TPU v7x, 32 devices: a whole 2x2x4 slice. The times are simulated.
32 devices in a mesh: expert: 4 (over y, x), context: 2 (over core), dp: 4 (over z).
Axes of the slice: x: 2, y: 2, z: 4, core: 2. Of those that a mesh axis runs over, the one named last changes fastest.
Arguments:
- hidden_in: bfloat16 [16, 1024, 1536], P(('expert', 'dp'), 'context'), may hold values from -6 to 6
- out_grad: bfloat16 [16, 1024, 1536], P(('expert', 'dp'), 'context'), may hold values from -6 to 6
- routes: int32 [16, 1024, 4], P(('expert', 'dp'), 'context'), may hold values from 0 to 15, all different within a row; in each aligned block of 512 rows (0 to 511, 512 to 1023, ..., all dimensions but the last counted through in order) at most 256 rows name the same one
- attn_gain: float32 [1536], P(('context', 'dp')), may hold values from 0.5 to 1.5
- w_query: float32 [1536, 1536], P(('context', 'dp')), may hold values from -0.15625 to 0.15625
- key_projection: float32 [1536, 256], P(('context', 'dp')), may hold values from -0.15625 to 0.15625
- value_projection: float32 [1536, 256], P(('context', 'dp')), may hold values from -0.15625 to 0.15625
- w_out: float32 [1536, 1536], P(('context', 'dp')), may hold values from -1.75 to 1.75
- ffn_gain: float32 [1536], P(('context', 'dp')), may hold values from 0.5 to 1.5
- w_router: float32 [1536, 16], P(('context', 'dp')), may hold values from -0.078125 to 0.078125
- w_gate: float32 [16, 1536, 768], P('expert', ('context', 'dp')), may hold values from -0.15625 to 0.15625
- w_up: float32 [16, 1536, 768], P('expert', ('context', 'dp')), may hold values from -0.15625 to 0.15625
- w_down: float32 [16, 768, 1536], P('expert', None, ('context', 'dp')), may hold values from -0.4375 to 0.4375
Outputs:
- block_out: bfloat16 [16, 1024, 1536], P(('expert', 'dp'), 'context')
- grad_in: float32 [16, 1024, 1536], P(('expert', 'dp'), 'context')
- grad_attn_gain: float32 [1536], P(('context', 'dp'))
- grad_query: float32 [1536, 1536], P(('context', 'dp'))
- grad_key: float32 [1536, 256], P(('context', 'dp'))
- grad_value: float32 [1536, 256], P(('context', 'dp'))
- grad_out: float32 [1536, 1536], P(('context', 'dp'))
- grad_ffn_gain: float32 [1536], P(('context', 'dp'))
- grad_router: float32 [1536, 16], P(('context', 'dp'))
- grad_gate: float32 [16, 1536, 768], P('expert', ('context', 'dp'))
- grad_up: float32 [16, 1536, 768], P('expert', ('context', 'dp'))
- grad_down: float32 [16, 768, 1536], P('expert', None, ('context', 'dp'))
Inputs may be any that keep to these rules, and one draw needn't show every extreme that they name: `routes`: each row names 4 different experts; among the 512 rows of one sequence block no expert is named by more than 256 rows, a bound that some block reaches.
All inputs are finite; a program needn't handle non-finite values.
Results may differ from a plain program's by a relative error of at most 0.022.
Values may be sent and summed in bfloat16 or wider, within the bound.
No kernel may reach another device: no remote copies, remote signals or barrier semaphores. Data moves between devices by JAX's collectives and lax.ppermute only.
A program may use at most 384 MiB of HBM per device.

v0:
```python
from functools import partial
import math

import jax
import jax.numpy as jnp
from jax import lax
from jax.sharding import PartitionSpec as P

MODEL_WIDTH = 1536
QUERY_HEADS = 12
KEY_VALUE_HEADS = 2
HEAD_SIZE = 128
TOP = 4
EXP_DEV = 4


norm_eps = 1e-06
rope_base = 1000000.0
mask_fill = -1e30


def passed_along(value, axis, steps):
    count = lax.axis_size(axis)
    leading, last = (max(0, -steps), min(count, count - steps))
    return lax.ppermute(value, axis, [(source, source + steps) for source in range(leading, last)])


def normalize(values, gain):
    return values * lax.rsqrt(jnp.mean(values * values, axis=-1, keepdims=True) + norm_eps) * gain


def rope_tables(start_pos, length, head_dim):
    half_dim = head_dim // 2
    freqs = rope_base ** (-(2.0 * jnp.arange(half_dim, dtype=jnp.float32)) / head_dim)
    places = (start_pos + jnp.arange(length, dtype=jnp.int32)).astype(jnp.float32)
    angles = places[:, None] * freqs[None, :]
    return (jnp.cos(angles), jnp.sin(angles))


def apply_rotary(heads, cosine_table, sine_values_table):
    half_dim = heads.shape[-1] // 2
    front_half = heads[..., :half_dim]
    back_half = heads[..., half_dim:]
    cos_wide = cosine_table[:, None, :]
    sin_wide = sine_values_table[:, None, :]
    return jnp.concatenate(
        [
            front_half * cos_wide - back_half * sin_wide,
            back_half * cos_wide + front_half * sin_wide,
        ],
        axis=-1,
    )


def gated(gate_v, up_v):
    return jax.nn.gelu(gate_v) * up_v


def local(
    hidden_in,
    out_grad,
    routes,
    attn_gain,
    w_query,
    key_projection,
    value_projection,
    w_out,
    ffn_gain,
    w_router,
    w_gate,
    w_up,
    w_down,
):
    dense = (
        lax.all_gather(attn_gain.astype(jnp.bfloat16), ("context", "dp"), axis=0, tiled=True),
        lax.all_gather(w_query.astype(jnp.bfloat16), ("context", "dp"), axis=0, tiled=True),
        lax.all_gather(key_projection.astype(jnp.bfloat16), ("context", "dp"), axis=0, tiled=True),
        lax.all_gather(
            value_projection.astype(jnp.bfloat16), ("context", "dp"), axis=0, tiled=True
        ),
        lax.all_gather(w_out.astype(jnp.bfloat16), ("context", "dp"), axis=0, tiled=True),
        lax.all_gather(ffn_gain.astype(jnp.bfloat16), ("context", "dp"), axis=0, tiled=True),
        lax.all_gather(w_router.astype(jnp.bfloat16), ("context", "dp"), axis=0, tiled=True),
    )
    gain_one = dense[0].astype(jnp.float32)
    query_w, key_weight_matrix, value_weight_matrix, out_w = (
        dense[1],
        dense[2],
        dense[3],
        dense[4],
    )
    gain_two = dense[5].astype(jnp.float32)
    router_w = dense[6]
    token_rows = hidden_in.shape[1]
    query_group_width = QUERY_HEADS // KEY_VALUE_HEADS
    expert_devs = lax.axis_size("expert")
    experts_all = EXP_DEV * expert_devs
    capacity = token_rows * TOP * 5 // (4 * experts_all)
    slot_count = experts_all * capacity
    context_idx = lax.axis_index("context")
    scale_factor = 1.0 / math.sqrt(HEAD_SIZE)
    zero_half = jnp.zeros((), jnp.bfloat16)
    inputs_f = hidden_in[0].astype(jnp.float32)
    cosine_table, sine_values_table = rope_tables(context_idx * token_rows, token_rows, HEAD_SIZE)

    def turn(heads):
        return apply_rotary(heads, cosine_table, sine_values_table)

    first_activation = normalize(inputs_f, gain_one).astype(jnp.bfloat16)
    query_flat = jnp.dot(first_activation, query_w, preferred_element_type=jnp.float32).reshape(
        token_rows, QUERY_HEADS, HEAD_SIZE
    )
    key_flat = jnp.dot(
        first_activation, key_weight_matrix, preferred_element_type=jnp.float32
    ).reshape(token_rows, KEY_VALUE_HEADS, HEAD_SIZE)
    query_blocks = turn(query_flat).astype(jnp.bfloat16)
    key_b = turn(key_flat).astype(jnp.bfloat16)
    value_blocks = (
        jnp.dot(first_activation, value_weight_matrix, preferred_element_type=jnp.float32)
        .astype(jnp.bfloat16)
        .reshape(token_rows, KEY_VALUE_HEADS, HEAD_SIZE)
    )
    remote_key, remote_value = passed_along((key_b, value_blocks), "context", 1)
    all_keys = jnp.concatenate([remote_key, key_b], axis=0)
    all_values = jnp.concatenate([remote_value, value_blocks], axis=0)
    query_pos = context_idx * token_rows + jnp.arange(token_rows, dtype=jnp.int32)
    key_pos = (context_idx - 1) * token_rows + jnp.arange(2 * token_rows, dtype=jnp.int32)
    allowed = (key_pos[None, :] <= query_pos[:, None]) & (key_pos[None, :] >= 0)
    grouped_query_rows = query_blocks.reshape(
        token_rows, KEY_VALUE_HEADS, query_group_width, HEAD_SIZE
    )

    def group_scores(key_value_head):
        raw_scores = jnp.einsum(
            "qrd,kd->rqk",
            grouped_query_rows[:, key_value_head],
            all_keys[:, key_value_head],
            preferred_element_type=jnp.float32,
        )
        return jnp.where(allowed[None], raw_scores * scale_factor, mask_fill)

    outputs = []
    log_totals = []
    for key_value_head in range(KEY_VALUE_HEADS):
        scores = group_scores(key_value_head)
        peak = jnp.max(scores, axis=-1, keepdims=True)
        exped = jnp.exp(scores - peak)
        totals = jnp.sum(exped, axis=-1, keepdims=True)
        probs = exped / totals
        log_totals.append(peak + jnp.log(totals))
        outputs.append(
            jnp.einsum(
                "rqk,kd->qrd",
                probs.astype(jnp.bfloat16),
                all_values[:, key_value_head],
                preferred_element_type=jnp.float32,
            )
        )
    mixed_b = (
        jnp.stack(outputs, axis=1).reshape(token_rows, QUERY_HEADS * HEAD_SIZE).astype(jnp.bfloat16)
    )
    resid_one = inputs_f + jnp.dot(mixed_b, out_w, preferred_element_type=jnp.float32)
    act_two = normalize(resid_one, gain_two).astype(jnp.bfloat16)
    logits = jnp.dot(act_two, router_w, preferred_element_type=jnp.float32)
    route_ids = routes[0]
    expert_ids = jnp.arange(experts_all, dtype=jnp.int32)
    picked_mask = route_ids[:, :, None] == expert_ids[None, None, :]
    chosen = jnp.sum(jnp.where(picked_mask, logits[:, None, :], 0.0), axis=-1)
    gates = jax.nn.softmax(chosen, axis=-1)
    flat_ids = route_ids.reshape(-1)
    onehot = (flat_ids[:, None] == expert_ids[None, :]).astype(jnp.int32)
    ranks = jnp.sum(jnp.cumsum(onehot, axis=0) * onehot, axis=1) - 1
    kept = ranks < capacity
    targets = jnp.where(kept, flat_ids * capacity + ranks, slot_count)
    slot_pair = (
        jnp.full((slot_count,), -1, jnp.int32)
        .at[targets]
        .set(jnp.arange(token_rows * TOP, dtype=jnp.int32), mode="drop")
    )
    slot_used = slot_pair >= 0
    slot_source = jnp.maximum(slot_pair, 0)
    pair_slot = jnp.where(kept, targets, 0).reshape(token_rows, TOP)
    pair_kept = kept.reshape(token_rows, TOP)
    outgoing = jnp.where(slot_used[:, None], act_two[slot_source // TOP], zero_half).reshape(
        expert_devs, EXP_DEV, capacity, MODEL_WIDTH
    )
    arrived = lax.all_to_all(outgoing, "expert", split_axis=0, concat_axis=2, tiled=True)[0]
    gate_w, up_w, down_w = (
        lax.all_gather(w_gate.astype(jnp.bfloat16), ("context", "dp"), axis=1, tiled=True),
        lax.all_gather(w_up.astype(jnp.bfloat16), ("context", "dp"), axis=1, tiled=True),
        lax.all_gather(w_down.astype(jnp.bfloat16), ("context", "dp"), axis=2, tiled=True),
    )
    gate_h = jnp.einsum("ecd,edf->ecf", arrived, gate_w, preferred_element_type=jnp.float32)
    up_h = jnp.einsum("ecd,edf->ecf", arrived, up_w, preferred_element_type=jnp.float32)
    hidden_b = gated(gate_h, up_h).astype(jnp.bfloat16)
    expert_res = jnp.einsum(
        "ecf,efd->ecd", hidden_b, down_w, preferred_element_type=jnp.float32
    ).astype(jnp.bfloat16)
    returned_all = lax.all_to_all(
        expert_res[None], "expert", split_axis=2, concat_axis=0, tiled=True
    ).reshape(slot_count, MODEL_WIDTH)
    returned = jnp.where(pair_kept[:, :, None], returned_all[pair_slot], zero_half).astype(
        jnp.float32
    )
    resid_two = resid_one + jnp.sum(gates[:, :, None] * returned, axis=1)
    block_out = resid_two.astype(jnp.bfloat16)[None]
    grad_y = out_grad[0].astype(jnp.float32)
    grad_gates = jnp.sum(grad_y[:, None, :] * returned, axis=-1)
    grad_pairs = (
        (gates[:, :, None] * grad_y[:, None, :])
        .astype(jnp.bfloat16)
        .reshape(token_rows * TOP, MODEL_WIDTH)
    )
    grad_send = jnp.where(slot_used[:, None], grad_pairs[slot_source], zero_half).reshape(
        expert_devs, EXP_DEV, capacity, MODEL_WIDTH
    )
    gate_w, up_w, down_w = (
        lax.all_gather(w_gate.astype(jnp.bfloat16), ("context", "dp"), axis=1, tiled=True),
        lax.all_gather(w_up.astype(jnp.bfloat16), ("context", "dp"), axis=1, tiled=True),
        lax.all_gather(w_down.astype(jnp.bfloat16), ("context", "dp"), axis=2, tiled=True),
    )
    grad_res = lax.all_to_all(grad_send, "expert", split_axis=0, concat_axis=2, tiled=True)[0]
    grad_hidden = jnp.einsum("ecd,efd->ecf", grad_res, down_w, preferred_element_type=jnp.float32)
    _, gated_back = jax.vjp(gated, gate_h, up_h)
    grad_gate_h, grad_up_h = gated_back(grad_hidden)
    grad_gate_b = grad_gate_h.astype(jnp.bfloat16)
    grad_up_b = grad_up_h.astype(jnp.bfloat16)
    grad_arrived = jnp.einsum(
        "ecf,edf->ecd", grad_gate_b, gate_w, preferred_element_type=jnp.float32
    ) + jnp.einsum("ecf,edf->ecd", grad_up_b, up_w, preferred_element_type=jnp.float32)
    grad_gate_w = jnp.einsum(
        "ecd,ecf->edf", arrived, grad_gate_b, preferred_element_type=jnp.float32
    )
    grad_up_w = jnp.einsum("ecd,ecf->edf", arrived, grad_up_b, preferred_element_type=jnp.float32)
    grad_down_w = jnp.einsum("ecf,ecd->efd", hidden_b, grad_res, preferred_element_type=jnp.float32)
    grad_back = lax.all_to_all(
        grad_arrived[None], "expert", split_axis=2, concat_axis=0, tiled=True
    ).reshape(slot_count, MODEL_WIDTH)
    grad_act_two = jnp.sum(jnp.where(pair_kept[:, :, None], grad_back[pair_slot], 0.0), axis=1)
    _, soft_back = jax.vjp(partial(jax.nn.softmax, axis=-1), chosen)
    grad_chosen = soft_back(grad_gates)[0]
    grad_logits = jnp.sum(jnp.where(picked_mask, grad_chosen[:, :, None], 0.0), axis=1).astype(
        jnp.bfloat16
    )
    grad_act_two = grad_act_two + jnp.einsum(
        "te,de->td", grad_logits, router_w, preferred_element_type=jnp.float32
    )
    grad_router_w = jnp.einsum(
        "td,te->de", act_two, grad_logits, preferred_element_type=jnp.float32
    )
    _, norm_back_two = jax.vjp(normalize, resid_one, gain_two)
    grad_resid_n, grad_gain_two = norm_back_two(grad_act_two)
    grad_resid = grad_y + grad_resid_n
    grad_resid_b = grad_resid.astype(jnp.bfloat16)
    grad_out_w = jnp.einsum("tk,td->kd", mixed_b, grad_resid_b, preferred_element_type=jnp.float32)
    mixed_gradient = jnp.einsum(
        "td,kd->tk", grad_resid_b, out_w, preferred_element_type=jnp.float32
    ).astype(jnp.bfloat16)
    mixed_gradient = mixed_gradient.reshape(
        token_rows, KEY_VALUE_HEADS, query_group_width, HEAD_SIZE
    )
    query_parts = []
    key_parts = []
    value_parts = []
    for key_value_head in range(KEY_VALUE_HEADS):
        scores = group_scores(key_value_head)
        probs = jnp.exp(scores - log_totals[key_value_head])
        grad_head = mixed_gradient[:, key_value_head]
        grad_probs = jnp.einsum(
            "qrd,kd->rqk",
            grad_head,
            all_values[:, key_value_head],
            preferred_element_type=jnp.float32,
        )
        inner = jnp.sum(probs * grad_probs, axis=-1, keepdims=True)
        grad_scores = (probs * (grad_probs - inner)).astype(jnp.bfloat16)
        query_parts.append(
            jnp.einsum(
                "rqk,kd->qrd",
                grad_scores,
                all_keys[:, key_value_head],
                preferred_element_type=jnp.float32,
            )
            * scale_factor
        )
        key_parts.append(
            jnp.einsum(
                "rqk,qrd->kd",
                grad_scores,
                grouped_query_rows[:, key_value_head],
                preferred_element_type=jnp.float32,
            )
            * scale_factor
        )
        value_parts.append(
            jnp.einsum(
                "rqk,qrd->kd",
                probs.astype(jnp.bfloat16),
                grad_head,
                preferred_element_type=jnp.float32,
            )
        )
    grad_query_r = jnp.stack(query_parts, axis=1).reshape(token_rows, QUERY_HEADS, HEAD_SIZE)
    grad_key_all = jnp.stack(key_parts, axis=1)
    value_gradient_total = jnp.stack(value_parts, axis=1)
    sent_key, value_outgoing_rows = (
        passed_along(grad_key_all[:token_rows].astype(jnp.bfloat16), "context", -1).astype(
            jnp.float32
        ),
        passed_along(value_gradient_total[:token_rows].astype(jnp.bfloat16), "context", -1).astype(
            jnp.float32
        ),
    )
    key_gradient_rotated = grad_key_all[token_rows:] + sent_key
    grad_value_b = (
        (value_gradient_total[token_rows:] + value_outgoing_rows)
        .astype(jnp.bfloat16)
        .reshape(token_rows, KEY_VALUE_HEADS * HEAD_SIZE)
    )
    _, turn_query = jax.vjp(turn, query_flat)
    _, rotate_key_rows = jax.vjp(turn, key_flat)
    grad_query_b = (
        turn_query(grad_query_r)[0]
        .astype(jnp.bfloat16)
        .reshape(token_rows, QUERY_HEADS * HEAD_SIZE)
    )
    key_gradient_blocks = (
        rotate_key_rows(key_gradient_rotated)[0]
        .astype(jnp.bfloat16)
        .reshape(token_rows, KEY_VALUE_HEADS * HEAD_SIZE)
    )
    grad_act_one = jnp.einsum(
        "tk,dk->td", grad_query_b, query_w, preferred_element_type=jnp.float32
    )
    grad_act_one = grad_act_one + jnp.einsum(
        "tk,dk->td", key_gradient_blocks, key_weight_matrix, preferred_element_type=jnp.float32
    )
    grad_act_one = grad_act_one + jnp.einsum(
        "tk,dk->td", grad_value_b, value_weight_matrix, preferred_element_type=jnp.float32
    )
    grad_query_w = jnp.einsum(
        "td,tk->dk", first_activation, grad_query_b, preferred_element_type=jnp.float32
    )
    grad_key_w = jnp.einsum(
        "td,tk->dk", first_activation, key_gradient_blocks, preferred_element_type=jnp.float32
    )
    grad_value_w = jnp.einsum(
        "td,tk->dk", first_activation, grad_value_b, preferred_element_type=jnp.float32
    )
    _, norm_back_one = jax.vjp(normalize, inputs_f, gain_one)
    grad_inputs_n, grad_gain_one = norm_back_one(grad_act_one)
    grad_in = (grad_resid + grad_inputs_n)[None]
    dense_terms = (
        grad_gain_one,
        grad_query_w,
        grad_key_w,
        grad_value_w,
        grad_out_w,
        grad_gain_two,
        grad_router_w,
    )
    shares = (
        lax.psum_scatter(
            dense_terms[0].astype(jnp.bfloat16), ("context", "dp"), scatter_dimension=0, tiled=True
        ).astype(jnp.float32),
        lax.psum_scatter(
            dense_terms[1].astype(jnp.bfloat16), ("context", "dp"), scatter_dimension=0, tiled=True
        ).astype(jnp.float32),
        lax.psum_scatter(
            dense_terms[2].astype(jnp.bfloat16), ("context", "dp"), scatter_dimension=0, tiled=True
        ).astype(jnp.float32),
        lax.psum_scatter(
            dense_terms[3].astype(jnp.bfloat16), ("context", "dp"), scatter_dimension=0, tiled=True
        ).astype(jnp.float32),
        lax.psum_scatter(
            dense_terms[4].astype(jnp.bfloat16), ("context", "dp"), scatter_dimension=0, tiled=True
        ).astype(jnp.float32),
        lax.psum_scatter(
            dense_terms[5].astype(jnp.bfloat16), ("context", "dp"), scatter_dimension=0, tiled=True
        ).astype(jnp.float32),
        lax.psum_scatter(
            dense_terms[6].astype(jnp.bfloat16), ("context", "dp"), scatter_dimension=0, tiled=True
        ).astype(jnp.float32),
    )
    totals_all = (
        lax.psum(shares[0].astype(jnp.bfloat16), "expert").astype(jnp.float32),
        lax.psum(shares[1].astype(jnp.bfloat16), "expert").astype(jnp.float32),
        lax.psum(shares[2].astype(jnp.bfloat16), "expert").astype(jnp.float32),
        lax.psum(shares[3].astype(jnp.bfloat16), "expert").astype(jnp.float32),
        lax.psum(shares[4].astype(jnp.bfloat16), "expert").astype(jnp.float32),
        lax.psum(shares[5].astype(jnp.bfloat16), "expert").astype(jnp.float32),
        lax.psum(shares[6].astype(jnp.bfloat16), "expert").astype(jnp.float32),
    )
    expert_shares = (
        lax.psum_scatter(
            grad_gate_w.astype(jnp.bfloat16), ("context", "dp"), scatter_dimension=1, tiled=True
        ).astype(jnp.float32),
        lax.psum_scatter(
            grad_up_w.astype(jnp.bfloat16), ("context", "dp"), scatter_dimension=1, tiled=True
        ).astype(jnp.float32),
        lax.psum_scatter(
            grad_down_w.astype(jnp.bfloat16), ("context", "dp"), scatter_dimension=2, tiled=True
        ).astype(jnp.float32),
    )
    return (
        block_out,
        grad_in,
        totals_all[0],
        totals_all[1],
        totals_all[2],
        totals_all[3],
        totals_all[4],
        totals_all[5],
        totals_all[6],
        expert_shares[0],
        expert_shares[1],
        expert_shares[2],
    )


def solution(mesh):
    placed = (
        P(("expert", "dp"), "context", None),
        P(("expert", "dp"), "context", None),
        P(("expert", "dp"), "context", None),
        P(("context", "dp")),
        P(("context", "dp"), None),
        P(("context", "dp"), None),
        P(("context", "dp"), None),
        P(("context", "dp"), None),
        P(("context", "dp")),
        P(("context", "dp"), None),
        P("expert", ("context", "dp"), None),
        P("expert", ("context", "dp"), None),
        P("expert", None, ("context", "dp")),
    )
    return jax.shard_map(
        local,
        mesh=mesh,
        in_specs=placed,
        out_specs=(
            P(("expert", "dp"), "context", None),
            P(("expert", "dp"), "context", None),
            P(("context", "dp")),
            P(("context", "dp"), None),
            P(("context", "dp"), None),
            P(("context", "dp"), None),
            P(("context", "dp"), None),
            P(("context", "dp")),
            P(("context", "dp"), None),
            P("expert", ("context", "dp"), None),
            P("expert", ("context", "dp"), None),
            P("expert", None, ("context", "dp")),
        ),
        check_vma=False,
    )
```

profile of v0, /device:TPU:0, one launch (start us, length us, event | category | flops | bytes accessed | tf_op | source)
XLA Modules:
  0.0 1898.5 jit_solution(16870958856285610800)
XLA Ops:
  17.9 20.8 %all-reduce.9 = (bf16[1536]{0:T(1024)(128)(2,1)S(1)}, bf16[1536]{0:T(1024)(128)(2,1)}) all-reduce(bf16[1536]{0:T(1024)(128)(2,1)S(1)} %dynamic-update-slice, bf16[1536]{0:T(1024)(128)(2,1)S(1)} %dynamic-update-slice.1), channel_id=1, replica_groups=mesh['expert'=4,'context'=2,'dp'=4] {'context','dp'}, use_global_device_ids=true, to_apply=%add.4 | all-reduce | flops 3072 | bytes 12288
  39.1 34.3 %all_gather.34 = bf16[1536,256]{1,0:T(8,128)(2,1)S(1)} all-gather(bf16[192,256]{1,0:T(8,128)(2,1)S(1)} %convert_element_type.244), channel_id=1, replica_groups=mesh['expert'=4,'context'=2,'dp'=4] {'context','dp'}, dimensions={0}, use_global_device_ids=true | all-gather | bytes 884736 | tf_op jit(solution)/shard_map/all_gather | solution.py:78
  78.8 31.3 %all_gather.35 = bf16[1536,256]{1,0:T(8,128)(2,1)S(1)} all-gather(bf16[192,256]{1,0:T(8,128)(2,1)S(1)} %convert_element_type.249), channel_id=1, replica_groups=mesh['expert'=4,'context'=2,'dp'=4] {'context','dp'}, dimensions={0}, use_global_device_ids=true | all-gather | bytes 884736 | tf_op jit(solution)/shard_map/all_gather | solution.py:77
  123.0 8.1 scatter_custom_fusion
  137.0 25.0 %all-gather = bf16[8,192,16]{1,2,0:T(8,128)(2,1)S(1)} all-gather(bf16[1,192,16]{1,2,0:T(8,128)(2,1)S(1)} %convert_bitcast_fusion.2), channel_id=1, replica_groups=mesh['expert'=4,'context'=2,'dp'=4] {'context','dp'}, dimensions={0}, use_global_device_ids=true | all-gather | bytes 55296 | tf_op jit(solution)/shard_map/all_gather | solution.py:83
  165.6 6.0 mul.508
  171.6 15.0 mul.509
  190.7 6.8 copy.170
  197.5 4.7 fusion.46
  208.4 6.0 fusion.116
  218.7 8.9 fusion.8
  231.5 7.3 fusion.57
  239.0 5.5 multiply_reduce_fusion.2
  248.6 8.0 multiply_convert_fusion
  256.7 9.5 gather_fusion
  266.2 20.1 %gather_fusion.2 = bf16[2560,1536]{1,0:T(8,128)(2,1)} fusion(bf16[2048,1536]{1,0:T(8,128)(2,1)} %multiply_convert_fusion, s32[3072]{0:T(1024)S(1)} %copy-done.68), kind=kCustom, calls=%fused_computation.2 | custom fusion | bytes 15738880 | tf_op jit(solution)/shard_map/gather | solution.py:214
  286.3 9.0 broadcast_select_fusion
  295.3 91.5 %all_to_all.60 = bf16[4,4,160,1536]{3,2,1,0:T(8,128)(2,1)} all-to-all(bf16[4,4,160,1536]{3,2,1,0:T(8,128)(2,1)S(1)} %get-tuple-element.45), channel_id=1, replica_groups=mesh['expert'=4,'context'=2,'dp'=4] {'expert'}, dimensions={0} | all-to-all | bytes 15728640 | tf_op jit(solution)/shard_map/all_to_all | solution.py:222
  386.8 6.0 all-to-all-start
  392.8 7.0 copy.186
  399.9 79.0 %all-to-all-done = bf16[4,4,160,1536]{3,2,1,0:T(8,128)(2,1)} async-done(((bf16[4,4,160,1536]{3,2,1,0:T(8,128)(2,1)}), bf16[4,4,160,1536]{3,2,1,0:T(8,128)(2,1)}, u32[]{:S(2)}, u32[]{:S(2)}) %all-to-all-start) | async-done | bytes 7864352 | tf_op jit(solution)/shard_map/all_to_all | solution.py:187
  478.9 7.0 copy.182
  485.9 13.2 fusion.119
  499.1 13.2 fusion.118
  512.3 22.7 %multiply_convert_fusion.1 = (bf16[4,640,768]{2,1,0:T(8,128)(2,1)}, bf16[4,640,768]{2,1,0:T(8,128)(2,1)}, bf16[4,640,768]{2,1,0:T(8,128)(2,1)}) fusion(f32[4,640,768]{2,1,0:T(8,128)} %fusion.118, f32[4,640,768]{2,1,0:T(8,128)} %fusion.119, bf16[4,640,1536]{2,1,0:T(8,128)(2,1)} %bitcast.306, bf16[4,768,1536]{1,2,0:T(8,128)(2,1)} %all-gather.15.cloned.1.call-done), kind=kOutput, calls=%fused_computation.43 | convolution fusion | flops 6090915840 | bytes 44826624 | tf_op jit(solution)/shard_map/ecd,efd->ecf/dot_general | solution.py:223
  535.0 12.2 convert_bitcast_fusion
  547.2 12.3 copy.183
  559.6 5.7 all-to-all-start.1
  565.3 13.3 fusion.120
  578.6 15.8 add_bitcast_fusion
  594.4 23.3 %copy.187 = f32[1,4,640,1536]{3,1,0,2:T(4,128)} copy(f32[1,4,640,1536]{3,2,1,0:T(8,128)} %add_bitcast_fusion) | data formatting | bytes 31457280 | tf_op jit(solution)/shard_map/broadcast_in_dim | solution.py:237
  617.7 33.8 %all-to-all-done.1 = bf16[1,4,640,1536]{3,1,0,2:T(4,128)(2,1)} async-done(((bf16[1,4,640,1536]{3,1,0,2:T(4,128)(2,1)}), bf16[1,4,640,1536]{3,1,0,2:T(4,128)(2,1)}, u32[]{:S(2)}, u32[]{:S(2)}) %all-to-all-start.1) | async-done | bytes 7864352 | tf_op jit(solution)/shard_map/all_to_all | solution.py:199
  651.5 6.8 all-to-all-start.3
  659.3 8.0 copy.184
  667.4 17.9 gather_fusion.1
  685.3 11.2 reshape.558
  696.5 132.4 %all-to-all-done.3 = f32[1,4,640,1536]{3,1,0,2:T(4,128)} async-done(((f32[1,4,640,1536]{3,1,0,2:T(4,128)}), f32[1,4,640,1536]{3,1,0,2:T(4,128)}, u32[]{:S(2)}, u32[]{:S(2)}) %all-to-all-start.3) | async-done | bytes 15728672 | tf_op jit(solution)/shard_map/all_to_all | solution.py:236
  828.8 15.8 copy.188
  844.7 19.7 %gather_fusion.3 = f32[2048,1536]{1,0:T(8,128)} fusion(f32[2560,1536]{1,0:T(8,128)} %bitcast.286, s32[2048]{0:T(1024)S(1)} %broadcast_clamp_fusion), kind=kCustom, calls=%fused_computation.3 | custom fusion | bytes 25174016 | tf_op jit(solution)/shard_map/gather | solution.py:239
  864.3 14.7 reshape.574
  879.1 29.3 %fusion.1 = (f32[512,4]{1,0:T(8,128)S(1)}, f32[512,1536]{1,0:T(8,128)}, f32[512,1536]{1,0:T(8,128)}) fusion(f32[512,1536]{1,0:T(8,128)} %copy-done.3, bf16[512,4,1536]{2,1,0:T(4,128)(2,1)} %reshape.558, pred[512,4]{1,0:T(8,128)(4,1)S(1)} %lt.59, f32[512,4]{1,0:T(8,128)S(1)} %copy-done.34, f32[512,4,1536]{2,1,0:T(4,128)} %reshape.574), kind=kLoop, calls=%fused_computation.9 | loop fusion | flops 23590912 | bytes 28329984 | tf_op jit(solution)/shard_map/reduce_sum | solution.py:208
  922.5 7.0 fusion.62
  929.4 7.0 fusion.59
  938.5 7.0 fusion.5
  945.6 10.0 fusion.7
  955.6 7.0 fusion.2
  962.6 10.2 fusion.4
  980.0 5.0 fusion.68
  991.2 7.2 convolution_convert_fusion
  1009.4 4.6 convolution_convert_fusion.1
  1014.2 13.2 convolution_convert_fusion.2
  1027.5 13.3 convolution_convert_fusion.3
  1041.1 13.3 convolution_convert_fusion.4
  1055.1 7.4 fusion.121
  1067.7 82.8 %reduce-scatter.17.cloned.1.call-done = bf16[192,1536]{1,0:T(8,128)(2,1)} async-done(((bf16[1536,1536]{1,0:T(8,128)(2,1)}), bf16[192,1536]{1,0:T(8,128)(2,1)}) %reduce-scatter.17.cloned.1.call-update) | async-done | bytes 589840 | tf_op jit(solution)/shard_map/reduce_scatter | solution.py:375
  1150.5 101.0 %reduce-scatter.11.cloned.1.call-done = bf16[192,1536]{1,0:T(8,128)(2,1)} async-done(((bf16[1536,1536]{1,0:T(8,128)(2,1)}), bf16[192,1536]{1,0:T(8,128)(2,1)}) %reduce-scatter.11.cloned.1.call-update) | async-done | bytes 589840 | tf_op jit(solution)/shard_map/reduce_scatter | solution.py:366
  1251.6 4.8 fusion.35
  1256.4 18.0 all-reduce.8
  1274.6 10.1 all-reduce.10
  1286.4 5.3 fusion.42
  1291.7 149.8 %reduce-scatter.23.cloned.1.call-done = bf16[4,768,192]{1,2,0:T(8,128)(2,1)} async-done(((bf16[4,768,1536]{1,2,0:T(8,128)(2,1)}), bf16[4,768,192]{1,2,0:T(8,128)(2,1)}) %reduce-scatter.23.cloned.1.call-update) | async-done | bytes 1179664 | tf_op jit(solution)/shard_map/reduce_scatter | solution.py:401
  1444.3 186.6 %reduce-scatter.21.cloned.1.call-done = bf16[4,192,768]{2,1,0:T(8,128)(2,1)} async-done(((bf16[4,1536,768]{2,1,0:T(8,128)(2,1)}), bf16[4,192,768]{2,1,0:T(8,128)(2,1)}) %reduce-scatter.21.cloned.1.call-update) | async-done | bytes 1179664 | tf_op jit(solution)/shard_map/reduce_scatter | solution.py:398
  1633.8 187.1 %reduce-scatter.19.cloned.1.call-done = bf16[4,192,768]{2,1,0:T(8,128)(2,1)} async-done(((bf16[4,1536,768]{2,1,0:T(8,128)(2,1)}), bf16[4,192,768]{2,1,0:T(8,128)(2,1)}) %reduce-scatter.19.cloned.1.call-update) | async-done | bytes 1179664 | tf_op jit(solution)/shard_map/reduce_scatter | solution.py:395
  1823.8 60.4 %all-reduce.14.cloned.1.call-done = (bf16[192,1536]{1,0:T(8,128)(2,1)}, bf16[192,256]{1,0:T(8,128)(2,1)}, bf16[192,256]{1,0:T(8,128)(2,1)}, bf16[192,1536]{1,0:T(8,128)(2,1)}) async-done(((bf16[192,1536]{1,0:T(8,128)(2,1)}, bf16[192,256]{1,0:T(8,128)(2,1)}, bf16[192,256]{1,0:T(8,128)(2,1)}, bf16[192,1536]{1,0:T(8,128)(2,1)}), (bf16[192,1536]{1,0:T(8,128)(2,1)}, bf16[192,256]{1,0:T(8,128)(2,1)}, ...) | async-done | bytes 1376272 | tf_op jit(solution)/shard_map/psum | solution.py:387
  (364 shorter events, 125.3 us)
Async XLA Ops:
  7.2 183.5 %all-gather.7.cloned.1.call-start = ((), (), s32[]{:S(2)}) async-start(), calls=%async_computation.12 | async-start | bytes 5308416 | tf_op jit(solution)/shard_map/all_gather | solution.py:76
  9.6 229.5 %all-gather.9.cloned.1.call-start = ((), (), s32[]{:S(2)}) async-start(), calls=%async_computation.13 | async-start | bytes 5308416 | tf_op jit(solution)/shard_map/all_gather | solution.py:81
  11.8 26.8 %copy-start.45 = (f32[192,256]{1,0:T(8,128)S(1)}, f32[192,256]{1,0:T(8,128)}, u32[]{:S(2)}) copy-start(f32[192,256]{1,0:T(8,128)} %param.19) | copy-start | bytes 589828
  11.8 474.1 %all-gather.13.cloned.1.call-start = ((), (), s32[]{:S(2)}) async-start(), calls=%async_computation.15 | async-start | bytes 10616832 | tf_op jit(solution)/shard_map/all_gather | solution.py:190
  13.0 25.6 %copy-start.10 = (bf16[1,512,1536]{2,1,0:T(8,128)(2,1)S(1)}, bf16[1,512,1536]{2,1,0:T(8,128)(2,1)}, u32[]{:S(2)}) copy-start(bf16[1,512,1536]{2,1,0:T(8,128)(2,1)} %param.13) | copy-start | bytes 4718596
  13.0 486.1 %all-gather.11.cloned.1.call-start = ((), (), s32[]{:S(2)}) async-start(), calls=%async_computation.14 | async-start | bytes 10616832 | tf_op jit(solution)/shard_map/all_gather | solution.py:189
  16.0 62.7 %copy-start.46 = (f32[192,256]{1,0:T(8,128)S(1)}, f32[192,256]{1,0:T(8,128)}, u32[]{:S(2)}) copy-start(f32[192,256]{1,0:T(8,128)} %param.18) | copy-start | bytes 589828
  16.0 496.3 %all-gather.15.cloned.1.call-start = ((), (), s32[]{:S(2)}) async-start(), calls=%async_computation.16 | async-start | bytes 10616832 | tf_op jit(solution)/shard_map/all_gather | solution.py:191
  38.6 72.3 %copy-start.59 = (f32[1536]{0:T(1024)}, f32[1536]{0:T(1024)S(1)}, u32[]{:S(2)}) copy-start(f32[1536]{0:T(1024)S(1)} %convert_element_type.242) | copy-start | bytes 18436
  39.0 39.7 %copy-start.79 = (f32[512]{0:T(512)}, f32[512]{0:T(512)S(1)}, u32[]{:S(2)}) copy-start(f32[512]{0:T(512)S(1)} %fusion.36) | copy-start | bytes 6148
  39.1 71.9 %copy-start.76 = (f32[512]{0:T(512)}, f32[512]{0:T(512)S(1)}, u32[]{:S(2)}) copy-start(f32[512]{0:T(512)S(1)} %fusion.99) | copy-start | bytes 6148
  75.7 151.8 %collective-permute-start = (bf16[512,2,128]{0,2,1:T(8,128)(2,1)}, bf16[512,2,128]{0,2,1:T(8,128)(2,1)}, u32[]{:S(2)}, u32[]{:S(2)}) collective-permute-start(bf16[512,2,128]{0,2,1:T(8,128)(2,1)} %bitcast.2), channel_id=1, source_target_pairs={{0,4},{1,5},{2,6},{3,7},{8,12},{9,13},{10,14},{11,15},{16,20},{17,... | collective-permute-start | bytes 786440 | tf_op jit(solution)/shard_map/ppermute | solution.py:25
  110.9 91.3 %copy-start.27 = (f32[512,64]{0,1:T(8,128)}, f32[512,64]{0,1:T(8,128)S(1)}, u32[]{:S(2)}) copy-start(f32[512,64]{0,1:T(8,128)S(1)} %get-tuple-element.47) | copy-start | bytes 393220
  110.9 91.3 %copy-start.29 = (f32[512,64]{0,1:T(8,128)}, f32[512,64]{0,1:T(8,128)S(1)}, u32[]{:S(2)}) copy-start(f32[512,64]{0,1:T(8,128)S(1)} %get-tuple-element.48) | copy-start | bytes 393220
  111.7 11.2 copy-start.39
  111.7 21.1 %copy-start.82 = (f32[192,16]{0,1:T(8,128)S(1)}, f32[192,16]{0,1:T(8,128)}, u32[]{:S(2)}) copy-start(f32[192,16]{0,1:T(8,128)} %param.22) | copy-start | bytes 36868
  112.5 76.3 %collective-permute-start.1 = (bf16[512,2,128]{0,2,1:T(8,128)(2,1)}, bf16[512,2,128]{0,2,1:T(8,128)(2,1)}, u32[]{:S(2)}, u32[]{:S(2)}) collective-permute-start(bf16[512,2,128]{0,2,1:T(8,128)(2,1)} %pad_maximum_fusion.6), channel_id=1, source_target_pairs={{0,4},{1,5},{2,6},{3,7},{8,12},{9,13},{10,14},{11,15},{16,20},{17,... | collective-permute-start | bytes 786440 | tf_op jit(solution)/shard_map/ppermute | solution.py:25
  117.0 15.9 copy-start.20
  134.7 36.9 %copy-start.3 = (f32[512,1536]{1,0:T(8,128)}, f32[512,1536]{1,0:T(8,128)S(1)}, u32[]{:S(2)}) copy-start(f32[512,1536]{1,0:T(8,128)S(1)} %bitcast_convert_fusion) | copy-start | bytes 9437188
  137.0 107.6 %copy-start.51 = (f32[1536]{0:T(1024)}, f32[1536]{0:T(1024)S(1)}, u32[]{:S(2)}) copy-start(f32[1536]{0:T(1024)S(1)} %convert_element_type.257) | copy-start | bytes 18436
  214.4 17.0 copy-start.47
  216.9 10.7 copy-start.2
  216.9 10.7 copy-start.49
  244.6 12.1 copy-start.83
  266.2 20.1 %copy-start.81 = (pred[4,4,160]{2,1,0:T(4,128)(4,1)S(1)}, pred[4,4,160]{2,1,0:T(4,128)(4,1)}, u32[]{:S(2)}) copy-start(pred[4,4,160]{2,1,0:T(4,128)(4,1)} %broadcast_in_dim.181) | copy-start | bytes 7684
  386.8 92.1 %all-to-all-start = ((bf16[4,4,160,1536]{3,2,1,0:T(8,128)(2,1)}), bf16[4,4,160,1536]{3,2,1,0:T(8,128)(2,1)}, u32[]{:S(2)}, u32[]{:S(2)}) async-start(bf16[4,4,160,1536]{3,2,1,0:T(8,128)(2,1)} %get-tuple-element.46), calls=%async_computation | async-start | bytes 15728640 | tf_op jit(solution)/shard_map/all_to_all | solution.py:187
  559.6 91.9 %all-to-all-start.1 = ((bf16[1,4,640,1536]{3,1,0,2:T(4,128)(2,1)}), bf16[1,4,640,1536]{3,1,0,2:T(4,128)(2,1)}, u32[]{:S(2)}, u32[]{:S(2)}) async-start(bf16[1,4,640,1536]{3,1,0,2:T(4,128)(2,1)} %copy.183), calls=%async_computation.1 | async-start | bytes 15728640 | tf_op jit(solution)/shard_map/all_to_all | solution.py:199
  617.7 40.7 %copy-start.54 = (s32[2048]{0:T(1024)S(1)}, s32[2048]{0:T(1024)}, u32[]{:S(2)}) copy-start(s32[2048]{0:T(1024)} %copy-done.53) | copy-start | bytes 24580
  617.7 41.0 %copy-start.56 = (s32[2048]{0:T(1024)S(1)}, s32[2048]{0:T(1024)}, u32[]{:S(2)}) copy-start(s32[2048]{0:T(1024)} %copy-done.55) | copy-start | bytes 24580
  617.7 41.3 %copy-start.21 = (s32[1,512,4]{2,1,0:T(8,128)S(1)}, s32[1,512,4]{2,1,0:T(8,128)}, u32[]{:S(2)}) copy-start(s32[1,512,4]{2,1,0:T(8,128)} %copy-done.20) | copy-start | bytes 24580
  617.7 41.6 %copy-start.75 = (f32[512]{0:T(512)S(1)}, f32[512]{0:T(512)}, u32[]{:S(2)}) copy-start(f32[512]{0:T(512)} %copy-done.74) | copy-start | bytes 6148
  617.7 41.6 %copy-start.50 = (f32[6,512]{1,0:T(8,128)S(1)}, f32[6,512]{1,0:T(8,128)}, u32[]{:S(2)}) copy-start(f32[6,512]{1,0:T(8,128)} %copy-done.49) | copy-start | bytes 36868
  617.7 41.6 %copy-start.65 = (f32[6,512]{1,0:T(8,128)S(1)}, f32[6,512]{1,0:T(8,128)}, u32[]{:S(2)}) copy-start(f32[6,512]{1,0:T(8,128)} %copy-done.64) | copy-start | bytes 36868
  617.7 41.6 %copy-start.48 = (f32[6,512]{1,0:T(8,128)S(1)}, f32[6,512]{1,0:T(8,128)}, u32[]{:S(2)}) copy-start(f32[6,512]{1,0:T(8,128)} %copy-done.47) | copy-start | bytes 36868
  617.7 41.6 %copy-start.63 = (f32[6,512]{1,0:T(8,128)S(1)}, f32[6,512]{1,0:T(8,128)}, u32[]{:S(2)}) copy-start(f32[6,512]{1,0:T(8,128)} %copy-done.62) | copy-start | bytes 36868
  651.5 177.3 %all-to-all-start.3 = ((f32[1,4,640,1536]{3,1,0,2:T(4,128)}), f32[1,4,640,1536]{3,1,0,2:T(4,128)}, u32[]{:S(2)}, u32[]{:S(2)}) async-start(f32[1,4,640,1536]{3,1,0,2:T(4,128)} %copy.187), calls=%async_computation.3 | async-start | bytes 31457280 | tf_op jit(solution)/shard_map/all_to_all | solution.py:236
  658.3 404.2 %reduce-scatter.25.cloned.1.call-start = ((), (), s32[]{:S(2)}) async-start(), calls=%async_computation.24 | async-start | bytes 442368
  864.3 14.7 copy-start.34
  879.1 29.5 %copy-start.44 = (f32[512,4]{0,1:T(4,128)S(1)}, f32[512,4]{0,1:T(4,128)}, u32[]{:S(2)}) copy-start(f32[512,4]{0,1:T(4,128)} %copy-done.43) | copy-start | bytes 24580
  879.1 29.5 %copy-start.67 = (f32[512]{0:T(512)S(1)}, f32[512]{0:T(512)}, u32[]{:S(2)}) copy-start(f32[512]{0:T(512)} %copy-done.66) | copy-start | bytes 6148
  879.1 29.5 %copy-start.58 = (s32[1,512,4]{1,2,0:T(4,128)S(1)}, s32[1,512,4]{1,2,0:T(4,128)}, u32[]{:S(2)}) copy-start(s32[1,512,4]{1,2,0:T(4,128)} %param.15) | copy-start | bytes 24580
  879.1 29.6 %copy-start.1 = (bf16[512,1536]{1,0:T(8,128)(2,1)S(1)}, bf16[512,1536]{1,0:T(8,128)(2,1)}, u32[]{:S(2)}) copy-start(bf16[512,1536]{1,0:T(8,128)(2,1)} %copy-done) | copy-start | bytes 4718596
  879.1 29.9 %copy-start.42 = (bf16[1536,16]{0,1:T(8,128)(2,1)S(1)}, bf16[1536,16]{0,1:T(8,128)(2,1)}, u32[]{:S(2)}) copy-start(bf16[1536,16]{0,1:T(8,128)(2,1)} %reshape.600) | copy-start | bytes 147460
  879.1 29.9 %copy-start.52 = (f32[1536]{0:T(1024)S(1)}, f32[1536]{0:T(1024)}, u32[]{:S(2)}) copy-start(f32[1536]{0:T(1024)} %copy-done.51) | copy-start | bytes 18436
  879.1 29.9 %copy-start.73 = (f32[512]{0:T(512)S(1)}, f32[512]{0:T(512)}, u32[]{:S(2)}) copy-start(f32[512]{0:T(512)} %copy-done.72) | copy-start | bytes 6148
  922.2 145.5 %reduce-scatter.15.cloned.1.call-start = ((), (), s32[]{:S(2)}) async-start(), calls=%async_computation.19 | async-start | bytes 884736 | tf_op jit(solution)/shard_map/reduce_scatter | solution.py:372
  922.4 16.0 slice-start.3
  922.5 16.0 slice-start.4
  937.2 38.8 %collective-permute-start.3 = (bf16[512,2,128]{0,2,1:T(8,128)(2,1)}, bf16[512,2,128]{0,2,1:T(8,128)(2,1)}, u32[]{:S(2)}, u32[]{:S(2)}) collective-permute-start(bf16[512,2,128]{0,2,1:T(8,128)(2,1)} %fusion.84), channel_id=1, source_target_pairs={{4,0},{5,1},{6,2},{7,3},{12,8},{13,9},{14,10},{15,11},{20,16},{21,... | collective-permute-start | bytes 786440 | tf_op jit(solution)/shard_map/ppermute | solution.py:25
  938.5 17.0 slice-start
  938.5 17.0 slice-start.1
  955.6 17.3 slice-start.6
  962.6 10.2 copy-start.7
  962.6 10.2 copy-start.9
  979.5 88.1 %reduce-scatter.13.cloned.1.call-start = ((), (), s32[]{:S(2)}) async-start(), calls=%async_computation.18 | async-start | bytes 884736 | tf_op jit(solution)/shard_map/reduce_scatter | solution.py:369
  985.0 4.2 collective-permute-start.2
  991.1 159.4 %reduce-scatter.17.cloned.1.call-start = ((), (), s32[]{:S(2)}) async-start(), calls=%async_computation.20 | async-start | bytes 5308416 | tf_op jit(solution)/shard_map/reduce_scatter | solution.py:375
  998.4 253.1 %reduce-scatter.11.cloned.1.call-start = ((), (), s32[]{:S(2)}) async-start(), calls=%async_computation.17 | async-start | bytes 5308416 | tf_op jit(solution)/shard_map/reduce_scatter | solution.py:366
  1014.0 427.5 %reduce-scatter.23.cloned.1.call-start = ((), (), s32[]{:S(2)}) async-start(), calls=%async_computation.23 | async-start | bytes 10616832 | tf_op jit(solution)/shard_map/reduce_scatter | solution.py:401
  1027.4 603.5 %reduce-scatter.21.cloned.1.call-start = ((), (), s32[]{:S(2)}) async-start(), calls=%async_computation.22 | async-start | bytes 10616832 | tf_op jit(solution)/shard_map/reduce_scatter | solution.py:398
  1040.8 780.1 %reduce-scatter.19.cloned.1.call-start = ((), (), s32[]{:S(2)}) async-start(), calls=%async_computation.21 | async-start | bytes 10616832 | tf_op jit(solution)/shard_map/reduce_scatter | solution.py:395
  1054.4 829.8 %all-reduce.14.cloned.1.call-start = ((), (), s32[]{:S(2)}) async-start(), calls=%async_computation.25 | async-start | bytes 2752512 | tf_op jit(solution)/shard_map/psum | solution.py:387
  1063.4 188.2 %copy-start.32 = (bf16[1536,256]{1,0:T(8,128)(2,1)S(1)}, bf16[1536,256]{1,0:T(8,128)(2,1)}, u32[]{:S(2)}) copy-start(bf16[1536,256]{1,0:T(8,128)(2,1)} %copy-done.31) | copy-start | bytes 2359300
  1251.6 34.8 %copy-start.80 = (f32[512]{0:T(512)S(1)}, f32[512]{0:T(512)}, u32[]{:S(2)}) copy-start(f32[512]{0:T(512)} %copy-done.79) | copy-start | bytes 6148
  (55 other events, 289.8 us)
Sparse Core Ops, SparseCore 0:
  10.2 69.9 all-gather.6
  82.4 58.5 all-gather.8
  143.2 90.0 all-gather.12
  235.3 89.2 all-gather.10
  326.0 89.1 all-gather.14
  922.3 31.2 reduce-scatter.24
  979.6 34.8 reduce-scatter.14
  1017.4 32.8 reduce-scatter.12
  1052.7 97.7 reduce-scatter.16
  1152.8 98.7 reduce-scatter.10
  1253.9 187.4 reduce-scatter.22
  1443.7 187.1 reduce-scatter.20
  1633.3 187.5 reduce-scatter.18
  1824.5 59.6 all-reduce.13
where the time goes:
time: 1910 us; the launch traced here: 1900 us
  waiting for transfers between devices  1020 us (53%)
  matrix products  245 us (13%)
  blocking collectives  231 us (12%)
  local copies, waits for them, and re-layouts  226 us (12%)
  other arithmetic  135 us (7%)
  starting transfers between devices  28.3 us (1%)
    reduce_scatter x1, waiting for transfers between devices, local(): lax.psum_scatter(grad_gate_w.astype(jnp.bfloat16), ('context', 'dp'), sca...  187 us
    reduce_scatter x1, waiting for transfers between devices, local(): lax.psum_scatter(grad_up_w.astype(jnp.bfloat16), ('context', 'dp'), scatt...  187 us
    reduce_scatter x1, waiting for transfers between devices, local(): lax.psum_scatter(grad_down_w.astype(jnp.bfloat16), ('context', 'dp'), sca...  150 us
    all_to_all x1, waiting for transfers between devices, local(): lax.all_to_all(grad_arrived[None], 'expert', split_axis=2, concat_axis=0,...  132 us
    reduce_scatter x1, waiting for transfers between devices, local(): lax.psum_scatter(dense_terms[1].astype(jnp.bfloat16), ('context', 'dp'),...  101 us
    all_to_all x1, blocking collectives, local(): lax.all_to_all(grad_send, 'expert', split_axis=0, concat_axis=2, tiled=True)  91.5 us
    reduce_scatter x1, waiting for transfers between devices, local(): lax.psum_scatter(dense_terms[4].astype(jnp.bfloat16), ('context', 'dp'),...  82.8 us
    all_to_all x1, waiting for transfers between devices, local(): lax.all_to_all(outgoing, 'expert', split_axis=0, concat_axis=2, tiled=True)  79 us
  transfers between devices with their start and end apart: 21, of which 10 were waited for; matrix products, arithmetic and copies ran while one was open for 24% of the time, Pallas kernels for 0%

commit v1 on v0

v1 whole, which is shorter than its diff:
```python
import functools
import math

import jax
import jax.numpy as jnp
from jax import lax
from jax.experimental import pallas as pl
from jax.experimental.pallas import tpu as pltpu
from jax.sharding import PartitionSpec as P

MODEL_WIDTH = 1536
QUERY_HEADS = 12
KEY_VALUE_HEADS = 2
HEAD_SIZE = 128
FF = 768
TOP = 4
EXP_DEV = 4
GROUP = QUERY_HEADS // KEY_VALUE_HEADS
Q_WIDTH = QUERY_HEADS * HEAD_SIZE
KV_WIDTH = KEY_VALUE_HEADS * HEAD_SIZE
SMALL = 128

norm_eps = 1e-06
rope_base = 1000000.0
mask_fill = -1e30
bf16 = jnp.bfloat16
f32 = jnp.float32
VMEM_LIMIT = 60 * 1024 * 1024


def dot(a, b, dims=((1,), (0,))):
    return lax.dot_general(a, b, (dims, ((), ())), preferred_element_type=f32)


def after(value, *others):
    return lax.optimization_barrier((value,) + others)[0]


def flip(value, step):
    count = lax.axis_size("expert")
    return lax.ppermute(value, "expert", [(i, i ^ step) for i in range(count)])


def swap(value):
    return lax.ppermute(value, "context", [(0, 1), (1, 0)])


def rope_tables(start_pos, length, head_dim):
    half_dim = head_dim // 2
    freqs = rope_base ** (-(2.0 * jnp.arange(half_dim, dtype=f32)) / head_dim)
    places = (start_pos + jnp.arange(length, dtype=jnp.int32)).astype(f32)
    angles = places[:, None] * freqs[None, :]
    return (jnp.cos(angles), jnp.sin(angles))


def rotate(heads, cosine, sine):
    half_dim = heads.shape[-1] // 2
    a = heads[..., :half_dim]
    b = heads[..., half_dim:]
    c = cosine[:, None, :]
    s = sine[:, None, :]
    return jnp.concatenate([a * c - b * s, b * c + a * s], axis=-1)


def norm_parts(values):
    scale = lax.rsqrt(jnp.mean(values * values, axis=-1, keepdims=True) + norm_eps)
    return scale, values * scale


def assemble(own, other, context, expert):
    count = len(own)
    z, r, n = own[0].shape
    if r % 16 != 0:
        blocks = jnp.stack([jnp.stack(own), jnp.stack(other)])
        order = jnp.arange(count) ^ expert
        blocks = jnp.take(blocks, order, axis=1)
        blocks = jnp.take(blocks, jnp.arange(2) ^ context, axis=0)
        return jnp.transpose(blocks, (0, 2, 1, 3, 4)).reshape(2 * z * count * r, n)

    def kernel(place, *refs):
        sources, out, sems = refs[: 2 * count], refs[2 * count], refs[2 * count + 1]
        copies = []
        for k in range(count):
            for half in range(2):
                at = place[0] if half == 0 else 1 - place[0]
                copies.append(
                    pltpu.make_async_copy(
                        sources[half * count + k],
                        out.at[at, :, jnp.bitwise_xor(place[1], k)],
                        sems.at[half * count + k],
                    )
                )
        for copy in copies:
            copy.start()
        for copy in copies:
            copy.wait()

    size = 2 * z * count * r * n * 2
    shape = (2, z, count, r, n)
    out = pl.pallas_call(
        kernel,
        out_shape=jax.ShapeDtypeStruct(shape, bf16),
        grid_spec=pltpu.PrefetchScalarGridSpec(
            num_scalar_prefetch=1,
            grid=(1,),
            in_specs=[pl.BlockSpec(memory_space=pl.ANY)] * (2 * count),
            out_specs=pl.BlockSpec(shape, lambda i, place: (0, 0, 0, 0, 0)),
            scratch_shapes=[pltpu.SemaphoreType.DMA((2 * count,))],
        ),
        compiler_params=pltpu.CompilerParams(vmem_limit_bytes=VMEM_LIMIT),
        cost_estimate=pl.CostEstimate(flops=0, bytes_accessed=2 * size, transcendentals=0),
        name="assemble",
    )(jnp.stack([context, expert]).astype(jnp.int32), *own, *other)
    return out.reshape(2 * z * count * r, n)


def spread(block):
    count = lax.axis_size("expert")
    own = [block] + [flip(block, k) for k in range(1, count)]
    return own, [swap(b) for b in own]


GELU_C = math.sqrt(2.0 / math.pi)


def expert_kernel(count, tokens, capacity, place, *refs):
    acts, dys = refs[: 2 * count], refs[2 * count : 4 * count]
    w_ref, refs = refs[4 * count], refs[4 * count + 1 :]
    earlier, refs = refs[: len(refs) - 12], refs[len(refs) - 12 :]
    y_refs, d_refs, (x_ref, gdy_ref, h_ref, dg_ref, du_ref, abuf, dbuf, sems) = refs[:2], refs[2:4], refs[4:]
    step = pl.program_id(0)
    slot = lax.rem(step, 2)

    def copies(k, at):
        out = []
        for s in range(2):
            out.append(pltpu.make_async_copy(acts[s * count + k], abuf.at[at, s], sems.at[at, s]))
            out.append(pltpu.make_async_copy(dys[s * count + k], dbuf.at[at, s], sems.at[at, 2 + s]))
        return out

    @pl.when(step == 0)
    def _():
        for c in copies(0, 0):
            c.start()

    for k in range(1, count):

        @pl.when(step == k - 1)
        def _(k=k):
            for c in copies(k, k % 2):
                c.start()

    for k in range(count):

        @pl.when(step == k)
        def _(k=k):
            for c in copies(k, k % 2):
                c.wait()

    row = place[0]
    extra = abuf.shape[2] - tokens
    row_ids = lax.broadcasted_iota(jnp.int32, (extra, 3 * tokens), 0)
    slot_ids = lax.broadcasted_iota(jnp.int32, (capacity, tokens), 0).astype(f32)
    hits = []
    gate_cols = []
    for s in range(2):
        meta = abuf[slot, s, tokens:, :].astype(f32)
        line = jnp.sum(jnp.where(row_ids == row, meta, 0.0), axis=0, keepdims=True)
        gate_line = line[:, :tokens] + line[:, tokens : 2 * tokens]
        hit = slot_ids == line[:, 2 * tokens :]
        hits.append(hit)
        gate_col = jnp.sum(jnp.where(hit, gate_line, 0.0), axis=1, keepdims=True)
        gate_cols.append(gate_col)
        one = jnp.where(hit, 1.0, 0.0).astype(bf16)
        at = pl.ds(s * capacity, capacity)
        x_ref[at, :] = dot(one, abuf[slot, s, :tokens, :]).astype(bf16)
        gdy_ref[at, :] = dot(one, dbuf[slot, s]).astype(bf16)
    gate_col = jnp.concatenate(gate_cols, axis=0)
    wide = w_ref.shape[0] * w_ref.shape[3]
    w_gate = w_ref[:, 0, 0].reshape(wide, FF)
    w_up = w_ref[:, 0, 1].reshape(wide, FF)
    w_down = w_ref[:, 0, 2].reshape(wide, FF)
    x = x_ref[...]
    dy = gdy_ref[...]
    gate_h = dot(x, w_gate)
    up_h = dot(x, w_up)
    back = dot(dy, w_down)
    square = gate_h * gate_h
    tanh = jnp.tanh(GELU_C * gate_h * (1.0 + 0.044715 * square))
    half = 0.5 * (1.0 + tanh)
    gelu = gate_h * half
    slope = half + 0.5 * gate_h * (1.0 - tanh * tanh) * (GELU_C * (1.0 + 3 * 0.044715 * square))
    hidden = (gelu * up_h).astype(bf16)
    dgate_col = jnp.sum(hidden.astype(f32) * back, axis=1, keepdims=True)
    dhidden = back * gate_col
    dgate_h = (dhidden * up_h * slope).astype(bf16)
    dup_h = (dhidden * gelu).astype(bf16)
    h_ref[...] = hidden
    dg_ref[...] = dgate_h
    du_ref[...] = dup_h
    gdy_ref[...] = (dy.astype(f32) * gate_col).astype(bf16)
    result = (dot(hidden, w_down, ((1,), (1,))) * gate_col).astype(bf16)
    dx = (dot(dgate_h, w_gate, ((1,), (1,))) + dot(dup_h, w_up, ((1,), (1,)))).astype(bf16)
    for s in range(2):
        one = jnp.where(hits[s], 1.0, 0.0).astype(bf16)
        rows = slice(s * capacity, (s + 1) * capacity)
        y = dot(one, result[rows], ((0,), (0,)))
        d = dot(one, dx[rows], ((0,), (0,)))
        line = jnp.sum(jnp.where(hits[s], dgate_col[rows], 0.0), axis=0, keepdims=True)
        high = line.astype(bf16).astype(f32)
        line = jnp.concatenate([high, line - high, jnp.zeros_like(high)], axis=1)
        line = jnp.where(row_ids == row, line, 0.0)
        if earlier:
            y = y + earlier[s][0].astype(f32)
            d = d + earlier[2 + s][0, :tokens].astype(f32)
            line = line + earlier[2 + s][0, tokens:].astype(f32)
        y_refs[s][0] = y.astype(bf16)
        d_refs[s][0, :tokens] = d.astype(bf16)
        d_refs[s][0, tokens:] = line.astype(bf16)


def run_expert(acts, dys, weights, place, capacity, earlier=()):
    count = len(acts) // 2
    tokens = dys[0].shape[0]
    rows = acts[0].shape[0]
    cz, _, _, local, _ = weights.shape
    slots = 2 * capacity
    total = count * slots

    def row_block(width):
        return pl.BlockSpec((slots, width), lambda i, place: (i, 0))

    macs = total * (9 * MODEL_WIDTH * FF - 3 * MODEL_WIDTH * FF + 4 * tokens * MODEL_WIDTH)
    moved = 2 * (
        4 * count * (rows + tokens) * MODEL_WIDTH + total * (2 * MODEL_WIDTH + 3 * FF) + 3 * MODEL_WIDTH * FF
    )
    sums = [pl.BlockSpec((1, n, MODEL_WIDTH), lambda i, place: (i, 0, 0)) for n in (tokens, tokens, rows, rows)]
    return pl.pallas_call(
        functools.partial(expert_kernel, count, tokens, capacity),
        out_shape=(
            jax.ShapeDtypeStruct((count, tokens, MODEL_WIDTH), bf16),
            jax.ShapeDtypeStruct((count, tokens, MODEL_WIDTH), bf16),
            jax.ShapeDtypeStruct((count, rows, MODEL_WIDTH), bf16),
            jax.ShapeDtypeStruct((count, rows, MODEL_WIDTH), bf16),
            jax.ShapeDtypeStruct((total, MODEL_WIDTH), bf16),
            jax.ShapeDtypeStruct((total, MODEL_WIDTH), bf16),
            jax.ShapeDtypeStruct((total, FF), bf16),
            jax.ShapeDtypeStruct((total, FF), bf16),
            jax.ShapeDtypeStruct((total, FF), bf16),
        ),
        grid_spec=pltpu.PrefetchScalarGridSpec(
            num_scalar_prefetch=1,
            grid=(count,),
            in_specs=[pl.BlockSpec(memory_space=pl.ANY)] * (4 * count)
            + [
                pl.BlockSpec(
                    (cz, 1, 3, local, FF),
                    lambda i, place: (0, place[1], 0, 0, 0),
                    pipeline_mode=pl.Buffered(1),
                )
            ]
            + (sums if earlier else []),
            out_specs=(
                *sums,
                row_block(MODEL_WIDTH),
                row_block(MODEL_WIDTH),
                row_block(FF),
                row_block(FF),
                row_block(FF),
            ),
            scratch_shapes=[
                pltpu.VMEM((2, 2, rows, MODEL_WIDTH), bf16),
                pltpu.VMEM((2, 2, tokens, MODEL_WIDTH), bf16),
                pltpu.SemaphoreType.DMA((2, 4)),
            ],
        ),
        compiler_params=pltpu.CompilerParams(
            dimension_semantics=("arbitrary",), vmem_limit_bytes=VMEM_LIMIT
        ),
        cost_estimate=pl.CostEstimate(
            flops=2 * macs, bytes_accessed=moved, transcendentals=total * FF
        ),
        name="experts",
    )(place, *acts, *dys, weights, *earlier)


def weight_grad_kernel(x_ref, gdy_ref, h_ref, dg_ref, du_ref, out_ref):
    shape = (out_ref.shape[0], out_ref.shape[3], FF)
    x = x_ref[...]
    first = ((0,), (0,))
    out_ref[:, 0, 0] = dot(x, dg_ref[...], first).astype(bf16).reshape(shape)
    out_ref[:, 0, 1] = dot(x, du_ref[...], first).astype(bf16).reshape(shape)
    out_ref[:, 0, 2] = dot(gdy_ref[...], h_ref[...], first).astype(bf16).reshape(shape)


def weight_grads(x, gdy, hidden, dgate, dup, z, local):
    total = x.shape[0]
    wide = 384
    per = MODEL_WIDTH // 2 // wide
    full = pl.BlockSpec((total, FF), lambda i: (0, 0))
    column = pl.BlockSpec((total, wide), lambda i: (0, i))
    return pl.pallas_call(
        weight_grad_kernel,
        out_shape=jax.ShapeDtypeStruct((z, 2, 3, local, FF), bf16),
        grid=(MODEL_WIDTH // wide,),
        in_specs=[column, column, full, full, full],
        out_specs=pl.BlockSpec(
            (wide // local, 1, 3, local, FF), lambda i: (lax.rem(i, per), lax.div(i, per), 0, 0, 0)
        ),
        compiler_params=pltpu.CompilerParams(
            dimension_semantics=("arbitrary",), vmem_limit_bytes=VMEM_LIMIT
        ),
        cost_estimate=pl.CostEstimate(
            flops=6 * total * MODEL_WIDTH * FF,
            bytes_accessed=2 * (total * (2 * MODEL_WIDTH + 3 * FF) + 3 * MODEL_WIDTH * FF),
            transcendentals=0,
        ),
        name="weight_grads",
    )(x, gdy, hidden, dgate, dup)


SCORE = math.log2(math.e) / math.sqrt(HEAD_SIZE)
STRIP = 256


def roll_half(x):
    return pltpu.roll(x, HEAD_SIZE // 2, 1)


def causal(strip):
    shape = ((strip + 1) * STRIP, STRIP)
    key = lax.broadcasted_iota(jnp.int32, shape, 0)
    return key <= lax.broadcasted_iota(jnp.int32, shape, 1) + strip * STRIP


def attend_kernel(place, q_ref, ko_ref, vo_ref, kr_ref, vr_ref, cos_ref, sin_ref, rot_ref, mix_ref, log_ref):
    q = q_ref[...]
    rot_ref[...] = (q * cos_ref[...] + roll_half(q) * sin_ref[...]).astype(bf16)
    last = ((1,), (1,))
    first = ((0,), (0,))
    for r in range(q_ref.shape[0] // STRIP):
        rows = pl.ds(r * STRIP, STRIP)
        seen = (r + 1) * STRIP
        q = rot_ref[rows, :]
        far = jnp.where(place[0] > 0, dot(kr_ref[...], q, last), mask_fill)
        near = jnp.where(causal(r), dot(ko_ref[:seen, :], q, last), mask_fill)
        peak = jnp.maximum(
            jnp.max(far, axis=0, keepdims=True), jnp.max(near, axis=0, keepdims=True)
        )
        peak = peak * SCORE
        far = jnp.exp2(far * SCORE - peak)
        near = jnp.exp2(near * SCORE - peak)
        total = jnp.sum(far, axis=0, keepdims=True) + jnp.sum(near, axis=0, keepdims=True)
        out = dot(vr_ref[...], far.astype(bf16), first)
        out = out + dot(vo_ref[:seen, :], near.astype(bf16), first)
        mix_ref[rows, :] = (out / total).T.astype(bf16)
        log_ref[0, :, rows] = peak + jnp.log2(total)


def attention_specs(tokens):
    head = pl.BlockSpec((tokens, HEAD_SIZE), lambda h, place: (0, h))
    key = pl.BlockSpec((tokens, HEAD_SIZE), lambda h, place: (0, h // GROUP))
    value = pl.BlockSpec((tokens, HEAD_SIZE), lambda h, place: (0, KEY_VALUE_HEADS + h // GROUP))
    table = pl.BlockSpec((tokens, HEAD_SIZE), lambda h, place: (0, 0))
    log = pl.BlockSpec((1, 1, tokens), lambda h, place: (h, 0, 0))
    return head, key, value, table, log


def attention(context, qkv, near, far, cosine, sine):
    tokens = qkv.shape[0]
    head, key, value, table, log = attention_specs(tokens)
    pairs = 2 * tokens * tokens * QUERY_HEADS
    return pl.pallas_call(
        attend_kernel,
        out_shape=(
            jax.ShapeDtypeStruct((tokens, Q_WIDTH), bf16),
            jax.ShapeDtypeStruct((tokens, Q_WIDTH), bf16),
            jax.ShapeDtypeStruct((QUERY_HEADS, 1, tokens), f32),
        ),
        grid_spec=pltpu.PrefetchScalarGridSpec(
            num_scalar_prefetch=1,
            grid=(QUERY_HEADS,),
            in_specs=[head, key, value, key, value, table, table],
            out_specs=(head, head, log),
        ),
        compiler_params=pltpu.CompilerParams(
            dimension_semantics=("arbitrary",), vmem_limit_bytes=VMEM_LIMIT
        ),
        cost_estimate=pl.CostEstimate(
            flops=4 * pairs * HEAD_SIZE, bytes_accessed=tokens * Q_WIDTH * 10, transcendentals=pairs
        ),
        name="attention",
    )(context, qkv, near, near, far, far, cosine, sine)


def attend_back_kernel(
    place, q_ref, dout_ref, ko_ref, vo_ref, kr_ref, vr_ref, log_ref, cos_ref, sin_ref,
    dq_ref, dko_ref, dvo_ref, dkr_ref, dvr_ref,
):
    last = ((1,), (1,))
    first = ((0,), (0,))
    scale = 1.0 / math.sqrt(HEAD_SIZE)

    @pl.when(lax.rem(pl.program_id(0), GROUP) == 0)
    def _():
        for ref in (dko_ref, dvo_ref, dkr_ref, dvr_ref):
            ref[...] = jnp.zeros_like(ref)

    for r in range(q_ref.shape[0] // STRIP):
        rows = pl.ds(r * STRIP, STRIP)
        seen = (r + 1) * STRIP
        q = q_ref[rows, :]
        dout = dout_ref[rows, :]
        logs = log_ref[0, :, rows]
        far = jnp.where(place[0] > 0, dot(kr_ref[...], q, last), mask_fill)
        near = jnp.where(causal(r), dot(ko_ref[:seen, :], q, last), mask_fill)
        far = jnp.exp2(far * SCORE - logs)
        near = jnp.exp2(near * SCORE - logs)
        dvr_ref[...] += dot(far.astype(bf16), dout)
        dvo_ref[:seen, :] += dot(near.astype(bf16), dout)
        dfar = dot(vr_ref[...], dout, last)
        dnear = dot(vo_ref[:seen, :], dout, last)
        inner = jnp.sum(far * dfar, axis=0, keepdims=True)
        inner = inner + jnp.sum(near * dnear, axis=0, keepdims=True)
        dfar = (far * (dfar - inner)).astype(bf16)
        dnear = (near * (dnear - inner)).astype(bf16)
        dkr_ref[...] += dot(dfar, q) * scale
        dko_ref[:seen, :] += dot(dnear, q) * scale
        dq = dot(kr_ref[...], dfar, first) + dot(ko_ref[:seen, :], dnear, first)
        dq = dq.T * scale
        dq_ref[rows, :] = (dq * cos_ref[rows, :] - roll_half(dq) * sin_ref[rows, :]).astype(bf16)


def attention_back(context, query, dmixed, near, far, logs, cosine, sine):
    tokens = query.shape[0]
    head, key, value, table, log = attention_specs(tokens)
    pairs = 2 * tokens * tokens * QUERY_HEADS
    side = jax.ShapeDtypeStruct((tokens, KV_WIDTH), f32)
    return pl.pallas_call(
        attend_back_kernel,
        out_shape=(jax.ShapeDtypeStruct((tokens, Q_WIDTH), bf16), side, side, side, side),
        grid_spec=pltpu.PrefetchScalarGridSpec(
            num_scalar_prefetch=1,
            grid=(QUERY_HEADS,),
            in_specs=[head, head, key, value, key, value, log, table, table],
            out_specs=(head, key, key, key, key),
        ),
        compiler_params=pltpu.CompilerParams(
            dimension_semantics=("arbitrary",), vmem_limit_bytes=VMEM_LIMIT
        ),
        cost_estimate=pl.CostEstimate(
            flops=10 * pairs * HEAD_SIZE, bytes_accessed=tokens * Q_WIDTH * 8, transcendentals=pairs
        ),
        name="attention_back",
    )(context, query, dmixed, near, near, far, far, logs, cosine, sine)


def reduce_dense(grad, context, expert):
    count = lax.axis_size("expert")
    z = lax.axis_size("dp")
    n = grad.shape[1]
    r = grad.shape[0] // (2 * z * count)
    grad = grad.astype(bf16).reshape(2, z, count, r, n)
    theirs = swap(lax.dynamic_index_in_dim(grad, 1 - context, 0, keepdims=False))
    mine = lax.dynamic_index_in_dim(grad, context, 0, keepdims=False)

    def part(k):
        at = expert ^ k
        a = lax.dynamic_index_in_dim(mine, at, 1, keepdims=False)
        b = lax.dynamic_index_in_dim(theirs, at, 1, keepdims=False)
        return a.astype(f32) + b.astype(f32)

    total = part(0)
    for k in range(1, count):
        total = total + flip(part(k).astype(bf16), k).astype(f32)
    share = lax.psum_scatter(total.astype(bf16), "dp", scatter_dimension=0, tiled=False)
    blocks = jnp.stack([share] + [flip(share, k) for k in range(1, count)])
    pieces = [lax.dynamic_index_in_dim(blocks, expert ^ e, 0, keepdims=False) for e in range(count)]
    return jnp.concatenate(pieces, axis=0).astype(f32)


def reduce_blocks(own, other):
    count = own.shape[0]
    came = swap(other)
    parts = [own[k].astype(f32) + came[k].astype(f32) for k in range(count)]
    total = parts[0]
    for k in range(1, count):
        total = total + flip(parts[k].astype(bf16), k).astype(f32)
    return total


def local(
    hidden_in,
    out_grad,
    routes,
    attn_gain,
    w_query,
    key_projection,
    value_projection,
    w_out,
    ffn_gain,
    w_router,
    w_gate,
    w_up,
    w_down,
):
    expert = lax.axis_index("expert")
    context = lax.axis_index("context")
    count = lax.axis_size("expert")
    z = lax.axis_size("dp")
    tokens = hidden_in.shape[1]
    experts_all = EXP_DEV * count
    per_core = EXP_DEV // 2
    capacity = tokens * TOP * 5 // (4 * experts_all)
    rows = w_query.shape[0]
    piece = rows // count

    def quarter(parts):
        cut = [
            lax.dynamic_slice_in_dim(p, expert * piece, piece, axis=0).astype(bf16) for p in parts
        ]
        return jnp.concatenate(cut, axis=1)

    pad = jnp.zeros((rows, SMALL - experts_all - 2), f32)
    first_pack = quarter(
        [w_query, key_projection, value_projection, w_router, attn_gain[:, None], ffn_gain[:, None], pad]
    )
    second_pack = quarter([w_out])
    first_z = lax.all_gather(first_pack, "dp", axis=0, tiled=False)
    second_z = lax.all_gather(second_pack, "dp", axis=0, tiled=False)
    own_one, other_one = spread(first_z)
    own_two, other_two = spread(after(second_z, own_one[-1]))
    packed = assemble(own_one, other_one, context, expert)
    out_w = assemble(own_two, other_two, context, expert)
    qkv_w = packed[:, : Q_WIDTH + 2 * KV_WIDTH]
    router_w = packed[:, Q_WIDTH + 2 * KV_WIDTH :][:, :experts_all]
    small = packed[:, Q_WIDTH + 2 * KV_WIDTH :].T
    gain_one = small[experts_all].astype(f32)
    gain_two = small[experts_all + 1].astype(f32)

    def chunk(j):
        picked = slice(j, None, per_core)
        return jnp.stack(
            [
                w_gate[picked].astype(bf16),
                w_up[picked].astype(bf16),
                jnp.swapaxes(w_down[picked], 1, 2).astype(bf16),
            ],
            axis=1,
        )

    gathered = []
    for j in range(per_core):
        sent = after(chunk(j), second_z)
        gathered.append(lax.all_gather(sent, ("context", "dp"), axis=0, tiled=False))

    dy_half = after(out_grad[0], own_two[-1])
    dys_own, dys_other = spread(dy_half)

    route_t = routes[0].T
    expert_ids = jnp.arange(experts_all, dtype=jnp.int32)
    named = jnp.any(route_t[:, None, :] == expert_ids[None, :, None], axis=0)
    earlier = (
        jnp.arange(tokens, dtype=jnp.int32)[:, None] < jnp.arange(tokens, dtype=jnp.int32)[None, :]
    )
    ranks = dot(named.astype(bf16), earlier.astype(bf16))
    slot_code = jnp.where(named & (ranks < capacity), ranks, -1.0)

    inputs_f = hidden_in[0].astype(f32)
    scale_one, norm_one = norm_parts(inputs_f)
    act_one = (norm_one * gain_one).astype(bf16)
    qkv = dot(act_one, qkv_w)
    cosine, sine = rope_tables(context * tokens, tokens, HEAD_SIZE)
    cos_wide = jnp.concatenate([cosine, cosine], axis=1)
    sin_wide = jnp.concatenate([-sine, sine], axis=1)
    key = rotate(
        qkv[:, Q_WIDTH : Q_WIDTH + KV_WIDTH].reshape(tokens, KEY_VALUE_HEADS, HEAD_SIZE),
        cosine,
        sine,
    ).astype(bf16)
    value = qkv[:, Q_WIDTH + KV_WIDTH :].astype(bf16)
    near = jnp.concatenate([key.reshape(tokens, KV_WIDTH), value], axis=1)
    far = lax.ppermute(near, "context", [(0, 1)])
    where = context[None].astype(jnp.int32)
    query, mixed, logs = attention(where, qkv, near, far, cos_wide, sin_wide)
    resid_one = inputs_f + dot(mixed, out_w)
    scale_two, norm_two = norm_parts(resid_one)
    act_two = (norm_two * gain_two).astype(bf16)

    logits = dot(router_w, act_two, ((0,), (1,)))
    shown = jnp.where(named, logits, mask_fill)
    exped = jnp.where(named, jnp.exp(shown - jnp.max(shown, axis=0, keepdims=True)), 0.0)
    gates = exped / jnp.sum(exped, axis=0, keepdims=True)
    gates_high = gates.astype(bf16)
    gates_low = (gates - gates_high.astype(f32)).astype(bf16)
    meta = jnp.concatenate([gates_high, gates_low, slot_code.astype(bf16)], axis=1)
    acts_own, acts_other = spread(jnp.concatenate([act_two, meta], axis=0))

    sums, shares = (), []
    place = jnp.stack([expert * EXP_DEV + context * per_core, context]).astype(jnp.int32)
    step = jnp.array([1, 0], jnp.int32)
    for j in range(per_core):
        *sums, x, gdy, hidden, dgate, dup = run_expert(
            acts_own + acts_other, dys_own + dys_other, gathered[j], place, capacity, sums
        )
        grads = weight_grads(x, gdy, hidden, dgate, dup, z, rows)
        place = after(place + step, grads)
        shares.append(lax.psum_scatter(grads, "dp", scatter_dimension=0, tiled=False))
    y_own, y_other, d_own, d_other = sums
    dact = reduce_blocks(d_own, d_other)
    y_other = after(y_other, dact)
    block_out = (resid_one + reduce_blocks(y_own, y_other)).astype(bf16)[None]

    dy = out_grad[0].astype(f32)
    dgates = dact[tokens:, :tokens] + dact[tokens:, tokens : 2 * tokens]
    dlogits = (gates * (dgates - jnp.sum(gates * dgates, axis=0, keepdims=True))).astype(bf16)
    dact_two = dact[:tokens] + dot(dlogits, router_w, ((0,), (1,)))
    grad_router = dot(act_two, dlogits, ((0,), (1,)))
    grad_gain_two = jnp.sum(dact_two * norm_two, axis=0)
    dn2 = dact_two * gain_two
    dresid = dy + scale_two * (dn2 - norm_two * jnp.mean(dn2 * norm_two, axis=-1, keepdims=True))
    dresid_b = dresid.astype(bf16)
    grad_out = reduce_dense(dot(mixed, dresid_b, ((0,), (0,))), context, expert)
    dmixed = dot(dresid_b, out_w, ((1,), (1,))).astype(bf16)

    dquery, dkey_near, dvalue_near, dkey_far, dvalue_far = attention_back(
        where, query, dmixed, near, far, logs, cos_wide, sin_wide
    )
    sent = jnp.concatenate([dkey_far, dvalue_far], axis=1).astype(bf16)
    came = lax.ppermute(sent, "context", [(1, 0)]).astype(f32)
    dkey_r = (dkey_near + came[:, :KV_WIDTH]).reshape(tokens, KEY_VALUE_HEADS, HEAD_SIZE)
    dkey = rotate(dkey_r, cosine, -sine).astype(bf16).reshape(tokens, KV_WIDTH)
    dvalue = dvalue_near + came[:, KV_WIDTH:]
    dqkv = jnp.concatenate([dquery, dkey, dvalue.astype(bf16)], axis=1)
    dact_one = dot(dqkv, qkv_w, ((1,), (1,)))
    grad_qkv = dot(act_one, dqkv, ((0,), (0,)))
    grad_gain_one = jnp.sum(dact_one * norm_one, axis=0)
    dn1 = dact_one * gain_one
    grad_in = dresid + scale_one * (dn1 - norm_one * jnp.mean(dn1 * norm_one, axis=-1, keepdims=True))
    grad_small = jnp.concatenate(
        [
            grad_router,
            grad_gain_one[:, None],
            grad_gain_two[:, None],
            jnp.zeros((MODEL_WIDTH, SMALL - experts_all - 2), f32),
        ],
        axis=1,
    )
    first = reduce_dense(jnp.concatenate([grad_qkv, grad_small], axis=1), context, expert)
    kv_at = Q_WIDTH + KV_WIDTH
    small_at = kv_at + KV_WIDTH

    finals = []
    for share in shares:
        keep = lax.dynamic_index_in_dim(share, context, 0, keepdims=False)
        came = swap(lax.dynamic_index_in_dim(share, 1 - context, 0, keepdims=False))
        finals.append((jnp.where(context == 0, keep, came), jnp.where(context == 0, came, keep)))
    stacked = jnp.stack([f[c] for c in range(2) for f in finals])
    stacked = stacked.astype(f32)
    return (
        block_out,
        grad_in[None],
        first[:, small_at + experts_all],
        first[:, :Q_WIDTH],
        first[:, Q_WIDTH:kv_at],
        first[:, kv_at:small_at],
        grad_out,
        first[:, small_at + experts_all + 1],
        first[:, small_at : small_at + experts_all],
        stacked[:, 0],
        stacked[:, 1],
        jnp.swapaxes(stacked[:, 2], 1, 2),
    )


def solution(mesh):
    tokens_at = P(("expert", "dp"), "context", None)
    vector = P(("context", "dp"))
    matrix = P(("context", "dp"), None)
    wide = P("expert", ("context", "dp"), None)
    down = P("expert", None, ("context", "dp"))
    return jax.shard_map(
        local,
        mesh=mesh,
        in_specs=(
            tokens_at,
            tokens_at,
            tokens_at,
            vector,
            matrix,
            matrix,
            matrix,
            matrix,
            vector,
            matrix,
            wide,
            wide,
            down,
        ),
        out_specs=(
            tokens_at,
            tokens_at,
            vector,
            matrix,
            matrix,
            matrix,
            matrix,
            vector,
            matrix,
            wide,
            wide,
            down,
        ),
        check_vma=False,
    )
```

time: 1910 us -> 823 us (0.43)
  waiting for transfers between devices: 1020 us -> 352 us
  matrix products: 245 us -> 38.5 us
  blocking collectives: 231 us -> 46.1 us
  Pallas kernels: 0 us -> 174 us
  local copies, waits for them, and re-layouts: 226 us -> 71.4 us
  other arithmetic: 135 us -> 65.8 us
  starting transfers between devices: 28.3 us -> 52 us
    reduce_scatter x7 -> x4, waiting for transfers between devices: 707 us -> 10 us  [the longest x2 10 us: reduce_dense(): lax.psum_scatter(total.astype(bf16), 'dp', scatter_dimension=0, tiled=False)]
    ppermute x4 -> x54, waiting for transfers between devices: 2.88 us -> 342 us  [the longest x30 320 us: flip(): return lax.ppermute(value, 'expert', [(i, i ^ step) for i in range(count)])]
    all_to_all x3 -> x0, waiting for transfers between devices: 245 us -> none  [the longest x1 132 us: local(): lax.all_to_all(grad_arrived[None], 'expert', split_axis=2, concat_axis=0,...]
    dot_general x36 -> x10, matrix products: 245 us -> 38.5 us  [dot(): return lax.dot_general(a, b, (dims, ((), ())), preferred_element_type=f32)]
    pallas_call x0 -> x8, Pallas kernels: none -> 174 us  [the longest x2 84.9 us: run_expert(): pl.pallas_call(functools.partial(expert_kernel, count, tokens, capacity),...]
    gather x6 -> x0, local copies, waits for them, and re-layouts: 93.1 us -> none  [the longest x2 34.4 us: local(): grad_back[pair_slot]]
    all_to_all x1 -> x0, blocking collectives: 91.5 us -> none  [local(): lax.all_to_all(grad_send, 'expert', split_axis=0, concat_axis=2, tiled=True)]
    psum x1 -> x0, waiting for transfers between devices: 60.4 us -> none  [local(): lax.psum(shares[1].astype(jnp.bfloat16), 'expert').astype(jnp.float32)]
  transfers between devices with their start and end apart: 21 -> 60, of which waited for: 10 -> 27; matrix products, arithmetic and copies ran while one was open for 24% -> 18% of each run, Pallas kernels for 0% -> 14%
where the time goes in v1:
time: 823 us; the launch traced here: 816 us
  waiting for transfers between devices  352 us (43%)
  Pallas kernels  174 us (21%)
  local copies, waits for them, and re-layouts  71.4 us (9%)
  other arithmetic  65.8 us (8%)
  starting transfers between devices  52 us (6%)
  blocking collectives  46.1 us (6%)
  matrix products  38.5 us (5%)
  between operations  15.2 us (2%)
    ppermute x30, waiting for transfers between devices, flip(): return lax.ppermute(value, 'expert', [(i, i ^ step) for i in range(count)])  320 us
    pallas_call x2, Pallas kernels, run_expert(): pl.pallas_call(functools.partial(expert_kernel, count, tokens, capacity),...  84.9 us
    ppermute x30, starting transfers between devices, flip(): return lax.ppermute(value, 'expert', [(i, i ^ step) for i in range(count)])  42.4 us
    dot_general x10, matrix products, dot(): return lax.dot_general(a, b, (dims, ((), ())), preferred_element_type=f32)  38.5 us
    pallas_call x2, Pallas kernels, weight_grads(): pl.pallas_call(weight_grad_kernel, out_shape=jax.ShapeDtypeStruct((z, 2,...  29.9 us
    pallas_call x1, Pallas kernels, attention_back(): pl.pallas_call(attend_back_kernel, out_shape=(jax.ShapeDtypeStruct((token...  28.8 us
    all_gather x1, blocking collectives, local(): first_z = lax.all_gather(first_pack, 'dp', axis=0, tiled=False)  27.7 us
    ppermute x22, waiting for transfers between devices, swap(): return lax.ppermute(value, 'context', [(0, 1), (1, 0)])  21.6 us
  transfers between devices with their start and end apart: 60, of which 27 were waited for; matrix products, arithmetic and copies ran while one was open for 18% of the time, Pallas kernels for 14%

profile of v1, /device:TPU:0, one launch (start us, length us, event | category | flops | bytes accessed | tf_op | source)
XLA Modules:
  0.0 815.6 jit_solution(6564875061373193865)
XLA Ops:
  8.5 18.4 %all-gather.1 = bf16[192,1536]{1,0:T(8,128)(2,1)} all-gather(bf16[48,1536]{1,0:T(8,128)(2,1)S(1)} %dynamic-slice_convert_fusion), channel_id=3, replica_groups=mesh['expert'=4,'context'=2,'dp'=4] {'dp'}, dimensions={0}, use_global_device_ids=true | all-gather | bytes 737280 | tf_op jit(solution)/shard_map/all_gather | solution.py:530
  31.1 2.0 pad_maximum_fusion.1
  37.1 27.7 %all-gather = bf16[192,2176]{1,0:T(8,128)(2,1)S(1)} all-gather(bf16[48,2176]{1,0:T(8,128)(2,1)S(1)} %concatenate.50), channel_id=2, replica_groups=mesh['expert'=4,'context'=2,'dp'=4] {'dp'}, dimensions={0}, use_global_device_ids=true | all-gather | bytes 1044480 | tf_op jit(solution)/shard_map/all_gather | solution.py:529
  64.9 2.5 collective-permute-start.2
  68.3 19.1 %collective-permute-done.2.refs_3_ = bf16[4,48,2176]{2,1,0:T(8,128)(2,1)} collective-permute-done((bf16[4,48,2176]{2,1,0:T(8,128)(2,1)S(1)}, bf16[4,48,2176]{2,1,0:T(8,128)(2,1)}, u32[]{:S(2)}, u32[]{:S(2)}) %collective-permute-start.2) | collective-permute-done | bytes 835616 | tf_op jit(solution)/shard_map/ppermute | solution.py:41
  87.5 2.5 collective-permute-start.10
  90.0 9.0 %collective-permute-done.refs_1_ = bf16[4,48,2176]{2,1,0:T(8,128)(2,1)} collective-permute-done((bf16[4,48,2176]{2,1,0:T(8,128)(2,1)S(1)}, bf16[4,48,2176]{2,1,0:T(8,128)(2,1)}, u32[]{:S(2)}, u32[]{:S(2)}) %collective-permute-start) | collective-permute-done | bytes 835616 | tf_op jit(solution)/shard_map/ppermute | solution.py:41
  101.4 5.6 collective-permute-done.10.refs_3_
  107.0 1.9 collective-permute-start.9
  110.5 7.4 collective-permute-done.8.refs_1_
  118.9 6.4 assemble.2
  126.7 5.6 fusion.2.q_ref
  137.4 2.5 collective-permute-start.7
  144.7 5.2 assemble.3
  150.7 19.0 %attention.1 = (bf16[512,1536]{1,0:T(8,128)(2,1)}, bf16[512,1536]{1,0:T(8,128)(2,1)}, f32[12,1,512]{2,1,0:T(1,128)}) custom-call(s32[1]{0:T(128)} %bitcast.1.place, f32[512,2048]{1,0:T(8,128)} %copy-done.20, bf16[512,512]{1,0:T(8,128)(2,1)} %copy-done.18, bf16[512,512]{1,0:T(8,128)(2,1)} %copy-done.18, bf16[512,512]{1,0:T(8,128)(2,1)} %copy-done.30, ...), custom_call_target="tpu_custom_call" | custom-call | flops 3221225472 | bytes 7864320 | tf_op jit(solution)/shard_map/attention/pallas_call | solution.py:373
  169.7 5.1 multiply_reduce_fusion.2
  180.9 30.0 %collective-permute-done.23.refs_10_ = bf16[512,1536]{1,0:T(8,128)(2,1)} collective-permute-done((bf16[512,1536]{1,0:T(8,128)(2,1)}, bf16[512,1536]{1,0:T(8,128)(2,1)}, u32[]{:S(2)}, u32[]{:S(2)}) %collective-permute-start.23) | collective-permute-done | bytes 1572896 | tf_op jit(solution)/shard_map/ppermute | solution.py:41
  210.9 3.0 collective-permute-start.17
  214.4 32.9 %collective-permute-done.15.refs_1_ = bf16[528,1536]{1,0:T(8,128)(2,1)} collective-permute-done((bf16[528,1536]{1,0:T(8,128)(2,1)S(1)}, bf16[528,1536]{1,0:T(8,128)(2,1)}, u32[]{:S(2)}, u32[]{:S(2)}) %collective-permute-start.15) | collective-permute-done | bytes 1622048 | tf_op jit(solution)/shard_map/ppermute | solution.py:41
  247.3 32.8 %collective-permute-done.16.refs_2_ = bf16[528,1536]{1,0:T(8,128)(2,1)} collective-permute-done((bf16[528,1536]{1,0:T(8,128)(2,1)S(1)}, bf16[528,1536]{1,0:T(8,128)(2,1)}, u32[]{:S(2)}, u32[]{:S(2)}) %collective-permute-start.16) | collective-permute-done | bytes 1622048 | tf_op jit(solution)/shard_map/ppermute | solution.py:41
  283.9 10.5 %copy.95 = bf16[16,3,192,768]{3,2,1,0:T(8,128)(2,1)} copy(bf16[16,3,192,768]{3,2,0,1:T(8,128)(2,1)} %all-gather.7.cloned.1.call-done) | data formatting | bytes 28311552 | tf_op jit(solution)/shard_map/all_gather | solution.py:555
  294.4 41.0 %experts.2 = (bf16[4,512,1536]{2,1,0:T(8,128)(2,1)}, bf16[4,512,1536]{2,1,0:T(8,128)(2,1)}, bf16[4,528,1536]{2,1,0:T(8,128)(2,1)}, bf16[4,528,1536]{2,1,0:T(8,12...) custom-call(s32[2]{0:T(128)} %get-tuple-element.133.place, ...), custom_call_target="tpu_custom_call" | custom-call | flops 26172456960 | bytes 71958528 | tf_op jit(solution)/shard_map/experts/pallas_call | solution.py:238
  335.5 15.1 %weight_grads.2 = bf16[4,2,3,192,768]{4,3,2,1,0:T(8,128)(2,1)} custom-call(bf16[1280,1536]{1,0:T(8,128)(2,1)} %get-tuple-element.48.x_ref, bf16[1280,1536]{1,0:T(8,128)(2,1)} %get-tuple-element.49.gdy_ref, bf16[1280,768]{1,0:T(8,128)(2,1)} %get-tuple-element.50.h_ref, bf16[1280,768]{1,0:T(8,128)(2,1)} %get-tuple-element.51.dg_ref, ...), custom_call_target="tpu_custom_call" | custom-call | flops 9059696640 | bytes 20840448 | tf_op jit(solution)/shard_map/weight_grads/pallas_call | solution.py:302
  350.6 10.5 %copy.96 = bf16[16,3,192,768]{3,2,1,0:T(8,128)(2,1)} copy(bf16[16,3,192,768]{3,2,0,1:T(8,128)(2,1)} %all-gather.9.cloned.1.call-done) | data formatting | bytes 28311552 | tf_op jit(solution)/shard_map/all_gather | solution.py:555
  361.1 43.9 %experts.3 = (bf16[4,512,1536]{2,1,0:T(8,128)(2,1)}, bf16[4,512,1536]{2,1,0:T(8,128)(2,1)}, bf16[4,528,1536]{2,1,0:T(8,128)(2,1)}, bf16[4,528,1536]{2,1,0:T(8,12...) custom-call(s32[2]{0:T(128)} %get-tuple-element.53.place, ...), custom_call_target="tpu_custom_call" | custom-call | flops 26172456960 | bytes 71958528 | tf_op jit(solution)/shard_map/experts/pallas_call | solution.py:238
  405.0 14.7 %weight_grads.3 = bf16[4,2,3,192,768]{4,3,2,1,0:T(8,128)(2,1)} custom-call(bf16[1280,1536]{1,0:T(8,128)(2,1)} %get-tuple-element.71.x_ref, bf16[1280,1536]{1,0:T(8,128)(2,1)} %get-tuple-element.72.gdy_ref, bf16[1280,768]{1,0:T(8,128)(2,1)} %get-tuple-element.73.h_ref, bf16[1280,768]{1,0:T(8,128)(2,1)} %get-tuple-element.74.dg_ref, ...), custom_call_target="tpu_custom_call" | custom-call | flops 9059696640 | bytes 20840448 | tf_op jit(solution)/shard_map/weight_grads/pallas_call | solution.py:302
  420.5 10.3 %collective-permute-done.29 = bf16[4,528,1536]{2,1,0:T(8,128)(2,1)S(1)} collective-permute-done((bf16[4,528,1536]{2,1,0:T(8,128)(2,1)}, bf16[4,528,1536]{2,1,0:T(8,128)(2,1)S(1)}, u32[]{:S(2)}, u32[]{:S(2)}) %collective-permute-start.29) | collective-permute-done | bytes 6488096 | tf_op jit(solution)/shard_map/ppermute | solution.py:45
  430.7 3.2 fusion.30
  437.5 34.8 %collective-permute-done.30 = bf16[528,1536]{1,0:T(8,128)(2,1)S(1)} collective-permute-done((bf16[528,1536]{1,0:T(8,128)(2,1)S(1)}, bf16[528,1536]{1,0:T(8,128)(2,1)S(1)}, u32[]{:S(2)}, u32[]{:S(2)}) %collective-permute-start.30) | collective-permute-done | bytes 1622048 | tf_op jit(solution)/shard_map/ppermute | solution.py:41
  472.3 33.9 %collective-permute-done.31 = bf16[528,1536]{1,0:T(8,128)(2,1)S(1)} collective-permute-done((bf16[528,1536]{1,0:T(8,128)(2,1)S(1)}, bf16[528,1536]{1,0:T(8,128)(2,1)S(1)}, u32[]{:S(2)}, u32[]{:S(2)}) %collective-permute-start.31) | collective-permute-done | bytes 1622048 | tf_op jit(solution)/shard_map/ppermute | solution.py:41
  507.4 4.1 fusion.9
  511.5 10.4 %collective-permute-done.33 = bf16[4,512,1536]{2,1,0:T(8,128)(2,1)} collective-permute-done((bf16[4,512,1536]{2,1,0:T(8,128)(2,1)}, bf16[4,512,1536]{2,1,0:T(8,128)(2,1)}, u32[]{:S(2)}, u32[]{:S(2)}) %collective-permute-start.33) | collective-permute-done | bytes 6291488 | tf_op jit(solution)/shard_map/ppermute | solution.py:45
  522.0 4.5 fusion.33
  530.8 3.5 multiply_reduce_fusion
  534.3 29.4 %collective-permute-done.34 = bf16[512,1536]{1,0:T(8,128)(2,1)S(1)} collective-permute-done((bf16[512,1536]{1,0:T(8,128)(2,1)S(1)}, bf16[512,1536]{1,0:T(8,128)(2,1)S(1)}, u32[]{:S(2)}, u32[]{:S(2)}) %collective-permute-start.34) | collective-permute-done | bytes 1572896 | tf_op jit(solution)/shard_map/ppermute | solution.py:41
  563.7 32.5 %collective-permute-done.35 = bf16[512,1536]{1,0:T(8,128)(2,1)S(1)} collective-permute-done((bf16[512,1536]{1,0:T(8,128)(2,1)S(1)}, bf16[512,1536]{1,0:T(8,128)(2,1)S(1)}, u32[]{:S(2)}, u32[]{:S(2)}) %collective-permute-start.35) | collective-permute-done | bytes 1572896 | tf_op jit(solution)/shard_map/ppermute | solution.py:41
  597.3 5.1 multiply_add_fusion
  602.4 3.8 convolution_convert_fusion.2.dout_ref
  606.2 28.8 %attention_back.1 = (bf16[512,1536]{1,0:T(8,128)(2,1)}, f32[512,256]{1,0:T(8,128)}, f32[512,256]{1,0:T(8,128)}, f32[512,256]{1,0:T(8,128)}, f32[512,256]{1,0:T(8,128)}) custom-call(s32[1]{0:T(128)} %bitcast.1.place, bf16[512,1536]{1,0:T(8,128)(2,1)} %get-tuple-element.64.q_ref, bf16[512,1536]{1,0:T(8,128)(2,1)} %convolution_convert_fusion.2.dout_ref, ...), custom_call_target="tpu_custom_call" | custom-call | flops 8053063680 | bytes 6291456 | tf_op jit(solution)/shard_map/attention_back/pallas_call | solution.py:439
  646.3 6.8 fusion
  653.2 2.2 fusion.16
  655.4 2.8 copy.97
  658.9 8.0 convolution_convert_fusion.1
  666.9 11.2 %concatenate.63 = bf16[2,4,4,48,2176]{4,3,2,1,0:T(8,128)(2,1)} concatenate(bf16[2,4,4,48,2048]{4,3,2,1,0:T(8,128)(2,1)} %convolution_convert_fusion.1, bf16[2,4,4,48,16]{4,3,2,1,0:T(8,128)(2,1)S(1)} %bitcast.254, bf16[2,4,4,48,1]{4,3,2,1,0:T(8,128)(2,1)S(1)} %concatenate.66, bf16[2,4,4,48,1]{4,3,2,1,0:T(8,128)(2,1)S(1)} %copy-done.16, ...), dimensions={4} | concatenate | bytes 13369344 | tf_op jit(solution)/shard_map/concatenate | solution.py:649
  678.2 4.1 copy_bitcast_fusion
  682.3 2.0 collective-permute-start.38
  684.3 2.9 convolution_convert_fusion
  691.9 2.1 dynamic-slice_bitcast_fusion.1
  694.9 2.5 fusion.39
  700.9 2.2 fusion.45
  703.1 4.2 fusion.25
  708.4 5.3 collective-permute-done.46
  715.0 9.8 %collective-permute-done.47 = bf16[4,48,1536]{2,1,0:T(8,128)(2,1)S(1)} collective-permute-done((bf16[4,48,1536]{2,1,0:T(8,128)(2,1)S(1)}, bf16[4,48,1536]{2,1,0:T(8,128)(2,1)S(1)}, u32[]{:S(2)}, u32[]{:S(2)}) %collective-permute-start.47) | collective-permute-done | bytes 589856 | tf_op jit(solution)/shard_map/ppermute | solution.py:41
  724.8 3.7 collective-permute-start.41
  728.5 2.5 fusion.43
  732.6 4.3 maximum_convert_fusion
  736.8 7.5 collective-permute-done.39
  744.3 16.6 %collective-permute-done.40 = bf16[4,48,2176]{2,1,0:T(8,128)(2,1)} collective-permute-done((bf16[4,48,2176]{2,1,0:T(8,128)(2,1)}, bf16[4,48,2176]{2,1,0:T(8,128)(2,1)}, u32[]{:S(2)}, u32[]{:S(2)}) %collective-permute-start.40) | collective-permute-done | bytes 835616 | tf_op jit(solution)/shard_map/ppermute | solution.py:41
  762.2 3.6 fusion.29
  765.8 6.2 slice_bitcast_fusion
  775.6 5.3 fusion.15
  781.7 10.0 %reduce-scatter.5.cloned.1.call-done = bf16[1,48,2176]{2,1,0:T(8,128)(2,1)} async-done(((bf16[4,48,2176]{2,1,0:T(8,128)(2,1)}), bf16[1,48,2176]{2,1,0:T(8,128)(2,1)}) %reduce-scatter.5.cloned.1.call-update) | async-done | bytes 208912 | tf_op jit(solution)/shard_map/reduce_scatter | solution.py:476
  796.4 3.7 collective-permute-done.42
  800.0 3.8 collective-permute-done.43
  (241 shorter events, 88.9 us)
Async XLA Ops:
  7.2 276.7 %all-gather.7.cloned.1.call-start = ((), (), s32[]{:S(2)}) async-start(), calls=%async_computation.8 | async-start | bytes 15925248 | tf_op jit(solution)/shard_map/all_gather | solution.py:555
  33.2 66.3 %copy-start.4 = (bf16[1,512,1536]{2,1,0:T(8,128)(2,1)S(1)}, bf16[1,512,1536]{2,1,0:T(8,128)(2,1)}, u32[]{:S(2)}) copy-start(bf16[1,512,1536]{2,1,0:T(8,128)(2,1)} %param.14) | copy-start | bytes 4718596
  33.2 317.4 %all-gather.9.cloned.1.call-start = ((), (), s32[]{:S(2)}) async-start(), calls=%async_computation.9 | async-start | bytes 15925248 | tf_op jit(solution)/shard_map/all_gather | solution.py:555
  33.9 656.1 %reduce-scatter.11.cloned.1.call-start = ((), (), s32[]{:S(2)}) async-start(), calls=%async_computation.7 | async-start | bytes 8847360 | tf_op jit(solution)/shard_map/reduce_scatter | solution.py:608
  64.8 54.1 %copy-start.10 = (bf16[192,2176]{1,0:T(8,128)(2,1)}, bf16[192,2176]{1,0:T(8,128)(2,1)S(1)}, u32[]{:S(2)}) copy-start(bf16[192,2176]{1,0:T(8,128)(2,1)S(1)} %all-gather) | copy-start | bytes 2506756
  64.9 22.6 %collective-permute-start.2 = (bf16[4,48,2176]{2,1,0:T(8,128)(2,1)S(1)}, bf16[4,48,2176]{2,1,0:T(8,128)(2,1)}, u32[]{:S(2)}, u32[]{:S(2)}) collective-permute-start(bf16[4,48,2176]{2,1,0:T(8,128)(2,1)S(1)} %bitcast.248), channel_id=1, source_target_pairs={{0,24},{8,16},{16,8},{24,0},{1,25},{9,17},{17,9},{25,1},{2,26},{10... | collective-permute-start | bytes 2506760 | tf_op jit(solution)/shard_map/ppermute | solution.py:41
  67.3 31.6 %collective-permute-start = (bf16[4,48,2176]{2,1,0:T(8,128)(2,1)S(1)}, bf16[4,48,2176]{2,1,0:T(8,128)(2,1)}, u32[]{:S(2)}, u32[]{:S(2)}) collective-permute-start(bf16[4,48,2176]{2,1,0:T(8,128)(2,1)S(1)} %bitcast.249), channel_id=1, source_target_pairs={{0,8},{8,0},{16,24},{24,16},{1,9},{9,1},{17,25},{25,17},{2,10},{10... | collective-permute-start | bytes 2506760 | tf_op jit(solution)/shard_map/ppermute | solution.py:41
  67.9 31.1 %collective-permute-start.1 = (bf16[4,48,2176]{2,1,0:T(8,128)(2,1)S(1)}, bf16[4,48,2176]{2,1,0:T(8,128)(2,1)}, u32[]{:S(2)}, u32[]{:S(2)}) collective-permute-start(bf16[4,48,2176]{2,1,0:T(8,128)(2,1)S(1)} %bitcast.250), channel_id=1, source_target_pairs={{0,16},{8,24},{16,0},{24,8},{1,17},{9,25},{17,1},{25,9},{2,18},{10... | collective-permute-start | bytes 2506760 | tf_op jit(solution)/shard_map/ppermute | solution.py:41
  68.3 31.5 %collective-permute-start.3 = (bf16[4,48,2176]{2,1,0:T(8,128)(2,1)S(1)}, bf16[4,48,2176]{2,1,0:T(8,128)(2,1)}, u32[]{:S(2)}, u32[]{:S(2)}) collective-permute-start(bf16[4,48,2176]{2,1,0:T(8,128)(2,1)S(1)} %bitcast.251), channel_id=1, source_target_pairs={{0,4},{4,0},{1,5},{5,1},{2,6},{6,2},{3,7},{7,3},{8,12},{12,8},{9,1... | collective-permute-start | bytes 2506760 | tf_op jit(solution)/shard_map/ppermute | solution.py:45
  87.5 19.5 %collective-permute-start.10 = (bf16[4,48,1536]{2,1,0:T(8,128)(2,1)}, bf16[4,48,1536]{2,1,0:T(8,128)(2,1)S(1)}, u32[]{:S(2)}, u32[]{:S(2)}) collective-permute-start(bf16[4,48,1536]{2,1,0:T(8,128)(2,1)} %bitcast.9.refs_0_), channel_id=1, source_target_pairs={{0,24},{8,16},{16,8},{24,0},{1,25},{9,17},{17,9},{25,1},{2,26},{10... | collective-permute-start | bytes 1769480 | tf_op jit(solution)/shard_map/ppermute | solution.py:41
  90.0 28.5 %collective-permute-start.6 = (bf16[4,48,2176]{2,1,0:T(8,128)(2,1)}, bf16[4,48,2176]{2,1,0:T(8,128)(2,1)}, u32[]{:S(2)}, u32[]{:S(2)}) collective-permute-start(bf16[4,48,2176]{2,1,0:T(8,128)(2,1)} %collective-permute-done.2.refs_3_), channel_id=1, source_target_pairs={{0,4},{4,0},{1,5},{5,1},{2,6},{6,2},{3,7},{7,3},{8,12},{12,8},{9,1... | collective-permute-start | bytes 2506760 | tf_op jit(solution)/shard_map/ppermute | solution.py:45
  98.9 19.8 %collective-permute-start.4 = (bf16[4,48,2176]{2,1,0:T(8,128)(2,1)}, bf16[4,48,2176]{2,1,0:T(8,128)(2,1)}, u32[]{:S(2)}, u32[]{:S(2)}) collective-permute-start(bf16[4,48,2176]{2,1,0:T(8,128)(2,1)} %collective-permute-done.refs_1_), channel_id=1, source_target_pairs={{0,4},{4,0},{1,5},{5,1},{2,6},{6,2},{3,7},{7,3},{8,12},{12,8},{9,1... | collective-permute-start | bytes 2506760 | tf_op jit(solution)/shard_map/ppermute | solution.py:45
  99.0 19.9 %collective-permute-start.5 = (bf16[4,48,2176]{2,1,0:T(8,128)(2,1)}, bf16[4,48,2176]{2,1,0:T(8,128)(2,1)}, u32[]{:S(2)}, u32[]{:S(2)}) collective-permute-start(bf16[4,48,2176]{2,1,0:T(8,128)(2,1)} %collective-permute-done.1.refs_2_), channel_id=1, source_target_pairs={{0,4},{4,0},{1,5},{5,1},{2,6},{6,2},{3,7},{7,3},{8,12},{12,8},{9,1... | collective-permute-start | bytes 2506760 | tf_op jit(solution)/shard_map/ppermute | solution.py:45
  99.9 18.0 %collective-permute-start.8 = (bf16[4,48,1536]{2,1,0:T(8,128)(2,1)}, bf16[4,48,1536]{2,1,0:T(8,128)(2,1)}, u32[]{:S(2)}, u32[]{:S(2)}) collective-permute-start(bf16[4,48,1536]{2,1,0:T(8,128)(2,1)} %bitcast.9.refs_0_), channel_id=1, source_target_pairs={{0,8},{8,0},{16,24},{24,16},{1,9},{9,1},{17,25},{25,17},{2,10},{10... | collective-permute-start | bytes 1769480 | tf_op jit(solution)/shard_map/ppermute | solution.py:41
  107.0 11.2 %collective-permute-start.9 = (bf16[4,48,1536]{2,1,0:T(8,128)(2,1)}, bf16[4,48,1536]{2,1,0:T(8,128)(2,1)}, u32[]{:S(2)}, u32[]{:S(2)}) collective-permute-start(bf16[4,48,1536]{2,1,0:T(8,128)(2,1)} %bitcast.9.refs_0_), channel_id=1, source_target_pairs={{0,16},{8,24},{16,0},{24,8},{1,17},{9,25},{17,1},{25,9},{2,18},{10... | collective-permute-start | bytes 1769480 | tf_op jit(solution)/shard_map/ppermute | solution.py:41
  117.9 23.2 %collective-permute-start.11 = (bf16[4,48,1536]{2,1,0:T(8,128)(2,1)}, bf16[4,48,1536]{2,1,0:T(8,128)(2,1)}, u32[]{:S(2)}, u32[]{:S(2)}) collective-permute-start(bf16[4,48,1536]{2,1,0:T(8,128)(2,1)} %bitcast.9.refs_0_), channel_id=1, source_target_pairs={{0,4},{4,0},{1,5},{5,1},{2,6},{6,2},{3,7},{7,3},{8,12},{12,8},{9,1... | collective-permute-start | bytes 1769480 | tf_op jit(solution)/shard_map/ppermute | solution.py:45
  118.2 24.1 %collective-permute-start.14 = (bf16[4,48,1536]{2,1,0:T(8,128)(2,1)}, bf16[4,48,1536]{2,1,0:T(8,128)(2,1)}, u32[]{:S(2)}, u32[]{:S(2)}) collective-permute-start(bf16[4,48,1536]{2,1,0:T(8,128)(2,1)} %copy-done.17), channel_id=1, source_target_pairs={{0,4},{4,0},{1,5},{5,1},{2,6},{6,2},{3,7},{7,3},{8,12},{12,8},{9,1... | collective-permute-start | bytes 1769480 | tf_op jit(solution)/shard_map/ppermute | solution.py:45
  118.4 25.4 %collective-permute-start.12 = (bf16[4,48,1536]{2,1,0:T(8,128)(2,1)}, bf16[4,48,1536]{2,1,0:T(8,128)(2,1)}, u32[]{:S(2)}, u32[]{:S(2)}) collective-permute-start(bf16[4,48,1536]{2,1,0:T(8,128)(2,1)} %collective-permute-done.8.refs_1_), channel_id=1, source_target_pairs={{0,4},{4,0},{1,5},{5,1},{2,6},{6,2},{3,7},{7,3},{8,12},{12,8},{9,1... | collective-permute-start | bytes 1769480 | tf_op jit(solution)/shard_map/ppermute | solution.py:45
  118.7 25.9 %collective-permute-start.13 = (bf16[4,48,1536]{2,1,0:T(8,128)(2,1)}, bf16[4,48,1536]{2,1,0:T(8,128)(2,1)}, u32[]{:S(2)}, u32[]{:S(2)}) collective-permute-start(bf16[4,48,1536]{2,1,0:T(8,128)(2,1)} %collective-permute-done.9.refs_2_), channel_id=1, source_target_pairs={{0,4},{4,0},{1,5},{5,1},{2,6},{6,2},{3,7},{7,3},{8,12},{12,8},{9,1... | collective-permute-start | bytes 1769480 | tf_op jit(solution)/shard_map/ppermute | solution.py:45
  137.4 12.5 %collective-permute-start.7 = (bf16[512,512]{1,0:T(8,128)(2,1)S(1)}, bf16[512,512]{1,0:T(8,128)(2,1)S(1)}, u32[]{:S(2)}, u32[]{:S(2)}) collective-permute-start(bf16[512,512]{1,0:T(8,128)(2,1)S(1)} %pad_maximum_fusion.7.ko_ref.vo_ref), channel_id=1, source_target_pairs={{0,4},{1,5},{2,6},{3,7},{8,12},{9,13},{10,14},{11,15},{16,20},{17,... | collective-permute-start | bytes 1572872 | tf_op jit(solution)/shard_map/ppermute | solution.py:583
  141.1 38.3 %collective-permute-start.22 = (bf16[512,1536]{1,0:T(8,128)(2,1)}, bf16[512,1536]{1,0:T(8,128)(2,1)}, u32[]{:S(2)}, u32[]{:S(2)}) collective-permute-start(bf16[512,1536]{1,0:T(8,128)(2,1)} %bitcast.14.refs_8_), channel_id=1, source_target_pairs={{0,8},{8,0},{16,24},{24,16},{1,9},{9,1},{17,25},{25,17},{2,10},{10... | collective-permute-start | bytes 4718600 | tf_op jit(solution)/shard_map/ppermute | solution.py:41
  142.4 68.6 %collective-permute-start.23 = (bf16[512,1536]{1,0:T(8,128)(2,1)}, bf16[512,1536]{1,0:T(8,128)(2,1)}, u32[]{:S(2)}, u32[]{:S(2)}) collective-permute-start(bf16[512,1536]{1,0:T(8,128)(2,1)} %bitcast.14.refs_8_), channel_id=1, source_target_pairs={{0,16},{8,24},{16,0},{24,8},{1,17},{9,25},{17,1},{25,9},{2,18},{10... | collective-permute-start | bytes 4718600 | tf_op jit(solution)/shard_map/ppermute | solution.py:41
  143.8 70.1 %collective-permute-start.24 = (bf16[512,1536]{1,0:T(8,128)(2,1)}, bf16[512,1536]{1,0:T(8,128)(2,1)}, u32[]{:S(2)}, u32[]{:S(2)}) collective-permute-start(bf16[512,1536]{1,0:T(8,128)(2,1)} %bitcast.14.refs_8_), channel_id=1, source_target_pairs={{0,24},{8,16},{16,8},{24,0},{1,25},{9,17},{17,9},{25,1},{2,26},{10... | collective-permute-start | bytes 4718600 | tf_op jit(solution)/shard_map/ppermute | solution.py:41
  144.7 69.2 %collective-permute-start.25 = (bf16[512,1536]{1,0:T(8,128)(2,1)}, bf16[512,1536]{1,0:T(8,128)(2,1)}, u32[]{:S(2)}, u32[]{:S(2)}) collective-permute-start(bf16[512,1536]{1,0:T(8,128)(2,1)} %bitcast.14.refs_8_), channel_id=1, source_target_pairs={{0,4},{4,0},{1,5},{5,1},{2,6},{6,2},{3,7},{7,3},{8,12},{12,8},{9,1... | collective-permute-start | bytes 4718600 | tf_op jit(solution)/shard_map/ppermute | solution.py:45
  176.4 106.8 %copy-start.26 = (s32[2]{0:T(128)S(1)}, s32[2]{0:T(128)}, u32[]{:S(2)}) copy-start(s32[2]{0:T(128)} %constant.334.clone) | copy-start | bytes 28
  178.2 69.1 %collective-permute-start.15 = (bf16[528,1536]{1,0:T(8,128)(2,1)S(1)}, bf16[528,1536]{1,0:T(8,128)(2,1)}, u32[]{:S(2)}, u32[]{:S(2)}) collective-permute-start(bf16[528,1536]{1,0:T(8,128)(2,1)S(1)} %maximum_maximum_fusion.refs_0_), channel_id=1, source_target_pairs={{0,8},{8,0},{16,24},{24,16},{1,9},{9,1},{17,25},{25,17},{2,10},{10... | collective-permute-start | bytes 4866056 | tf_op jit(solution)/shard_map/ppermute | solution.py:41
  179.4 100.7 %collective-permute-start.16 = (bf16[528,1536]{1,0:T(8,128)(2,1)S(1)}, bf16[528,1536]{1,0:T(8,128)(2,1)}, u32[]{:S(2)}, u32[]{:S(2)}) collective-permute-start(bf16[528,1536]{1,0:T(8,128)(2,1)S(1)} %maximum_maximum_fusion.refs_0_), channel_id=1, source_target_pairs={{0,16},{8,24},{16,0},{24,8},{1,17},{9,25},{17,1},{25,9},{2,18},{10... | collective-permute-start | bytes 4866056 | tf_op jit(solution)/shard_map/ppermute | solution.py:41
  210.9 70.6 %collective-permute-start.17 = (bf16[528,1536]{1,0:T(8,128)(2,1)S(1)}, bf16[528,1536]{1,0:T(8,128)(2,1)}, u32[]{:S(2)}, u32[]{:S(2)}) collective-permute-start(bf16[528,1536]{1,0:T(8,128)(2,1)S(1)} %maximum_maximum_fusion.refs_0_), channel_id=1, source_target_pairs={{0,24},{8,16},{16,8},{24,0},{1,25},{9,17},{17,9},{25,1},{2,26},{10... | collective-permute-start | bytes 4866056 | tf_op jit(solution)/shard_map/ppermute | solution.py:41
  213.9 67.6 %collective-permute-start.18 = (bf16[528,1536]{1,0:T(8,128)(2,1)S(1)}, bf16[528,1536]{1,0:T(8,128)(2,1)S(1)}, u32[]{:S(2)}, u32[]{:S(2)}) collective-permute-start(bf16[528,1536]{1,0:T(8,128)(2,1)S(1)} %maximum_maximum_fusion.refs_0_), channel_id=1, source_target_pairs={{0,4},{4,0},{1,5},{5,1},{2,6},{6,2},{3,7},{7,3},{8,12},{12,8},{9,1... | collective-permute-start | bytes 4866056 | tf_op jit(solution)/shard_map/ppermute | solution.py:45
  213.9 69.3 %collective-permute-start.26 = (bf16[512,1536]{1,0:T(8,128)(2,1)}, bf16[512,1536]{1,0:T(8,128)(2,1)}, u32[]{:S(2)}, u32[]{:S(2)}) collective-permute-start(bf16[512,1536]{1,0:T(8,128)(2,1)} %collective-permute-done.22.refs_9_), channel_id=1, source_target_pairs={{0,4},{4,0},{1,5},{5,1},{2,6},{6,2},{3,7},{7,3},{8,12},{12,8},{9,1... | collective-permute-start | bytes 4718600 | tf_op jit(solution)/shard_map/ppermute | solution.py:45
  247.3 47.1 %collective-permute-start.19 = (bf16[528,1536]{1,0:T(8,128)(2,1)}, bf16[528,1536]{1,0:T(8,128)(2,1)}, u32[]{:S(2)}, u32[]{:S(2)}) collective-permute-start(bf16[528,1536]{1,0:T(8,128)(2,1)} %collective-permute-done.15.refs_1_), channel_id=1, source_target_pairs={{0,4},{4,0},{1,5},{5,1},{2,6},{6,2},{3,7},{7,3},{8,12},{12,8},{9,1... | collective-permute-start | bytes 4866056 | tf_op jit(solution)/shard_map/ppermute | solution.py:45
  280.2 14.2 %collective-permute-start.20 = (bf16[528,1536]{1,0:T(8,128)(2,1)}, bf16[528,1536]{1,0:T(8,128)(2,1)}, u32[]{:S(2)}, u32[]{:S(2)}) collective-permute-start(bf16[528,1536]{1,0:T(8,128)(2,1)} %collective-permute-done.16.refs_2_), channel_id=1, source_target_pairs={{0,4},{4,0},{1,5},{5,1},{2,6},{6,2},{3,7},{7,3},{8,12},{12,8},{9,1... | collective-permute-start | bytes 4866056 | tf_op jit(solution)/shard_map/ppermute | solution.py:45
  281.5 12.9 %collective-permute-start.21 = (bf16[528,1536]{1,0:T(8,128)(2,1)}, bf16[528,1536]{1,0:T(8,128)(2,1)}, u32[]{:S(2)}, u32[]{:S(2)}) collective-permute-start(bf16[528,1536]{1,0:T(8,128)(2,1)} %collective-permute-done.17.refs_3_), channel_id=1, source_target_pairs={{0,4},{4,0},{1,5},{5,1},{2,6},{6,2},{3,7},{7,3},{8,12},{12,8},{9,1... | collective-permute-start | bytes 4866056 | tf_op jit(solution)/shard_map/ppermute | solution.py:45
  282.7 11.7 %collective-permute-start.27 = (bf16[512,1536]{1,0:T(8,128)(2,1)}, bf16[512,1536]{1,0:T(8,128)(2,1)}, u32[]{:S(2)}, u32[]{:S(2)}) collective-permute-start(bf16[512,1536]{1,0:T(8,128)(2,1)} %collective-permute-done.23.refs_10_), channel_id=1, source_target_pairs={{0,4},{4,0},{1,5},{5,1},{2,6},{6,2},{3,7},{7,3},{8,12},{12,8},{9,1... | collective-permute-start | bytes 4718600 | tf_op jit(solution)/shard_map/ppermute | solution.py:45
  283.2 11.2 %collective-permute-start.28 = (bf16[512,1536]{1,0:T(8,128)(2,1)}, bf16[512,1536]{1,0:T(8,128)(2,1)}, u32[]{:S(2)}, u32[]{:S(2)}) collective-permute-start(bf16[512,1536]{1,0:T(8,128)(2,1)} %collective-permute-done.24.refs_11_), channel_id=1, source_target_pairs={{0,4},{4,0},{1,5},{5,1},{2,6},{6,2},{3,7},{7,3},{8,12},{12,8},{9,1... | collective-permute-start | bytes 4718600 | tf_op jit(solution)/shard_map/ppermute | solution.py:45
  419.8 272.1 %reduce-scatter.9.cloned.1.call-start = ((), (), s32[]{:S(2)}) async-start(), calls=%async_computation.6 | async-start | bytes 8847360 | tf_op jit(solution)/shard_map/reduce_scatter | solution.py:608
  419.8 10.9 %collective-permute-start.29 = (bf16[4,528,1536]{2,1,0:T(8,128)(2,1)}, bf16[4,528,1536]{2,1,0:T(8,128)(2,1)S(1)}, u32[]{:S(2)}, u32[]{:S(2)}) collective-permute-start(bf16[4,528,1536]{2,1,0:T(8,128)(2,1)} %get-tuple-element.62), channel_id=1, source_target_pairs={{0,4},{4,0},{1,5},{5,1},{2,6},{6,2},{3,7},{7,3},{8,12},{12,8},{9,1... | collective-permute-start | bytes 19464200 | tf_op jit(solution)/shard_map/ppermute | solution.py:45
  433.9 38.3 %collective-permute-start.30 = (bf16[528,1536]{1,0:T(8,128)(2,1)S(1)}, bf16[528,1536]{1,0:T(8,128)(2,1)S(1)}, u32[]{:S(2)}, u32[]{:S(2)}) collective-permute-start(bf16[528,1536]{1,0:T(8,128)(2,1)S(1)} %get-tuple-element.134), channel_id=1, source_target_pairs={{0,8},{8,0},{16,24},{24,16},{1,9},{9,1},{17,25},{25,17},{2,10},{10... | collective-permute-start | bytes 4866056 | tf_op jit(solution)/shard_map/ppermute | solution.py:41
  435.0 71.1 %collective-permute-start.31 = (bf16[528,1536]{1,0:T(8,128)(2,1)S(1)}, bf16[528,1536]{1,0:T(8,128)(2,1)S(1)}, u32[]{:S(2)}, u32[]{:S(2)}) collective-permute-start(bf16[528,1536]{1,0:T(8,128)(2,1)S(1)} %get-tuple-element.136), channel_id=1, source_target_pairs={{0,16},{8,24},{16,0},{24,8},{1,17},{9,25},{17,1},{25,9},{2,18},{10... | collective-permute-start | bytes 4866056 | tf_op jit(solution)/shard_map/ppermute | solution.py:41
  436.6 70.8 %collective-permute-start.32 = (bf16[528,1536]{1,0:T(8,128)(2,1)S(1)}, bf16[528,1536]{1,0:T(8,128)(2,1)S(1)}, u32[]{:S(2)}, u32[]{:S(2)}) collective-permute-start(bf16[528,1536]{1,0:T(8,128)(2,1)S(1)} %get-tuple-element.135), channel_id=1, source_target_pairs={{0,24},{8,16},{16,8},{24,0},{1,25},{9,17},{17,9},{25,1},{2,26},{10... | collective-permute-start | bytes 4866056 | tf_op jit(solution)/shard_map/ppermute | solution.py:41
  511.5 10.5 %collective-permute-start.33 = (bf16[4,512,1536]{2,1,0:T(8,128)(2,1)}, bf16[4,512,1536]{2,1,0:T(8,128)(2,1)}, u32[]{:S(2)}, u32[]{:S(2)}) collective-permute-start(bf16[4,512,1536]{2,1,0:T(8,128)(2,1)} %get-tuple-element.63), channel_id=1, source_target_pairs={{0,4},{4,0},{1,5},{5,1},{2,6},{6,2},{3,7},{7,3},{8,12},{12,8},{9,1... | collective-permute-start | bytes 18874376 | tf_op jit(solution)/shard_map/ppermute | solution.py:45
  511.5 260.6 %reduce-scatter.7.cloned.1.call-start = ((), (), s32[]{:S(2)}) async-start(), calls=%async_computation.5 | async-start | bytes 737280 | tf_op jit(solution)/shard_map/reduce_scatter | solution.py:476
  526.4 37.3 %collective-permute-start.34 = (bf16[512,1536]{1,0:T(8,128)(2,1)S(1)}, bf16[512,1536]{1,0:T(8,128)(2,1)S(1)}, u32[]{:S(2)}, u32[]{:S(2)}) collective-permute-start(bf16[512,1536]{1,0:T(8,128)(2,1)S(1)} %get-tuple-element.137), channel_id=1, source_target_pairs={{0,8},{8,0},{16,24},{24,16},{1,9},{9,1},{17,25},{25,17},{2,10},{10... | collective-permute-start | bytes 4718600 | tf_op jit(solution)/shard_map/ppermute | solution.py:41
  527.4 68.8 %collective-permute-start.35 = (bf16[512,1536]{1,0:T(8,128)(2,1)S(1)}, bf16[512,1536]{1,0:T(8,128)(2,1)S(1)}, u32[]{:S(2)}, u32[]{:S(2)}) collective-permute-start(bf16[512,1536]{1,0:T(8,128)(2,1)S(1)} %get-tuple-element.139), channel_id=1, source_target_pairs={{0,16},{8,24},{16,0},{24,8},{1,17},{9,25},{17,1},{25,9},{2,18},{10... | collective-permute-start | bytes 4718600 | tf_op jit(solution)/shard_map/ppermute | solution.py:41
  528.8 68.5 %collective-permute-start.36 = (bf16[512,1536]{1,0:T(8,128)(2,1)S(1)}, bf16[512,1536]{1,0:T(8,128)(2,1)S(1)}, u32[]{:S(2)}, u32[]{:S(2)}) collective-permute-start(bf16[512,1536]{1,0:T(8,128)(2,1)S(1)} %get-tuple-element.138), channel_id=1, source_target_pairs={{0,24},{8,16},{16,8},{24,0},{1,25},{9,17},{17,9},{25,1},{2,26},{10... | collective-permute-start | bytes 4718600 | tf_op jit(solution)/shard_map/ppermute | solution.py:41
  530.8 71.6 %slice-start = ((s8[4718592]{0:T(1024)(128)(4,1)}), s8[4194304]{0:T(1024)(128)(4,1)S(1)}, s32[]{:S(2)}) async-start(s8[4718592]{0:T(1024)(128)(4,1)} %bitcast.242), calls=%async_computation.10 | async-start | bytes 8388608
  637.2 4.8 collective-permute-start.37
  682.3 20.9 %collective-permute-start.38 = (bf16[4,4,48,2176]{3,2,0,1:T(8,128)(2,1)}, bf16[4,4,48,2176]{3,2,0,1:T(8,128)(2,1)}, u32[]{:S(2)}, u32[]{:S(2)}) collective-permute-start(bf16[4,4,48,2176]{3,2,0,1:T(8,128)(2,1)} %copy_bitcast_fusion), channel_id=1, source_target_pairs={{0,4},{4,0},{1,5},{5,1},{2,6},{6,2},{3,7},{7,3},{8,12},{12,8},{9,1... | collective-permute-start | bytes 10027016 | tf_op jit(solution)/shard_map/ppermute | solution.py:45
  690.0 4.9 collective-permute-start.45
  691.3 8.4 %collective-permute-start.53 = (bf16[3,192,768]{2,1,0:T(8,128)(2,1)S(1)}, bf16[3,192,768]{2,1,0:T(8,128)(2,1)}, u32[]{:S(2)}, u32[]{:S(2)}) collective-permute-start(bf16[3,192,768]{2,1,0:T(8,128)(2,1)S(1)} %dynamic-slice_bitcast_fusion), channel_id=1, source_target_pairs={{0,4},{4,0},{1,5},{5,1},{2,6},{6,2},{3,7},{7,3},{8,12},{12,8},{9,1... | collective-permute-start | bytes 2654216 | tf_op jit(solution)/shard_map/ppermute | solution.py:45
  694.0 37.0 %collective-permute-start.52 = (bf16[3,192,768]{2,1,0:T(8,128)(2,1)}, bf16[3,192,768]{2,1,0:T(8,128)(2,1)}, u32[]{:S(2)}, u32[]{:S(2)}) collective-permute-start(bf16[3,192,768]{2,1,0:T(8,128)(2,1)} %dynamic-slice_bitcast_fusion.1), channel_id=1, source_target_pairs={{0,4},{4,0},{1,5},{5,1},{2,6},{6,2},{3,7},{7,3},{8,12},{12,8},{9,1... | collective-permute-start | bytes 2654216 | tf_op jit(solution)/shard_map/ppermute | solution.py:45
  697.4 16.2 %collective-permute-start.46 = (bf16[4,48,1536]{2,1,0:T(8,128)(2,1)S(1)}, bf16[4,48,1536]{2,1,0:T(8,128)(2,1)S(1)}, u32[]{:S(2)}, u32[]{:S(2)}) collective-permute-start(bf16[4,48,1536]{2,1,0:T(8,128)(2,1)S(1)} %get-tuple-element.146), channel_id=1, source_target_pairs={{0,8},{8,0},{16,24},{24,16},{1,9},{9,1},{17,25},{25,17},{2,10},{10... | collective-permute-start | bytes 1769480 | tf_op jit(solution)/shard_map/ppermute | solution.py:41
  698.5 26.3 %collective-permute-start.47 = (bf16[4,48,1536]{2,1,0:T(8,128)(2,1)S(1)}, bf16[4,48,1536]{2,1,0:T(8,128)(2,1)S(1)}, u32[]{:S(2)}, u32[]{:S(2)}) collective-permute-start(bf16[4,48,1536]{2,1,0:T(8,128)(2,1)S(1)} %get-tuple-element.148), channel_id=1, source_target_pairs={{0,16},{8,24},{16,0},{24,8},{1,17},{9,25},{17,1},{25,9},{2,18},{10... | collective-permute-start | bytes 1769480 | tf_op jit(solution)/shard_map/ppermute | solution.py:41
  699.7 28.8 %collective-permute-start.48 = (bf16[4,48,1536]{2,1,0:T(8,128)(2,1)S(1)}, bf16[4,48,1536]{2,1,0:T(8,128)(2,1)S(1)}, u32[]{:S(2)}, u32[]{:S(2)}) collective-permute-start(bf16[4,48,1536]{2,1,0:T(8,128)(2,1)S(1)} %get-tuple-element.147), channel_id=1, source_target_pairs={{0,24},{8,16},{16,8},{24,0},{1,25},{9,17},{17,9},{25,1},{2,26},{10... | collective-permute-start | bytes 1769480 | tf_op jit(solution)/shard_map/ppermute | solution.py:41
  707.3 37.0 %collective-permute-start.39 = (bf16[4,48,2176]{2,1,0:T(8,128)(2,1)}, bf16[4,48,2176]{2,1,0:T(8,128)(2,1)}, u32[]{:S(2)}, u32[]{:S(2)}) collective-permute-start(bf16[4,48,2176]{2,1,0:T(8,128)(2,1)} %get-tuple-element.140), channel_id=1, source_target_pairs={{0,8},{8,0},{16,24},{24,16},{1,9},{9,1},{17,25},{25,17},{2,10},{10... | collective-permute-start | bytes 2506760 | tf_op jit(solution)/shard_map/ppermute | solution.py:41
  713.6 47.3 %collective-permute-start.40 = (bf16[4,48,2176]{2,1,0:T(8,128)(2,1)}, bf16[4,48,2176]{2,1,0:T(8,128)(2,1)}, u32[]{:S(2)}, u32[]{:S(2)}) collective-permute-start(bf16[4,48,2176]{2,1,0:T(8,128)(2,1)} %get-tuple-element.142), channel_id=1, source_target_pairs={{0,16},{8,24},{16,0},{24,8},{1,17},{9,25},{17,1},{25,9},{2,18},{10... | collective-permute-start | bytes 2506760 | tf_op jit(solution)/shard_map/ppermute | solution.py:41
  724.8 37.5 %collective-permute-start.41 = (bf16[4,48,2176]{2,1,0:T(8,128)(2,1)}, bf16[4,48,2176]{2,1,0:T(8,128)(2,1)}, u32[]{:S(2)}, u32[]{:S(2)}) collective-permute-start(bf16[4,48,2176]{2,1,0:T(8,128)(2,1)} %get-tuple-element.141), channel_id=1, source_target_pairs={{0,24},{8,16},{16,8},{24,0},{1,25},{9,17},{17,9},{25,1},{2,26},{10... | collective-permute-start | bytes 2506760 | tf_op jit(solution)/shard_map/ppermute | solution.py:41
  731.0 60.8 %reduce-scatter.5.cloned.1.call-start = ((), (), s32[]{:S(2)}) async-start(), calls=%async_computation.4 | async-start | bytes 1044480 | tf_op jit(solution)/shard_map/reduce_scatter | solution.py:476
  772.1 8.8 %collective-permute-start.49 = (bf16[48,1536]{1,0:T(8,128)(2,1)}, bf16[48,1536]{1,0:T(8,128)(2,1)S(1)}, u32[]{:S(2)}, u32[]{:S(2)}) collective-permute-start(bf16[48,1536]{1,0:T(8,128)(2,1)} %bitcast.267), channel_id=1, source_target_pairs={{0,8},{8,0},{16,24},{24,16},{1,9},{9,1},{17,25},{25,17},{2,10},{10... | collective-permute-start | bytes 442376 | tf_op jit(solution)/shard_map/ppermute | solution.py:41
  773.0 7.9 collective-permute-start.50
  774.4 7.2 collective-permute-start.51
  791.7 8.3 %collective-permute-start.42 = (bf16[48,2176]{1,0:T(8,128)(2,1)}, bf16[48,2176]{1,0:T(8,128)(2,1)S(1)}, u32[]{:S(2)}, u32[]{:S(2)}) collective-permute-start(bf16[48,2176]{1,0:T(8,128)(2,1)} %bitcast.261), channel_id=1, source_target_pairs={{0,8},{8,0},{16,24},{24,16},{1,9},{9,1},{17,25},{25,17},{2,10},{10... | collective-permute-start | bytes 626696 | tf_op jit(solution)/shard_map/ppermute | solution.py:41
  793.2 10.7 %collective-permute-start.43 = (bf16[48,2176]{1,0:T(8,128)(2,1)}, bf16[48,2176]{1,0:T(8,128)(2,1)S(1)}, u32[]{:S(2)}, u32[]{:S(2)}) collective-permute-start(bf16[48,2176]{1,0:T(8,128)(2,1)} %bitcast.262), channel_id=1, source_target_pairs={{0,16},{8,24},{16,0},{24,8},{1,17},{9,25},{17,1},{25,9},{2,18},{10... | collective-permute-start | bytes 626696 | tf_op jit(solution)/shard_map/ppermute | solution.py:41
  794.7 9.2 %collective-permute-start.44 = (bf16[48,2176]{1,0:T(8,128)(2,1)}, bf16[48,2176]{1,0:T(8,128)(2,1)S(1)}, u32[]{:S(2)}, u32[]{:S(2)}) collective-permute-start(bf16[48,2176]{1,0:T(8,128)(2,1)} %bitcast.263), channel_id=1, source_target_pairs={{0,24},{8,16},{16,8},{24,0},{1,25},{9,17},{17,9},{25,1},{2,26},{10... | collective-permute-start | bytes 626696 | tf_op jit(solution)/shard_map/ppermute | solution.py:41
  (30 other events, 182.1 us)
Sparse Core Ops, SparseCore 0:
  33.3 136.4 all-gather.6
  171.5 128.8 all-gather.8
  419.9 125.6 reduce-scatter.10
  547.8 124.0 reduce-scatter.8
  731.1 22.9 reduce-scatter.6
  766.0 25.7 reduce-scatter.4

commit v2 on v1

--- a/solution.py
+++ b/solution.py
@@ -28,12 +28,27 @@
 VMEM_LIMIT = 60 * 1024 * 1024
 
 
+COST_SCALE = 1
+
+
+def cost(flops, bytes_accessed, transcendentals):
+    return pl.CostEstimate(
+        flops=flops // COST_SCALE,
+        bytes_accessed=bytes_accessed // COST_SCALE,
+        transcendentals=transcendentals // COST_SCALE,
+    )
+
+
 def dot(a, b, dims=((1,), (0,))):
     return lax.dot_general(a, b, (dims, ((), ())), preferred_element_type=f32)
 
 
 def after(value, *others):
     return lax.optimization_barrier((value,) + others)[0]
+
+
+def tie(*values):
+    return lax.optimization_barrier(values)
 
 
 def flip(value, step):
@@ -108,16 +123,57 @@
             scratch_shapes=[pltpu.SemaphoreType.DMA((2 * count,))],
         ),
         compiler_params=pltpu.CompilerParams(vmem_limit_bytes=VMEM_LIMIT),
-        cost_estimate=pl.CostEstimate(flops=0, bytes_accessed=2 * size, transcendentals=0),
+        cost_estimate=cost(flops=0, bytes_accessed=2 * size, transcendentals=0),
         name="assemble",
     )(jnp.stack([context, expert]).astype(jnp.int32), *own, *other)
     return out.reshape(2 * z * count * r, n)
 
 
+def halves_of(size):
+    return size // 2 if size < 32 else size // 32 * 16
+
+
+def fourth_block(one, two, *later):
+    cut = halves_of(one.shape[0])
+    first, second = flip(after(one[:cut], *later), 2), flip(after(two[cut:], *later), 1)
+    return jnp.concatenate([first, second], axis=0)
+
+
+def gather_blocks(block):
+    count = lax.axis_size("expert")
+    if count != 4:
+        return [block] + [flip(block, k) for k in range(1, count)]
+    one, two = flip(block, 1), flip(block, 2)
+    return [block, one, two, fourth_block(one, two)]
+
+
 def spread(block):
+    own = gather_blocks(block)
+    return own, [swap(b) for b in own]
+
+
+def scatter_blocks(parts, before=(), between=(), finish=()):
     count = lax.axis_size("expert")
-    own = [block] + [flip(block, k) for k in range(1, count)]
-    return own, [swap(b) for b in own]
+    if count != 4:
+        came = [flip(after(parts[k], *before), k) for k in range(1, count)]
+        return add_all(parts[0], came), came, came
+    cut = halves_of(parts[0].shape[0])
+    top, bottom = [p[:cut] for p in parts], [p[cut:] for p in parts]
+    top_sent = after(jnp.stack([top[1], top[3]]), *before)
+    bottom_sent = after(jnp.stack([bottom[2], bottom[3]]), *before)
+    top_came, bottom_came = flip(top_sent, 1), flip(bottom_sent, 2)
+    top_next = add_all(top[2], [top_came[1]]).astype(bf16)
+    bottom_next = add_all(bottom[1], [bottom_came[1]]).astype(bf16)
+    top_last = after(flip(after(top_next, *between), 2), *finish)
+    bottom_last = flip(after(bottom_next, *between), 1)
+    total = jnp.concatenate(
+        [
+            add_all(top[0], [top_came[0], top_last]),
+            add_all(bottom[0], [bottom_came[0], bottom_last]),
+        ],
+        axis=0,
+    )
+    return total, [top_came, bottom_came], [top_last, bottom_last]
 
 
 GELU_C = math.sqrt(2.0 / math.pi)
@@ -277,7 +333,7 @@
         compiler_params=pltpu.CompilerParams(
             dimension_semantics=("arbitrary",), vmem_limit_bytes=VMEM_LIMIT
         ),
-        cost_estimate=pl.CostEstimate(
+        cost_estimate=cost(
             flops=2 * macs, bytes_accessed=moved, transcendentals=total * FF
         ),
         name="experts",
@@ -310,7 +366,7 @@
         compiler_params=pltpu.CompilerParams(
             dimension_semantics=("arbitrary",), vmem_limit_bytes=VMEM_LIMIT
         ),
-        cost_estimate=pl.CostEstimate(
+        cost_estimate=cost(
             flops=6 * total * MODEL_WIDTH * FF,
             bytes_accessed=2 * (total * (2 * MODEL_WIDTH + 3 * FF) + 3 * MODEL_WIDTH * FF),
             transcendentals=0,
@@ -357,6 +413,56 @@
         log_ref[0, :, rows] = peak + jnp.log2(total)
 
 
+def key_value_kernel(x_ref, cos_ref, sin_ref, out_ref):
+    for h in range(KEY_VALUE_HEADS):
+        at = pl.ds(h * HEAD_SIZE, HEAD_SIZE)
+        x = x_ref[:, at]
+        out_ref[:, at] = (x * cos_ref[...] + roll_half(x) * sin_ref[...]).astype(bf16)
+    out_ref[:, KV_WIDTH:] = x_ref[:, KV_WIDTH:].astype(bf16)
+
+
+def key_value(qkv, cosine, sine):
+    tokens = qkv.shape[0]
+    table = pl.BlockSpec((tokens, HEAD_SIZE), lambda i: (0, 0))
+    return pl.pallas_call(
+        key_value_kernel,
+        out_shape=jax.ShapeDtypeStruct((tokens, 2 * KV_WIDTH), bf16),
+        grid=(1,),
+        in_specs=[
+            pl.BlockSpec((tokens, 2 * KV_WIDTH), lambda i: (0, Q_WIDTH // (2 * KV_WIDTH))),
+            table,
+            table,
+        ],
+        out_specs=pl.BlockSpec((tokens, 2 * KV_WIDTH), lambda i: (0, 0)),
+        cost_estimate=cost(
+            flops=tokens * KV_WIDTH * 4, bytes_accessed=tokens * KV_WIDTH * 14, transcendentals=0
+        ),
+        name="key_value",
+    )(qkv, cosine, sine)
+
+
+def key_value_back_kernel(near_ref, came_ref, cos_ref, sin_ref, out_ref):
+    for h in range(KEY_VALUE_HEADS):
+        at = pl.ds(h * HEAD_SIZE, HEAD_SIZE)
+        x = near_ref[:, at] + came_ref[:, at].astype(f32)
+        out_ref[:, at] = (x * cos_ref[...] - roll_half(x) * sin_ref[...]).astype(bf16)
+    out_ref[:, KV_WIDTH:] = (
+        near_ref[:, KV_WIDTH:] + came_ref[:, KV_WIDTH:].astype(f32)
+    ).astype(bf16)
+
+
+def key_value_back(near, came, cosine, sine):
+    tokens = near.shape[0]
+    return pl.pallas_call(
+        key_value_back_kernel,
+        out_shape=jax.ShapeDtypeStruct((tokens, 2 * KV_WIDTH), bf16),
+        cost_estimate=cost(
+            flops=tokens * KV_WIDTH * 6, bytes_accessed=tokens * KV_WIDTH * 18, transcendentals=0
+        ),
+        name="key_value_back",
+    )(near, came, cosine, sine)
+
+
 def attention_specs(tokens):
     head = pl.BlockSpec((tokens, HEAD_SIZE), lambda h, place: (0, h))
     key = pl.BlockSpec((tokens, HEAD_SIZE), lambda h, place: (0, h // GROUP))
@@ -386,7 +492,7 @@
         compiler_params=pltpu.CompilerParams(
             dimension_semantics=("arbitrary",), vmem_limit_bytes=VMEM_LIMIT
         ),
-        cost_estimate=pl.CostEstimate(
+        cost_estimate=cost(
             flops=4 * pairs * HEAD_SIZE, bytes_accessed=tokens * Q_WIDTH * 10, transcendentals=pairs
         ),
         name="attention",
@@ -395,13 +501,14 @@
 
 def attend_back_kernel(
     place, q_ref, dout_ref, ko_ref, vo_ref, kr_ref, vr_ref, log_ref, cos_ref, sin_ref,
-    dq_ref, dko_ref, dvo_ref, dkr_ref, dvr_ref,
+    dq_ref, near_ref, far_ref, dko_ref, dvo_ref, dkr_ref, dvr_ref,
 ):
     last = ((1,), (1,))
     first = ((0,), (0,))
     scale = 1.0 / math.sqrt(HEAD_SIZE)
-
-    @pl.when(lax.rem(pl.program_id(0), GROUP) == 0)
+    head = pl.program_id(0)
+
+    @pl.when(lax.rem(head, GROUP) == 0)
     def _():
         for ref in (dko_ref, dvo_ref, dkr_ref, dvr_ref):
             ref[...] = jnp.zeros_like(ref)
@@ -424,69 +531,107 @@
         inner = inner + jnp.sum(near * dnear, axis=0, keepdims=True)
         dfar = (far * (dfar - inner)).astype(bf16)
         dnear = (near * (dnear - inner)).astype(bf16)
-        dkr_ref[...] += dot(dfar, q) * scale
-        dko_ref[:seen, :] += dot(dnear, q) * scale
+        dkr_ref[...] += dot(dfar, q)
+        dko_ref[:seen, :] += dot(dnear, q)
         dq = dot(kr_ref[...], dfar, first) + dot(ko_ref[:seen, :], dnear, first)
         dq = dq.T * scale
         dq_ref[rows, :] = (dq * cos_ref[rows, :] - roll_half(dq) * sin_ref[rows, :]).astype(bf16)
+
+    for h in range(KEY_VALUE_HEADS):
+
+        @pl.when(head == (h + 1) * GROUP - 1)
+        def _(h=h):
+            key = pl.ds(h * HEAD_SIZE, HEAD_SIZE)
+            value = pl.ds(KV_WIDTH + h * HEAD_SIZE, HEAD_SIZE)
+            near_ref[:, key] = dko_ref[...] * scale
+            near_ref[:, value] = dvo_ref[...]
+            far_ref[:, key] = (dkr_ref[...] * scale).astype(bf16)
+            far_ref[:, value] = dvr_ref[...].astype(bf16)
 
 
 def attention_back(context, query, dmixed, near, far, logs, cosine, sine):
     tokens = query.shape[0]
     head, key, value, table, log = attention_specs(tokens)
     pairs = 2 * tokens * tokens * QUERY_HEADS
-    side = jax.ShapeDtypeStruct((tokens, KV_WIDTH), f32)
+    side = pl.BlockSpec((tokens, 2 * KV_WIDTH), lambda h, place: (0, 0))
     return pl.pallas_call(
         attend_back_kernel,
-        out_shape=(jax.ShapeDtypeStruct((tokens, Q_WIDTH), bf16), side, side, side, side),
+        out_shape=(
+            jax.ShapeDtypeStruct((tokens, Q_WIDTH), bf16),
+            jax.ShapeDtypeStruct((tokens, 2 * KV_WIDTH), f32),
+            jax.ShapeDtypeStruct((tokens, 2 * KV_WIDTH), bf16),
+        ),
         grid_spec=pltpu.PrefetchScalarGridSpec(
             num_scalar_prefetch=1,
             grid=(QUERY_HEADS,),
             in_specs=[head, head, key, value, key, value, log, table, table],
-            out_specs=(head, key, key, key, key),
+            out_specs=(head, side, side),
+            scratch_shapes=[pltpu.VMEM((tokens, HEAD_SIZE), f32)] * 4,
         ),
         compiler_params=pltpu.CompilerParams(
             dimension_semantics=("arbitrary",), vmem_limit_bytes=VMEM_LIMIT
         ),
-        cost_estimate=pl.CostEstimate(
+        cost_estimate=cost(
             flops=10 * pairs * HEAD_SIZE, bytes_accessed=tokens * Q_WIDTH * 8, transcendentals=pairs
         ),
         name="attention_back",
     )(context, query, dmixed, near, near, far, far, logs, cosine, sine)
 
 
-def reduce_dense(grad, context, expert):
+def swap_halves(grad, context):
+    z = lax.axis_size("dp")
     count = lax.axis_size("expert")
+    r = grad.shape[0] // (2 * z * count)
+    grad = grad.astype(bf16).reshape(2, z, count, r, grad.shape[1])
+    theirs = swap(lax.dynamic_index_in_dim(grad, 1 - context, 0, keepdims=False))
+    return lax.dynamic_index_in_dim(grad, context, 0, keepdims=False), theirs
+
+
+def dense_parts(halves, expert):
+    out = []
+    for k in range(lax.axis_size("expert")):
+        sums = []
+        for pair in halves:
+            a, b = (lax.dynamic_index_in_dim(p, expert ^ k, 1, keepdims=False) for p in pair)
+            sums.append(a.astype(f32) + b.astype(f32))
+        out.append(jnp.concatenate(sums, axis=-1).astype(bf16))
+    return out
+
+
+def line_step(grads, step, came):
     z = lax.axis_size("dp")
-    n = grad.shape[1]
-    r = grad.shape[0] // (2 * z * count)
-    grad = grad.astype(bf16).reshape(2, z, count, r, n)
-    theirs = swap(lax.dynamic_index_in_dim(grad, 1 - context, 0, keepdims=False))
-    mine = lax.dynamic_index_in_dim(grad, context, 0, keepdims=False)
-
-    def part(k):
-        at = expert ^ k
-        a = lax.dynamic_index_in_dim(mine, at, 1, keepdims=False)
-        b = lax.dynamic_index_in_dim(theirs, at, 1, keepdims=False)
-        return a.astype(f32) + b.astype(f32)
-
-    total = part(0)
-    for k in range(1, count):
-        total = total + flip(part(k).astype(bf16), k).astype(f32)
-    share = lax.psum_scatter(total.astype(bf16), "dp", scatter_dimension=0, tiled=False)
+    me = lax.axis_index("dp")
+
+    def part(at, arrived):
+        own = lax.dynamic_index_in_dim(grads, jnp.clip(at, 0, z - 1), 0, keepdims=False)
+        return own if arrived is None else add_all(own, [arrived]).astype(bf16)
+
+    up = part(z - step + me, came[0])
+    down = part(step + me - z, came[1])
+    return (
+        lax.ppermute(up, "dp", [(i, i + 1) for i in range(step)]),
+        lax.ppermute(down, "dp", [(i, i - 1) for i in range(z - step, z)]),
+    )
+
+
+def add_all(own, came):
+    total = own.astype(f32)
+    for c in came:
+        total = total + c.astype(f32)
+    return total
+
+
+def finish_dense(total, expert):
+    count = lax.axis_size("expert")
+    share = lax.psum_scatter(total, "dp", scatter_dimension=0, tiled=False)
     blocks = jnp.stack([share] + [flip(share, k) for k in range(1, count)])
     pieces = [lax.dynamic_index_in_dim(blocks, expert ^ e, 0, keepdims=False) for e in range(count)]
-    return jnp.concatenate(pieces, axis=0).astype(f32)
-
-
-def reduce_blocks(own, other):
-    count = own.shape[0]
+    return jnp.concatenate(pieces, axis=0).astype(f32), share
+
+
+def block_parts(own, other):
     came = swap(other)
-    parts = [own[k].astype(f32) + came[k].astype(f32) for k in range(count)]
-    total = parts[0]
-    for k in range(1, count):
-        total = total + flip(parts[k].astype(bf16), k).astype(f32)
-    return total
+    return [(own[i].astype(f32) + came[i].astype(f32)).astype(bf16) for i in range(own.shape[0])]
 
 
 def local(
@@ -522,16 +667,30 @@
         return jnp.concatenate(cut, axis=1)
 
     pad = jnp.zeros((rows, SMALL - experts_all - 2), f32)
-    first_pack = quarter(
-        [w_query, key_projection, value_projection, w_router, attn_gain[:, None], ffn_gain[:, None], pad]
-    )
-    second_pack = quarter([w_out])
-    first_z = lax.all_gather(first_pack, "dp", axis=0, tiled=False)
-    second_z = lax.all_gather(second_pack, "dp", axis=0, tiled=False)
-    own_one, other_one = spread(first_z)
-    own_two, other_two = spread(after(second_z, own_one[-1]))
+    pack = quarter(
+        [
+            w_query,
+            key_projection,
+            value_projection,
+            w_router,
+            attn_gain[:, None],
+            ffn_gain[:, None],
+            pad,
+            w_out,
+        ]
+    )
+    dense_z = lax.all_gather(pack, "dp", axis=0, tiled=False)
+    cut = Q_WIDTH + 2 * KV_WIDTH + SMALL
+    own_one, other_one = spread(dense_z[..., :cut])
+    dy_half = after(out_grad[0], *own_one[1:])
+    dy_first = [flip(dy_half, k) for k in ((1, 2) if count == 4 else range(1, count))]
+    own_two, other_two = spread(after(dense_z[..., cut:], *dy_first))
+    if count == 4:
+        dys_own = [dy_half, *dy_first, fourth_block(*dy_first, *own_two[1:])]
+    else:
+        dys_own = [dy_half, *dy_first]
+    dys_other = [swap(b) for b in dys_own]
     packed = assemble(own_one, other_one, context, expert)
-    out_w = assemble(own_two, other_two, context, expert)
     qkv_w = packed[:, : Q_WIDTH + 2 * KV_WIDTH]
     router_w = packed[:, Q_WIDTH + 2 * KV_WIDTH :][:, :experts_all]
     small = packed[:, Q_WIDTH + 2 * KV_WIDTH :].T
@@ -539,23 +698,16 @@
     gain_two = small[experts_all + 1].astype(f32)
 
     def chunk(j):
-        picked = slice(j, None, per_core)
-        return jnp.stack(
-            [
-                w_gate[picked].astype(bf16),
-                w_up[picked].astype(bf16),
-                jnp.swapaxes(w_down[picked], 1, 2).astype(bf16),
-            ],
-            axis=1,
-        )
+        parts = []
+        for at in range(j, EXP_DEV, per_core):
+            parts += [w_gate[at], w_up[at], w_down[at].T]
+        return jnp.concatenate([p.astype(bf16) for p in parts], axis=0)
 
     gathered = []
     for j in range(per_core):
-        sent = after(chunk(j), second_z)
-        gathered.append(lax.all_gather(sent, ("context", "dp"), axis=0, tiled=False))
-
-    dy_half = after(out_grad[0], own_two[-1])
-    dys_own, dys_other = spread(dy_half)
+        sent = after(chunk(j), dense_z)
+        came = lax.all_gather(sent, ("context", "dp"), axis=0, tiled=False)
+        gathered.append(came.reshape(2 * z, 2, 3, rows, FF))
 
     route_t = routes[0].T
     expert_ids = jnp.arange(experts_all, dtype=jnp.int32)
@@ -573,16 +725,11 @@
     cosine, sine = rope_tables(context * tokens, tokens, HEAD_SIZE)
     cos_wide = jnp.concatenate([cosine, cosine], axis=1)
     sin_wide = jnp.concatenate([-sine, sine], axis=1)
-    key = rotate(
-        qkv[:, Q_WIDTH : Q_WIDTH + KV_WIDTH].reshape(tokens, KEY_VALUE_HEADS, HEAD_SIZE),
-        cosine,
-        sine,
-    ).astype(bf16)
-    value = qkv[:, Q_WIDTH + KV_WIDTH :].astype(bf16)
-    near = jnp.concatenate([key.reshape(tokens, KV_WIDTH), value], axis=1)
+    near = key_value(qkv, cos_wide, sin_wide)
     far = lax.ppermute(near, "context", [(0, 1)])
     where = context[None].astype(jnp.int32)
     query, mixed, logs = attention(where, qkv, near, far, cos_wide, sin_wide)
+    out_w = assemble(own_two, other_two, context, expert)
     resid_one = inputs_f + dot(mixed, out_w)
     scale_two, norm_two = norm_parts(resid_one)
     act_two = (norm_two * gain_two).astype(bf16)
@@ -594,22 +741,27 @@
     gates_high = gates.astype(bf16)
     gates_low = (gates - gates_high.astype(f32)).astype(bf16)
     meta = jnp.concatenate([gates_high, gates_low, slot_code.astype(bf16)], axis=1)
-    acts_own, acts_other = spread(jnp.concatenate([act_two, meta], axis=0))
-
-    sums, shares = (), []
+    payload = jnp.concatenate([act_two, meta], axis=0)
+    acts_own, acts_other = spread(after(payload, *dys_own[1:]))
+
     place = jnp.stack([expert * EXP_DEV + context * per_core, context]).astype(jnp.int32)
     step = jnp.array([1, 0], jnp.int32)
+    sums, shares = (), []
     for j in range(per_core):
         *sums, x, gdy, hidden, dgate, dup = run_expert(
             acts_own + acts_other, dys_own + dys_other, gathered[j], place, capacity, sums
         )
+        if j == per_core - 1:
+            d_parts = block_parts(sums[2], sums[3])
+            x = after(x, d_parts[-1])
         grads = weight_grads(x, gdy, hidden, dgate, dup, z, rows)
-        place = after(place + step, grads)
+        place, grads = tie(place + step, grads)
+        if j == per_core - 1:
+            dact, came, last = scatter_blocks(d_parts, (), (), [shares[-1], grads])
+            grads, shares[-1] = tie(grads, shares[-1])
         shares.append(lax.psum_scatter(grads, "dp", scatter_dimension=0, tiled=False))
-    y_own, y_other, d_own, d_other = sums
-    dact = reduce_blocks(d_own, d_other)
-    y_other = after(y_other, dact)
-    block_out = (resid_one + reduce_blocks(y_own, y_other)).astype(bf16)[None]
+    y_parts = block_parts(sums[0], after(sums[1], *came))
+    y_sum, y_came, _ = scatter_blocks(y_parts, last)
 
     dy = out_grad[0].astype(f32)
     dgates = dact[tokens:, :tokens] + dact[tokens:, tokens : 2 * tokens]
@@ -620,20 +772,19 @@
     dn2 = dact_two * gain_two
     dresid = dy + scale_two * (dn2 - norm_two * jnp.mean(dn2 * norm_two, axis=-1, keepdims=True))
     dresid_b = dresid.astype(bf16)
-    grad_out = reduce_dense(dot(mixed, dresid_b, ((0,), (0,))), context, expert)
     dmixed = dot(dresid_b, out_w, ((1,), (1,))).astype(bf16)
-
-    dquery, dkey_near, dvalue_near, dkey_far, dvalue_far = attention_back(
+    out_halves = swap_halves(dot(mixed, after(dresid_b, dmixed), ((0,), (0,))), context)
+    out_total, out_first, out_came = scatter_blocks(dense_parts([out_halves], expert))
+
+    dquery, near_grad, far_grad = attention_back(
         where, query, dmixed, near, far, logs, cos_wide, sin_wide
     )
-    sent = jnp.concatenate([dkey_far, dvalue_far], axis=1).astype(bf16)
-    came = lax.ppermute(sent, "context", [(1, 0)]).astype(f32)
-    dkey_r = (dkey_near + came[:, :KV_WIDTH]).reshape(tokens, KEY_VALUE_HEADS, HEAD_SIZE)
-    dkey = rotate(dkey_r, cosine, -sine).astype(bf16).reshape(tokens, KV_WIDTH)
-    dvalue = dvalue_near + came[:, KV_WIDTH:]
-    dqkv = jnp.concatenate([dquery, dkey, dvalue.astype(bf16)], axis=1)
-    dact_one = dot(dqkv, qkv_w, ((1,), (1,)))
-    grad_qkv = dot(act_one, dqkv, ((0,), (0,)))
+    came = lax.ppermute(after(far_grad, *y_came), "context", [(1, 0)])
+    grad_query = dot(act_one, dquery, ((0,), (0,))).astype(bf16)
+    dkv = key_value_back(near_grad, came, cos_wide, sin_wide)
+    grad_kv = dot(act_one, dkv, ((0,), (0,))).astype(bf16)
+    dact_one = dot(dquery, qkv_w[:, :Q_WIDTH], ((1,), (1,)))
+    dact_one = dact_one + dot(after(dkv, grad_kv), qkv_w[:, Q_WIDTH:], ((1,), (1,)))
     grad_gain_one = jnp.sum(dact_one * norm_one, axis=0)
     dn1 = dact_one * gain_one
     grad_in = dresid + scale_one * (dn1 - norm_one * jnp.mean(dn1 * norm_one, axis=-1, keepdims=True))
@@ -646,7 +797,15 @@
         ],
         axis=1,
     )
-    first = reduce_dense(jnp.concatenate([grad_qkv, grad_small], axis=1), context, expert)
+    block_out = (resid_one + y_sum).astype(bf16)[None]
+    out_total, shares[-1] = tie(out_total.astype(bf16), shares[-1])
+    grad_out, out_share = finish_dense(out_total, expert)
+    halves = [swap_halves(grad, context) for grad in (grad_query, grad_kv)]
+    first_total, _, _ = scatter_blocks(dense_parts(halves, expert), out_came)
+    small_total, _, _ = scatter_blocks(dense_parts([swap_halves(grad_small, context)], expert))
+    first_total = jnp.concatenate([first_total, small_total], axis=-1).astype(bf16)
+    first_total, out_share = tie(first_total, out_share)
+    first, _ = finish_dense(first_total, expert)
     kv_at = Q_WIDTH + KV_WIDTH
     small_at = kv_at + KV_WIDTH
 

time: 823 us -> 715 us (0.87)
  waiting for transfers between devices: 352 us -> 266 us
  blocking collectives: 46.1 us -> 0 us
  other arithmetic: 65.8 us -> 80.5 us
    ppermute x30 -> x42, waiting for transfers between devices: 320 us -> 201 us  [flip(): return lax.ppermute(value, 'expert', [(i, i ^ step) for i in range(count)])]
    all_gather x2 -> x0, blocking collectives: 46.1 us -> none  [the longest x1 27.7 us: local(): first_z = lax.all_gather(first_pack, 'dp', axis=0, tiled=False)]
    all_gather x2 -> x3, waiting for transfers between devices: 0.01 us -> 28.2 us  [the longest x1 28.2 us: local(): dense_z = lax.all_gather(pack, 'dp', axis=0, tiled=False)]
    all_gather x2 -> x0, local copies, waits for them, and re-layouts: 21 us -> none  [local(): lax.all_gather(sent, ('context', 'dp'), axis=0, tiled=False)]
    unnamed x72 -> x161, local copies, waits for them, and re-layouts: 9.73 us -> 23.7 us
    slice x2 -> x17, local copies, waits for them, and re-layouts: 0.94 us -> 11.5 us  [the longest x4 4.1 us: fourth_block(): two[cut:]]
    convert_element_type x9 -> x17, other arithmetic: 22.7 us -> 31.9 us  [the longest x2 9.29 us: block_parts(): (own[i].astype(f32) + came[i].astype(f32)).astype(bf16)]
    another operation x10 -> x23, other arithmetic: 9.03 us -> 17.5 us
  transfers between devices with their start and end apart: 60 -> 75, of which waited for: 27 -> 28; matrix products, arithmetic and copies ran while one was open for 18% -> 23% of each run, Pallas kernels for 14% -> 26%
where the time goes in v2:
time: 715 us; the launch traced here: 708 us
  waiting for transfers between devices  266 us (37%)
  Pallas kernels  181 us (25%)
  other arithmetic  80.5 us (11%)
  local copies, waits for them, and re-layouts  63.8 us (9%)
  starting transfers between devices  56 us (8%)
  matrix products  45.2 us (6%)
  between operations  15.6 us (2%)
    ppermute x42, waiting for transfers between devices, flip(): return lax.ppermute(value, 'expert', [(i, i ^ step) for i in range(count)])  201 us
    pallas_call x2, Pallas kernels, run_expert(): pl.pallas_call(functools.partial(expert_kernel, count, tokens, capacity),...  86.7 us
    ppermute x42, starting transfers between devices, flip(): return lax.ppermute(value, 'expert', [(i, i ^ step) for i in range(count)])  47.2 us
    dot_general x12, matrix products, dot(): return lax.dot_general(a, b, (dims, ((), ())), preferred_element_type=f32)  45.2 us
    pallas_call x1, Pallas kernels, attention_back(): pl.pallas_call(attend_back_kernel, out_shape=(jax.ShapeDtypeStruct((token...  29.4 us
    pallas_call x2, Pallas kernels, weight_grads(): pl.pallas_call(weight_grad_kernel, out_shape=jax.ShapeDtypeStruct((z, 2,...  29.4 us
    all_gather x1, waiting for transfers between devices, local(): dense_z = lax.all_gather(pack, 'dp', axis=0, tiled=False)  28.2 us
    unnamed x161, local copies, waits for them, and re-layouts  23.7 us
  transfers between devices with their start and end apart: 75, of which 28 were waited for; matrix products, arithmetic and copies ran while one was open for 23% of the time, Pallas kernels for 26%

profile of v2, /device:TPU:0, one launch (start us, length us, event | category | flops | bytes accessed | tf_op | source)
XLA Modules:
  0.0 708.1 jit_solution(5180457212530520674)
XLA Ops:
  11.3 1.9 convert.139
  20.5 28.2 %all-gather.7.cloned.1.call-done = bf16[192,3712]{1,0:T(8,128)(2,1)} async-done(((bf16[48,3712]{1,0:T(8,128)(2,1)}), bf16[192,3712]{1,0:T(8,128)(2,1)}) %all-gather.7.cloned.1.call-update) | async-done | bytes 1425424 | tf_op jit(solution)/shard_map/all_gather | solution.py:682
  54.0 16.9 %collective-permute-done.refs_1_ = bf16[4,48,2176]{2,1,0:T(8,128)(2,1)S(1)} collective-permute-done((bf16[4,48,2176]{2,1,0:T(8,128)(2,1)}, bf16[4,48,2176]{2,1,0:T(8,128)(2,1)S(1)}, u32[]{:S(2)}, u32[]{:S(2)}) %collective-permute-start) | collective-permute-done | bytes 835616 | tf_op jit(solution)/shard_map/ppermute | solution.py:56
  74.0 7.0 collective-permute-done.2
  84.9 30.9 %collective-permute-done.10.refs_10_ = bf16[512,1536]{1,0:T(8,128)(2,1)} collective-permute-done((bf16[512,1536]{1,0:T(8,128)(2,1)S(1)}, bf16[512,1536]{1,0:T(8,128)(2,1)}, u32[]{:S(2)}, u32[]{:S(2)}) %collective-permute-start.10) | collective-permute-done | bytes 1572896 | tf_op jit(solution)/shard_map/ppermute | solution.py:56
  117.8 1.9 slice.506.refs_0_
  123.7 6.5 assemble.2
  131.5 4.2 collective-permute-done.11.refs_1_
  139.3 8.0 %fusion.x_ref.q_ref = f32[512,2048]{1,0:T(8,128)} fusion(bf16[1536,2176]{1,0:T(8,128)(2,1)} %bitcast.414, bf16[1,512,1536]{2,1,0:T(8,128)(2,1)S(1)} %copy-done.16, f32[1536]{0:T(1024)S(1)} %get-tuple-element.147, f32[512]{0:T(512)S(1)} %add_rsqrt_fusion.1), kind=kOutput, calls=%fused_computation.2 | convolution fusion | flops 3224371200 | bytes 12066816 | tf_op jit(solution)/shard_map/dot_general | solution.py:43
  147.3 2.4 key_value.1.ko_ref.vo_ref
  149.6 2.1 collective-permute-start.8
  153.1 19.2 %attention.1 = (bf16[512,1536]{1,0:T(8,128)(2,1)}, bf16[512,1536]{1,0:T(8,128)(2,1)}, f32[12,1,512]{2,1,0:T(1,128)}) custom-call(s32[1]{0:T(128)} %bitcast.1.place, f32[512,2048]{1,0:T(8,128)} %fusion.x_ref.q_ref, bf16[512,512]{1,0:T(8,128)(2,1)} %key_value.1.ko_ref.vo_ref, bf16[512,512]{1,0:T(8,128)(2,1)} %key_value.1.ko_ref.vo_ref, ...), custom_call_target="tpu_custom_call" | custom-call | flops 3221225472 | bytes 7864320 | tf_op jit(solution)/shard_map/attention/pallas_call | solution.py:479
  172.3 2.1 slice.512
  174.3 2.1 slice.511
  179.2 5.2 assemble.3
  184.4 6.6 multiply_reduce_fusion.2
  194.6 2.2 collective-permute-done.19
  196.9 2.1 constant_dynamic-update-slice_fusion.5
  199.0 2.1 constant_dynamic-update-slice_fusion.4.refs_11_
  204.2 33.5 %collective-permute-done.21.refs_1_ = bf16[528,1536]{1,0:T(8,128)(2,1)} collective-permute-done((bf16[528,1536]{1,0:T(8,128)(2,1)}, bf16[528,1536]{1,0:T(8,128)(2,1)}, u32[]{:S(2)}, u32[]{:S(2)}) %collective-permute-start.21) | collective-permute-done | bytes 1622048 | tf_op jit(solution)/shard_map/ppermute | solution.py:56
  242.8 13.6 %collective-permute-done.23 = bf16[256,1536]{1,0:T(8,128)(2,1)S(1)} collective-permute-done((bf16[256,1536]{1,0:T(8,128)(2,1)S(1)}, bf16[256,1536]{1,0:T(8,128)(2,1)S(1)}, u32[]{:S(2)}, u32[]{:S(2)}) %collective-permute-start.23) | collective-permute-done | bytes 786464 | tf_op jit(solution)/shard_map/ppermute | solution.py:56
  257.4 2.4 collective-permute-done.24
  263.5 7.6 %collective-permute-done.32.refs_15_ = bf16[512,1536]{1,0:T(8,128)(2,1)} collective-permute-done((bf16[512,1536]{1,0:T(8,128)(2,1)}, bf16[512,1536]{1,0:T(8,128)(2,1)}, u32[]{:S(2)}, u32[]{:S(2)}) %collective-permute-start.32) | collective-permute-done | bytes 1572896 | tf_op jit(solution)/shard_map/ppermute | solution.py:60
  271.2 41.1 %experts.2 = (bf16[4,512,1536]{2,1,0:T(8,128)(2,1)}, bf16[4,512,1536]{2,1,0:T(8,128)(2,1)}, bf16[4,528,1536]{2,1,0:T(8,128)(2,1)}, bf16[4,528,1536]{2,1,0:T(8,12...) custom-call(s32[2]{0:T(128)} %get-tuple-element.149.place, ...), custom_call_target="tpu_custom_call" | custom-call | flops 26172456960 | bytes 71958528 | tf_op jit(solution)/shard_map/experts/pallas_call | solution.py:294
  312.3 14.7 %weight_grads.2 = bf16[4,2,3,192,768]{4,3,2,1,0:T(8,128)(2,1)} custom-call(bf16[1280,1536]{1,0:T(8,128)(2,1)} %get-tuple-element.66.x_ref, bf16[1280,1536]{1,0:T(8,128)(2,1)} %get-tuple-element.67.gdy_ref, bf16[1280,768]{1,0:T(8,128)(2,1)} %get-tuple-element.68.h_ref, bf16[1280,768]{1,0:T(8,128)(2,1)} %get-tuple-element.69.dg_ref, ...), custom_call_target="tpu_custom_call" | custom-call | flops 9059696640 | bytes 20840448 | tf_op jit(solution)/shard_map/weight_grads/pallas_call | solution.py:358
  327.1 45.6 %experts.3 = (bf16[4,512,1536]{2,1,0:T(8,128)(2,1)}, bf16[4,512,1536]{2,1,0:T(8,128)(2,1)}, bf16[4,528,1536]{2,1,0:T(8,128)(2,1)}, bf16[4,528,1536]{2,1,0:T(8,12...) custom-call(s32[2]{0:T(128)} %get-tuple-element.71.place, ...), custom_call_target="tpu_custom_call" | custom-call | flops 26172456960 | bytes 71958528 | tf_op jit(solution)/shard_map/experts/pallas_call | solution.py:294
  372.9 10.5 %collective-permute-done.33 = bf16[4,528,1536]{2,1,0:T(8,128)(2,1)S(1)} collective-permute-done((bf16[4,528,1536]{2,1,0:T(8,128)(2,1)}, bf16[4,528,1536]{2,1,0:T(8,128)(2,1)S(1)}, u32[]{:S(2)}, u32[]{:S(2)}) %collective-permute-start.33) | collective-permute-done | bytes 6488096 | tf_op jit(solution)/shard_map/ppermute | solution.py:60
  383.4 4.7 add_convert_fusion
  394.2 35.1 %collective-permute-done.34 = bf16[2,256,1536]{2,1,0:T(8,128)(2,1)} collective-permute-done((bf16[2,256,1536]{2,1,0:T(8,128)(2,1)}, bf16[2,256,1536]{2,1,0:T(8,128)(2,1)}, u32[]{:S(2)}, u32[]{:S(2)}) %collective-permute-start.34) | collective-permute-done | bytes 1572896 | tf_op jit(solution)/shard_map/ppermute | solution.py:56
  429.5 2.5 fusion.36
  433.2 14.7 %weight_grads.3 = bf16[4,2,3,192,768]{4,3,2,1,0:T(8,128)(2,1)} custom-call(bf16[1280,1536]{1,0:T(8,128)(2,1)} %get-tuple-element.83.x_ref, bf16[1280,1536]{1,0:T(8,128)(2,1)} %get-tuple-element.84.gdy_ref, bf16[1280,768]{1,0:T(8,128)(2,1)} %get-tuple-element.85.h_ref, bf16[1280,768]{1,0:T(8,128)(2,1)} %get-tuple-element.86.dg_ref, ...), custom_call_target="tpu_custom_call" | custom-call | flops 9059696640 | bytes 20840448 | tf_op jit(solution)/shard_map/weight_grads/pallas_call | solution.py:358
  448.0 2.6 fusion.37
  457.8 2.1 dynamic-slice_bitcast_fusion.1
  460.2 10.4 %collective-permute-done.37 = bf16[256,1536]{1,0:T(8,128)(2,1)} collective-permute-done((bf16[256,1536]{1,0:T(8,128)(2,1)}, bf16[256,1536]{1,0:T(8,128)(2,1)}, u32[]{:S(2)}, u32[]{:S(2)}) %collective-permute-start.37) | collective-permute-done | bytes 786464 | tf_op jit(solution)/shard_map/ppermute | solution.py:56
  472.4 3.0 multiply_reduce_fusion
  477.1 3.7 convolution_convert_fusion.3.dout_ref
  480.9 2.9 convolution_convert_fusion
  486.7 4.6 add_convert_fusion.7
  497.1 29.4 %attention_back.1 = (bf16[512,1536]{1,0:T(8,128)(2,1)}, f32[512,512]{1,0:T(8,128)}, bf16[512,512]{1,0:T(8,128)(2,1)}) custom-call(s32[1]{0:T(128)} %bitcast.1.place, bf16[512,1536]{1,0:T(8,128)(2,1)} %get-tuple-element.91.q_ref, bf16[512,1536]{1,0:T(8,128)(2,1)} %convolution_convert_fusion.3.dout_ref, bf16[512,512]{1,0:T(8,128)(2,1)} %key_value.1.ko_ref.vo_ref, ...), custom_call_target="tpu_custom_call" | custom-call | flops 8053063680 | bytes 6291456 | tf_op jit(solution)/shard_map/attention_back/pallas_call | solution.py:557
  526.6 4.6 convolution_convert_fusion.1
  535.9 2.9 fusion.34
  540.5 2.3 fusion.39
  543.9 2.4 fusion.38
  547.4 3.8 fusion.23
  555.0 3.5 fusion.30
  558.5 2.5 key_value_back.1
  561.1 3.9 convolution_convert_fusion.2
  565.0 2.6 fusion.21
  567.6 7.6 %fusion.17 = (bf16[1536]{0:T(1024)(128)(2,1)}, f32[512]{0:T(512)}, f32[512,1536]{1,0:T(8,128)}) fusion(bf16[1,512,1536]{2,1,0:T(8,128)(2,1)S(1)} %copy-done.17, f32[512]{0:T(512)S(1)} %copy-done.59, f32[1536]{0:T(1024)S(1)} %copy-done.52, f32[512,1536]{1,0:T(8,128)S(1)} %fusion.21, bf16[512,1536]{1,0:T(8,128)(2,1)S(1)} %copy-done.67, ...), kind=kOutput, calls=%fused_computation.26 | convolution fusion | flops 2422208512 | bytes 14169088 | tf_op jit(solution)/shard_map/dot_general | solution.py:43
  583.2 3.1 collective-permute-done.58
  588.0 2.3 collective-permute-done.56
  592.7 4.2 bitcast_add_fusion.3
  601.4 7.0 collective-permute-done.48
  612.1 14.6 %collective-permute-done.53 = bf16[2,2,48,2048]{3,2,1,0:T(8,128)(2,1)S(1)} collective-permute-done((bf16[2,2,48,2048]{3,2,1,0:T(8,128)(2,1)S(1)}, bf16[2,2,48,2048]{3,2,1,0:T(8,128)(2,1)S(1)}, u32[]{:S(2)}, u32[]{:S(2)}) %collective-permute-start.53) | collective-permute-done | bytes 786464 | tf_op jit(solution)/shard_map/ppermute | solution.py:56
  633.4 5.3 collective-permute-done.52
  641.7 2.1 dynamic-slice_bitcast_fusion
  643.8 10.9 %reduce-scatter.9.cloned.1.call-done = bf16[1,48,1536]{2,1,0:T(8,128)(2,1)} async-done(((bf16[4,48,1536]{2,1,0:T(8,128)(2,1)}), bf16[1,48,1536]{2,1,0:T(8,128)(2,1)}) %reduce-scatter.9.cloned.1.call-update) | async-done | bytes 147472 | tf_op jit(solution)/shard_map/reduce_scatter | solution.py:626
  654.8 7.2 %fusion.16 = (f32[1,512,1536]{2,1,0:T(8,128)}, bf16[1,512,1536]{2,1,0:T(8,128)(2,1)}) fusion(f32[512,1536]{1,0:T(8,128)} %get-tuple-element.233, bf16[1,512,1536]{2,1,0:T(8,128)(2,1)} %param.14, f32[512]{0:T(512)S(1)} %copy-done.61, f32[1536]{0:T(1024)S(1)} %copy-done.53, f32[512]{0:T(512)S(1)} %copy-done.60, f32[512]{0:T(512)S(1)} %broadcast_multiply_fusion.1, ...), kind=kLoop, calls=%fused_computation.25 | loop fusion | flops 13369344 | bytes 20467712 | tf_op jit(solution)/shard_map/broadcast_in_dim | solution.py:821
  668.1 3.1 slice_bitcast_fusion
  671.7 1.9 collective-permute-done.65
  673.8 5.7 reduce-scatter.11.cloned.1.call-done
  684.1 3.7 collective-permute-done.60
  687.8 3.8 collective-permute-done.61
  694.3 2.3 maximum_convert_fusion.1
  (411 shorter events, 142.9 us)
Async XLA Ops:
  7.2 41.5 %all-gather.7.cloned.1.call-start = ((), (), s32[]{:S(2)}) async-start(), calls=%async_computation.8 | async-start | bytes 1781760 | tf_op jit(solution)/shard_map/all_gather | solution.py:682
  11.2 260.0 %all-gather.9.cloned.1.call-start = ((), (), s32[]{:S(2)}) async-start(), calls=%async_computation.9 | async-start | bytes 15925248 | tf_op jit(solution)/shard_map/all_gather | solution.py:709
  48.8 278.3 %all-gather.11.cloned.1.call-start = ((), (), s32[]{:S(2)}) async-start(), calls=%async_computation.10 | async-start | bytes 15925248 | tf_op jit(solution)/shard_map/all_gather | solution.py:709
  49.5 408.3 %reduce-scatter.5.cloned.1.call-start = ((), (), s32[]{:S(2)}) async-start(), calls=%async_computation.4 | async-start | bytes 8847360 | tf_op jit(solution)/shard_map/reduce_scatter | solution.py:762
  51.0 19.8 %collective-permute-start = (bf16[4,48,2176]{2,1,0:T(8,128)(2,1)}, bf16[4,48,2176]{2,1,0:T(8,128)(2,1)S(1)}, u32[]{:S(2)}, u32[]{:S(2)}) collective-permute-start(bf16[4,48,2176]{2,1,0:T(8,128)(2,1)} %slice.500.refs_0_), channel_id=1, source_target_pairs={{0,8},{8,0},{16,24},{24,16},{1,9},{9,1},{17,25},{25,17},{2,10},{10... | collective-permute-start | bytes 2506760 | tf_op jit(solution)/shard_map/ppermute | solution.py:56
  52.5 19.9 %collective-permute-start.1 = (bf16[4,48,2176]{2,1,0:T(8,128)(2,1)}, bf16[4,48,2176]{2,1,0:T(8,128)(2,1)S(1)}, u32[]{:S(2)}, u32[]{:S(2)}) collective-permute-start(bf16[4,48,2176]{2,1,0:T(8,128)(2,1)} %slice.500.refs_0_), channel_id=1, source_target_pairs={{0,16},{8,24},{16,0},{24,8},{1,17},{9,25},{17,1},{25,9},{2,18},{10... | collective-permute-start | bytes 2506760 | tf_op jit(solution)/shard_map/ppermute | solution.py:56
  70.9 10.1 %collective-permute-start.2 = (bf16[2,48,2176]{2,1,0:T(8,128)(2,1)S(1)}, bf16[2,48,2176]{2,1,0:T(8,128)(2,1)S(1)}, u32[]{:S(2)}, u32[]{:S(2)}) collective-permute-start(bf16[2,48,2176]{2,1,0:T(8,128)(2,1)S(1)} %slice.501), channel_id=1, source_target_pairs={{0,16},{8,24},{16,0},{24,8},{1,17},{9,25},{17,1},{25,9},{2,18},{10... | collective-permute-start | bytes 1253384 | tf_op jit(solution)/shard_map/ppermute | solution.py:56
  72.5 9.6 %collective-permute-start.3 = (bf16[2,48,2176]{2,1,0:T(8,128)(2,1)S(1)}, bf16[2,48,2176]{2,1,0:T(8,128)(2,1)S(1)}, u32[]{:S(2)}, u32[]{:S(2)}) collective-permute-start(bf16[2,48,2176]{2,1,0:T(8,128)(2,1)S(1)} %slice.502), channel_id=1, source_target_pairs={{0,8},{8,0},{16,24},{24,16},{1,9},{9,1},{17,25},{25,17},{2,10},{10... | collective-permute-start | bytes 1253384 | tf_op jit(solution)/shard_map/ppermute | solution.py:56
  82.2 33.7 %collective-permute-start.10 = (bf16[512,1536]{1,0:T(8,128)(2,1)S(1)}, bf16[512,1536]{1,0:T(8,128)(2,1)}, u32[]{:S(2)}, u32[]{:S(2)}) collective-permute-start(bf16[512,1536]{1,0:T(8,128)(2,1)S(1)} %bitcast.423), channel_id=1, source_target_pairs={{0,16},{8,24},{16,0},{24,8},{1,17},{9,25},{17,1},{25,9},{2,18},{10... | collective-permute-start | bytes 4718600 | tf_op jit(solution)/shard_map/ppermute | solution.py:56
  83.3 36.4 %collective-permute-start.9 = (bf16[512,1536]{1,0:T(8,128)(2,1)S(1)}, bf16[512,1536]{1,0:T(8,128)(2,1)}, u32[]{:S(2)}, u32[]{:S(2)}) collective-permute-start(bf16[512,1536]{1,0:T(8,128)(2,1)S(1)} %bitcast.424), channel_id=1, source_target_pairs={{0,8},{8,0},{16,24},{24,16},{1,9},{9,1},{17,25},{25,17},{2,10},{10... | collective-permute-start | bytes 4718600 | tf_op jit(solution)/shard_map/ppermute | solution.py:56
  84.3 37.0 %collective-permute-start.4 = (bf16[4,48,2176]{2,1,0:T(8,128)(2,1)}, bf16[4,48,2176]{2,1,0:T(8,128)(2,1)}, u32[]{:S(2)}, u32[]{:S(2)}) collective-permute-start(bf16[4,48,2176]{2,1,0:T(8,128)(2,1)} %slice.500.refs_0_), channel_id=1, source_target_pairs={{0,4},{4,0},{1,5},{5,1},{2,6},{6,2},{3,7},{7,3},{8,12},{12,8},{9,1... | collective-permute-start | bytes 2506760 | tf_op jit(solution)/shard_map/ppermute | solution.py:60
  84.3 38.5 %collective-permute-start.5 = (bf16[4,48,2176]{2,1,0:T(8,128)(2,1)}, bf16[4,48,2176]{2,1,0:T(8,128)(2,1)S(1)}, u32[]{:S(2)}, u32[]{:S(2)}) collective-permute-start(bf16[4,48,2176]{2,1,0:T(8,128)(2,1)} %copy-done.34), channel_id=1, source_target_pairs={{0,4},{4,0},{1,5},{5,1},{2,6},{6,2},{3,7},{7,3},{8,12},{12,8},{9,1... | collective-permute-start | bytes 2506760 | tf_op jit(solution)/shard_map/ppermute | solution.py:60
  84.8 37.9 %collective-permute-start.6 = (bf16[4,48,2176]{2,1,0:T(8,128)(2,1)}, bf16[4,48,2176]{2,1,0:T(8,128)(2,1)}, u32[]{:S(2)}, u32[]{:S(2)}) collective-permute-start(bf16[4,48,2176]{2,1,0:T(8,128)(2,1)} %copy-done.35), channel_id=1, source_target_pairs={{0,4},{4,0},{1,5},{5,1},{2,6},{6,2},{3,7},{7,3},{8,12},{12,8},{9,1... | collective-permute-start | bytes 2506760 | tf_op jit(solution)/shard_map/ppermute | solution.py:60
  119.8 15.9 %collective-permute-start.11 = (bf16[4,48,1536]{2,1,0:T(8,128)(2,1)}, bf16[4,48,1536]{2,1,0:T(8,128)(2,1)S(1)}, u32[]{:S(2)}, u32[]{:S(2)}) collective-permute-start(bf16[4,48,1536]{2,1,0:T(8,128)(2,1)} %slice.506.refs_0_), channel_id=1, source_target_pairs={{0,8},{8,0},{16,24},{24,16},{1,9},{9,1},{17,25},{25,17},{2,10},{10... | collective-permute-start | bytes 1769480 | tf_op jit(solution)/shard_map/ppermute | solution.py:56
  121.2 16.2 %collective-permute-start.12 = (bf16[4,48,1536]{2,1,0:T(8,128)(2,1)}, bf16[4,48,1536]{2,1,0:T(8,128)(2,1)S(1)}, u32[]{:S(2)}, u32[]{:S(2)}) collective-permute-start(bf16[4,48,1536]{2,1,0:T(8,128)(2,1)} %slice.506.refs_0_), channel_id=1, source_target_pairs={{0,16},{8,24},{16,0},{24,8},{1,17},{9,25},{17,1},{25,9},{2,18},{10... | collective-permute-start | bytes 1769480 | tf_op jit(solution)/shard_map/ppermute | solution.py:56
  136.5 15.7 %collective-permute-start.13 = (bf16[2,48,1536]{2,1,0:T(8,128)(2,1)}, bf16[2,48,1536]{2,1,0:T(8,128)(2,1)S(1)}, u32[]{:S(2)}, u32[]{:S(2)}) collective-permute-start(bf16[2,48,1536]{2,1,0:T(8,128)(2,1)} %slice.507), channel_id=1, source_target_pairs={{0,16},{8,24},{16,0},{24,8},{1,17},{9,25},{17,1},{25,9},{2,18},{10... | collective-permute-start | bytes 884744 | tf_op jit(solution)/shard_map/ppermute | solution.py:56
  138.2 14.1 %collective-permute-start.14 = (bf16[2,48,1536]{2,1,0:T(8,128)(2,1)}, bf16[2,48,1536]{2,1,0:T(8,128)(2,1)S(1)}, u32[]{:S(2)}, u32[]{:S(2)}) collective-permute-start(bf16[2,48,1536]{2,1,0:T(8,128)(2,1)} %slice.508), channel_id=1, source_target_pairs={{0,8},{8,0},{16,24},{24,16},{1,9},{9,1},{17,25},{25,17},{2,10},{10... | collective-permute-start | bytes 884744 | tf_op jit(solution)/shard_map/ppermute | solution.py:56
  151.7 25.6 %collective-permute-start.15 = (bf16[4,48,1536]{2,1,0:T(8,128)(2,1)}, bf16[4,48,1536]{2,1,0:T(8,128)(2,1)S(1)}, u32[]{:S(2)}, u32[]{:S(2)}) collective-permute-start(bf16[4,48,1536]{2,1,0:T(8,128)(2,1)} %slice.506.refs_0_), channel_id=1, source_target_pairs={{0,4},{4,0},{1,5},{5,1},{2,6},{6,2},{3,7},{7,3},{8,12},{12,8},{9,1... | collective-permute-start | bytes 1769480 | tf_op jit(solution)/shard_map/ppermute | solution.py:60
  151.7 26.7 %collective-permute-start.16 = (bf16[4,48,1536]{2,1,0:T(8,128)(2,1)S(1)}, bf16[4,48,1536]{2,1,0:T(8,128)(2,1)S(1)}, u32[]{:S(2)}, u32[]{:S(2)}) collective-permute-start(bf16[4,48,1536]{2,1,0:T(8,128)(2,1)S(1)} %collective-permute-done.11.refs_1_), channel_id=1, source_target_pairs={{0,4},{4,0},{1,5},{5,1},{2,6},{6,2},{3,7},{7,3},{8,12},{12,8},{9,1... | collective-permute-start | bytes 1769480 | tf_op jit(solution)/shard_map/ppermute | solution.py:60
  152.2 26.2 %collective-permute-start.17 = (bf16[4,48,1536]{2,1,0:T(8,128)(2,1)S(1)}, bf16[4,48,1536]{2,1,0:T(8,128)(2,1)}, u32[]{:S(2)}, u32[]{:S(2)}) collective-permute-start(bf16[4,48,1536]{2,1,0:T(8,128)(2,1)S(1)} %collective-permute-done.12.refs_2_), channel_id=1, source_target_pairs={{0,4},{4,0},{1,5},{5,1},{2,6},{6,2},{3,7},{7,3},{8,12},{12,8},{9,1... | collective-permute-start | bytes 1769480 | tf_op jit(solution)/shard_map/ppermute | solution.py:60
  152.4 26.0 %collective-permute-start.18 = (bf16[4,48,1536]{2,1,0:T(8,128)(2,1)S(1)}, bf16[4,48,1536]{2,1,0:T(8,128)(2,1)}, u32[]{:S(2)}, u32[]{:S(2)}) collective-permute-start(bf16[4,48,1536]{2,1,0:T(8,128)(2,1)S(1)} %constant_dynamic-update-slice_fusion.2.refs_3_), channel_id=1, source_target_pairs={{0,4},{4,0},{1,5},{5,1},{2,6},{6,2},{3,7},{7,3},{8,12},{12,8},{9,1... | collective-permute-start | bytes 1769480 | tf_op jit(solution)/shard_map/ppermute | solution.py:60
  176.4 22.6 %collective-permute-start.20 = (bf16[256,1536]{1,0:T(8,128)(2,1)}, bf16[256,1536]{1,0:T(8,128)(2,1)}, u32[]{:S(2)}, u32[]{:S(2)}) collective-permute-start(bf16[256,1536]{1,0:T(8,128)(2,1)} %slice.512), channel_id=1, source_target_pairs={{0,8},{8,0},{16,24},{24,16},{1,9},{9,1},{17,25},{25,17},{2,10},{10... | collective-permute-start | bytes 2359304 | tf_op jit(solution)/shard_map/ppermute | solution.py:56
  177.3 19.6 %collective-permute-start.19 = (bf16[256,1536]{1,0:T(8,128)(2,1)}, bf16[256,1536]{1,0:T(8,128)(2,1)}, u32[]{:S(2)}, u32[]{:S(2)}) collective-permute-start(bf16[256,1536]{1,0:T(8,128)(2,1)} %slice.511), channel_id=1, source_target_pairs={{0,16},{8,24},{16,0},{24,8},{1,17},{9,25},{17,1},{25,9},{2,18},{10... | collective-permute-start | bytes 2359304 | tf_op jit(solution)/shard_map/ppermute | solution.py:56
  201.1 36.6 %collective-permute-start.21 = (bf16[528,1536]{1,0:T(8,128)(2,1)}, bf16[528,1536]{1,0:T(8,128)(2,1)}, u32[]{:S(2)}, u32[]{:S(2)}) collective-permute-start(bf16[528,1536]{1,0:T(8,128)(2,1)} %maximum_maximum_fusion.refs_0_), channel_id=1, source_target_pairs={{0,8},{8,0},{16,24},{24,16},{1,9},{9,1},{17,25},{25,17},{2,10},{10... | collective-permute-start | bytes 4866056 | tf_op jit(solution)/shard_map/ppermute | solution.py:56
  202.2 38.0 %collective-permute-start.22 = (bf16[528,1536]{1,0:T(8,128)(2,1)}, bf16[528,1536]{1,0:T(8,128)(2,1)}, u32[]{:S(2)}, u32[]{:S(2)}) collective-permute-start(bf16[528,1536]{1,0:T(8,128)(2,1)} %maximum_maximum_fusion.refs_0_), channel_id=1, source_target_pairs={{0,16},{8,24},{16,0},{24,8},{1,17},{9,25},{17,1},{25,9},{2,18},{10... | collective-permute-start | bytes 4866056 | tf_op jit(solution)/shard_map/ppermute | solution.py:56
  203.7 57.1 %collective-permute-start.29 = (bf16[512,1536]{1,0:T(8,128)(2,1)S(1)}, bf16[512,1536]{1,0:T(8,128)(2,1)S(1)}, u32[]{:S(2)}, u32[]{:S(2)}) collective-permute-start(bf16[512,1536]{1,0:T(8,128)(2,1)S(1)} %bitcast.425), channel_id=1, source_target_pairs={{0,4},{4,0},{1,5},{5,1},{2,6},{6,2},{3,7},{7,3},{8,12},{12,8},{9,1... | collective-permute-start | bytes 4718600 | tf_op jit(solution)/shard_map/ppermute | solution.py:60
  203.7 58.7 %collective-permute-start.30 = (bf16[512,1536]{1,0:T(8,128)(2,1)}, bf16[512,1536]{1,0:T(8,128)(2,1)}, u32[]{:S(2)}, u32[]{:S(2)}) collective-permute-start(bf16[512,1536]{1,0:T(8,128)(2,1)} %collective-permute-done.9.refs_9_), channel_id=1, source_target_pairs={{0,4},{4,0},{1,5},{5,1},{2,6},{6,2},{3,7},{7,3},{8,12},{12,8},{9,1... | collective-permute-start | bytes 4718600 | tf_op jit(solution)/shard_map/ppermute | solution.py:60
  204.2 58.2 %collective-permute-start.31 = (bf16[512,1536]{1,0:T(8,128)(2,1)}, bf16[512,1536]{1,0:T(8,128)(2,1)}, u32[]{:S(2)}, u32[]{:S(2)}) collective-permute-start(bf16[512,1536]{1,0:T(8,128)(2,1)} %collective-permute-done.10.refs_10_), channel_id=1, source_target_pairs={{0,4},{4,0},{1,5},{5,1},{2,6},{6,2},{3,7},{7,3},{8,12},{12,8},{9,1... | collective-permute-start | bytes 4718600 | tf_op jit(solution)/shard_map/ppermute | solution.py:60
  238.9 17.5 %collective-permute-start.23 = (bf16[256,1536]{1,0:T(8,128)(2,1)S(1)}, bf16[256,1536]{1,0:T(8,128)(2,1)S(1)}, u32[]{:S(2)}, u32[]{:S(2)}) collective-permute-start(bf16[256,1536]{1,0:T(8,128)(2,1)S(1)} %slice.513), channel_id=1, source_target_pairs={{0,16},{8,24},{16,0},{24,8},{1,17},{9,25},{17,1},{25,9},{2,18},{10... | collective-permute-start | bytes 2359304 | tf_op jit(solution)/shard_map/ppermute | solution.py:56
  241.4 18.4 %collective-permute-start.24 = (bf16[272,1536]{1,0:T(8,128)(2,1)S(1)}, bf16[272,1536]{1,0:T(8,128)(2,1)S(1)}, u32[]{:S(2)}, u32[]{:S(2)}) collective-permute-start(bf16[272,1536]{1,0:T(8,128)(2,1)S(1)} %slice.514), channel_id=1, source_target_pairs={{0,8},{8,0},{16,24},{24,16},{1,9},{9,1},{17,25},{25,17},{2,10},{10... | collective-permute-start | bytes 2506760 | tf_op jit(solution)/shard_map/ppermute | solution.py:56
  256.4 14.7 %collective-permute-start.25 = (bf16[528,1536]{1,0:T(8,128)(2,1)}, bf16[528,1536]{1,0:T(8,128)(2,1)}, u32[]{:S(2)}, u32[]{:S(2)}) collective-permute-start(bf16[528,1536]{1,0:T(8,128)(2,1)} %maximum_maximum_fusion.refs_0_), channel_id=1, source_target_pairs={{0,4},{4,0},{1,5},{5,1},{2,6},{6,2},{3,7},{7,3},{8,12},{12,8},{9,1... | collective-permute-start | bytes 4866056 | tf_op jit(solution)/shard_map/ppermute | solution.py:60
  259.8 11.4 %collective-permute-start.26 = (bf16[528,1536]{1,0:T(8,128)(2,1)}, bf16[528,1536]{1,0:T(8,128)(2,1)}, u32[]{:S(2)}, u32[]{:S(2)}) collective-permute-start(bf16[528,1536]{1,0:T(8,128)(2,1)} %collective-permute-done.21.refs_1_), channel_id=1, source_target_pairs={{0,4},{4,0},{1,5},{5,1},{2,6},{6,2},{3,7},{7,3},{8,12},{12,8},{9,1... | collective-permute-start | bytes 4866056 | tf_op jit(solution)/shard_map/ppermute | solution.py:60
  261.9 9.2 %collective-permute-start.27 = (bf16[528,1536]{1,0:T(8,128)(2,1)}, bf16[528,1536]{1,0:T(8,128)(2,1)}, u32[]{:S(2)}, u32[]{:S(2)}) collective-permute-start(bf16[528,1536]{1,0:T(8,128)(2,1)} %collective-permute-done.22.refs_2_), channel_id=1, source_target_pairs={{0,4},{4,0},{1,5},{5,1},{2,6},{6,2},{3,7},{7,3},{8,12},{12,8},{9,1... | collective-permute-start | bytes 4866056 | tf_op jit(solution)/shard_map/ppermute | solution.py:60
  262.4 8.7 %collective-permute-start.28 = (bf16[528,1536]{1,0:T(8,128)(2,1)}, bf16[528,1536]{1,0:T(8,128)(2,1)}, u32[]{:S(2)}, u32[]{:S(2)}) collective-permute-start(bf16[528,1536]{1,0:T(8,128)(2,1)} %constant_dynamic-update-slice_fusion.6.refs_3_), channel_id=1, source_target_pairs={{0,4},{4,0},{1,5},{5,1},{2,6},{6,2},{3,7},{7,3},{8,12},{12,8},{9,1... | collective-permute-start | bytes 4866056 | tf_op jit(solution)/shard_map/ppermute | solution.py:60
  262.4 8.7 %collective-permute-start.32 = (bf16[512,1536]{1,0:T(8,128)(2,1)}, bf16[512,1536]{1,0:T(8,128)(2,1)}, u32[]{:S(2)}, u32[]{:S(2)}) collective-permute-start(bf16[512,1536]{1,0:T(8,128)(2,1)} %constant_dynamic-update-slice_fusion.4.refs_11_), channel_id=1, source_target_pairs={{0,4},{4,0},{1,5},{5,1},{2,6},{6,2},{3,7},{7,3},{8,12},{12,8},{9,1... | collective-permute-start | bytes 4718600 | tf_op jit(solution)/shard_map/ppermute | solution.py:60
  327.0 304.7 %reduce-scatter.7.cloned.1.call-start = ((), (), s32[]{:S(2)}) async-start(), calls=%async_computation.5 | async-start | bytes 8847360 | tf_op jit(solution)/shard_map/reduce_scatter | solution.py:762
  372.7 10.7 %collective-permute-start.33 = (bf16[4,528,1536]{2,1,0:T(8,128)(2,1)}, bf16[4,528,1536]{2,1,0:T(8,128)(2,1)S(1)}, u32[]{:S(2)}, u32[]{:S(2)}) collective-permute-start(bf16[4,528,1536]{2,1,0:T(8,128)(2,1)} %get-tuple-element.80), channel_id=1, source_target_pairs={{0,4},{4,0},{1,5},{5,1},{2,6},{6,2},{3,7},{7,3},{8,12},{12,8},{9,1... | collective-permute-start | bytes 19464200 | tf_op jit(solution)/shard_map/ppermute | solution.py:60
  390.6 38.9 %collective-permute-start.35 = (bf16[2,272,1536]{2,1,0:T(8,128)(2,1)}, bf16[2,272,1536]{2,1,0:T(8,128)(2,1)}, u32[]{:S(2)}, u32[]{:S(2)}) collective-permute-start(bf16[2,272,1536]{2,1,0:T(8,128)(2,1)} %pad_maximum_fusion.1), channel_id=1, source_target_pairs={{0,16},{8,24},{16,0},{24,8},{1,17},{9,25},{17,1},{25,9},{2,18},{10... | collective-permute-start | bytes 5013512 | tf_op jit(solution)/shard_map/ppermute | solution.py:56
  392.8 36.4 %collective-permute-start.34 = (bf16[2,256,1536]{2,1,0:T(8,128)(2,1)}, bf16[2,256,1536]{2,1,0:T(8,128)(2,1)}, u32[]{:S(2)}, u32[]{:S(2)}) collective-permute-start(bf16[2,256,1536]{2,1,0:T(8,128)(2,1)} %pad_maximum_fusion.2), channel_id=1, source_target_pairs={{0,8},{8,0},{16,24},{24,16},{1,9},{9,1},{17,25},{25,17},{2,10},{10... | collective-permute-start | bytes 4718600 | tf_op jit(solution)/shard_map/ppermute | solution.py:56
  429.5 57.1 %collective-permute-start.36 = (bf16[4,512,1536]{2,1,0:T(8,128)(2,1)}, bf16[4,512,1536]{2,1,0:T(8,128)(2,1)}, u32[]{:S(2)}, u32[]{:S(2)}) collective-permute-start(bf16[4,512,1536]{2,1,0:T(8,128)(2,1)} %get-tuple-element.81), channel_id=1, source_target_pairs={{0,4},{4,0},{1,5},{5,1},{2,6},{6,2},{3,7},{7,3},{8,12},{12,8},{9,1... | collective-permute-start | bytes 18874376 | tf_op jit(solution)/shard_map/ppermute | solution.py:60
  432.0 21.3 %collective-permute-start.38 = (bf16[272,1536]{1,0:T(8,128)(2,1)}, bf16[272,1536]{1,0:T(8,128)(2,1)}, u32[]{:S(2)}, u32[]{:S(2)}) collective-permute-start(bf16[272,1536]{1,0:T(8,128)(2,1)} %fusion.36), channel_id=1, source_target_pairs={{0,8},{8,0},{16,24},{24,16},{1,9},{9,1},{17,25},{25,17},{2,10},{10... | collective-permute-start | bytes 2506760 | tf_op jit(solution)/shard_map/ppermute | solution.py:56
  450.5 20.0 %collective-permute-start.37 = (bf16[256,1536]{1,0:T(8,128)(2,1)}, bf16[256,1536]{1,0:T(8,128)(2,1)}, u32[]{:S(2)}, u32[]{:S(2)}) collective-permute-start(bf16[256,1536]{1,0:T(8,128)(2,1)} %fusion.37), channel_id=1, source_target_pairs={{0,16},{8,24},{16,0},{24,8},{1,17},{9,25},{17,1},{25,9},{2,18},{10... | collective-permute-start | bytes 2359304 | tf_op jit(solution)/shard_map/ppermute | solution.py:56
  459.9 76.0 %collective-permute-start.66 = (bf16[3,192,768]{2,1,0:T(8,128)(2,1)}, bf16[3,192,768]{2,1,0:T(8,128)(2,1)}, u32[]{:S(2)}, u32[]{:S(2)}) collective-permute-start(bf16[3,192,768]{2,1,0:T(8,128)(2,1)} %dynamic-slice_bitcast_fusion.1), channel_id=1, source_target_pairs={{0,4},{4,0},{1,5},{5,1},{2,6},{6,2},{3,7},{7,3},{8,12},{12,8},{9,1... | collective-permute-start | bytes 2654216 | tf_op jit(solution)/shard_map/ppermute | solution.py:60
  459.9 194.8 %reduce-scatter.9.cloned.1.call-start = ((), (), s32[]{:S(2)}) async-start(), calls=%async_computation.6 | async-start | bytes 737280 | tf_op jit(solution)/shard_map/reduce_scatter | solution.py:626
  486.6 60.7 %collective-permute-start.46 = (bf16[4,4,48,1536]{3,2,0,1:T(8,128)(2,1)}, bf16[4,4,48,1536]{3,2,0,1:T(8,128)(2,1)}, u32[]{:S(2)}, u32[]{:S(2)}) collective-permute-start(bf16[4,4,48,1536]{3,2,0,1:T(8,128)(2,1)} %copy_bitcast_fusion), channel_id=1, source_target_pairs={{0,4},{4,0},{1,5},{5,1},{2,6},{6,2},{3,7},{7,3},{8,12},{12,8},{9,1... | collective-permute-start | bytes 7077896 | tf_op jit(solution)/shard_map/ppermute | solution.py:60
  493.8 45.1 %collective-permute-start.41 = (bf16[2,256,1536]{2,1,0:T(8,128)(2,1)}, bf16[2,256,1536]{2,1,0:T(8,128)(2,1)}, u32[]{:S(2)}, u32[]{:S(2)}) collective-permute-start(bf16[2,256,1536]{2,1,0:T(8,128)(2,1)} %pad_maximum_fusion.4), channel_id=1, source_target_pairs={{0,16},{8,24},{16,0},{24,8},{1,17},{9,25},{17,1},{25,9},{2,18},{10... | collective-permute-start | bytes 4718600 | tf_op jit(solution)/shard_map/ppermute | solution.py:56
  496.2 42.6 %collective-permute-start.39 = (bf16[2,256,1536]{2,1,0:T(8,128)(2,1)}, bf16[2,256,1536]{2,1,0:T(8,128)(2,1)}, u32[]{:S(2)}, u32[]{:S(2)}) collective-permute-start(bf16[2,256,1536]{2,1,0:T(8,128)(2,1)} %pad_maximum_fusion.3), channel_id=1, source_target_pairs={{0,8},{8,0},{16,24},{24,16},{1,9},{9,1},{17,25},{25,17},{2,10},{10... | collective-permute-start | bytes 4718600 | tf_op jit(solution)/shard_map/ppermute | solution.py:56
  534.2 20.0 %collective-permute-start.44 = (bf16[4,4,48,1536]{3,2,0,1:T(8,128)(2,1)}, bf16[4,4,48,1536]{3,2,0,1:T(8,128)(2,1)}, u32[]{:S(2)}, u32[]{:S(2)}) collective-permute-start(bf16[4,4,48,1536]{3,2,0,1:T(8,128)(2,1)} %copy_bitcast_fusion.1), channel_id=1, source_target_pairs={{0,4},{4,0},{1,5},{5,1},{2,6},{6,2},{3,7},{7,3},{8,12},{12,8},{9,1... | collective-permute-start | bytes 7077896 | tf_op jit(solution)/shard_map/ppermute | solution.py:60
  538.8 19.7 %collective-permute-start.43 = (bf16[512,512]{1,0:T(8,128)(2,1)S(1)}, bf16[512,512]{1,0:T(8,128)(2,1)}, u32[]{:S(2)}, u32[]{:S(2)}) collective-permute-start(bf16[512,512]{1,0:T(8,128)(2,1)S(1)} %copy-done.65), channel_id=1, source_target_pairs={{4,0},{5,1},{6,2},{7,3},{12,8},{13,9},{14,10},{15,11},{20,16},{21,... | collective-permute-start | bytes 1572872 | tf_op jit(solution)/shard_map/ppermute | solution.py:782
  542.7 48.8 %collective-permute-start.42 = (bf16[256,1536]{1,0:T(8,128)(2,1)}, bf16[256,1536]{1,0:T(8,128)(2,1)}, u32[]{:S(2)}, u32[]{:S(2)}) collective-permute-start(bf16[256,1536]{1,0:T(8,128)(2,1)} %fusion.39), channel_id=1, source_target_pairs={{0,8},{8,0},{16,24},{24,16},{1,9},{9,1},{17,25},{25,17},{2,10},{10... | collective-permute-start | bytes 2359304 | tf_op jit(solution)/shard_map/ppermute | solution.py:56
  546.3 44.0 %collective-permute-start.40 = (bf16[256,1536]{1,0:T(8,128)(2,1)}, bf16[256,1536]{1,0:T(8,128)(2,1)}, u32[]{:S(2)}, u32[]{:S(2)}) collective-permute-start(bf16[256,1536]{1,0:T(8,128)(2,1)} %fusion.38), channel_id=1, source_target_pairs={{0,16},{8,24},{16,0},{24,8},{1,17},{9,25},{17,1},{25,9},{2,18},{10... | collective-permute-start | bytes 2359304 | tf_op jit(solution)/shard_map/ppermute | solution.py:56
  552.2 44.6 %collective-permute-start.49 = (bf16[2,2,48,1536]{3,2,1,0:T(8,128)(2,1)}, bf16[2,2,48,1536]{3,2,1,0:T(8,128)(2,1)}, u32[]{:S(2)}, u32[]{:S(2)}) collective-permute-start(bf16[2,2,48,1536]{3,2,1,0:T(8,128)(2,1)} %pad_maximum_fusion.9), channel_id=1, source_target_pairs={{0,16},{8,24},{16,0},{24,8},{1,17},{9,25},{17,1},{25,9},{2,18},{10... | collective-permute-start | bytes 1769480 | tf_op jit(solution)/shard_map/ppermute | solution.py:56
  554.2 44.6 %collective-permute-start.47 = (bf16[2,2,48,1536]{3,2,1,0:T(8,128)(2,1)}, bf16[2,2,48,1536]{3,2,1,0:T(8,128)(2,1)}, u32[]{:S(2)}, u32[]{:S(2)}) collective-permute-start(bf16[2,2,48,1536]{3,2,1,0:T(8,128)(2,1)} %pad_maximum_fusion.8), channel_id=1, source_target_pairs={{0,8},{8,0},{16,24},{24,16},{1,9},{9,1},{17,25},{25,17},{2,10},{10... | collective-permute-start | bytes 1769480 | tf_op jit(solution)/shard_map/ppermute | solution.py:56
  590.3 10.6 %collective-permute-start.45 = (bf16[4,4,48,512]{3,2,0,1:T(8,128)(2,1)S(1)}, bf16[4,4,48,512]{3,2,0,1:T(8,128)(2,1)S(1)}, u32[]{:S(2)}, u32[]{:S(2)}) collective-permute-start(bf16[4,4,48,512]{3,2,0,1:T(8,128)(2,1)S(1)} %copy_bitcast_fusion.2), channel_id=1, source_target_pairs={{0,4},{4,0},{1,5},{5,1},{2,6},{6,2},{3,7},{7,3},{8,12},{12,8},{9,1... | collective-permute-start | bytes 2359304 | tf_op jit(solution)/shard_map/ppermute | solution.py:60
  590.4 41.6 %collective-permute-start.59 = (bf16[2,48,128]{2,1,0:T(8,128)(2,1)}, bf16[2,48,128]{2,1,0:T(8,128)(2,1)S(1)}, u32[]{:S(2)}, u32[]{:S(2)}) collective-permute-start(bf16[2,48,128]{2,1,0:T(8,128)(2,1)} %fusion.84), channel_id=1, source_target_pairs={{0,8},{8,0},{16,24},{24,16},{1,9},{9,1},{17,25},{25,17},{2,10},{10... | collective-permute-start | bytes 73736 | tf_op jit(solution)/shard_map/ppermute | solution.py:56
  597.9 10.6 %collective-permute-start.50 = (bf16[2,48,1536]{2,1,0:T(8,128)(2,1)S(1)}, bf16[2,48,1536]{2,1,0:T(8,128)(2,1)S(1)}, u32[]{:S(2)}, u32[]{:S(2)}) collective-permute-start(bf16[2,48,1536]{2,1,0:T(8,128)(2,1)S(1)} %fusion.50), channel_id=1, source_target_pairs={{0,8},{8,0},{16,24},{24,16},{1,9},{9,1},{17,25},{25,17},{2,10},{10... | collective-permute-start | bytes 884744 | tf_op jit(solution)/shard_map/ppermute | solution.py:56
  608.5 18.2 %collective-permute-start.53 = (bf16[2,2,48,2048]{3,2,1,0:T(8,128)(2,1)S(1)}, bf16[2,2,48,2048]{3,2,1,0:T(8,128)(2,1)S(1)}, u32[]{:S(2)}, u32[]{:S(2)}) collective-permute-start(bf16[2,2,48,2048]{3,2,1,0:T(8,128)(2,1)S(1)} %pad_maximum_fusion.7), channel_id=1, source_target_pairs={{0,16},{8,24},{16,0},{24,8},{1,17},{9,25},{17,1},{25,9},{2,18},{10... | collective-permute-start | bytes 2359304 | tf_op jit(solution)/shard_map/ppermute | solution.py:56
  609.6 19.3 %collective-permute-start.51 = (bf16[2,2,48,2048]{3,2,1,0:T(8,128)(2,1)S(1)}, bf16[2,2,48,2048]{3,2,1,0:T(8,128)(2,1)S(1)}, u32[]{:S(2)}, u32[]{:S(2)}) collective-permute-start(bf16[2,2,48,2048]{3,2,1,0:T(8,128)(2,1)S(1)} %pad_maximum_fusion.6), channel_id=1, source_target_pairs={{0,8},{8,0},{16,24},{24,16},{1,9},{9,1},{17,25},{25,17},{2,10},{10... | collective-permute-start | bytes 2359304 | tf_op jit(solution)/shard_map/ppermute | solution.py:56
  627.7 11.1 %collective-permute-start.54 = (bf16[2,48,2048]{2,1,0:T(8,128)(2,1)}, bf16[2,48,2048]{2,1,0:T(8,128)(2,1)}, u32[]{:S(2)}, u32[]{:S(2)}) collective-permute-start(bf16[2,48,2048]{2,1,0:T(8,128)(2,1)} %fusion.40), channel_id=1, source_target_pairs={{0,8},{8,0},{16,24},{24,16},{1,9},{9,1},{17,25},{25,17},{2,10},{10... | collective-permute-start | bytes 1179656 | tf_op jit(solution)/shard_map/ppermute | solution.py:56
  629.8 8.9 %collective-permute-start.52 = (bf16[2,48,2048]{2,1,0:T(8,128)(2,1)}, bf16[2,48,2048]{2,1,0:T(8,128)(2,1)}, u32[]{:S(2)}, u32[]{:S(2)}) collective-permute-start(bf16[2,48,2048]{2,1,0:T(8,128)(2,1)} %fusion.43), channel_id=1, source_target_pairs={{0,16},{8,24},{16,0},{24,8},{1,17},{9,25},{17,1},{25,9},{2,18},{10... | collective-permute-start | bytes 1179656 | tf_op jit(solution)/shard_map/ppermute | solution.py:56
  631.7 47.8 %reduce-scatter.11.cloned.1.call-start = ((), (), s32[]{:S(2)}) async-start(), calls=%async_computation.7 | async-start | bytes 1044480 | tf_op jit(solution)/shard_map/reduce_scatter | solution.py:626
  643.8 18.2 %collective-permute-start.67 = (bf16[3,192,768]{2,1,0:T(8,128)(2,1)}, bf16[3,192,768]{2,1,0:T(8,128)(2,1)}, u32[]{:S(2)}, u32[]{:S(2)}) collective-permute-start(bf16[3,192,768]{2,1,0:T(8,128)(2,1)} %dynamic-slice_bitcast_fusion), channel_id=1, source_target_pairs={{0,4},{4,0},{1,5},{5,1},{2,6},{6,2},{3,7},{7,3},{8,12},{12,8},{9,1... | collective-permute-start | bytes 2654216 | tf_op jit(solution)/shard_map/ppermute | solution.py:60
  681.0 10.7 %collective-permute-start.61 = (bf16[48,2176]{1,0:T(8,128)(2,1)}, bf16[48,2176]{1,0:T(8,128)(2,1)S(1)}, u32[]{:S(2)}, u32[]{:S(2)}) collective-permute-start(bf16[48,2176]{1,0:T(8,128)(2,1)} %bitcast.446), channel_id=1, source_target_pairs={{0,16},{8,24},{16,0},{24,8},{1,17},{9,25},{17,1},{25,9},{2,18},{10... | collective-permute-start | bytes 626696 | tf_op jit(solution)/shard_map/ppermute | solution.py:56
  682.4 9.2 %collective-permute-start.62 = (bf16[48,2176]{1,0:T(8,128)(2,1)}, bf16[48,2176]{1,0:T(8,128)(2,1)S(1)}, u32[]{:S(2)}, u32[]{:S(2)}) collective-permute-start(bf16[48,2176]{1,0:T(8,128)(2,1)} %bitcast.447), channel_id=1, source_target_pairs={{0,24},{8,16},{16,8},{24,0},{1,25},{9,17},{17,9},{25,1},{2,26},{10... | collective-permute-start | bytes 626696 | tf_op jit(solution)/shard_map/ppermute | solution.py:56
  (86 other events, 585.8 us)
Sparse Core Ops, SparseCore 0:
  11.3 37.3 all-gather.6
  50.9 128.5 all-gather.8
  181.6 127.8 all-gather.10
  327.1 124.6 reduce-scatter.4
  460.1 125.2 reduce-scatter.6
  631.8 22.9 reduce-scatter.8
  657.1 22.3 reduce-scatter.10

commit v3 on v2

--- a/solution.py
+++ b/solution.py
@@ -133,18 +133,23 @@
     return size // 2 if size < 32 else size // 32 * 16
 
 
-def fourth_block(one, two, *later):
+def fourth_block(one, two):
     cut = halves_of(one.shape[0])
-    first, second = flip(after(one[:cut], *later), 2), flip(after(two[cut:], *later), 1)
-    return jnp.concatenate([first, second], axis=0)
+    return jnp.concatenate([flip(one[:cut], 2), flip(two[cut:], 1)], axis=0)
+
+
+def gather_first(block):
+    count = lax.axis_size("expert")
+    return [flip(block, k) for k in ((1, 2) if count == 4 else range(1, count))]
+
+
+def gather_second(came):
+    return [fourth_block(*came)] if lax.axis_size("expert") == 4 else []
 
 
 def gather_blocks(block):
-    count = lax.axis_size("expert")
-    if count != 4:
-        return [block] + [flip(block, k) for k in range(1, count)]
-    one, two = flip(block, 1), flip(block, 2)
-    return [block, one, two, fourth_block(one, two)]
+    came = gather_first(block)
+    return [block, *came, *gather_second(came)]
 
 
 def spread(block):
@@ -152,28 +157,37 @@
     return own, [swap(b) for b in own]
 
 
-def scatter_blocks(parts, before=(), between=(), finish=()):
+def scatter_first(parts):
     count = lax.axis_size("expert")
     if count != 4:
-        came = [flip(after(parts[k], *before), k) for k in range(1, count)]
-        return add_all(parts[0], came), came, came
+        return [flip(parts[k], k) for k in range(1, count)]
     cut = halves_of(parts[0].shape[0])
-    top, bottom = [p[:cut] for p in parts], [p[cut:] for p in parts]
-    top_sent = after(jnp.stack([top[1], top[3]]), *before)
-    bottom_sent = after(jnp.stack([bottom[2], bottom[3]]), *before)
-    top_came, bottom_came = flip(top_sent, 1), flip(bottom_sent, 2)
-    top_next = add_all(top[2], [top_came[1]]).astype(bf16)
-    bottom_next = add_all(bottom[1], [bottom_came[1]]).astype(bf16)
-    top_last = after(flip(after(top_next, *between), 2), *finish)
-    bottom_last = flip(after(bottom_next, *between), 1)
-    total = jnp.concatenate(
-        [
-            add_all(top[0], [top_came[0], top_last]),
-            add_all(bottom[0], [bottom_came[0], bottom_last]),
-        ],
-        axis=0,
-    )
-    return total, [top_came, bottom_came], [top_last, bottom_last]
+    top = jnp.stack([parts[1][:cut], parts[3][:cut]])
+    bottom = jnp.stack([parts[2][cut:], parts[3][cut:]])
+    return [flip(top, 1), flip(bottom, 2)]
+
+
+def scatter_second(parts, came):
+    if lax.axis_size("expert") != 4:
+        return []
+    cut = halves_of(parts[0].shape[0])
+    top = add_all(parts[2][:cut], [came[0][1]]).astype(bf16)
+    bottom = add_all(parts[1][cut:], [came[1][1]]).astype(bf16)
+    return [flip(top, 2), flip(bottom, 1)]
+
+
+def scatter_total(parts, came, last):
+    if lax.axis_size("expert") != 4:
+        return add_all(parts[0], came)
+    cut = halves_of(parts[0].shape[0])
+    top = add_all(parts[0][:cut], [came[0][0], last[0]])
+    bottom = add_all(parts[0][cut:], [came[1][0], last[1]])
+    return jnp.concatenate([top, bottom], axis=0)
+
+
+def tie_lists(*lists):
+    flat = iter(tie(*(v for values in lists for v in values)))
+    return [[next(flat) for _ in values] for values in lists]
 
 
 GELU_C = math.sqrt(2.0 / math.pi)
@@ -340,29 +354,49 @@
     )(place, *acts, *dys, weights, *earlier)
 
 
-def weight_grad_kernel(x_ref, gdy_ref, h_ref, dg_ref, du_ref, out_ref):
-    shape = (out_ref.shape[0], out_ref.shape[3], FF)
-    x = x_ref[...]
+def weight_grad_kernel(per, x_ref, gdy_ref, h_ref, dg_ref, du_ref, *out_refs):
     first = ((0,), (0,))
-    out_ref[:, 0, 0] = dot(x, dg_ref[...], first).astype(bf16).reshape(shape)
-    out_ref[:, 0, 1] = dot(x, du_ref[...], first).astype(bf16).reshape(shape)
-    out_ref[:, 0, 2] = dot(gdy_ref[...], h_ref[...], first).astype(bf16).reshape(shape)
-
-
-def weight_grads(x, gdy, hidden, dgate, dup, z, local):
+
+    def write(out_ref):
+        shape = (out_ref.shape[0], out_ref.shape[2], FF)
+        x = x_ref[...]
+        out_ref[:, 0] = dot(x, dg_ref[...], first).astype(bf16).reshape(shape)
+        out_ref[:, 1] = dot(x, du_ref[...], first).astype(bf16).reshape(shape)
+        out_ref[:, 2] = dot(gdy_ref[...], h_ref[...], first).astype(bf16).reshape(shape)
+
+    if len(out_refs) == 1:
+        write(out_refs[0].at[:, 0])
+    else:
+        for c, out_ref in enumerate(out_refs):
+            pl.when(lax.div(pl.program_id(0), per) == c)(functools.partial(write, out_ref))
+
+
+def weight_grads(x, gdy, hidden, dgate, dup, z, local, split):
     total = x.shape[0]
     wide = 384
     per = MODEL_WIDTH // 2 // wide
     full = pl.BlockSpec((total, FF), lambda i: (0, 0))
     column = pl.BlockSpec((total, wide), lambda i: (0, i))
+    block = wide // local
+    if split:
+        shapes = [jax.ShapeDtypeStruct((z, 3, local, FF), bf16)] * 2
+        specs = [
+            pl.BlockSpec((block, 3, local, FF), lambda i: (jnp.minimum(i, per - 1), 0, 0, 0)),
+            pl.BlockSpec((block, 3, local, FF), lambda i: (jnp.maximum(i - per, 0), 0, 0, 0)),
+        ]
+    else:
+        shapes = [jax.ShapeDtypeStruct((z, 2, 3, local, FF), bf16)]
+        specs = [
+            pl.BlockSpec(
+                (block, 1, 3, local, FF), lambda i: (lax.rem(i, per), lax.div(i, per), 0, 0, 0)
+            )
+        ]
     return pl.pallas_call(
-        weight_grad_kernel,
-        out_shape=jax.ShapeDtypeStruct((z, 2, 3, local, FF), bf16),
+        functools.partial(weight_grad_kernel, per),
+        out_shape=shapes,
         grid=(MODEL_WIDTH // wide,),
         in_specs=[column, column, full, full, full],
-        out_specs=pl.BlockSpec(
-            (wide // local, 1, 3, local, FF), lambda i: (lax.rem(i, per), lax.div(i, per), 0, 0, 0)
-        ),
+        out_specs=specs,
         compiler_params=pltpu.CompilerParams(
             dimension_semantics=("arbitrary",), vmem_limit_bytes=VMEM_LIMIT
         ),
@@ -596,22 +630,6 @@
             sums.append(a.astype(f32) + b.astype(f32))
         out.append(jnp.concatenate(sums, axis=-1).astype(bf16))
     return out
-
-
-def line_step(grads, step, came):
-    z = lax.axis_size("dp")
-    me = lax.axis_index("dp")
-
-    def part(at, arrived):
-        own = lax.dynamic_index_in_dim(grads, jnp.clip(at, 0, z - 1), 0, keepdims=False)
-        return own if arrived is None else add_all(own, [arrived]).astype(bf16)
-
-    up = part(z - step + me, came[0])
-    down = part(step + me - z, came[1])
-    return (
-        lax.ppermute(up, "dp", [(i, i + 1) for i in range(step)]),
-        lax.ppermute(down, "dp", [(i, i - 1) for i in range(z - step, z)]),
-    )
 
 
 def add_all(own, came):
@@ -660,6 +678,14 @@
     rows = w_query.shape[0]
     piece = rows // count
 
+    def chunk(j):
+        parts = []
+        for at in range(j, EXP_DEV, per_core):
+            parts += [w_gate[at], w_up[at], w_down[at].T]
+        return jnp.concatenate([p.astype(bf16) for p in parts], axis=0)
+
+    chunks = [chunk(j) for j in range(per_core)]
+
     def quarter(parts):
         cut = [
             lax.dynamic_slice_in_dim(p, expert * piece, piece, axis=0).astype(bf16) for p in parts
@@ -667,7 +693,7 @@
         return jnp.concatenate(cut, axis=1)
 
     pad = jnp.zeros((rows, SMALL - experts_all - 2), f32)
-    pack = quarter(
+    first_pack = quarter(
         [
             w_query,
             key_projection,
@@ -676,38 +702,27 @@
             attn_gain[:, None],
             ffn_gain[:, None],
             pad,
-            w_out,
         ]
     )
-    dense_z = lax.all_gather(pack, "dp", axis=0, tiled=False)
-    cut = Q_WIDTH + 2 * KV_WIDTH + SMALL
-    own_one, other_one = spread(dense_z[..., :cut])
-    dy_half = after(out_grad[0], *own_one[1:])
-    dy_first = [flip(dy_half, k) for k in ((1, 2) if count == 4 else range(1, count))]
-    own_two, other_two = spread(after(dense_z[..., cut:], *dy_first))
-    if count == 4:
-        dys_own = [dy_half, *dy_first, fourth_block(*dy_first, *own_two[1:])]
-    else:
-        dys_own = [dy_half, *dy_first]
-    dys_other = [swap(b) for b in dys_own]
+    second_both = lax.all_gather(quarter([w_out]), ("context", "dp"), axis=0, tiled=False)
+    second_both = second_both.reshape(2, z, piece, MODEL_WIDTH)
+    first_pack, chunks[0] = tie(first_pack, chunks[0])
+    first_z = lax.all_gather(first_pack, "dp", axis=0, tiled=False)
+    own_one, other_one = spread(first_z)
+    gathered = [lax.all_gather(chunks[0], ("context", "dp"), axis=0, tiled=False)]
+    for sent in chunks[1:]:
+        sent = after(sent, first_z)
+        gathered.append(lax.all_gather(sent, ("context", "dp"), axis=0, tiled=False))
+    gathered = [came.reshape(2 * z, 2, 3, rows, FF) for came in gathered]
+    second_z = lax.dynamic_index_in_dim(second_both, context, 0, keepdims=False)
+    second_other = lax.dynamic_index_in_dim(second_both, 1 - context, 0, keepdims=False)
+    second_came = gather_first(after(second_z, *own_one[1:3]))
     packed = assemble(own_one, other_one, context, expert)
     qkv_w = packed[:, : Q_WIDTH + 2 * KV_WIDTH]
     router_w = packed[:, Q_WIDTH + 2 * KV_WIDTH :][:, :experts_all]
     small = packed[:, Q_WIDTH + 2 * KV_WIDTH :].T
     gain_one = small[experts_all].astype(f32)
     gain_two = small[experts_all + 1].astype(f32)
-
-    def chunk(j):
-        parts = []
-        for at in range(j, EXP_DEV, per_core):
-            parts += [w_gate[at], w_up[at], w_down[at].T]
-        return jnp.concatenate([p.astype(bf16) for p in parts], axis=0)
-
-    gathered = []
-    for j in range(per_core):
-        sent = after(chunk(j), dense_z)
-        came = lax.all_gather(sent, ("context", "dp"), axis=0, tiled=False)
-        gathered.append(came.reshape(2 * z, 2, 3, rows, FF))
 
     route_t = routes[0].T
     expert_ids = jnp.arange(experts_all, dtype=jnp.int32)
@@ -722,6 +737,11 @@
     scale_one, norm_one = norm_parts(inputs_f)
     act_one = (norm_one * gain_one).astype(bf16)
     qkv = dot(act_one, qkv_w)
+    (qkv,), second_came = tie_lists((qkv,), second_came)
+    own_two = [second_z, *second_came, *gather_second(second_came)]
+    other_two = [second_other] + [swap(b) for b in own_two[1:]]
+    dy_half = after(out_grad[0], *own_two[1:])
+    dy_came = gather_first(dy_half)
     cosine, sine = rope_tables(context * tokens, tokens, HEAD_SIZE)
     cos_wide = jnp.concatenate([cosine, cosine], axis=1)
     sin_wide = jnp.concatenate([-sine, sine], axis=1)
@@ -729,6 +749,9 @@
     far = lax.ppermute(near, "context", [(0, 1)])
     where = context[None].astype(jnp.int32)
     query, mixed, logs = attention(where, qkv, near, far, cos_wide, sin_wide)
+    (mixed,), dy_came = tie_lists((mixed,), dy_came)
+    dys_own = [dy_half, *dy_came, *gather_second(dy_came)]
+    dys_other = [swap(b) for b in dys_own]
     out_w = assemble(own_two, other_two, context, expert)
     resid_one = inputs_f + dot(mixed, out_w)
     scale_two, norm_two = norm_parts(resid_one)
@@ -753,66 +776,75 @@
         )
         if j == per_core - 1:
             d_parts = block_parts(sums[2], sums[3])
-            x = after(x, d_parts[-1])
-        grads = weight_grads(x, gdy, hidden, dgate, dup, z, rows)
-        place, grads = tie(place + step, grads)
+            (x, y_other), d_parts = tie_lists((x, sums[1]), d_parts)
+            d_came = scatter_first(d_parts)
+        grads = weight_grads(x, gdy, hidden, dgate, dup, z, rows, True)
+        (place,), grads = tie_lists((place + step,), grads)
         if j == per_core - 1:
-            dact, came, last = scatter_blocks(d_parts, (), (), [shares[-1], grads])
-            grads, shares[-1] = tie(grads, shares[-1])
-        shares.append(lax.psum_scatter(grads, "dp", scatter_dimension=0, tiled=False))
-    y_parts = block_parts(sums[0], after(sums[1], *came))
-    y_sum, y_came, _ = scatter_blocks(y_parts, last)
+            y_parts = block_parts(sums[0], y_other)
+            d_came, grads = tie_lists(d_came, grads)
+            d_last = scatter_second(d_parts, d_came)
+            d_last, y_parts, shares[-1] = tie_lists(d_last, y_parts, shares[-1])
+        shares.append([lax.psum_scatter(g, "dp", scatter_dimension=0, tiled=False) for g in grads])
+    dact = scatter_total(d_parts, d_came, d_last)
+    y_came = scatter_first(y_parts)
 
     dy = out_grad[0].astype(f32)
     dgates = dact[tokens:, :tokens] + dact[tokens:, tokens : 2 * tokens]
     dlogits = (gates * (dgates - jnp.sum(gates * dgates, axis=0, keepdims=True))).astype(bf16)
     dact_two = dact[:tokens] + dot(dlogits, router_w, ((0,), (1,)))
-    grad_router = dot(act_two, dlogits, ((0,), (1,)))
+    grad_router = dot(dlogits, act_two)
     grad_gain_two = jnp.sum(dact_two * norm_two, axis=0)
     dn2 = dact_two * gain_two
     dresid = dy + scale_two * (dn2 - norm_two * jnp.mean(dn2 * norm_two, axis=-1, keepdims=True))
     dresid_b = dresid.astype(bf16)
     dmixed = dot(dresid_b, out_w, ((1,), (1,))).astype(bf16)
     out_halves = swap_halves(dot(mixed, after(dresid_b, dmixed), ((0,), (0,))), context)
-    out_total, out_first, out_came = scatter_blocks(dense_parts([out_halves], expert))
 
     dquery, near_grad, far_grad = attention_back(
         where, query, dmixed, near, far, logs, cos_wide, sin_wide
     )
-    came = lax.ppermute(after(far_grad, *y_came), "context", [(1, 0)])
+    (far_grad,), y_came = tie_lists((far_grad,), y_came)
+    came = lax.ppermute(far_grad, "context", [(1, 0)])
     grad_query = dot(act_one, dquery, ((0,), (0,))).astype(bf16)
     dkv = key_value_back(near_grad, came, cos_wide, sin_wide)
     grad_kv = dot(act_one, dkv, ((0,), (0,))).astype(bf16)
     dact_one = dot(dquery, qkv_w[:, :Q_WIDTH], ((1,), (1,)))
-    dact_one = dact_one + dot(after(dkv, grad_kv), qkv_w[:, Q_WIDTH:], ((1,), (1,)))
+    dact_one = dact_one + dot(dkv, qkv_w[:, Q_WIDTH:], ((1,), (1,)))
     grad_gain_one = jnp.sum(dact_one * norm_one, axis=0)
+    small = jnp.concatenate(
+        [
+            grad_router,
+            grad_gain_one[None],
+            grad_gain_two[None],
+            jnp.zeros((SMALL - experts_all - 2, MODEL_WIDTH), f32),
+        ],
+        axis=0,
+    )
+    halves = [swap_halves(grad, context) for grad in (grad_query, grad_kv, small.T)]
+    first_parts = dense_parts(halves, expert)
+    first_came = scatter_first(first_parts)
+    out_parts = dense_parts([out_halves], expert)
+    out_came = scatter_first(out_parts)
+    out_total = scatter_total(out_parts, out_came, scatter_second(out_parts, out_came))
+
     dn1 = dact_one * gain_one
     grad_in = dresid + scale_one * (dn1 - norm_one * jnp.mean(dn1 * norm_one, axis=-1, keepdims=True))
-    grad_small = jnp.concatenate(
-        [
-            grad_router,
-            grad_gain_one[:, None],
-            grad_gain_two[:, None],
-            jnp.zeros((MODEL_WIDTH, SMALL - experts_all - 2), f32),
-        ],
-        axis=1,
-    )
+    y_came, first_came = tie_lists(y_came, first_came)
+    first_total = scatter_total(first_parts, first_came, scatter_second(first_parts, first_came))
+    y_sum = scatter_total(y_parts, y_came, scatter_second(y_parts, y_came))
     block_out = (resid_one + y_sum).astype(bf16)[None]
-    out_total, shares[-1] = tie(out_total.astype(bf16), shares[-1])
+    out_total, shares[-1][-1] = tie(out_total.astype(bf16), shares[-1][-1])
     grad_out, out_share = finish_dense(out_total, expert)
-    halves = [swap_halves(grad, context) for grad in (grad_query, grad_kv)]
-    first_total, _, _ = scatter_blocks(dense_parts(halves, expert), out_came)
-    small_total, _, _ = scatter_blocks(dense_parts([swap_halves(grad_small, context)], expert))
-    first_total = jnp.concatenate([first_total, small_total], axis=-1).astype(bf16)
-    first_total, out_share = tie(first_total, out_share)
-    first, _ = finish_dense(first_total, expert)
+    first, _ = finish_dense(first_total.astype(bf16), expert)
     kv_at = Q_WIDTH + KV_WIDTH
     small_at = kv_at + KV_WIDTH
 
     finals = []
-    for share in shares:
-        keep = lax.dynamic_index_in_dim(share, context, 0, keepdims=False)
-        came = swap(lax.dynamic_index_in_dim(share, 1 - context, 0, keepdims=False))
+    for pair in shares:
+        low, high = pair if len(pair) == 2 else (pair[0][0], pair[0][1])
+        keep = jnp.where(context == 0, low, high)
+        came = swap(jnp.where(context == 0, high, low))
         finals.append((jnp.where(context == 0, keep, came), jnp.where(context == 0, came, keep)))
     stacked = jnp.stack([f[c] for c in range(2) for f in finals])
     stacked = stacked.astype(f32)

time: 715 us -> 662 us (0.926)
  waiting for transfers between devices: 266 us -> 199 us
  blocking collectives: 0 us -> 25.7 us
  local copies, waits for them, and re-layouts: 63.8 us -> 54.6 us
    ppermute x42 -> x38, waiting for transfers between devices: 201 us -> 154 us  [flip(): return lax.ppermute(value, 'expert', [(i, i ^ step) for i in range(count)])]
    all_gather x3, waiting for transfers between devices: 28.2 us -> 1.04 us  [the longest x1 1 us: local(): lax.all_gather(sent, ('context', 'dp'), axis=0, tiled=False)]
    all_gather x0 -> x1, blocking collectives: none -> 25.7 us  [local(): first_z = lax.all_gather(first_pack, 'dp', axis=0, tiled=False)]
    reduce_scatter x2 -> x4, waiting for transfers between devices: 0.01 us -> 12.9 us  [local(): lax.psum_scatter(g, 'dp', scatter_dimension=0, tiled=False)]
    reduce_scatter x2, waiting for transfers between devices: 16.6 us -> 8.06 us  [finish_dense(): share = lax.psum_scatter(total, 'dp', scatter_dimension=0, tiled=False)]
    ppermute x42 -> x38, starting transfers between devices: 47.2 us -> 43.3 us  [flip(): return lax.ppermute(value, 'expert', [(i, i ^ step) for i in range(count)])]
    ppermute x24 -> x23, waiting for transfers between devices: 18.6 us -> 21.7 us  [swap(): return lax.ppermute(value, 'context', [(0, 1), (1, 0)])]
    another operation x21 -> x16, other arithmetic: 17.3 us -> 15.1 us
  transfers between devices with their start and end apart: 75 -> 72, of which waited for: 28 -> 29; matrix products, arithmetic and copies ran while one was open for 23% -> 24% of each run, Pallas kernels for 26% -> 28%
where the time goes in v3:
time: 662 us; the launch traced here: 655 us
  waiting for transfers between devices  199 us (30%)
  Pallas kernels  182 us (27%)
  other arithmetic  81.1 us (12%)
  local copies, waits for them, and re-layouts  54.6 us (8%)
  starting transfers between devices  53.7 us (8%)
  matrix products  43.1 us (7%)
  blocking collectives  25.7 us (4%)
  between operations  15.4 us (2%)
    ppermute x38, waiting for transfers between devices, flip(): return lax.ppermute(value, 'expert', [(i, i ^ step) for i in range(count)])  154 us
    pallas_call x2, Pallas kernels, run_expert(): pl.pallas_call(functools.partial(expert_kernel, count, tokens, capacity),...  85.6 us
    ppermute x38, starting transfers between devices, flip(): return lax.ppermute(value, 'expert', [(i, i ^ step) for i in range(count)])  43.3 us
    dot_general x12, matrix products, dot(): return lax.dot_general(a, b, (dims, ((), ())), preferred_element_type=f32)  43.1 us
    pallas_call x2, Pallas kernels, weight_grads(): pl.pallas_call(functools.partial(weight_grad_kernel, per), out_shape=shap...  31 us
    pallas_call x1, Pallas kernels, attention_back(): pl.pallas_call(attend_back_kernel, out_shape=(jax.ShapeDtypeStruct((token...  29.4 us
    all_gather x1, blocking collectives, local(): first_z = lax.all_gather(first_pack, 'dp', axis=0, tiled=False)  25.7 us
    ppermute x23, waiting for transfers between devices, swap(): return lax.ppermute(value, 'context', [(0, 1), (1, 0)])  21.7 us
  transfers between devices with their start and end apart: 72, of which 29 were waited for; matrix products, arithmetic and copies ran while one was open for 24% of the time, Pallas kernels for 28%

profile of v3, /device:TPU:0, one launch (start us, length us, event | category | flops | bytes accessed | tf_op | source)
XLA Modules:
  0.0 654.8 jit_solution(18080751636993826649)
XLA Ops:
  11.1 2.9 convert.130
  21.9 25.7 %all-gather = bf16[192,2176]{1,0:T(8,128)(2,1)S(1)} all-gather(bf16[48,2176]{1,0:T(8,128)(2,1)S(1)} %concatenate.73), channel_id=2, replica_groups=mesh['expert'=4,'context'=2,'dp'=4] {'dp'}, dimensions={0}, use_global_device_ids=true | all-gather | bytes 1044480 | tf_op jit(solution)/shard_map/all_gather | solution.py:710
  50.6 16.8 %collective-permute-done.refs_1_ = bf16[4,48,2176]{2,1,0:T(8,128)(2,1)} collective-permute-done((bf16[4,48,2176]{2,1,0:T(8,128)(2,1)S(1)}, bf16[4,48,2176]{2,1,0:T(8,128)(2,1)}, u32[]{:S(2)}, u32[]{:S(2)}) %collective-permute-start) | collective-permute-done | bytes 835616 | tf_op jit(solution)/shard_map/ppermute | solution.py:56
  73.1 5.2 collective-permute-done.2
  82.4 2.1 dynamic-slice_bitcast_fusion
  86.6 6.6 %assemble.2 = bf16[2,4,4,48,2176]{4,3,2,1,0:T(8,128)(2,1)} custom-call(s32[2]{0:T(128)} %pad_add_fusion.place, bf16[4,48,2176]{2,1,0:T(8,128)(2,1)} %bitcast.447, bf16[4,48,2176]{2,1,0:T(8,128)(2,1)} %collective-permute-done.refs_1_, bf16[4,48,2176]{2,1,0:T(8,128)(2,1)} %collective-permute-done.1.refs_2_, ...), custom_call_target="tpu_custom_call" | custom-call | bytes 13369344 | tf_op jit(solution)/shard_map/assemble/pallas_call | solution.py:115
  94.5 8.0 %fusion.x_ref.q_ref = f32[512,2048]{1,0:T(8,128)} fusion(bf16[1536,2176]{1,0:T(8,128)(2,1)} %bitcast.416, bf16[1,512,1536]{2,1,0:T(8,128)(2,1)S(1)} %copy-done.18, f32[1536]{0:T(1024)S(1)} %get-tuple-element.207, f32[512]{0:T(512)S(1)} %add_rsqrt_fusion.1), kind=kOutput, calls=%fused_computation.2 | convolution fusion | flops 3224371200 | bytes 12066816 | tf_op jit(solution)/shard_map/dot_general | solution.py:43
  106.7 5.8 collective-permute-done.11
  112.5 2.2 collective-permute-done.12
  117.9 2.4 key_value.1.ko_ref.vo_ref
  124.4 19.0 %attention.1 = (bf16[512,1536]{1,0:T(8,128)(2,1)}, bf16[512,1536]{1,0:T(8,128)(2,1)}, f32[12,1,512]{2,1,0:T(1,128)}) custom-call(s32[1]{0:T(128)} %bitcast.1.place, f32[512,2048]{1,0:T(8,128)} %fusion.x_ref.q_ref, bf16[512,512]{1,0:T(8,128)(2,1)} %key_value.1.ko_ref.vo_ref, bf16[512,512]{1,0:T(8,128)(2,1)} %key_value.1.ko_ref.vo_ref, ...), custom_call_target="tpu_custom_call" | custom-call | flops 3221225472 | bytes 7864320 | tf_op jit(solution)/shard_map/attention/pallas_call | solution.py:513
  144.4 5.2 assemble.3
  155.4 4.6 multiply_reduce_fusion.2
  160.4 1.8 fusion.95
  163.6 7.3 %collective-permute-done.18 = bf16[256,1536]{1,0:T(8,128)(2,1)S(1)} collective-permute-done((bf16[256,1536]{1,0:T(8,128)(2,1)S(1)}, bf16[256,1536]{1,0:T(8,128)(2,1)S(1)}, u32[]{:S(2)}, u32[]{:S(2)}) %collective-permute-start.18) | collective-permute-done | bytes 786464 | tf_op jit(solution)/shard_map/ppermute | solution.py:56
  177.0 34.3 %collective-permute-done.20.refs_1_ = bf16[528,1536]{1,0:T(8,128)(2,1)} collective-permute-done((bf16[528,1536]{1,0:T(8,128)(2,1)}, bf16[528,1536]{1,0:T(8,128)(2,1)}, u32[]{:S(2)}, u32[]{:S(2)}) %collective-permute-start.20) | collective-permute-done | bytes 1622048 | tf_op jit(solution)/shard_map/ppermute | solution.py:56
  215.6 14.7 %collective-permute-done.22 = bf16[256,1536]{1,0:T(8,128)(2,1)S(1)} collective-permute-done((bf16[256,1536]{1,0:T(8,128)(2,1)S(1)}, bf16[256,1536]{1,0:T(8,128)(2,1)S(1)}, u32[]{:S(2)}, u32[]{:S(2)}) %collective-permute-start.22) | collective-permute-done | bytes 786464 | tf_op jit(solution)/shard_map/ppermute | solution.py:56
  236.4 7.6 %collective-permute-done.31.refs_15_ = bf16[512,1536]{1,0:T(8,128)(2,1)} collective-permute-done((bf16[512,1536]{1,0:T(8,128)(2,1)}, bf16[512,1536]{1,0:T(8,128)(2,1)}, u32[]{:S(2)}, u32[]{:S(2)}) %collective-permute-start.31) | collective-permute-done | bytes 1572896 | tf_op jit(solution)/shard_map/ppermute | solution.py:60
  244.1 41.1 %experts.2 = (bf16[4,512,1536]{2,1,0:T(8,128)(2,1)}, bf16[4,512,1536]{2,1,0:T(8,128)(2,1)}, bf16[4,528,1536]{2,1,0:T(8,128)(2,1)}, bf16[4,528,1536]{2,1,0:T(8,12...) custom-call(s32[2]{0:T(128)} %get-tuple-element.209.place, ...), custom_call_target="tpu_custom_call" | custom-call | flops 26172456960 | bytes 71958528 | tf_op jit(solution)/shard_map/experts/pallas_call | solution.py:308
  285.2 15.7 %weight_grads.2 = (bf16[4,3,192,768]{3,2,1,0:T(8,128)(2,1)}, bf16[4,3,192,768]{3,2,1,0:T(8,128)(2,1)}) custom-call(bf16[1280,1536]{1,0:T(8,128)(2,1)} %get-tuple-element.95.x_ref, bf16[1280,1536]{1,0:T(8,128)(2,1)} %get-tuple-element.96.gdy_ref, bf16[1280,768]{1,0:T(8,128)(2,1)} %get-tuple-element.97.h_ref, bf16[1280,768]{1,0:T(8,128)(2,1)} %get-tuple-element.98.dg_ref, ...), custom_call_target="tpu_custom_call" | custom-call | flops 9059696640 | bytes 20840448 | tf_op jit(solution)/shard_map/weight_grads/pallas_call | solution.py:394
  302.0 44.5 %experts.3 = (bf16[4,512,1536]{2,1,0:T(8,128)(2,1)}, bf16[4,512,1536]{2,1,0:T(8,128)(2,1)}, bf16[4,528,1536]{2,1,0:T(8,128)(2,1)}, bf16[4,528,1536]{2,1,0:T(8,12...) custom-call(s32[2]{0:T(128)} %get-tuple-element.102.place, ...), custom_call_target="tpu_custom_call" | custom-call | flops 26172456960 | bytes 71958528 | tf_op jit(solution)/shard_map/experts/pallas_call | solution.py:308
  346.9 10.4 %collective-permute-done.32 = bf16[4,528,1536]{2,1,0:T(8,128)(2,1)} collective-permute-done((bf16[4,528,1536]{2,1,0:T(8,128)(2,1)}, bf16[4,528,1536]{2,1,0:T(8,128)(2,1)}, u32[]{:S(2)}, u32[]{:S(2)}) %collective-permute-start.32) | collective-permute-done | bytes 6488096 | tf_op jit(solution)/shard_map/ppermute | solution.py:60
  357.3 6.6 %fusion.25 = (bf16[528,1536]{1,0:T(8,128)(2,1)S(1)}, bf16[528,1536]{1,0:T(8,128)(2,1)S(1)}, bf16[528,1536]{1,0:T(8,128)(2,1)S(1)}, bf16[528,1536]{1,0:T(8,128)(2,1)}) fusion(bf16[4,528,1536]{2,1,0:T(8,128)(2,1)} %collective-permute-done.32, bf16[4,528,1536]{2,1,0:T(8,128)(2,1)} %get-tuple-element.110), kind=kLoop, calls=%fused_computation.56 | loop fusion | flops 12976128 | bytes 19464192 | tf_op jit(solution)/shard_map/convert_element_type | solution.py:652
  370.8 15.3 %weight_grads.3 = (bf16[4,3,192,768]{3,2,1,0:T(8,128)(2,1)}, bf16[4,3,192,768]{3,2,1,0:T(8,128)(2,1)}) custom-call(bf16[1280,1536]{1,0:T(8,128)(2,1)} %get-tuple-element.115.x_ref, bf16[1280,1536]{1,0:T(8,128)(2,1)} %get-tuple-element.116.gdy_ref, bf16[1280,768]{1,0:T(8,128)(2,1)} %get-tuple-element.117.h_ref, bf16[1280,768]{1,0:T(8,128)(2,1)} %get-tuple-element.118.dg_ref, ...), custom_call_target="tpu_custom_call" | custom-call | flops 9059696640 | bytes 20840448 | tf_op jit(solution)/shard_map/weight_grads/pallas_call | solution.py:394
  386.2 19.8 %collective-permute-done.33 = bf16[2,256,1536]{2,1,0:T(8,128)(2,1)} collective-permute-done((bf16[2,256,1536]{2,1,0:T(8,128)(2,1)}, bf16[2,256,1536]{2,1,0:T(8,128)(2,1)}, u32[]{:S(2)}, u32[]{:S(2)}) %collective-permute-start.33) | collective-permute-done | bytes 1572896 | tf_op jit(solution)/shard_map/ppermute | solution.py:56
  406.1 2.6 fusion.21
  410.1 2.4 fusion.38
  414.1 2.5 collective-permute-done.37
  416.6 8.1 %fusion.29 = (bf16[512,1536]{1,0:T(8,128)(2,1)}, bf16[512,1536]{1,0:T(8,128)(2,1)}, bf16[512,1536]{1,0:T(8,128)(2,1)}, bf16[512,1536]{1,0:T(8,128)(2,1)}) fusion(bf16[4,512,1536]{2,1,0:T(8,128)(2,1)} %collective-permute-done.37, bf16[4,512,1536]{2,1,0:T(8,128)(2,1)} %get-tuple-element.124), kind=kLoop, calls=%fused_computation.61 | loop fusion | flops 12582912 | bytes 18874368 | tf_op jit(solution)/shard_map/convert_element_type | solution.py:652
  424.7 12.9 %reduce-scatter.9.cloned.1.call-done = bf16[1,3,192,768]{3,2,1,0:T(8,128)(2,1)} async-done(((bf16[4,3,192,768]{3,2,1,0:T(8,128)(2,1)}), bf16[1,3,192,768]{3,2,1,0:T(8,128)(2,1)}) %reduce-scatter.9.cloned.1.call-update) | async-done | bytes 884752 | tf_op jit(solution)/shard_map/reduce_scatter | solution.py:788
  437.6 2.3 broadcast_select_fusion
  439.9 1.7 fusion.20
  441.7 2.2 fusion.37
  443.9 3.0 multiply_reduce_fusion
  448.6 3.8 convolution_convert_fusion.3.dout_ref
  452.3 2.9 convolution_convert_fusion
  465.3 29.4 %attention_back.1 = (bf16[512,1536]{1,0:T(8,128)(2,1)}, f32[512,512]{1,0:T(8,128)}, bf16[512,512]{1,0:T(8,128)(2,1)}) custom-call(s32[1]{0:T(128)} %bitcast.1.place, bf16[512,1536]{1,0:T(8,128)(2,1)} %get-tuple-element.129.q_ref, bf16[512,1536]{1,0:T(8,128)(2,1)} %convolution_convert_fusion.3.dout_ref, bf16[512,512]{1,0:T(8,128)(2,1)} %key_value.1.ko_ref.vo_ref, ...), custom_call_target="tpu_custom_call" | custom-call | flops 8053063680 | bytes 6291456 | tf_op jit(solution)/shard_map/attention_back/pallas_call | solution.py:591
  494.7 4.6 convolution_convert_fusion.1
  503.8 1.7 convolution_convert_fusion.4
  506.6 1.7 broadcast_in_dim.59
  508.3 2.8 select_bitcast_fusion.3
  511.1 2.5 key_value_back.1
  513.6 2.9 convolution_convert_fusion.2
  516.7 1.9 collective-permute-start.42
  518.5 2.6 fusion.31
  521.2 7.0 %fusion.13 = (f32[512]{0:T(512)S(1)}, bf16[1536]{0:T(1024)(128)(2,1)S(1)}, f32[512,1536]{1,0:T(8,128)}) fusion(bf16[1,512,1536]{2,1,0:T(8,128)(2,1)S(1)} %copy-done.20, f32[1536]{0:T(1024)S(1)} %copy-done.47, f32[512]{0:T(512)S(1)} %copy-done.51, f32[512,1536]{1,0:T(8,128)S(1)} %fusion.31, bf16[512,1536]{1,0:T(8,128)(2,1)S(1)} %copy-done.59, ...), kind=kOutput, calls=%fused_computation.22 | convolution fusion | flops 2422208512 | bytes 14169088 | tf_op jit(solution)/shard_map/dot_general | solution.py:43
  531.1 2.3 fusion.42
  535.1 2.3 fusion.43
  539.8 1.7 collective-permute-start.45
  543.7 6.0 collective-permute-done.56
  553.1 21.6 %collective-permute-done.57 = bf16[2,48,1536]{2,1,0:T(8,128)(2,1)S(1)} collective-permute-done((bf16[2,48,1536]{2,1,0:T(8,128)(2,1)S(1)}, bf16[2,48,1536]{2,1,0:T(8,128)(2,1)S(1)}, u32[]{:S(2)}, u32[]{:S(2)}) %collective-permute-start.57) | collective-permute-done | bytes 294944 | tf_op jit(solution)/shard_map/ppermute | solution.py:56
  575.8 2.4 bitcast_select_fusion
  583.9 2.2 fusion.33
  586.7 2.3 fusion.35
  591.9 3.1 slice_bitcast_fusion
  597.5 3.0 reduce-scatter.15.cloned.1.call-done
  604.1 5.3 collective-permute-done.47
  609.4 2.4 collective-permute-done.46
  611.9 3.1 fusion.36
  615.2 5.4 fusion.17
  620.8 5.1 reduce-scatter.11.cloned.1.call-done
  630.5 3.7 collective-permute-done.50
  634.1 3.8 collective-permute-done.51
  640.6 2.3 maximum_convert_fusion.1
  (385 shorter events, 133.9 us)
Async XLA Ops:
  7.2 75.2 %all-gather.8.cloned.1.call-start = ((), (), s32[]{:S(2)}) async-start(), calls=%async_computation.12 | async-start | bytes 1327104 | tf_op jit(solution)/shard_map/all_gather | solution.py:707
  9.2 234.9 %all-gather.10.cloned.1.call-start = ((), (), s32[]{:S(2)}) async-start(), calls=%async_computation.13 | async-start | bytes 15925248 | tf_op jit(solution)/shard_map/all_gather | solution.py:712
  21.8 280.2 %all-gather.12.cloned.1.call-start = ((), (), s32[]{:S(2)}) async-start(), calls=%async_computation.14 | async-start | bytes 15925248 | tf_op jit(solution)/shard_map/all_gather | solution.py:715
  47.6 377.1 %reduce-scatter.7.cloned.1.call-start = ((), (), s32[]{:S(2)}) async-start(), calls=%async_computation.6 | async-start | bytes 4423680 | tf_op jit(solution)/shard_map/reduce_scatter | solution.py:788
  47.6 19.8 %collective-permute-start = (bf16[4,48,2176]{2,1,0:T(8,128)(2,1)S(1)}, bf16[4,48,2176]{2,1,0:T(8,128)(2,1)}, u32[]{:S(2)}, u32[]{:S(2)}) collective-permute-start(bf16[4,48,2176]{2,1,0:T(8,128)(2,1)S(1)} %bitcast.444), channel_id=1, source_target_pairs={{0,8},{8,0},{16,24},{24,16},{1,9},{9,1},{17,25},{25,17},{2,10},{10... | collective-permute-start | bytes 2506760 | tf_op jit(solution)/shard_map/ppermute | solution.py:56
  49.1 20.9 %collective-permute-start.1 = (bf16[4,48,2176]{2,1,0:T(8,128)(2,1)S(1)}, bf16[4,48,2176]{2,1,0:T(8,128)(2,1)}, u32[]{:S(2)}, u32[]{:S(2)}) collective-permute-start(bf16[4,48,2176]{2,1,0:T(8,128)(2,1)S(1)} %bitcast.445), channel_id=1, source_target_pairs={{0,16},{8,24},{16,0},{24,8},{1,17},{9,25},{17,1},{25,9},{2,18},{10... | collective-permute-start | bytes 2506760 | tf_op jit(solution)/shard_map/ppermute | solution.py:56
  68.5 9.8 %collective-permute-start.2 = (bf16[2,48,2176]{2,1,0:T(8,128)(2,1)S(1)}, bf16[2,48,2176]{2,1,0:T(8,128)(2,1)S(1)}, u32[]{:S(2)}, u32[]{:S(2)}) collective-permute-start(bf16[2,48,2176]{2,1,0:T(8,128)(2,1)S(1)} %slice.434), channel_id=1, source_target_pairs={{0,16},{8,24},{16,0},{24,8},{1,17},{9,25},{17,1},{25,9},{2,18},{10... | collective-permute-start | bytes 1253384 | tf_op jit(solution)/shard_map/ppermute | solution.py:56
  71.1 9.6 %collective-permute-start.3 = (bf16[2,48,2176]{2,1,0:T(8,128)(2,1)S(1)}, bf16[2,48,2176]{2,1,0:T(8,128)(2,1)S(1)}, u32[]{:S(2)}, u32[]{:S(2)}) collective-permute-start(bf16[2,48,2176]{2,1,0:T(8,128)(2,1)S(1)} %slice.435), channel_id=1, source_target_pairs={{0,8},{8,0},{16,24},{24,16},{1,9},{9,1},{17,25},{25,17},{2,10},{10... | collective-permute-start | bytes 1253384 | tf_op jit(solution)/shard_map/ppermute | solution.py:56
  72.6 13.5 %collective-permute-start.4 = (bf16[4,48,2176]{2,1,0:T(8,128)(2,1)S(1)}, bf16[4,48,2176]{2,1,0:T(8,128)(2,1)}, u32[]{:S(2)}, u32[]{:S(2)}) collective-permute-start(bf16[4,48,2176]{2,1,0:T(8,128)(2,1)S(1)} %bitcast.446), channel_id=1, source_target_pairs={{0,4},{4,0},{1,5},{5,1},{2,6},{6,2},{3,7},{7,3},{8,12},{12,8},{9,1... | collective-permute-start | bytes 2506760 | tf_op jit(solution)/shard_map/ppermute | solution.py:60
  72.6 14.0 %collective-permute-start.5 = (bf16[4,48,2176]{2,1,0:T(8,128)(2,1)}, bf16[4,48,2176]{2,1,0:T(8,128)(2,1)}, u32[]{:S(2)}, u32[]{:S(2)}) collective-permute-start(bf16[4,48,2176]{2,1,0:T(8,128)(2,1)} %collective-permute-done.refs_1_), channel_id=1, source_target_pairs={{0,4},{4,0},{1,5},{5,1},{2,6},{6,2},{3,7},{7,3},{8,12},{12,8},{9,1... | collective-permute-start | bytes 2506760 | tf_op jit(solution)/shard_map/ppermute | solution.py:60
  73.1 13.5 %collective-permute-start.6 = (bf16[4,48,2176]{2,1,0:T(8,128)(2,1)}, bf16[4,48,2176]{2,1,0:T(8,128)(2,1)}, u32[]{:S(2)}, u32[]{:S(2)}) collective-permute-start(bf16[4,48,2176]{2,1,0:T(8,128)(2,1)} %collective-permute-done.1.refs_2_), channel_id=1, source_target_pairs={{0,4},{4,0},{1,5},{5,1},{2,6},{6,2},{3,7},{7,3},{8,12},{12,8},{9,1... | collective-permute-start | bytes 2506760 | tf_op jit(solution)/shard_map/ppermute | solution.py:60
  84.6 17.9 %collective-permute-start.8 = (bf16[4,48,1536]{2,1,0:T(8,128)(2,1)S(1)}, bf16[4,48,1536]{2,1,0:T(8,128)(2,1)}, u32[]{:S(2)}, u32[]{:S(2)}) collective-permute-start(bf16[4,48,1536]{2,1,0:T(8,128)(2,1)S(1)} %get-tuple-element.84.refs_0_), channel_id=1, source_target_pairs={{0,8},{8,0},{16,24},{24,16},{1,9},{9,1},{17,25},{25,17},{2,10},{10... | collective-permute-start | bytes 1769480 | tf_op jit(solution)/shard_map/ppermute | solution.py:56
  86.0 16.4 %collective-permute-start.9 = (bf16[4,48,1536]{2,1,0:T(8,128)(2,1)S(1)}, bf16[4,48,1536]{2,1,0:T(8,128)(2,1)}, u32[]{:S(2)}, u32[]{:S(2)}) collective-permute-start(bf16[4,48,1536]{2,1,0:T(8,128)(2,1)S(1)} %get-tuple-element.84.refs_0_), channel_id=1, source_target_pairs={{0,16},{8,24},{16,0},{24,8},{1,17},{9,25},{17,1},{25,9},{2,18},{10... | collective-permute-start | bytes 1769480 | tf_op jit(solution)/shard_map/ppermute | solution.py:56
  103.6 8.9 %collective-permute-start.11 = (bf16[2,48,1536]{2,1,0:T(8,128)(2,1)S(1)}, bf16[2,48,1536]{2,1,0:T(8,128)(2,1)S(1)}, u32[]{:S(2)}, u32[]{:S(2)}) collective-permute-start(bf16[2,48,1536]{2,1,0:T(8,128)(2,1)S(1)} %slice.336), channel_id=1, source_target_pairs={{0,16},{8,24},{16,0},{24,8},{1,17},{9,25},{17,1},{25,9},{2,18},{10... | collective-permute-start | bytes 884744 | tf_op jit(solution)/shard_map/ppermute | solution.py:56
  114.8 35.4 %collective-permute-start.13 = (bf16[512,1536]{1,0:T(8,128)(2,1)S(1)}, bf16[512,1536]{1,0:T(8,128)(2,1)}, u32[]{:S(2)}, u32[]{:S(2)}) collective-permute-start(bf16[512,1536]{1,0:T(8,128)(2,1)S(1)} %bitcast.423), channel_id=1, source_target_pairs={{0,8},{8,0},{16,24},{24,16},{1,9},{9,1},{17,25},{25,17},{2,10},{10... | collective-permute-start | bytes 4718600 | tf_op jit(solution)/shard_map/ppermute | solution.py:56
  115.4 35.0 %collective-permute-start.14 = (bf16[512,1536]{1,0:T(8,128)(2,1)S(1)}, bf16[512,1536]{1,0:T(8,128)(2,1)}, u32[]{:S(2)}, u32[]{:S(2)}) collective-permute-start(bf16[512,1536]{1,0:T(8,128)(2,1)S(1)} %bitcast.424), channel_id=1, source_target_pairs={{0,16},{8,24},{16,0},{24,8},{1,17},{9,25},{17,1},{25,9},{2,18},{10... | collective-permute-start | bytes 4718600 | tf_op jit(solution)/shard_map/ppermute | solution.py:56
  121.8 21.5 %collective-permute-start.15 = (bf16[4,48,1536]{2,1,0:T(8,128)(2,1)}, bf16[4,48,1536]{2,1,0:T(8,128)(2,1)S(1)}, u32[]{:S(2)}, u32[]{:S(2)}) collective-permute-start(bf16[4,48,1536]{2,1,0:T(8,128)(2,1)} %collective-permute-done.8.refs_1_), channel_id=1, source_target_pairs={{0,4},{4,0},{1,5},{5,1},{2,6},{6,2},{3,7},{7,3},{8,12},{12,8},{9,1... | collective-permute-start | bytes 1769480 | tf_op jit(solution)/shard_map/ppermute | solution.py:60
  121.9 21.5 %collective-permute-start.16 = (bf16[4,48,1536]{2,1,0:T(8,128)(2,1)}, bf16[4,48,1536]{2,1,0:T(8,128)(2,1)S(1)}, u32[]{:S(2)}, u32[]{:S(2)}) collective-permute-start(bf16[4,48,1536]{2,1,0:T(8,128)(2,1)} %collective-permute-done.9.refs_2_), channel_id=1, source_target_pairs={{0,4},{4,0},{1,5},{5,1},{2,6},{6,2},{3,7},{7,3},{8,12},{12,8},{9,1... | collective-permute-start | bytes 1769480 | tf_op jit(solution)/shard_map/ppermute | solution.py:60
  123.4 20.1 %collective-permute-start.17 = (bf16[4,48,1536]{2,1,0:T(8,128)(2,1)S(1)}, bf16[4,48,1536]{2,1,0:T(8,128)(2,1)}, u32[]{:S(2)}, u32[]{:S(2)}) collective-permute-start(bf16[4,48,1536]{2,1,0:T(8,128)(2,1)S(1)} %constant_dynamic-update-slice_fusion.2.refs_3_), channel_id=1, source_target_pairs={{0,4},{4,0},{1,5},{5,1},{2,6},{6,2},{3,7},{7,3},{8,12},{12,8},{9,1... | collective-permute-start | bytes 1769480 | tf_op jit(solution)/shard_map/ppermute | solution.py:60
  151.8 19.1 %collective-permute-start.18 = (bf16[256,1536]{1,0:T(8,128)(2,1)S(1)}, bf16[256,1536]{1,0:T(8,128)(2,1)S(1)}, u32[]{:S(2)}, u32[]{:S(2)}) collective-permute-start(bf16[256,1536]{1,0:T(8,128)(2,1)S(1)} %slice.340), channel_id=1, source_target_pairs={{0,16},{8,24},{16,0},{24,8},{1,17},{9,25},{17,1},{25,9},{2,18},{10... | collective-permute-start | bytes 2359304 | tf_op jit(solution)/shard_map/ppermute | solution.py:56
  153.8 19.6 %collective-permute-start.19 = (bf16[256,1536]{1,0:T(8,128)(2,1)S(1)}, bf16[256,1536]{1,0:T(8,128)(2,1)S(1)}, u32[]{:S(2)}, u32[]{:S(2)}) collective-permute-start(bf16[256,1536]{1,0:T(8,128)(2,1)S(1)} %slice.341), channel_id=1, source_target_pairs={{0,8},{8,0},{16,24},{24,16},{1,9},{9,1},{17,25},{25,17},{2,10},{10... | collective-permute-start | bytes 2359304 | tf_op jit(solution)/shard_map/ppermute | solution.py:56
  174.4 36.9 %collective-permute-start.20 = (bf16[528,1536]{1,0:T(8,128)(2,1)}, bf16[528,1536]{1,0:T(8,128)(2,1)}, u32[]{:S(2)}, u32[]{:S(2)}) collective-permute-start(bf16[528,1536]{1,0:T(8,128)(2,1)} %maximum_maximum_fusion.refs_0_), channel_id=1, source_target_pairs={{0,8},{8,0},{16,24},{24,16},{1,9},{9,1},{17,25},{25,17},{2,10},{10... | collective-permute-start | bytes 4866056 | tf_op jit(solution)/shard_map/ppermute | solution.py:56
  175.9 37.0 %collective-permute-start.21 = (bf16[528,1536]{1,0:T(8,128)(2,1)}, bf16[528,1536]{1,0:T(8,128)(2,1)}, u32[]{:S(2)}, u32[]{:S(2)}) collective-permute-start(bf16[528,1536]{1,0:T(8,128)(2,1)} %maximum_maximum_fusion.refs_0_), channel_id=1, source_target_pairs={{0,16},{8,24},{16,0},{24,8},{1,17},{9,25},{17,1},{25,9},{2,18},{10... | collective-permute-start | bytes 4866056 | tf_op jit(solution)/shard_map/ppermute | solution.py:56
  176.5 57.2 %collective-permute-start.28 = (bf16[512,1536]{1,0:T(8,128)(2,1)S(1)}, bf16[512,1536]{1,0:T(8,128)(2,1)S(1)}, u32[]{:S(2)}, u32[]{:S(2)}) collective-permute-start(bf16[512,1536]{1,0:T(8,128)(2,1)S(1)} %bitcast.425), channel_id=1, source_target_pairs={{0,4},{4,0},{1,5},{5,1},{2,6},{6,2},{3,7},{7,3},{8,12},{12,8},{9,1... | collective-permute-start | bytes 4718600 | tf_op jit(solution)/shard_map/ppermute | solution.py:60
  176.5 58.8 %collective-permute-start.29 = (bf16[512,1536]{1,0:T(8,128)(2,1)}, bf16[512,1536]{1,0:T(8,128)(2,1)}, u32[]{:S(2)}, u32[]{:S(2)}) collective-permute-start(bf16[512,1536]{1,0:T(8,128)(2,1)} %collective-permute-done.13.refs_9_), channel_id=1, source_target_pairs={{0,4},{4,0},{1,5},{5,1},{2,6},{6,2},{3,7},{7,3},{8,12},{12,8},{9,1... | collective-permute-start | bytes 4718600 | tf_op jit(solution)/shard_map/ppermute | solution.py:60
  177.0 58.3 %collective-permute-start.30 = (bf16[512,1536]{1,0:T(8,128)(2,1)}, bf16[512,1536]{1,0:T(8,128)(2,1)}, u32[]{:S(2)}, u32[]{:S(2)}) collective-permute-start(bf16[512,1536]{1,0:T(8,128)(2,1)} %collective-permute-done.14.refs_10_), channel_id=1, source_target_pairs={{0,4},{4,0},{1,5},{5,1},{2,6},{6,2},{3,7},{7,3},{8,12},{12,8},{9,1... | collective-permute-start | bytes 4718600 | tf_op jit(solution)/shard_map/ppermute | solution.py:60
  212.5 17.8 %collective-permute-start.22 = (bf16[256,1536]{1,0:T(8,128)(2,1)S(1)}, bf16[256,1536]{1,0:T(8,128)(2,1)S(1)}, u32[]{:S(2)}, u32[]{:S(2)}) collective-permute-start(bf16[256,1536]{1,0:T(8,128)(2,1)S(1)} %slice.441), channel_id=1, source_target_pairs={{0,16},{8,24},{16,0},{24,8},{1,17},{9,25},{17,1},{25,9},{2,18},{10... | collective-permute-start | bytes 2359304 | tf_op jit(solution)/shard_map/ppermute | solution.py:56
  214.1 18.6 %collective-permute-start.23 = (bf16[272,1536]{1,0:T(8,128)(2,1)S(1)}, bf16[272,1536]{1,0:T(8,128)(2,1)S(1)}, u32[]{:S(2)}, u32[]{:S(2)}) collective-permute-start(bf16[272,1536]{1,0:T(8,128)(2,1)S(1)} %slice.442), channel_id=1, source_target_pairs={{0,8},{8,0},{16,24},{24,16},{1,9},{9,1},{17,25},{25,17},{2,10},{10... | collective-permute-start | bytes 2506760 | tf_op jit(solution)/shard_map/ppermute | solution.py:56
  230.3 13.7 %collective-permute-start.24 = (bf16[528,1536]{1,0:T(8,128)(2,1)}, bf16[528,1536]{1,0:T(8,128)(2,1)}, u32[]{:S(2)}, u32[]{:S(2)}) collective-permute-start(bf16[528,1536]{1,0:T(8,128)(2,1)} %maximum_maximum_fusion.refs_0_), channel_id=1, source_target_pairs={{0,4},{4,0},{1,5},{5,1},{2,6},{6,2},{3,7},{7,3},{8,12},{12,8},{9,1... | collective-permute-start | bytes 4866056 | tf_op jit(solution)/shard_map/ppermute | solution.py:60
  232.7 11.4 %collective-permute-start.25 = (bf16[528,1536]{1,0:T(8,128)(2,1)}, bf16[528,1536]{1,0:T(8,128)(2,1)}, u32[]{:S(2)}, u32[]{:S(2)}) collective-permute-start(bf16[528,1536]{1,0:T(8,128)(2,1)} %collective-permute-done.20.refs_1_), channel_id=1, source_target_pairs={{0,4},{4,0},{1,5},{5,1},{2,6},{6,2},{3,7},{7,3},{8,12},{12,8},{9,1... | collective-permute-start | bytes 4866056 | tf_op jit(solution)/shard_map/ppermute | solution.py:60
  234.8 9.3 %collective-permute-start.26 = (bf16[528,1536]{1,0:T(8,128)(2,1)}, bf16[528,1536]{1,0:T(8,128)(2,1)}, u32[]{:S(2)}, u32[]{:S(2)}) collective-permute-start(bf16[528,1536]{1,0:T(8,128)(2,1)} %collective-permute-done.21.refs_2_), channel_id=1, source_target_pairs={{0,4},{4,0},{1,5},{5,1},{2,6},{6,2},{3,7},{7,3},{8,12},{12,8},{9,1... | collective-permute-start | bytes 4866056 | tf_op jit(solution)/shard_map/ppermute | solution.py:60
  300.9 136.7 %reduce-scatter.9.cloned.1.call-start = ((), (), s32[]{:S(2)}) async-start(), calls=%async_computation.7 | async-start | bytes 4423680 | tf_op jit(solution)/shard_map/reduce_scatter | solution.py:788
  346.5 10.8 %collective-permute-start.32 = (bf16[4,528,1536]{2,1,0:T(8,128)(2,1)}, bf16[4,528,1536]{2,1,0:T(8,128)(2,1)}, u32[]{:S(2)}, u32[]{:S(2)}) collective-permute-start(bf16[4,528,1536]{2,1,0:T(8,128)(2,1)} %get-tuple-element.111), channel_id=1, source_target_pairs={{0,4},{4,0},{1,5},{5,1},{2,6},{6,2},{3,7},{7,3},{8,12},{12,8},{9,1... | collective-permute-start | bytes 19464200 | tf_op jit(solution)/shard_map/ppermute | solution.py:60
  346.8 229.0 %reduce-scatter.13.cloned.1.call-start = ((), (), s32[]{:S(2)}) async-start(), calls=%async_computation.9 | async-start | bytes 4423680 | tf_op jit(solution)/shard_map/reduce_scatter | solution.py:788
  366.4 39.6 %collective-permute-start.34 = (bf16[2,272,1536]{2,1,0:T(8,128)(2,1)}, bf16[2,272,1536]{2,1,0:T(8,128)(2,1)}, u32[]{:S(2)}, u32[]{:S(2)}) collective-permute-start(bf16[2,272,1536]{2,1,0:T(8,128)(2,1)} %pad_maximum_fusion.1), channel_id=1, source_target_pairs={{0,16},{8,24},{16,0},{24,8},{1,17},{9,25},{17,1},{25,9},{2,18},{10... | collective-permute-start | bytes 5013512 | tf_op jit(solution)/shard_map/ppermute | solution.py:56
  369.4 36.6 %collective-permute-start.33 = (bf16[2,256,1536]{2,1,0:T(8,128)(2,1)}, bf16[2,256,1536]{2,1,0:T(8,128)(2,1)}, u32[]{:S(2)}, u32[]{:S(2)}) collective-permute-start(bf16[2,256,1536]{2,1,0:T(8,128)(2,1)} %pad_maximum_fusion.2), channel_id=1, source_target_pairs={{0,8},{8,0},{16,24},{24,16},{1,9},{9,1},{17,25},{25,17},{2,10},{10... | collective-permute-start | bytes 4718600 | tf_op jit(solution)/shard_map/ppermute | solution.py:56
  406.0 169.8 %reduce-scatter.17.cloned.1.call-start = ((), (), s32[]{:S(2)}) async-start(), calls=%async_computation.11 | async-start | bytes 4423680 | tf_op jit(solution)/shard_map/reduce_scatter | solution.py:788
  406.0 10.6 %collective-permute-start.37 = (bf16[4,512,1536]{2,1,0:T(8,128)(2,1)}, bf16[4,512,1536]{2,1,0:T(8,128)(2,1)}, u32[]{:S(2)}, u32[]{:S(2)}) collective-permute-start(bf16[4,512,1536]{2,1,0:T(8,128)(2,1)} %get-tuple-element.125), channel_id=1, source_target_pairs={{0,4},{4,0},{1,5},{5,1},{2,6},{6,2},{3,7},{7,3},{8,12},{12,8},{9,1... | collective-permute-start | bytes 18874376 | tf_op jit(solution)/shard_map/ppermute | solution.py:60
  408.7 29.0 %collective-permute-start.36 = (bf16[272,1536]{1,0:T(8,128)(2,1)}, bf16[272,1536]{1,0:T(8,128)(2,1)}, u32[]{:S(2)}, u32[]{:S(2)}) collective-permute-start(bf16[272,1536]{1,0:T(8,128)(2,1)} %fusion.21), channel_id=1, source_target_pairs={{0,8},{8,0},{16,24},{24,16},{1,9},{9,1},{17,25},{25,17},{2,10},{10... | collective-permute-start | bytes 2506760 | tf_op jit(solution)/shard_map/ppermute | solution.py:56
  412.6 25.0 %collective-permute-start.35 = (bf16[256,1536]{1,0:T(8,128)(2,1)}, bf16[256,1536]{1,0:T(8,128)(2,1)}, u32[]{:S(2)}, u32[]{:S(2)}) collective-permute-start(bf16[256,1536]{1,0:T(8,128)(2,1)} %fusion.38), channel_id=1, source_target_pairs={{0,16},{8,24},{16,0},{24,8},{1,17},{9,25},{17,1},{25,9},{2,18},{10... | collective-permute-start | bytes 2359304 | tf_op jit(solution)/shard_map/ppermute | solution.py:56
  414.0 186.5 %reduce-scatter.15.cloned.1.call-start = ((), (), s32[]{:S(2)}) async-start(), calls=%async_computation.10 | async-start | bytes 737280 | tf_op jit(solution)/shard_map/reduce_scatter | solution.py:644
  439.9 68.4 %collective-permute-start.61 = (bf16[3,192,768]{2,1,0:T(8,128)(2,1)}, bf16[3,192,768]{2,1,0:T(8,128)(2,1)}, u32[]{:S(2)}, u32[]{:S(2)}) collective-permute-start(bf16[3,192,768]{2,1,0:T(8,128)(2,1)} %broadcast_select_fusion), channel_id=1, source_target_pairs={{0,4},{4,0},{1,5},{5,1},{2,6},{6,2},{3,7},{7,3},{8,12},{12,8},{9,1... | collective-permute-start | bytes 2654216 | tf_op jit(solution)/shard_map/ppermute | solution.py:60
  458.1 72.9 %collective-permute-start.53 = (bf16[4,4,48,1536]{3,2,0,1:T(8,128)(2,1)}, bf16[4,4,48,1536]{3,2,0,1:T(8,128)(2,1)}, u32[]{:S(2)}, u32[]{:S(2)}) collective-permute-start(bf16[4,4,48,1536]{3,2,0,1:T(8,128)(2,1)} %copy_bitcast_fusion), channel_id=1, source_target_pairs={{0,4},{4,0},{1,5},{5,1},{2,6},{6,2},{3,7},{7,3},{8,12},{12,8},{9,1... | collective-permute-start | bytes 7077896 | tf_op jit(solution)/shard_map/ppermute | solution.py:60
  460.9 41.4 %collective-permute-start.39 = (bf16[2,256,1536]{2,1,0:T(8,128)(2,1)}, bf16[2,256,1536]{2,1,0:T(8,128)(2,1)}, u32[]{:S(2)}, u32[]{:S(2)}) collective-permute-start(bf16[2,256,1536]{2,1,0:T(8,128)(2,1)} %pad_maximum_fusion.4), channel_id=1, source_target_pairs={{0,16},{8,24},{16,0},{24,8},{1,17},{9,25},{17,1},{25,9},{2,18},{10... | collective-permute-start | bytes 4718600 | tf_op jit(solution)/shard_map/ppermute | solution.py:56
  463.8 38.5 %collective-permute-start.38 = (bf16[2,256,1536]{2,1,0:T(8,128)(2,1)}, bf16[2,256,1536]{2,1,0:T(8,128)(2,1)}, u32[]{:S(2)}, u32[]{:S(2)}) collective-permute-start(bf16[2,256,1536]{2,1,0:T(8,128)(2,1)} %pad_maximum_fusion.3), channel_id=1, source_target_pairs={{0,8},{8,0},{16,24},{24,16},{1,9},{9,1},{17,25},{25,17},{2,10},{10... | collective-permute-start | bytes 4718600 | tf_op jit(solution)/shard_map/ppermute | solution.py:56
  502.3 32.8 %collective-permute-start.40 = (bf16[4,4,48,1536]{3,2,0,1:T(8,128)(2,1)}, bf16[4,4,48,1536]{3,2,0,1:T(8,128)(2,1)}, u32[]{:S(2)}, u32[]{:S(2)}) collective-permute-start(bf16[4,4,48,1536]{3,2,0,1:T(8,128)(2,1)} %copy_bitcast_fusion.1), channel_id=1, source_target_pairs={{0,4},{4,0},{1,5},{5,1},{2,6},{6,2},{3,7},{7,3},{8,12},{12,8},{9,1... | collective-permute-start | bytes 7077896 | tf_op jit(solution)/shard_map/ppermute | solution.py:60
  516.7 20.8 %collective-permute-start.42 = (bf16[4,4,48,512]{3,2,0,1:T(8,128)(2,1)S(1)}, bf16[4,4,48,512]{3,2,0,1:T(8,128)(2,1)S(1)}, u32[]{:S(2)}, u32[]{:S(2)}) collective-permute-start(bf16[4,4,48,512]{3,2,0,1:T(8,128)(2,1)S(1)} %copy_bitcast_fusion.2), channel_id=1, source_target_pairs={{0,4},{4,0},{1,5},{5,1},{2,6},{6,2},{3,7},{7,3},{8,12},{12,8},{9,1... | collective-permute-start | bytes 2359304 | tf_op jit(solution)/shard_map/ppermute | solution.py:60
  533.6 16.2 %collective-permute-start.56 = (bf16[2,2,48,1536]{3,2,1,0:T(8,128)(2,1)S(1)}, bf16[2,2,48,1536]{3,2,1,0:T(8,128)(2,1)S(1)}, u32[]{:S(2)}, u32[]{:S(2)}) collective-permute-start(bf16[2,2,48,1536]{3,2,1,0:T(8,128)(2,1)S(1)} %pad_maximum_fusion.14), channel_id=1, source_target_pairs={{0,16},{8,24},{16,0},{24,8},{1,17},{9,25},{17,1},{25,9},{2,18},{10... | collective-permute-start | bytes 1769480 | tf_op jit(solution)/shard_map/ppermute | solution.py:56
  535.0 16.2 %collective-permute-start.54 = (bf16[2,2,48,1536]{3,2,1,0:T(8,128)(2,1)S(1)}, bf16[2,2,48,1536]{3,2,1,0:T(8,128)(2,1)S(1)}, u32[]{:S(2)}, u32[]{:S(2)}) collective-permute-start(bf16[2,2,48,1536]{3,2,1,0:T(8,128)(2,1)S(1)} %pad_maximum_fusion.13), channel_id=1, source_target_pairs={{0,8},{8,0},{16,24},{24,16},{1,9},{9,1},{17,25},{25,17},{2,10},{10... | collective-permute-start | bytes 1769480 | tf_op jit(solution)/shard_map/ppermute | solution.py:56
  539.8 38.8 %collective-permute-start.45 = (bf16[2,2,48,2176]{3,2,1,0:T(8,128)(2,1)}, bf16[2,2,48,2176]{3,2,1,0:T(8,128)(2,1)}, u32[]{:S(2)}, u32[]{:S(2)}) collective-permute-start(bf16[2,2,48,2176]{3,2,1,0:T(8,128)(2,1)} %pad_maximum_fusion.9), channel_id=1, source_target_pairs={{0,16},{8,24},{16,0},{24,8},{1,17},{9,25},{17,1},{25,9},{2,18},{10... | collective-permute-start | bytes 2506760 | tf_op jit(solution)/shard_map/ppermute | solution.py:56
  542.7 35.9 %collective-permute-start.44 = (bf16[2,2,48,2176]{3,2,1,0:T(8,128)(2,1)}, bf16[2,2,48,2176]{3,2,1,0:T(8,128)(2,1)}, u32[]{:S(2)}, u32[]{:S(2)}) collective-permute-start(bf16[2,2,48,2176]{3,2,1,0:T(8,128)(2,1)} %pad_maximum_fusion.7), channel_id=1, source_target_pairs={{0,8},{8,0},{16,24},{24,16},{1,9},{9,1},{17,25},{25,17},{2,10},{10... | collective-permute-start | bytes 2506760 | tf_op jit(solution)/shard_map/ppermute | solution.py:56
  549.9 24.8 %collective-permute-start.57 = (bf16[2,48,1536]{2,1,0:T(8,128)(2,1)S(1)}, bf16[2,48,1536]{2,1,0:T(8,128)(2,1)S(1)}, u32[]{:S(2)}, u32[]{:S(2)}) collective-permute-start(bf16[2,48,1536]{2,1,0:T(8,128)(2,1)S(1)} %fusion.54), channel_id=1, source_target_pairs={{0,8},{8,0},{16,24},{24,16},{1,9},{9,1},{17,25},{25,17},{2,10},{10... | collective-permute-start | bytes 884744 | tf_op jit(solution)/shard_map/ppermute | solution.py:56
  551.3 23.4 %collective-permute-start.55 = (bf16[2,48,1536]{2,1,0:T(8,128)(2,1)S(1)}, bf16[2,48,1536]{2,1,0:T(8,128)(2,1)S(1)}, u32[]{:S(2)}, u32[]{:S(2)}) collective-permute-start(bf16[2,48,1536]{2,1,0:T(8,128)(2,1)S(1)} %fusion.57), channel_id=1, source_target_pairs={{0,16},{8,24},{16,0},{24,8},{1,17},{9,25},{17,1},{25,9},{2,18},{10... | collective-permute-start | bytes 884744 | tf_op jit(solution)/shard_map/ppermute | solution.py:56
  578.2 11.6 %collective-permute-start.62 = (bf16[3,192,768]{2,1,0:T(8,128)(2,1)}, bf16[3,192,768]{2,1,0:T(8,128)(2,1)}, u32[]{:S(2)}, u32[]{:S(2)}) collective-permute-start(bf16[3,192,768]{2,1,0:T(8,128)(2,1)} %bitcast_select_fusion), channel_id=1, source_target_pairs={{0,4},{4,0},{1,5},{5,1},{2,6},{6,2},{3,7},{7,3},{8,12},{12,8},{9,1... | collective-permute-start | bytes 2654216 | tf_op jit(solution)/shard_map/ppermute | solution.py:60
  578.3 47.6 %reduce-scatter.11.cloned.1.call-start = ((), (), s32[]{:S(2)}) async-start(), calls=%async_computation.8 | async-start | bytes 1044480 | tf_op jit(solution)/shard_map/reduce_scatter | solution.py:644
  580.0 15.1 %collective-permute-start.49 = (bf16[2,48,2176]{2,1,0:T(8,128)(2,1)S(1)}, bf16[2,48,2176]{2,1,0:T(8,128)(2,1)S(1)}, u32[]{:S(2)}, u32[]{:S(2)}) collective-permute-start(bf16[2,48,2176]{2,1,0:T(8,128)(2,1)S(1)} %fusion.48), channel_id=1, source_target_pairs={{0,8},{8,0},{16,24},{24,16},{1,9},{9,1},{17,25},{25,17},{2,10},{10... | collective-permute-start | bytes 1253384 | tf_op jit(solution)/shard_map/ppermute | solution.py:56
  582.4 12.7 %collective-permute-start.48 = (bf16[2,48,2176]{2,1,0:T(8,128)(2,1)S(1)}, bf16[2,48,2176]{2,1,0:T(8,128)(2,1)S(1)}, u32[]{:S(2)}, u32[]{:S(2)}) collective-permute-start(bf16[2,48,2176]{2,1,0:T(8,128)(2,1)S(1)} %fusion.51), channel_id=1, source_target_pairs={{0,16},{8,24},{16,0},{24,8},{1,17},{9,25},{17,1},{25,9},{2,18},{10... | collective-permute-start | bytes 1253384 | tf_op jit(solution)/shard_map/ppermute | solution.py:56
  586.2 23.3 %collective-permute-start.47 = (bf16[256,1536]{1,0:T(8,128)(2,1)}, bf16[256,1536]{1,0:T(8,128)(2,1)}, u32[]{:S(2)}, u32[]{:S(2)}) collective-permute-start(bf16[256,1536]{1,0:T(8,128)(2,1)} %fusion.33), channel_id=1, source_target_pairs={{0,8},{8,0},{16,24},{24,16},{1,9},{9,1},{17,25},{25,17},{2,10},{10... | collective-permute-start | bytes 2359304 | tf_op jit(solution)/shard_map/ppermute | solution.py:56
  589.0 22.9 %collective-permute-start.46 = (bf16[256,1536]{1,0:T(8,128)(2,1)}, bf16[256,1536]{1,0:T(8,128)(2,1)}, u32[]{:S(2)}, u32[]{:S(2)}) collective-permute-start(bf16[256,1536]{1,0:T(8,128)(2,1)} %fusion.35), channel_id=1, source_target_pairs={{0,16},{8,24},{16,0},{24,8},{1,17},{9,25},{17,1},{25,9},{2,18},{10... | collective-permute-start | bytes 2359304 | tf_op jit(solution)/shard_map/ppermute | solution.py:56
  600.5 20.1 %collective-permute-start.58 = (bf16[48,1536]{1,0:T(8,128)(2,1)}, bf16[48,1536]{1,0:T(8,128)(2,1)S(1)}, u32[]{:S(2)}, u32[]{:S(2)}) collective-permute-start(bf16[48,1536]{1,0:T(8,128)(2,1)} %bitcast.460), channel_id=1, source_target_pairs={{0,8},{8,0},{16,24},{24,16},{1,9},{9,1},{17,25},{25,17},{2,10},{10... | collective-permute-start | bytes 442376 | tf_op jit(solution)/shard_map/ppermute | solution.py:56
  601.9 18.7 %collective-permute-start.59 = (bf16[48,1536]{1,0:T(8,128)(2,1)}, bf16[48,1536]{1,0:T(8,128)(2,1)S(1)}, u32[]{:S(2)}, u32[]{:S(2)}) collective-permute-start(bf16[48,1536]{1,0:T(8,128)(2,1)} %bitcast.461), channel_id=1, source_target_pairs={{0,16},{8,24},{16,0},{24,8},{1,17},{9,25},{17,1},{25,9},{2,18},{10... | collective-permute-start | bytes 442376 | tf_op jit(solution)/shard_map/ppermute | solution.py:56
  603.5 17.1 %collective-permute-start.60 = (bf16[48,1536]{1,0:T(8,128)(2,1)}, bf16[48,1536]{1,0:T(8,128)(2,1)S(1)}, u32[]{:S(2)}, u32[]{:S(2)}) collective-permute-start(bf16[48,1536]{1,0:T(8,128)(2,1)} %bitcast.462), channel_id=1, source_target_pairs={{0,24},{8,16},{16,8},{24,0},{1,25},{9,17},{17,9},{25,1},{2,26},{10... | collective-permute-start | bytes 442376 | tf_op jit(solution)/shard_map/ppermute | solution.py:56
  627.3 10.7 %collective-permute-start.51 = (bf16[48,2176]{1,0:T(8,128)(2,1)}, bf16[48,2176]{1,0:T(8,128)(2,1)S(1)}, u32[]{:S(2)}, u32[]{:S(2)}) collective-permute-start(bf16[48,2176]{1,0:T(8,128)(2,1)} %bitcast.455), channel_id=1, source_target_pairs={{0,16},{8,24},{16,0},{24,8},{1,17},{9,25},{17,1},{25,9},{2,18},{10... | collective-permute-start | bytes 626696 | tf_op jit(solution)/shard_map/ppermute | solution.py:56
  628.8 9.2 %collective-permute-start.52 = (bf16[48,2176]{1,0:T(8,128)(2,1)}, bf16[48,2176]{1,0:T(8,128)(2,1)S(1)}, u32[]{:S(2)}, u32[]{:S(2)}) collective-permute-start(bf16[48,2176]{1,0:T(8,128)(2,1)} %bitcast.456), channel_id=1, source_target_pairs={{0,24},{8,16},{16,8},{24,0},{1,25},{9,17},{17,9},{25,1},{2,26},{10... | collective-permute-start | bytes 626696 | tf_op jit(solution)/shard_map/ppermute | solution.py:56
  (75 other events, 1253.5 us)
Sparse Core Ops, SparseCore 0:
  10.2 31.4 all-gather.7
  43.9 128.0 all-gather.9
  174.1 127.8 all-gather.11
  304.1 64.5 reduce-scatter.6
  370.9 66.6 reduce-scatter.8
  439.8 66.6 reduce-scatter.12
  508.8 66.6 reduce-scatter.16
  578.4 22.0 reduce-scatter.14
  603.4 22.3 reduce-scatter.10

commit v4 on v3

--- a/solution.py
+++ b/solution.py
@@ -129,12 +129,8 @@
     return out.reshape(2 * z * count * r, n)
 
 
-def halves_of(size):
-    return size // 2 if size < 32 else size // 32 * 16
-
-
 def fourth_block(one, two):
-    cut = halves_of(one.shape[0])
+    cut = one.shape[0] // 2
     return jnp.concatenate([flip(one[:cut], 2), flip(two[cut:], 1)], axis=0)
 
 
@@ -155,33 +151,147 @@
 def spread(block):
     own = gather_blocks(block)
     return own, [swap(b) for b in own]
+
+
+def fold_kernel(dense, pairs, place, *refs):
+    k, half = pl.program_id(0), pl.program_id(1)
+    odd, far = lax.rem(k, 2) == 1, k >= 2
+    top, bottom, keep_top, keep_bottom = refs[2 * pairs :]
+
+    def write(out):
+        begin = 0
+        for own, came in zip(refs[: 2 * pairs : 2], refs[1 : 2 * pairs : 2]):
+            lanes = pl.ds(begin, own.shape[-1])
+            begin += own.shape[-1]
+            if dense:
+                out[0, :, :, lanes] = own[0, :, 0] + came[:, 0]
+            else:
+                out[0, :, lanes] = own[0] + came[0]
+
+    for here, out in (
+        ((half == 0) & odd, top),
+        ((half == 1) & far, bottom),
+        ((half == 0) & jnp.logical_not(odd), keep_top),
+        ((half == 1) & jnp.logical_not(far), keep_bottom),
+    ):
+        pl.when(here)(functools.partial(write, out))
+
+
+def fold(dense, pairs, place):
+    if dense:
+        z, _, r, _ = pairs[0][1].shape
+        size, rest = z // 2, (r, sum(came.shape[-1] for _, came in pairs))
+    else:
+        size, rest = pairs[0][0].shape[1] // 2, pairs[0][0].shape[2:]
+    specs = []
+    for own, came in pairs:
+        n = own.shape[-1]
+        if dense:
+            specs += [
+                pl.BlockSpec(
+                    (1, size, 1, r, n), lambda k, h, place: (place[0], h, place[1] ^ k, 0, 0)
+                ),
+                pl.BlockSpec((size, 1, r, n), lambda k, h, place: (h, place[1] ^ k, 0, 0)),
+            ]
+        else:
+            specs += [pl.BlockSpec((1, size, n), lambda k, h, place: (k, h, 0))] * 2
+    tail = (0,) * (1 + len(rest))
+
+    def out(at):
+        return pl.BlockSpec((1, size, *rest), lambda k, h, place: (at(k), *tail))
+
+    elements = 2 * size * math.prod(rest)
+    return list(
+        pl.pallas_call(
+            functools.partial(fold_kernel, dense, len(pairs)),
+            out_shape=[jax.ShapeDtypeStruct((2, size, *rest), bf16)] * 4,
+            grid_spec=pltpu.PrefetchScalarGridSpec(
+                num_scalar_prefetch=1,
+                grid=(4, 2),
+                in_specs=specs,
+                out_specs=[
+                    out(lambda k: lax.div(k, 2)),
+                    out(lambda k: jnp.maximum(k - 2, 0)),
+                    out(lambda k: lax.div(k, 2)),
+                    out(lambda k: jnp.minimum(k, 1)),
+                ],
+            ),
+            compiler_params=pltpu.CompilerParams(
+                dimension_semantics=("arbitrary", "arbitrary"), vmem_limit_bytes=VMEM_LIMIT
+            ),
+            cost_estimate=cost(flops=4 * elements, bytes_accessed=24 * elements, transcendentals=0),
+            name="fold",
+        )(place, *(v for pair in pairs for v in pair))
+    )
+
+
+def fold_half_kernel(own_ref, came_ref, out_ref):
+    out_ref[...] = own_ref[...] + came_ref[...]
+
+
+def fold_half(own, came, block, half):
+    spec = pl.BlockSpec((1, *came.shape[1:]), lambda i: (i, 0, 0))
+    return pl.pallas_call(
+        fold_half_kernel,
+        out_shape=jax.ShapeDtypeStruct(came.shape, bf16),
+        grid=(2,),
+        in_specs=[pl.BlockSpec((1, *came.shape[1:]), lambda i: (block(i), half, 0)), spec],
+        out_specs=spec,
+        compiler_params=pltpu.CompilerParams(dimension_semantics=("arbitrary",)),
+        cost_estimate=cost(flops=came.size, bytes_accessed=6 * came.size, transcendentals=0),
+        name="fold_half",
+    )(own, came)
+
+
+def block_parts(own, other):
+    came = swap(other)
+    if lax.axis_size("expert") == 4:
+        return fold(False, [(own, came)], jnp.zeros((2,), jnp.int32))
+    return [(own[i].astype(f32) + came[i].astype(f32)).astype(bf16) for i in range(own.shape[0])]
+
+
+def swap_halves(grad, context):
+    z = lax.axis_size("dp")
+    count = lax.axis_size("expert")
+    r = grad.shape[0] // (2 * z * count)
+    grad = grad.astype(bf16).reshape(2, z, count, r, grad.shape[1])
+    return grad, swap(lax.dynamic_index_in_dim(grad, 1 - context, 0, keepdims=False))
+
+
+def dense_parts(halves, context, expert):
+    if lax.axis_size("expert") == 4 and halves[0][0].shape[3] % 16 == 0:
+        return fold(True, halves, jnp.stack([context, expert]).astype(jnp.int32))
+    out = []
+    for k in range(lax.axis_size("expert")):
+        sums = []
+        for grad, theirs in halves:
+            mine = lax.dynamic_index_in_dim(grad, context, 0, keepdims=False)
+            a, b = (lax.dynamic_index_in_dim(p, expert ^ k, 1, keepdims=False) for p in (mine, theirs))
+            sums.append(a.astype(f32) + b.astype(f32))
+        out.append(jnp.concatenate(sums, axis=-1).astype(bf16))
+    return out
 
 
 def scatter_first(parts):
     count = lax.axis_size("expert")
     if count != 4:
         return [flip(parts[k], k) for k in range(1, count)]
-    cut = halves_of(parts[0].shape[0])
-    top = jnp.stack([parts[1][:cut], parts[3][:cut]])
-    bottom = jnp.stack([parts[2][cut:], parts[3][cut:]])
-    return [flip(top, 1), flip(bottom, 2)]
+    return [flip(parts[0], 1), flip(parts[1], 2)]
 
 
 def scatter_second(parts, came):
     if lax.axis_size("expert") != 4:
         return []
-    cut = halves_of(parts[0].shape[0])
-    top = add_all(parts[2][:cut], [came[0][1]]).astype(bf16)
-    bottom = add_all(parts[1][cut:], [came[1][1]]).astype(bf16)
+    top = add_all(parts[2][1], [came[0][1]]).astype(bf16)
+    bottom = add_all(parts[3][1], [came[1][1]]).astype(bf16)
     return [flip(top, 2), flip(bottom, 1)]
 
 
 def scatter_total(parts, came, last):
     if lax.axis_size("expert") != 4:
         return add_all(parts[0], came)
-    cut = halves_of(parts[0].shape[0])
-    top = add_all(parts[0][:cut], [came[0][0], last[0]])
-    bottom = add_all(parts[0][cut:], [came[1][0], last[1]])
+    top = add_all(parts[2][0], [came[0][0], last[0]])
+    bottom = add_all(parts[3][0], [came[1][0], last[1]])
     return jnp.concatenate([top, bottom], axis=0)
 
 
@@ -193,11 +303,13 @@
 GELU_C = math.sqrt(2.0 / math.pi)
 
 
-def expert_kernel(count, tokens, capacity, place, *refs):
+def expert_kernel(count, tokens, capacity, apart, place, *refs):
     acts, dys = refs[: 2 * count], refs[2 * count : 4 * count]
     w_ref, refs = refs[4 * count], refs[4 * count + 1 :]
-    earlier, refs = refs[: len(refs) - 12], refs[len(refs) - 12 :]
-    y_refs, d_refs, (x_ref, gdy_ref, h_ref, dg_ref, du_ref, abuf, dbuf, sems) = refs[:2], refs[2:4], refs[4:]
+    sums = 7 if apart else 4
+    earlier, refs = refs[: len(refs) - sums - 8], refs[len(refs) - sums - 8 :]
+    y_refs, d_refs = refs[:2], refs[2:sums]
+    x_ref, gdy_ref, h_ref, dg_ref, du_ref, abuf, dbuf, sems = refs[sums:]
     step = pl.program_id(0)
     slot = lax.rem(step, 2)
 
@@ -285,39 +397,60 @@
             d = d + earlier[2 + s][0, :tokens].astype(f32)
             line = line + earlier[2 + s][0, tokens:].astype(f32)
         y_refs[s][0] = y.astype(bf16)
-        d_refs[s][0, :tokens] = d.astype(bf16)
-        d_refs[s][0, tokens:] = line.astype(bf16)
-
-
-def run_expert(acts, dys, weights, place, capacity, earlier=()):
+        d, line = d.astype(bf16), line.astype(bf16)
+        if s == 0 or not apart:
+            d_refs[s][0, :tokens] = d
+            d_refs[s][0, tokens:] = line
+            continue
+        cut = d_refs[1].shape[1]
+        odd, far = lax.rem(step, 2) == 1, step >= 2
+
+        def write_top(ref, d=d):
+            ref[0] = d[:cut]
+
+        def write_bottom(ref, d=d, line=line):
+            ref[0, : tokens - cut] = d[cut:]
+            ref[0, tokens - cut :] = line
+
+        for here, write, ref in zip(
+            (odd, far, jnp.logical_not(odd), jnp.logical_not(far)),
+            (write_top, write_bottom, write_top, write_bottom),
+            d_refs[1:],
+        ):
+            pl.when(here)(functools.partial(write, ref))
+
+
+def run_expert(acts, dys, weights, place, capacity, earlier, apart):
     count = len(acts) // 2
     tokens = dys[0].shape[0]
     rows = acts[0].shape[0]
     cz, _, _, local, _ = weights.shape
     slots = 2 * capacity
     total = count * slots
-
-    def row_block(width):
-        return pl.BlockSpec((slots, width), lambda i, place: (i, 0))
-
-    macs = total * (9 * MODEL_WIDTH * FF - 3 * MODEL_WIDTH * FF + 4 * tokens * MODEL_WIDTH)
-    moved = 2 * (
-        4 * count * (rows + tokens) * MODEL_WIDTH + total * (2 * MODEL_WIDTH + 3 * FF) + 3 * MODEL_WIDTH * FF
-    )
-    sums = [pl.BlockSpec((1, n, MODEL_WIDTH), lambda i, place: (i, 0, 0)) for n in (tokens, tokens, rows, rows)]
+    widths = (MODEL_WIDTH, MODEL_WIDTH, FF, FF, FF)
+    macs = total * (6 * MODEL_WIDTH * FF + 4 * tokens * MODEL_WIDTH)
+    moved = 2 * (4 * count * (rows + tokens) * MODEL_WIDTH + total * sum(widths) + 3 * MODEL_WIDTH * FF)
+
+    def block(n):
+        return pl.BlockSpec((1, n, MODEL_WIDTH), lambda i, place: (i, 0, 0))
+
+    def half(at):
+        return pl.BlockSpec((1, rows // 2, MODEL_WIDTH), lambda i, place: (at(i), 0, 0))
+
+    sums = [block(n) for n in (tokens, tokens, rows, rows)]
+    shapes = [jax.ShapeDtypeStruct((count, n, MODEL_WIDTH), bf16) for n in (tokens, tokens, rows, rows)]
+    outs = list(sums)
+    if apart:
+        outs[3:] = [
+            half(lambda i: lax.div(i, 2)),
+            half(lambda i: jnp.maximum(i - 2, 0)),
+            half(lambda i: lax.div(i, 2)),
+            half(lambda i: jnp.minimum(i, 1)),
+        ]
+        shapes[3:] = [jax.ShapeDtypeStruct((2, rows // 2, MODEL_WIDTH), bf16)] * 4
     return pl.pallas_call(
-        functools.partial(expert_kernel, count, tokens, capacity),
-        out_shape=(
-            jax.ShapeDtypeStruct((count, tokens, MODEL_WIDTH), bf16),
-            jax.ShapeDtypeStruct((count, tokens, MODEL_WIDTH), bf16),
-            jax.ShapeDtypeStruct((count, rows, MODEL_WIDTH), bf16),
-            jax.ShapeDtypeStruct((count, rows, MODEL_WIDTH), bf16),
-            jax.ShapeDtypeStruct((total, MODEL_WIDTH), bf16),
-            jax.ShapeDtypeStruct((total, MODEL_WIDTH), bf16),
-            jax.ShapeDtypeStruct((total, FF), bf16),
-            jax.ShapeDtypeStruct((total, FF), bf16),
-            jax.ShapeDtypeStruct((total, FF), bf16),
-        ),
+        functools.partial(expert_kernel, count, tokens, capacity, apart),
+        out_shape=(*shapes, *(jax.ShapeDtypeStruct((total, n), bf16) for n in widths)),
         grid_spec=pltpu.PrefetchScalarGridSpec(
             num_scalar_prefetch=1,
             grid=(count,),
@@ -330,14 +463,7 @@
                 )
             ]
             + (sums if earlier else []),
-            out_specs=(
-                *sums,
-                row_block(MODEL_WIDTH),
-                row_block(MODEL_WIDTH),
-                row_block(FF),
-                row_block(FF),
-                row_block(FF),
-            ),
+            out_specs=(*outs, *(pl.BlockSpec((slots, n), lambda i, place: (i, 0)) for n in widths)),
             scratch_shapes=[
                 pltpu.VMEM((2, 2, rows, MODEL_WIDTH), bf16),
                 pltpu.VMEM((2, 2, tokens, MODEL_WIDTH), bf16),
@@ -410,41 +536,44 @@
 
 
 SCORE = math.log2(math.e) / math.sqrt(HEAD_SIZE)
-STRIP = 256
+STRIP = 512
 
 
 def roll_half(x):
     return pltpu.roll(x, HEAD_SIZE // 2, 1)
 
 
-def causal(strip):
-    shape = ((strip + 1) * STRIP, STRIP)
-    key = lax.broadcasted_iota(jnp.int32, shape, 0)
-    return key <= lax.broadcasted_iota(jnp.int32, shape, 1) + strip * STRIP
+def masked(scores):
+    key = lax.broadcasted_iota(jnp.int32, (STRIP, STRIP), 0)
+    seen = key <= lax.broadcasted_iota(jnp.int32, (STRIP, STRIP), 1)
+    square = jnp.where(seen, scores[-STRIP:], mask_fill)
+    return jnp.concatenate([scores[:-STRIP], square], axis=0) if scores.shape[0] > STRIP else square
 
 
 def attend_kernel(place, q_ref, ko_ref, vo_ref, kr_ref, vr_ref, cos_ref, sin_ref, rot_ref, mix_ref, log_ref):
-    q = q_ref[...]
-    rot_ref[...] = (q * cos_ref[...] + roll_half(q) * sin_ref[...]).astype(bf16)
     last = ((1,), (1,))
     first = ((0,), (0,))
+    for m in range(PAIR):
+        lanes = pl.ds(m * HEAD_SIZE, HEAD_SIZE)
+        q = q_ref[:, lanes]
+        rot_ref[:, lanes] = (q * cos_ref[...] + roll_half(q) * sin_ref[...]).astype(bf16)
     for r in range(q_ref.shape[0] // STRIP):
         rows = pl.ds(r * STRIP, STRIP)
         seen = (r + 1) * STRIP
-        q = rot_ref[rows, :]
-        far = jnp.where(place[0] > 0, dot(kr_ref[...], q, last), mask_fill)
-        near = jnp.where(causal(r), dot(ko_ref[:seen, :], q, last), mask_fill)
-        peak = jnp.maximum(
-            jnp.max(far, axis=0, keepdims=True), jnp.max(near, axis=0, keepdims=True)
-        )
-        peak = peak * SCORE
-        far = jnp.exp2(far * SCORE - peak)
-        near = jnp.exp2(near * SCORE - peak)
-        total = jnp.sum(far, axis=0, keepdims=True) + jnp.sum(near, axis=0, keepdims=True)
-        out = dot(vr_ref[...], far.astype(bf16), first)
-        out = out + dot(vo_ref[:seen, :], near.astype(bf16), first)
-        mix_ref[rows, :] = (out / total).T.astype(bf16)
-        log_ref[0, :, rows] = peak + jnp.log2(total)
+        for m in range(PAIR):
+            lanes = pl.ds(m * HEAD_SIZE, HEAD_SIZE)
+            q = rot_ref[rows, lanes]
+            far = dot(kr_ref[...], q, last)
+            near = masked(dot(ko_ref[:seen, :], q, last))
+            far_peak = jnp.where(place[0] > 0, jnp.max(far, axis=0, keepdims=True), mask_fill)
+            peak = jnp.maximum(far_peak, jnp.max(near, axis=0, keepdims=True)) * SCORE
+            far = jnp.exp2(far * SCORE - jnp.where(place[0] > 0, peak, -mask_fill))
+            near = jnp.exp2(near * SCORE - peak)
+            total = jnp.sum(far, axis=0, keepdims=True) + jnp.sum(near, axis=0, keepdims=True)
+            out = dot(vr_ref[...], far.astype(bf16), first)
+            out = out + dot(vo_ref[:seen, :], near.astype(bf16), first)
+            mix_ref[rows, lanes] = (out / total).T.astype(bf16)
+            log_ref[m, :, rows] = peak + jnp.log2(total)
 
 
 def key_value_kernel(x_ref, cos_ref, sin_ref, out_ref):
@@ -497,12 +626,17 @@
     )(near, came, cosine, sine)
 
 
+PAIR = 6
+
+
 def attention_specs(tokens):
-    head = pl.BlockSpec((tokens, HEAD_SIZE), lambda h, place: (0, h))
-    key = pl.BlockSpec((tokens, HEAD_SIZE), lambda h, place: (0, h // GROUP))
-    value = pl.BlockSpec((tokens, HEAD_SIZE), lambda h, place: (0, KEY_VALUE_HEADS + h // GROUP))
+    head = pl.BlockSpec((tokens, PAIR * HEAD_SIZE), lambda h, place: (0, h))
+    key = pl.BlockSpec((tokens, HEAD_SIZE), lambda h, place: (0, h * PAIR // GROUP))
+    value = pl.BlockSpec(
+        (tokens, HEAD_SIZE), lambda h, place: (0, KEY_VALUE_HEADS + h * PAIR // GROUP)
+    )
     table = pl.BlockSpec((tokens, HEAD_SIZE), lambda h, place: (0, 0))
-    log = pl.BlockSpec((1, 1, tokens), lambda h, place: (h, 0, 0))
+    log = pl.BlockSpec((PAIR, 1, tokens), lambda h, place: (h, 0, 0))
     return head, key, value, table, log
 
 
@@ -519,7 +653,7 @@
         ),
         grid_spec=pltpu.PrefetchScalarGridSpec(
             num_scalar_prefetch=1,
-            grid=(QUERY_HEADS,),
+            grid=(QUERY_HEADS // PAIR,),
             in_specs=[head, key, value, key, value, table, table],
             out_specs=(head, head, log),
         ),
@@ -540,9 +674,9 @@
     last = ((1,), (1,))
     first = ((0,), (0,))
     scale = 1.0 / math.sqrt(HEAD_SIZE)
-    head = pl.program_id(0)
-
-    @pl.when(lax.rem(head, GROUP) == 0)
+    pair = pl.program_id(0)
+
+    @pl.when(lax.rem(pair, GROUP // PAIR) == 0)
     def _():
         for ref in (dko_ref, dvo_ref, dkr_ref, dvr_ref):
             ref[...] = jnp.zeros_like(ref)
@@ -550,30 +684,37 @@
     for r in range(q_ref.shape[0] // STRIP):
         rows = pl.ds(r * STRIP, STRIP)
         seen = (r + 1) * STRIP
-        q = q_ref[rows, :]
-        dout = dout_ref[rows, :]
-        logs = log_ref[0, :, rows]
-        far = jnp.where(place[0] > 0, dot(kr_ref[...], q, last), mask_fill)
-        near = jnp.where(causal(r), dot(ko_ref[:seen, :], q, last), mask_fill)
-        far = jnp.exp2(far * SCORE - logs)
-        near = jnp.exp2(near * SCORE - logs)
-        dvr_ref[...] += dot(far.astype(bf16), dout)
-        dvo_ref[:seen, :] += dot(near.astype(bf16), dout)
-        dfar = dot(vr_ref[...], dout, last)
-        dnear = dot(vo_ref[:seen, :], dout, last)
-        inner = jnp.sum(far * dfar, axis=0, keepdims=True)
-        inner = inner + jnp.sum(near * dnear, axis=0, keepdims=True)
-        dfar = (far * (dfar - inner)).astype(bf16)
-        dnear = (near * (dnear - inner)).astype(bf16)
-        dkr_ref[...] += dot(dfar, q)
-        dko_ref[:seen, :] += dot(dnear, q)
-        dq = dot(kr_ref[...], dfar, first) + dot(ko_ref[:seen, :], dnear, first)
-        dq = dq.T * scale
-        dq_ref[rows, :] = (dq * cos_ref[rows, :] - roll_half(dq) * sin_ref[rows, :]).astype(bf16)
+        dvr = dvo = dkr = dko = 0.0
+        for m in range(PAIR):
+            lanes = pl.ds(m * HEAD_SIZE, HEAD_SIZE)
+            q = q_ref[rows, lanes]
+            dout = dout_ref[rows, lanes]
+            logs = log_ref[m, :, rows]
+            far = dot(kr_ref[...], q, last)
+            near = masked(dot(ko_ref[:seen, :], q, last))
+            far = jnp.exp2(far * SCORE - jnp.where(place[0] > 0, logs, -mask_fill))
+            near = jnp.exp2(near * SCORE - logs)
+            dvr = dvr + dot(far.astype(bf16), dout)
+            dvo = dvo + dot(near.astype(bf16), dout)
+            dfar = dot(vr_ref[...], dout, last)
+            dnear = dot(vo_ref[:seen, :], dout, last)
+            inner = jnp.sum(far * dfar, axis=0, keepdims=True)
+            inner = inner + jnp.sum(near * dnear, axis=0, keepdims=True)
+            dfar = (far * (dfar - inner)).astype(bf16)
+            dnear = (near * (dnear - inner)).astype(bf16)
+            dkr = dkr + dot(dfar, q)
+            dko = dko + dot(dnear, q)
+            dq = dot(kr_ref[...], dfar, first) + dot(ko_ref[:seen, :], dnear, first)
+            dq = dq.T * scale
+            dq_ref[rows, lanes] = (dq * cos_ref[rows, :] - roll_half(dq) * sin_ref[rows, :]).astype(bf16)
+        dvr_ref[...] += dvr
+        dvo_ref[:seen, :] += dvo
+        dkr_ref[...] += dkr
+        dko_ref[:seen, :] += dko
 
     for h in range(KEY_VALUE_HEADS):
 
-        @pl.when(head == (h + 1) * GROUP - 1)
+        @pl.when(pair == (h + 1) * GROUP // PAIR - 1)
         def _(h=h):
             key = pl.ds(h * HEAD_SIZE, HEAD_SIZE)
             value = pl.ds(KV_WIDTH + h * HEAD_SIZE, HEAD_SIZE)
@@ -597,7 +738,7 @@
         ),
         grid_spec=pltpu.PrefetchScalarGridSpec(
             num_scalar_prefetch=1,
-            grid=(QUERY_HEADS,),
+            grid=(QUERY_HEADS // PAIR,),
             in_specs=[head, head, key, value, key, value, log, table, table],
             out_specs=(head, side, side),
             scratch_shapes=[pltpu.VMEM((tokens, HEAD_SIZE), f32)] * 4,
@@ -610,26 +751,6 @@
         ),
         name="attention_back",
     )(context, query, dmixed, near, near, far, far, logs, cosine, sine)
-
-
-def swap_halves(grad, context):
-    z = lax.axis_size("dp")
-    count = lax.axis_size("expert")
-    r = grad.shape[0] // (2 * z * count)
-    grad = grad.astype(bf16).reshape(2, z, count, r, grad.shape[1])
-    theirs = swap(lax.dynamic_index_in_dim(grad, 1 - context, 0, keepdims=False))
-    return lax.dynamic_index_in_dim(grad, context, 0, keepdims=False), theirs
-
-
-def dense_parts(halves, expert):
-    out = []
-    for k in range(lax.axis_size("expert")):
-        sums = []
-        for pair in halves:
-            a, b = (lax.dynamic_index_in_dim(p, expert ^ k, 1, keepdims=False) for p in pair)
-            sums.append(a.astype(f32) + b.astype(f32))
-        out.append(jnp.concatenate(sums, axis=-1).astype(bf16))
-    return out
 
 
 def add_all(own, came):
@@ -645,11 +766,6 @@
     blocks = jnp.stack([share] + [flip(share, k) for k in range(1, count)])
     pieces = [lax.dynamic_index_in_dim(blocks, expert ^ e, 0, keepdims=False) for e in range(count)]
     return jnp.concatenate(pieces, axis=0).astype(f32), share
-
-
-def block_parts(own, other):
-    came = swap(other)
-    return [(own[i].astype(f32) + came[i].astype(f32)).astype(bf16) for i in range(own.shape[0])]
 
 
 def local(
@@ -764,6 +880,7 @@
     gates_high = gates.astype(bf16)
     gates_low = (gates - gates_high.astype(f32)).astype(bf16)
     meta = jnp.concatenate([gates_high, gates_low, slot_code.astype(bf16)], axis=1)
+    meta = jnp.pad(meta, ((0, -experts_all % 32), (0, 0)))
     payload = jnp.concatenate([act_two, meta], axis=0)
     acts_own, acts_other = spread(after(payload, *dys_own[1:]))
 
@@ -771,35 +888,52 @@
     step = jnp.array([1, 0], jnp.int32)
     sums, shares = (), []
     for j in range(per_core):
+        final = j == per_core - 1
         *sums, x, gdy, hidden, dgate, dup = run_expert(
-            acts_own + acts_other, dys_own + dys_other, gathered[j], place, capacity, sums
+            acts_own + acts_other,
+            dys_own + dys_other,
+            gathered[j],
+            place,
+            capacity,
+            sums,
+            final and count == 4,
         )
-        if j == per_core - 1:
-            d_parts = block_parts(sums[2], sums[3])
-            (x, y_other), d_parts = tie_lists((x, sums[1]), d_parts)
+        if final and count == 4:
+            y_own, y_other, d_own, *d_apart = sums
+            top = fold_half(d_own, swap(d_apart[0]), lambda i: 2 * i + 1, 0)
+            bottom = fold_half(d_own, swap(d_apart[1]), lambda i: i + 2, 1)
+            d_came = scatter_first([top, bottom])
+            (x, y_other, *d_apart[2:]), (top, bottom) = tie_lists(
+                (x, y_other, *d_apart[2:]), (top, bottom)
+            )
+            keep_top = fold_half(d_own, swap(d_apart[2]), lambda i: 2 * i, 0)
+            keep_bottom = fold_half(d_own, swap(d_apart[3]), lambda i: i, 1)
+            d_parts = [top, bottom, keep_top, keep_bottom]
+        elif final:
+            y_own, y_other, d_own, d_other = sums
+            d_parts = block_parts(d_own, d_other)
             d_came = scatter_first(d_parts)
-        grads = weight_grads(x, gdy, hidden, dgate, dup, z, rows, True)
+        grads = weight_grads(x, gdy, hidden, dgate, dup, z, rows, False)
         (place,), grads = tie_lists((place + step,), grads)
-        if j == per_core - 1:
-            y_parts = block_parts(sums[0], y_other)
+        if final:
             d_came, grads = tie_lists(d_came, grads)
             d_last = scatter_second(d_parts, d_came)
+            y_parts = block_parts(y_own, y_other)
             d_last, y_parts, shares[-1] = tie_lists(d_last, y_parts, shares[-1])
         shares.append([lax.psum_scatter(g, "dp", scatter_dimension=0, tiled=False) for g in grads])
     dact = scatter_total(d_parts, d_came, d_last)
     y_came = scatter_first(y_parts)
 
     dy = out_grad[0].astype(f32)
-    dgates = dact[tokens:, :tokens] + dact[tokens:, tokens : 2 * tokens]
+    dgates = dact[tokens : tokens + experts_all, : 2 * tokens]
+    dgates = dgates[:, :tokens] + dgates[:, tokens:]
     dlogits = (gates * (dgates - jnp.sum(gates * dgates, axis=0, keepdims=True))).astype(bf16)
     dact_two = dact[:tokens] + dot(dlogits, router_w, ((0,), (1,)))
-    grad_router = dot(dlogits, act_two)
     grad_gain_two = jnp.sum(dact_two * norm_two, axis=0)
     dn2 = dact_two * gain_two
     dresid = dy + scale_two * (dn2 - norm_two * jnp.mean(dn2 * norm_two, axis=-1, keepdims=True))
     dresid_b = dresid.astype(bf16)
     dmixed = dot(dresid_b, out_w, ((1,), (1,))).astype(bf16)
-    out_halves = swap_halves(dot(mixed, after(dresid_b, dmixed), ((0,), (0,))), context)
 
     dquery, near_grad, far_grad = attention_back(
         where, query, dmixed, near, far, logs, cos_wide, sin_wide
@@ -809,36 +943,49 @@
     grad_query = dot(act_one, dquery, ((0,), (0,))).astype(bf16)
     dkv = key_value_back(near_grad, came, cos_wide, sin_wide)
     grad_kv = dot(act_one, dkv, ((0,), (0,))).astype(bf16)
+    halves = [swap_halves(grad, context) for grad in (grad_query, grad_kv)]
+    first_parts = dense_parts(halves, context, expert)
+    first_came = scatter_first(first_parts)
+
+    first_parts, (dquery, dkv, dlogits, dresid_b), shares[0] = tie_lists(
+        first_parts, (dquery, dkv, dlogits, dresid_b), shares[0]
+    )
+    out_halves = swap_halves(dot(mixed, dresid_b, ((0,), (0,))), context)
     dact_one = dot(dquery, qkv_w[:, :Q_WIDTH], ((1,), (1,)))
     dact_one = dact_one + dot(dkv, qkv_w[:, Q_WIDTH:], ((1,), (1,)))
     grad_gain_one = jnp.sum(dact_one * norm_one, axis=0)
+    dn1 = dact_one * gain_one
+    grad_in = dresid + scale_one * (dn1 - norm_one * jnp.mean(dn1 * norm_one, axis=-1, keepdims=True))
     small = jnp.concatenate(
         [
-            grad_router,
+            dot(dlogits, act_two),
             grad_gain_one[None],
             grad_gain_two[None],
             jnp.zeros((SMALL - experts_all - 2, MODEL_WIDTH), f32),
         ],
         axis=0,
     )
-    halves = [swap_halves(grad, context) for grad in (grad_query, grad_kv, small.T)]
-    first_parts = dense_parts(halves, expert)
-    first_came = scatter_first(first_parts)
-    out_parts = dense_parts([out_halves], expert)
+    small = swap_halves(small.T, context)
+    (out_theirs, small_theirs), first_came = tie_lists((out_halves[1], small[1]), first_came)
+    first_last = scatter_second(first_parts, first_came)
+    out_halves = [(out_halves[0], out_theirs), (small[0], small_theirs)]
+    out_parts = dense_parts(out_halves, context, expert)
     out_came = scatter_first(out_parts)
+    first_total = scatter_total(first_parts, first_came, first_last)
+    (first_total,), shares[-1], out_parts = tie_lists(
+        (first_total.astype(bf16),), shares[-1], out_parts
+    )
+    first, first_share = finish_dense(first_total, expert)
     out_total = scatter_total(out_parts, out_came, scatter_second(out_parts, out_came))
-
-    dn1 = dact_one * gain_one
-    grad_in = dresid + scale_one * (dn1 - norm_one * jnp.mean(dn1 * norm_one, axis=-1, keepdims=True))
-    y_came, first_came = tie_lists(y_came, first_came)
-    first_total = scatter_total(first_parts, first_came, scatter_second(first_parts, first_came))
-    y_sum = scatter_total(y_parts, y_came, scatter_second(y_parts, y_came))
+    (out_total, first_share, grad_in), y_came = tie_lists(
+        (out_total.astype(bf16), first_share, grad_in), y_came
+    )
+    last, out_share = finish_dense(out_total, expert)
+    y_last = scatter_second(y_parts, y_came)
+    y_last, (out_share,) = tie_lists(y_last, (out_share,))
+    y_sum = scatter_total(y_parts, y_came, y_last)
     block_out = (resid_one + y_sum).astype(bf16)[None]
-    out_total, shares[-1][-1] = tie(out_total.astype(bf16), shares[-1][-1])
-    grad_out, out_share = finish_dense(out_total, expert)
-    first, _ = finish_dense(first_total.astype(bf16), expert)
     kv_at = Q_WIDTH + KV_WIDTH
-    small_at = kv_at + KV_WIDTH
 
     finals = []
     for pair in shares:
@@ -851,13 +998,13 @@
     return (
         block_out,
         grad_in[None],
-        first[:, small_at + experts_all],
+        last[:, MODEL_WIDTH + experts_all],
         first[:, :Q_WIDTH],
         first[:, Q_WIDTH:kv_at],
-        first[:, kv_at:small_at],
-        grad_out,
-        first[:, small_at + experts_all + 1],
-        first[:, small_at : small_at + experts_all],
+        first[:, kv_at:],
+        last[:, :MODEL_WIDTH],
+        last[:, MODEL_WIDTH + experts_all + 1],
+        last[:, MODEL_WIDTH : MODEL_WIDTH + experts_all],
         stacked[:, 0],
         stacked[:, 1],
         jnp.swapaxes(stacked[:, 2], 1, 2),

time: 662 us -> 641 us (0.968)
  Pallas kernels: 182 us -> 208 us
  waiting for transfers between devices: 199 us -> 176 us
  other arithmetic: 81.1 us -> 61.4 us
    pallas_call x2 -> x9, Pallas kernels: 85.6 us -> 126 us  [the longest x2 89.1 us: run_expert(): pl.pallas_call(functools.partial(expert_kernel, count, tokens, capacity,...]
    convert_element_type x11 -> x9, other arithmetic: 29.2 us -> 15.8 us  [the longest x4 8.04 us: scatter_second(): bottom = add_all(parts[3][1], [came[1][1]]).astype(bf16)]
    reduce_scatter x4 -> x2, waiting for transfers between devices: 12.9 us -> 0.01 us  [local(): lax.psum_scatter(g, 'dp', scatter_dimension=0, tiled=False)]
    ppermute x38, waiting for transfers between devices: 154 us -> 143 us  [flip(): return lax.ppermute(value, 'expert', [(i, i ^ step) for i in range(count)])]
    ppermute x23 -> x26, waiting for transfers between devices: 21.7 us -> 13.5 us  [swap(): return lax.ppermute(value, 'context', [(0, 1), (1, 0)])]
    another operation x16 -> x7, other arithmetic: 15.1 us -> 7.89 us
    pallas_call x1, Pallas kernels: 19 us -> 12 us  [attention(): pl.pallas_call(attend_kernel, out_shape=(jax.ShapeDtypeStruct((tokens, Q_...]
    unnamed x145 -> x135, local copies, waits for them, and re-layouts: 21.5 us -> 17.7 us
  transfers between devices with their start and end apart: 72 -> 73, of which waited for: 29 -> 30; matrix products, arithmetic and copies ran while one was open for 24% -> 22% of each run, Pallas kernels for 28% -> 33%
where the time goes in v4:
time: 641 us; the launch traced here: 633 us
  Pallas kernels  208 us (32%)
  waiting for transfers between devices  176 us (27%)
  other arithmetic  61.4 us (10%)
  local copies, waits for them, and re-layouts  51.6 us (8%)
  starting transfers between devices  51.3 us (8%)
  matrix products  44.3 us (7%)
  blocking collectives  25.7 us (4%)
  between operations  15.6 us (2%)
    ppermute x38, waiting for transfers between devices, flip(): return lax.ppermute(value, 'expert', [(i, i ^ step) for i in range(count)])  143 us
    pallas_call x2, Pallas kernels, run_expert(): pl.pallas_call(functools.partial(expert_kernel, count, tokens, capacity,...  89.1 us
    dot_general x12, matrix products, dot(): return lax.dot_general(a, b, (dims, ((), ())), preferred_element_type=f32)  44.3 us
    ppermute x38, starting transfers between devices, flip(): return lax.ppermute(value, 'expert', [(i, i ^ step) for i in range(count)])  43.1 us
    pallas_call x2, Pallas kernels, weight_grads(): pl.pallas_call(functools.partial(weight_grad_kernel, per), out_shape=shap...  29.5 us
    all_gather x1, blocking collectives, local(): first_z = lax.all_gather(first_pack, 'dp', axis=0, tiled=False)  25.7 us
    pallas_call x3, Pallas kernels, fold(): pl.pallas_call(functools.partial(fold_kernel, dense, len(pairs)), out_sha...  25.1 us
    pallas_call x1, Pallas kernels, attention_back(): pl.pallas_call(attend_back_kernel, out_shape=(jax.ShapeDtypeStruct((token...  23.8 us
  transfers between devices with their start and end apart: 73, of which 30 were waited for; matrix products, arithmetic and copies ran while one was open for 22% of the time, Pallas kernels for 33%

profile of v4, /device:TPU:0, one launch (start us, length us, event | category | flops | bytes accessed | tf_op | source)
XLA Modules:
  0.0 633.5 jit_solution(3402662502397169964)
XLA Ops:
  11.1 2.9 convert.46
  21.9 25.7 %all-gather = bf16[192,2176]{1,0:T(8,128)(2,1)S(1)} all-gather(bf16[48,2176]{1,0:T(8,128)(2,1)S(1)} %concatenate.57), channel_id=2, replica_groups=mesh['expert'=4,'context'=2,'dp'=4] {'dp'}, dimensions={0}, use_global_device_ids=true | all-gather | bytes 1044480 | tf_op jit(solution)/shard_map/all_gather | solution.py:826
  50.6 16.8 %collective-permute-done.refs_1_ = bf16[4,48,2176]{2,1,0:T(8,128)(2,1)} collective-permute-done((bf16[4,48,2176]{2,1,0:T(8,128)(2,1)S(1)}, bf16[4,48,2176]{2,1,0:T(8,128)(2,1)}, u32[]{:S(2)}, u32[]{:S(2)}) %collective-permute-start) | collective-permute-done | bytes 835616 | tf_op jit(solution)/shard_map/ppermute | solution.py:56
  73.1 5.2 collective-permute-done.2
  82.4 2.1 dynamic-slice_bitcast_fusion.3
  86.6 6.5 %assemble.2 = bf16[2,4,4,48,2176]{4,3,2,1,0:T(8,128)(2,1)} custom-call(s32[2]{0:T(128)} %pad_add_fusion.place, bf16[4,48,2176]{2,1,0:T(8,128)(2,1)} %bitcast.254, bf16[4,48,2176]{2,1,0:T(8,128)(2,1)} %collective-permute-done.refs_1_, bf16[4,48,2176]{2,1,0:T(8,128)(2,1)} %collective-permute-done.1.refs_2_, ...), custom_call_target="tpu_custom_call" | custom-call | bytes 13369344 | tf_op jit(solution)/shard_map/assemble/pallas_call | solution.py:115
  94.4 8.0 %fusion.x_ref.q_ref = f32[512,2048]{1,0:T(8,128)} fusion(bf16[1536,2176]{1,0:T(8,128)(2,1)} %bitcast.227, bf16[1,512,1536]{2,1,0:T(8,128)(2,1)S(1)} %copy-done.13, f32[1536]{0:T(1024)S(1)} %get-tuple-element.249, f32[512]{0:T(512)S(1)} %add_rsqrt_fusion.1), kind=kOutput, calls=%fused_computation.2 | convolution fusion | flops 3224371200 | bytes 12066816 | tf_op jit(solution)/shard_map/dot_general | solution.py:43
  106.7 5.8 collective-permute-done.11
  112.5 2.2 collective-permute-done.12
  117.9 2.4 key_value.1.ko_ref.vo_ref
  124.3 12.0 %attention.1 = (bf16[512,1536]{1,0:T(8,128)(2,1)}, bf16[512,1536]{1,0:T(8,128)(2,1)}, f32[12,1,512]{2,1,0:T(1,128)}) custom-call(s32[1]{0:T(128)} %bitcast.1.place, f32[512,2048]{1,0:T(8,128)} %fusion.x_ref.q_ref, bf16[512,512]{1,0:T(8,128)(2,1)} %key_value.1.ko_ref.vo_ref, bf16[512,512]{1,0:T(8,128)(2,1)} %key_value.1.ko_ref.vo_ref, ...), custom_call_target="tpu_custom_call" | custom-call | flops 3221225472 | bytes 7864320 | tf_op jit(solution)/shard_map/attention/pallas_call | solution.py:647
  137.4 5.2 assemble.3
  142.6 7.5 %collective-permute-done.13.refs_9_ = bf16[512,1536]{1,0:T(8,128)(2,1)} collective-permute-done((bf16[512,1536]{1,0:T(8,128)(2,1)S(1)}, bf16[512,1536]{1,0:T(8,128)(2,1)}, u32[]{:S(2)}, u32[]{:S(2)}) %collective-permute-start.13) | collective-permute-done | bytes 1572896 | tf_op jit(solution)/shard_map/ppermute | solution.py:56
  154.9 4.6 multiply_reduce_fusion.2
  163.1 5.7 collective-permute-done.18
  174.7 31.8 %collective-permute-done.20.refs_1_ = bf16[544,1536]{1,0:T(8,128)(2,1)} collective-permute-done((bf16[544,1536]{1,0:T(8,128)(2,1)}, bf16[544,1536]{1,0:T(8,128)(2,1)}, u32[]{:S(2)}, u32[]{:S(2)}) %collective-permute-start.20) | collective-permute-done | bytes 1671200 | tf_op jit(solution)/shard_map/ppermute | solution.py:56
  212.1 13.4 %collective-permute-done.22 = bf16[272,1536]{1,0:T(8,128)(2,1)S(1)} collective-permute-done((bf16[272,1536]{1,0:T(8,128)(2,1)S(1)}, bf16[272,1536]{1,0:T(8,128)(2,1)S(1)}, u32[]{:S(2)}, u32[]{:S(2)}) %collective-permute-start.22) | collective-permute-done | bytes 835616 | tf_op jit(solution)/shard_map/ppermute | solution.py:56
  230.3 9.1 %collective-permute-done.31.refs_15_ = bf16[512,1536]{1,0:T(8,128)(2,1)} collective-permute-done((bf16[512,1536]{1,0:T(8,128)(2,1)}, bf16[512,1536]{1,0:T(8,128)(2,1)}, u32[]{:S(2)}, u32[]{:S(2)}) %collective-permute-start.31) | collective-permute-done | bytes 1572896 | tf_op jit(solution)/shard_map/ppermute | solution.py:60
  239.5 41.5 %experts.2 = (bf16[4,512,1536]{2,1,0:T(8,128)(2,1)}, bf16[4,512,1536]{2,1,0:T(8,128)(2,1)}, bf16[4,544,1536]{2,1,0:T(8,128)(2,1)}, bf16[4,544,1536]{2,1,0:T(8,12...) custom-call(s32[2]{0:T(128)} %get-tuple-element.251.place, ...), custom_call_target="tpu_custom_call" | custom-call | flops 26172456960 | bytes 72744960 | tf_op jit(solution)/shard_map/experts/pallas_call | solution.py:451
  280.9 14.8 %weight_grads.2 = bf16[4,2,3,192,768]{4,3,2,1,0:T(8,128)(2,1)} custom-call(bf16[1280,1536]{1,0:T(8,128)(2,1)} %get-tuple-element.115.x_ref, bf16[1280,1536]{1,0:T(8,128)(2,1)} %get-tuple-element.116.gdy_ref, bf16[1280,768]{1,0:T(8,128)(2,1)} %get-tuple-element.117.h_ref, bf16[1280,768]{1,0:T(8,128)(2,1)} %get-tuple-element.118.dg_ref, ...), custom_call_target="tpu_custom_call" | custom-call | flops 9059696640 | bytes 20840448 | tf_op jit(solution)/shard_map/weight_grads/pallas_call | solution.py:520
  295.8 6.2 all-gather.12.cloned.1.call-done
  302.0 47.6 %experts.3 = (bf16[4,512,1536]{2,1,0:T(8,128)(2,1)}, bf16[4,512,1536]{2,1,0:T(8,128)(2,1)}, bf16[4,544,1536]{2,1,0:T(8,128)(2,1)}, bf16[2,272,1536]{2,1,0:T(8,12...) custom-call(s32[2]{0:T(128)} %get-tuple-element.120.place, ...), custom_call_target="tpu_custom_call" | custom-call | flops 26172456960 | bytes 72744960 | tf_op jit(solution)/shard_map/experts/pallas_call | solution.py:451
  350.1 3.4 collective-permute-done.33.came_ref
  353.5 2.9 fold_half.5
  356.4 3.0 fold_half.4
  363.1 14.7 %weight_grads.3 = bf16[4,2,3,192,768]{4,3,2,1,0:T(8,128)(2,1)} custom-call(bf16[1280,1536]{1,0:T(8,128)(2,1)} %get-tuple-element.134.x_ref, bf16[1280,1536]{1,0:T(8,128)(2,1)} %get-tuple-element.135.gdy_ref, bf16[1280,768]{1,0:T(8,128)(2,1)} %get-tuple-element.136.h_ref, bf16[1280,768]{1,0:T(8,128)(2,1)} %get-tuple-element.137.dg_ref, ...), custom_call_target="tpu_custom_call" | custom-call | flops 9059696640 | bytes 20840448 | tf_op jit(solution)/shard_map/weight_grads/pallas_call | solution.py:520
  377.8 20.8 %collective-permute-done.36 = bf16[2,272,1536]{2,1,0:T(8,128)(2,1)} collective-permute-done((bf16[2,272,1536]{2,1,0:T(8,128)(2,1)}, bf16[2,272,1536]{2,1,0:T(8,128)(2,1)}, u32[]{:S(2)}, u32[]{:S(2)}) %collective-permute-start.36) | collective-permute-done | bytes 1671200 | tf_op jit(solution)/shard_map/ppermute | solution.py:56
  399.9 2.9 fold_half.7
  402.8 2.5 fusion.28
  406.8 2.9 fold_half.6
  409.7 2.5 fusion.27
  413.5 10.5 %fold.3 = (bf16[2,256,1536]{2,1,0:T(8,128)(2,1)}, bf16[2,256,1536]{2,1,0:T(8,128)(2,1)}, bf16[2,256,1536]{2,1,0:T(8,128)(2,1)}, bf16[2,256,1536]{2,1,0:T(8,128)(2,1)}) custom-call(s32[2]{0:T(128)} %broadcast_3_place.2.place, bf16[4,512,1536]{2,1,0:T(8,128)(2,1)} %get-tuple-element.142.refs_0_, bf16[4,512,1536]{2,1,0:T(8,128)(2,1)} %collective-permute-done.40.refs_1_), custom_call_target="tpu_custom_call" | custom-call | flops 3145728 | bytes 18874368 | tf_op jit(solution)/shard_map/fold/pallas_call | solution.py:205
  425.3 6.7 %collective-permute-done.37 = bf16[272,1536]{1,0:T(8,128)(2,1)} collective-permute-done((bf16[272,1536]{1,0:T(8,128)(2,1)}, bf16[272,1536]{1,0:T(8,128)(2,1)}, u32[]{:S(2)}, u32[]{:S(2)}) %collective-permute-start.37) | collective-permute-done | bytes 835616 | tf_op jit(solution)/shard_map/ppermute | solution.py:56
  432.0 2.1 bitcast_add_fusion
  435.3 2.1 bitcast_add_fusion.1
  437.4 3.0 multiply_reduce_fusion
  442.0 3.8 convolution_convert_fusion.3.dout_ref
  445.8 23.8 %attention_back.1 = (bf16[512,1536]{1,0:T(8,128)(2,1)}, f32[512,512]{1,0:T(8,128)}, bf16[512,512]{1,0:T(8,128)(2,1)}) custom-call(s32[1]{0:T(128)} %bitcast.1.place, bf16[512,1536]{1,0:T(8,128)(2,1)} %get-tuple-element.150.q_ref, bf16[512,1536]{1,0:T(8,128)(2,1)} %convolution_convert_fusion.3.dout_ref, bf16[512,512]{1,0:T(8,128)(2,1)} %key_value.1.ko_ref.vo_ref, ...), custom_call_target="tpu_custom_call" | custom-call | flops 8053063680 | bytes 6291456 | tf_op jit(solution)/shard_map/attention_back/pallas_call | solution.py:732
  469.6 4.6 convolution_convert_fusion.1
  478.5 4.1 collective-permute-done.44.came_ref
  482.6 2.6 key_value_back.1
  485.2 2.6 convolution_convert_fusion.2
  492.6 7.6 %fold.4 = (bf16[2,2,48,2048]{3,2,1,0:T(8,128)(2,1)}, bf16[2,2,48,2048]{3,2,1,0:T(8,128)(2,1)}, bf16[2,2,48,2048]{3,2,1,0:T(8,128)(2,1)}, bf16[2,2,48,2048]{3,2,1,0:T(8,128)(2,1)}) custom-call(s32[2]{0:T(128)} %pad_add_fusion.place, bf16[2,4,4,48,1536]{4,3,2,1,0:T(8,128)(2,1)} %bitcast.233, bf16[4,4,48,1536]{3,2,1,0:T(8,128)(2,1)} %collective-permute-done.41.refs_1_, ...), custom_call_target="tpu_custom_call" | custom-call | flops 1572864 | bytes 9437184 | tf_op jit(solution)/shard_map/fold/pallas_call | solution.py:205
  503.4 2.4 select_bitcast_fusion.1
  505.8 4.3 convolution_convert_fusion
  513.6 2.7 fusion.20
  516.4 7.7 %fusion.13 = (f32[512]{0:T(512)}, bf16[1536]{0:T(1024)(128)(2,1)}, f32[512,1536]{1,0:T(8,128)}) fusion(bf16[1,512,1536]{2,1,0:T(8,128)(2,1)S(1)} %copy-done.15, f32[1536]{0:T(1024)S(1)} %copy-done.47, f32[512]{0:T(512)S(1)} %copy-done.50, f32[512,1536]{1,0:T(8,128)S(1)} %fusion.20, bf16[512,1536]{1,0:T(8,128)(2,1)S(1)} %copy-done.59, ...), kind=kOutput, calls=%fused_computation.18 | convolution fusion | flops 2422208512 | bytes 14169088 | tf_op jit(solution)/shard_map/dot_general | solution.py:43
  529.5 5.5 fusion.16
  535.0 2.6 fusion.25
  537.7 1.9 fusion.35
  540.1 1.8 fusion.36
  542.5 7.1 %fold.5 = (bf16[2,2,48,1664]{3,2,1,0:T(8,128)(2,1)}, bf16[2,2,48,1664]{3,2,1,0:T(8,128)(2,1)}, bf16[2,2,48,1664]{3,2,1,0:T(8,128)(2,1)}, bf16[2,2,48,1664]{3,2,1,0:T(8,128)(2,1)}) custom-call(s32[2]{0:T(128)} %pad_add_fusion.place, bf16[2,4,4,48,1536]{4,3,2,1,0:T(8,128)(2,1)} %bitcast.235, bf16[4,4,48,1536]{3,2,1,0:T(8,128)(2,1)} %collective-permute-done.46.refs_1_, ...), custom_call_target="tpu_custom_call" | custom-call | flops 1277952 | bytes 7667712 | tf_op jit(solution)/shard_map/fold/pallas_call | solution.py:205
  556.4 2.4 select_bitcast_fusion
  559.0 8.2 %collective-permute-done.52 = bf16[2,2,48,1664]{3,2,1,0:T(8,128)(2,1)} collective-permute-done((bf16[2,2,48,1664]{3,2,1,0:T(8,128)(2,1)}, bf16[2,2,48,1664]{3,2,1,0:T(8,128)(2,1)}, u32[]{:S(2)}, u32[]{:S(2)}) %collective-permute-start.52) | collective-permute-done | bytes 639008 | tf_op jit(solution)/shard_map/ppermute | solution.py:56
  571.7 5.5 collective-permute-done.53
  581.9 2.0 fusion.23
  585.0 3.1 slice_bitcast_fusion
  588.7 2.9 collective-permute-start.63
  591.6 2.6 fusion.30
  594.5 2.2 fusion.29
  597.0 3.2 collective-permute-done.63
  603.4 7.8 %reduce-scatter.11.cloned.1.call-done = bf16[1,48,1664]{2,1,0:T(8,128)(2,1)} async-done(((bf16[4,48,1664]{2,1,0:T(8,128)(2,1)}), bf16[1,48,1664]{2,1,0:T(8,128)(2,1)}) %reduce-scatter.11.cloned.1.call-update) | async-done | bytes 159760 | tf_op jit(solution)/shard_map/reduce_scatter | solution.py:765
  614.7 2.6 collective-permute-done.57
  618.1 1.9 bitcast_add_fusion.3
  (352 shorter events, 131.5 us)
Async XLA Ops:
  7.2 75.2 %all-gather.8.cloned.1.call-start = ((), (), s32[]{:S(2)}) async-start(), calls=%async_computation.8 | async-start | bytes 1327104 | tf_op jit(solution)/shard_map/all_gather | solution.py:823
  9.2 230.3 %all-gather.10.cloned.1.call-start = ((), (), s32[]{:S(2)}) async-start(), calls=%async_computation.9 | async-start | bytes 15925248 | tf_op jit(solution)/shard_map/all_gather | solution.py:828
  21.8 280.2 %all-gather.12.cloned.1.call-start = ((), (), s32[]{:S(2)}) async-start(), calls=%async_computation.10 | async-start | bytes 15925248 | tf_op jit(solution)/shard_map/all_gather | solution.py:831
  47.6 384.5 %reduce-scatter.5.cloned.1.call-start = ((), (), s32[]{:S(2)}) async-start(), calls=%async_computation.4 | async-start | bytes 8847360 | tf_op jit(solution)/shard_map/reduce_scatter | solution.py:923
  47.6 19.8 %collective-permute-start = (bf16[4,48,2176]{2,1,0:T(8,128)(2,1)S(1)}, bf16[4,48,2176]{2,1,0:T(8,128)(2,1)}, u32[]{:S(2)}, u32[]{:S(2)}) collective-permute-start(bf16[4,48,2176]{2,1,0:T(8,128)(2,1)S(1)} %bitcast.251), channel_id=1, source_target_pairs={{0,8},{8,0},{16,24},{24,16},{1,9},{9,1},{17,25},{25,17},{2,10},{10... | collective-permute-start | bytes 2506760 | tf_op jit(solution)/shard_map/ppermute | solution.py:56
  49.1 20.9 %collective-permute-start.1 = (bf16[4,48,2176]{2,1,0:T(8,128)(2,1)S(1)}, bf16[4,48,2176]{2,1,0:T(8,128)(2,1)}, u32[]{:S(2)}, u32[]{:S(2)}) collective-permute-start(bf16[4,48,2176]{2,1,0:T(8,128)(2,1)S(1)} %bitcast.252), channel_id=1, source_target_pairs={{0,16},{8,24},{16,0},{24,8},{1,17},{9,25},{17,1},{25,9},{2,18},{10... | collective-permute-start | bytes 2506760 | tf_op jit(solution)/shard_map/ppermute | solution.py:56
  68.5 9.8 %collective-permute-start.2 = (bf16[2,48,2176]{2,1,0:T(8,128)(2,1)S(1)}, bf16[2,48,2176]{2,1,0:T(8,128)(2,1)S(1)}, u32[]{:S(2)}, u32[]{:S(2)}) collective-permute-start(bf16[2,48,2176]{2,1,0:T(8,128)(2,1)S(1)} %slice.329), channel_id=1, source_target_pairs={{0,16},{8,24},{16,0},{24,8},{1,17},{9,25},{17,1},{25,9},{2,18},{10... | collective-permute-start | bytes 1253384 | tf_op jit(solution)/shard_map/ppermute | solution.py:56
  71.1 9.6 %collective-permute-start.3 = (bf16[2,48,2176]{2,1,0:T(8,128)(2,1)S(1)}, bf16[2,48,2176]{2,1,0:T(8,128)(2,1)S(1)}, u32[]{:S(2)}, u32[]{:S(2)}) collective-permute-start(bf16[2,48,2176]{2,1,0:T(8,128)(2,1)S(1)} %slice.330), channel_id=1, source_target_pairs={{0,8},{8,0},{16,24},{24,16},{1,9},{9,1},{17,25},{25,17},{2,10},{10... | collective-permute-start | bytes 1253384 | tf_op jit(solution)/shard_map/ppermute | solution.py:56
  72.6 13.5 %collective-permute-start.4 = (bf16[4,48,2176]{2,1,0:T(8,128)(2,1)S(1)}, bf16[4,48,2176]{2,1,0:T(8,128)(2,1)}, u32[]{:S(2)}, u32[]{:S(2)}) collective-permute-start(bf16[4,48,2176]{2,1,0:T(8,128)(2,1)S(1)} %bitcast.253), channel_id=1, source_target_pairs={{0,4},{4,0},{1,5},{5,1},{2,6},{6,2},{3,7},{7,3},{8,12},{12,8},{9,1... | collective-permute-start | bytes 2506760 | tf_op jit(solution)/shard_map/ppermute | solution.py:60
  72.6 14.0 %collective-permute-start.5 = (bf16[4,48,2176]{2,1,0:T(8,128)(2,1)}, bf16[4,48,2176]{2,1,0:T(8,128)(2,1)}, u32[]{:S(2)}, u32[]{:S(2)}) collective-permute-start(bf16[4,48,2176]{2,1,0:T(8,128)(2,1)} %collective-permute-done.refs_1_), channel_id=1, source_target_pairs={{0,4},{4,0},{1,5},{5,1},{2,6},{6,2},{3,7},{7,3},{8,12},{12,8},{9,1... | collective-permute-start | bytes 2506760 | tf_op jit(solution)/shard_map/ppermute | solution.py:60
  73.1 13.5 %collective-permute-start.6 = (bf16[4,48,2176]{2,1,0:T(8,128)(2,1)}, bf16[4,48,2176]{2,1,0:T(8,128)(2,1)}, u32[]{:S(2)}, u32[]{:S(2)}) collective-permute-start(bf16[4,48,2176]{2,1,0:T(8,128)(2,1)} %collective-permute-done.1.refs_2_), channel_id=1, source_target_pairs={{0,4},{4,0},{1,5},{5,1},{2,6},{6,2},{3,7},{7,3},{8,12},{12,8},{9,1... | collective-permute-start | bytes 2506760 | tf_op jit(solution)/shard_map/ppermute | solution.py:60
  84.6 17.8 %collective-permute-start.8 = (bf16[4,48,1536]{2,1,0:T(8,128)(2,1)S(1)}, bf16[4,48,1536]{2,1,0:T(8,128)(2,1)}, u32[]{:S(2)}, u32[]{:S(2)}) collective-permute-start(bf16[4,48,1536]{2,1,0:T(8,128)(2,1)S(1)} %get-tuple-element.104.refs_0_), channel_id=1, source_target_pairs={{0,8},{8,0},{16,24},{24,16},{1,9},{9,1},{17,25},{25,17},{2,10},{10... | collective-permute-start | bytes 1769480 | tf_op jit(solution)/shard_map/ppermute | solution.py:56
  86.1 16.4 %collective-permute-start.9 = (bf16[4,48,1536]{2,1,0:T(8,128)(2,1)S(1)}, bf16[4,48,1536]{2,1,0:T(8,128)(2,1)}, u32[]{:S(2)}, u32[]{:S(2)}) collective-permute-start(bf16[4,48,1536]{2,1,0:T(8,128)(2,1)S(1)} %get-tuple-element.104.refs_0_), channel_id=1, source_target_pairs={{0,16},{8,24},{16,0},{24,8},{1,17},{9,25},{17,1},{25,9},{2,18},{10... | collective-permute-start | bytes 1769480 | tf_op jit(solution)/shard_map/ppermute | solution.py:56
  103.5 8.9 %collective-permute-start.11 = (bf16[2,48,1536]{2,1,0:T(8,128)(2,1)S(1)}, bf16[2,48,1536]{2,1,0:T(8,128)(2,1)S(1)}, u32[]{:S(2)}, u32[]{:S(2)}) collective-permute-start(bf16[2,48,1536]{2,1,0:T(8,128)(2,1)S(1)} %slice.258), channel_id=1, source_target_pairs={{0,16},{8,24},{16,0},{24,8},{1,17},{9,25},{17,1},{25,9},{2,18},{10... | collective-permute-start | bytes 884744 | tf_op jit(solution)/shard_map/ppermute | solution.py:56
  114.8 35.4 %collective-permute-start.13 = (bf16[512,1536]{1,0:T(8,128)(2,1)S(1)}, bf16[512,1536]{1,0:T(8,128)(2,1)}, u32[]{:S(2)}, u32[]{:S(2)}) collective-permute-start(bf16[512,1536]{1,0:T(8,128)(2,1)S(1)} %bitcast.242), channel_id=1, source_target_pairs={{0,8},{8,0},{16,24},{24,16},{1,9},{9,1},{17,25},{25,17},{2,10},{10... | collective-permute-start | bytes 4718600 | tf_op jit(solution)/shard_map/ppermute | solution.py:56
  115.4 35.0 %collective-permute-start.14 = (bf16[512,1536]{1,0:T(8,128)(2,1)S(1)}, bf16[512,1536]{1,0:T(8,128)(2,1)}, u32[]{:S(2)}, u32[]{:S(2)}) collective-permute-start(bf16[512,1536]{1,0:T(8,128)(2,1)S(1)} %bitcast.243), channel_id=1, source_target_pairs={{0,16},{8,24},{16,0},{24,8},{1,17},{9,25},{17,1},{25,9},{2,18},{10... | collective-permute-start | bytes 4718600 | tf_op jit(solution)/shard_map/ppermute | solution.py:56
  121.9 14.5 %collective-permute-start.15 = (bf16[4,48,1536]{2,1,0:T(8,128)(2,1)}, bf16[4,48,1536]{2,1,0:T(8,128)(2,1)S(1)}, u32[]{:S(2)}, u32[]{:S(2)}) collective-permute-start(bf16[4,48,1536]{2,1,0:T(8,128)(2,1)} %collective-permute-done.8.refs_1_), channel_id=1, source_target_pairs={{0,4},{4,0},{1,5},{5,1},{2,6},{6,2},{3,7},{7,3},{8,12},{12,8},{9,1... | collective-permute-start | bytes 1769480 | tf_op jit(solution)/shard_map/ppermute | solution.py:60
  121.9 14.4 %collective-permute-start.16 = (bf16[4,48,1536]{2,1,0:T(8,128)(2,1)}, bf16[4,48,1536]{2,1,0:T(8,128)(2,1)S(1)}, u32[]{:S(2)}, u32[]{:S(2)}) collective-permute-start(bf16[4,48,1536]{2,1,0:T(8,128)(2,1)} %collective-permute-done.9.refs_2_), channel_id=1, source_target_pairs={{0,4},{4,0},{1,5},{5,1},{2,6},{6,2},{3,7},{7,3},{8,12},{12,8},{9,1... | collective-permute-start | bytes 1769480 | tf_op jit(solution)/shard_map/ppermute | solution.py:60
  123.3 13.0 %collective-permute-start.17 = (bf16[4,48,1536]{2,1,0:T(8,128)(2,1)S(1)}, bf16[4,48,1536]{2,1,0:T(8,128)(2,1)}, u32[]{:S(2)}, u32[]{:S(2)}) collective-permute-start(bf16[4,48,1536]{2,1,0:T(8,128)(2,1)S(1)} %constant_dynamic-update-slice_fusion.2.refs_3_), channel_id=1, source_target_pairs={{0,4},{4,0},{1,5},{5,1},{2,6},{6,2},{3,7},{7,3},{8,12},{12,8},{9,1... | collective-permute-start | bytes 1769480 | tf_op jit(solution)/shard_map/ppermute | solution.py:60
  151.5 17.3 %collective-permute-start.18 = (bf16[256,1536]{1,0:T(8,128)(2,1)S(1)}, bf16[256,1536]{1,0:T(8,128)(2,1)S(1)}, u32[]{:S(2)}, u32[]{:S(2)}) collective-permute-start(bf16[256,1536]{1,0:T(8,128)(2,1)S(1)} %slice.262), channel_id=1, source_target_pairs={{0,16},{8,24},{16,0},{24,8},{1,17},{9,25},{17,1},{25,9},{2,18},{10... | collective-permute-start | bytes 2359304 | tf_op jit(solution)/shard_map/ppermute | solution.py:56
  153.3 16.9 %collective-permute-start.19 = (bf16[256,1536]{1,0:T(8,128)(2,1)S(1)}, bf16[256,1536]{1,0:T(8,128)(2,1)S(1)}, u32[]{:S(2)}, u32[]{:S(2)}) collective-permute-start(bf16[256,1536]{1,0:T(8,128)(2,1)S(1)} %slice.263), channel_id=1, source_target_pairs={{0,8},{8,0},{16,24},{24,16},{1,9},{9,1},{17,25},{25,17},{2,10},{10... | collective-permute-start | bytes 2359304 | tf_op jit(solution)/shard_map/ppermute | solution.py:56
  171.2 35.3 %collective-permute-start.20 = (bf16[544,1536]{1,0:T(8,128)(2,1)}, bf16[544,1536]{1,0:T(8,128)(2,1)}, u32[]{:S(2)}, u32[]{:S(2)}) collective-permute-start(bf16[544,1536]{1,0:T(8,128)(2,1)} %pad_maximum_fusion.1.refs_0_), channel_id=1, source_target_pairs={{0,8},{8,0},{16,24},{24,16},{1,9},{9,1},{17,25},{25,17},{2,10},{10... | collective-permute-start | bytes 5013512 | tf_op jit(solution)/shard_map/ppermute | solution.py:56
  172.6 36.7 %collective-permute-start.21 = (bf16[544,1536]{1,0:T(8,128)(2,1)}, bf16[544,1536]{1,0:T(8,128)(2,1)}, u32[]{:S(2)}, u32[]{:S(2)}) collective-permute-start(bf16[544,1536]{1,0:T(8,128)(2,1)} %pad_maximum_fusion.1.refs_0_), channel_id=1, source_target_pairs={{0,16},{8,24},{16,0},{24,8},{1,17},{9,25},{17,1},{25,9},{2,18},{10... | collective-permute-start | bytes 5013512 | tf_op jit(solution)/shard_map/ppermute | solution.py:56
  174.2 53.7 %collective-permute-start.28 = (bf16[512,1536]{1,0:T(8,128)(2,1)S(1)}, bf16[512,1536]{1,0:T(8,128)(2,1)S(1)}, u32[]{:S(2)}, u32[]{:S(2)}) collective-permute-start(bf16[512,1536]{1,0:T(8,128)(2,1)S(1)} %bitcast.244), channel_id=1, source_target_pairs={{0,4},{4,0},{1,5},{5,1},{2,6},{6,2},{3,7},{7,3},{8,12},{12,8},{9,1... | collective-permute-start | bytes 4718600 | tf_op jit(solution)/shard_map/ppermute | solution.py:60
  174.2 55.0 %collective-permute-start.29 = (bf16[512,1536]{1,0:T(8,128)(2,1)}, bf16[512,1536]{1,0:T(8,128)(2,1)}, u32[]{:S(2)}, u32[]{:S(2)}) collective-permute-start(bf16[512,1536]{1,0:T(8,128)(2,1)} %collective-permute-done.13.refs_9_), channel_id=1, source_target_pairs={{0,4},{4,0},{1,5},{5,1},{2,6},{6,2},{3,7},{7,3},{8,12},{12,8},{9,1... | collective-permute-start | bytes 4718600 | tf_op jit(solution)/shard_map/ppermute | solution.py:60
  174.7 54.9 %collective-permute-start.30 = (bf16[512,1536]{1,0:T(8,128)(2,1)}, bf16[512,1536]{1,0:T(8,128)(2,1)}, u32[]{:S(2)}, u32[]{:S(2)}) collective-permute-start(bf16[512,1536]{1,0:T(8,128)(2,1)} %collective-permute-done.14.refs_10_), channel_id=1, source_target_pairs={{0,4},{4,0},{1,5},{5,1},{2,6},{6,2},{3,7},{7,3},{8,12},{12,8},{9,1... | collective-permute-start | bytes 4718600 | tf_op jit(solution)/shard_map/ppermute | solution.py:60
  207.7 17.7 %collective-permute-start.22 = (bf16[272,1536]{1,0:T(8,128)(2,1)S(1)}, bf16[272,1536]{1,0:T(8,128)(2,1)S(1)}, u32[]{:S(2)}, u32[]{:S(2)}) collective-permute-start(bf16[272,1536]{1,0:T(8,128)(2,1)S(1)} %slice.336), channel_id=1, source_target_pairs={{0,16},{8,24},{16,0},{24,8},{1,17},{9,25},{17,1},{25,9},{2,18},{10... | collective-permute-start | bytes 2506760 | tf_op jit(solution)/shard_map/ppermute | solution.py:56
  210.6 16.0 %collective-permute-start.23 = (bf16[272,1536]{1,0:T(8,128)(2,1)S(1)}, bf16[272,1536]{1,0:T(8,128)(2,1)S(1)}, u32[]{:S(2)}, u32[]{:S(2)}) collective-permute-start(bf16[272,1536]{1,0:T(8,128)(2,1)S(1)} %slice.337), channel_id=1, source_target_pairs={{0,8},{8,0},{16,24},{24,16},{1,9},{9,1},{17,25},{25,17},{2,10},{10... | collective-permute-start | bytes 2506760 | tf_op jit(solution)/shard_map/ppermute | solution.py:56
  225.5 13.9 %collective-permute-start.24 = (bf16[544,1536]{1,0:T(8,128)(2,1)}, bf16[544,1536]{1,0:T(8,128)(2,1)}, u32[]{:S(2)}, u32[]{:S(2)}) collective-permute-start(bf16[544,1536]{1,0:T(8,128)(2,1)} %pad_maximum_fusion.1.refs_0_), channel_id=1, source_target_pairs={{0,4},{4,0},{1,5},{5,1},{2,6},{6,2},{3,7},{7,3},{8,12},{12,8},{9,1... | collective-permute-start | bytes 5013512 | tf_op jit(solution)/shard_map/ppermute | solution.py:60
  226.6 12.8 %collective-permute-start.25 = (bf16[544,1536]{1,0:T(8,128)(2,1)}, bf16[544,1536]{1,0:T(8,128)(2,1)}, u32[]{:S(2)}, u32[]{:S(2)}) collective-permute-start(bf16[544,1536]{1,0:T(8,128)(2,1)} %collective-permute-done.20.refs_1_), channel_id=1, source_target_pairs={{0,4},{4,0},{1,5},{5,1},{2,6},{6,2},{3,7},{7,3},{8,12},{12,8},{9,1... | collective-permute-start | bytes 5013512 | tf_op jit(solution)/shard_map/ppermute | solution.py:60
  229.0 10.4 %collective-permute-start.26 = (bf16[544,1536]{1,0:T(8,128)(2,1)}, bf16[544,1536]{1,0:T(8,128)(2,1)}, u32[]{:S(2)}, u32[]{:S(2)}) collective-permute-start(bf16[544,1536]{1,0:T(8,128)(2,1)} %collective-permute-done.21.refs_2_), channel_id=1, source_target_pairs={{0,4},{4,0},{1,5},{5,1},{2,6},{6,2},{3,7},{7,3},{8,12},{12,8},{9,1... | collective-permute-start | bytes 5013512 | tf_op jit(solution)/shard_map/ppermute | solution.py:60
  229.2 10.2 %collective-permute-start.27 = (bf16[544,1536]{1,0:T(8,128)(2,1)}, bf16[544,1536]{1,0:T(8,128)(2,1)}, u32[]{:S(2)}, u32[]{:S(2)}) collective-permute-start(bf16[544,1536]{1,0:T(8,128)(2,1)} %constant_dynamic-update-slice_fusion.6.refs_3_), channel_id=1, source_target_pairs={{0,4},{4,0},{1,5},{5,1},{2,6},{6,2},{3,7},{7,3},{8,12},{12,8},{9,1... | collective-permute-start | bytes 5013512 | tf_op jit(solution)/shard_map/ppermute | solution.py:60
  229.6 9.8 %collective-permute-start.31 = (bf16[512,1536]{1,0:T(8,128)(2,1)}, bf16[512,1536]{1,0:T(8,128)(2,1)}, u32[]{:S(2)}, u32[]{:S(2)}) collective-permute-start(bf16[512,1536]{1,0:T(8,128)(2,1)} %constant_dynamic-update-slice_fusion.4.refs_11_), channel_id=1, source_target_pairs={{0,4},{4,0},{1,5},{5,1},{2,6},{6,2},{3,7},{7,3},{8,12},{12,8},{9,1... | collective-permute-start | bytes 4718600 | tf_op jit(solution)/shard_map/ppermute | solution.py:60
  295.8 260.7 %reduce-scatter.7.cloned.1.call-start = ((), (), s32[]{:S(2)}) async-start(), calls=%async_computation.5 | async-start | bytes 8847360 | tf_op jit(solution)/shard_map/reduce_scatter | solution.py:923
  359.4 53.6 %collective-permute-start.40 = (bf16[4,512,1536]{2,1,0:T(8,128)(2,1)}, bf16[4,512,1536]{2,1,0:T(8,128)(2,1)}, u32[]{:S(2)}, u32[]{:S(2)}) collective-permute-start(bf16[4,512,1536]{2,1,0:T(8,128)(2,1)} %get-tuple-element.143), channel_id=1, source_target_pairs={{0,4},{4,0},{1,5},{5,1},{2,6},{6,2},{3,7},{7,3},{8,12},{12,8},{9,1... | collective-permute-start | bytes 18874376 | tf_op jit(solution)/shard_map/ppermute | solution.py:60
  359.6 39.0 %collective-permute-start.36 = (bf16[2,272,1536]{2,1,0:T(8,128)(2,1)}, bf16[2,272,1536]{2,1,0:T(8,128)(2,1)}, u32[]{:S(2)}, u32[]{:S(2)}) collective-permute-start(bf16[2,272,1536]{2,1,0:T(8,128)(2,1)} %fold_half.5), channel_id=1, source_target_pairs={{0,16},{8,24},{16,0},{24,8},{1,17},{9,25},{17,1},{25,9},{2,18},{10... | collective-permute-start | bytes 5013512 | tf_op jit(solution)/shard_map/ppermute | solution.py:56
  361.1 38.8 %collective-permute-start.35 = (bf16[2,272,1536]{2,1,0:T(8,128)(2,1)}, bf16[2,272,1536]{2,1,0:T(8,128)(2,1)}, u32[]{:S(2)}, u32[]{:S(2)}) collective-permute-start(bf16[2,272,1536]{2,1,0:T(8,128)(2,1)} %fold_half.4), channel_id=1, source_target_pairs={{0,8},{8,0},{16,24},{24,16},{1,9},{9,1},{17,25},{25,17},{2,10},{10... | collective-permute-start | bytes 5013512 | tf_op jit(solution)/shard_map/ppermute | solution.py:56
  362.6 37.3 %collective-permute-start.38 = (bf16[2,272,1536]{2,1,0:T(8,128)(2,1)}, bf16[2,272,1536]{2,1,0:T(8,128)(2,1)}, u32[]{:S(2)}, u32[]{:S(2)}) collective-permute-start(bf16[2,272,1536]{2,1,0:T(8,128)(2,1)} %get-tuple-element.140), channel_id=1, source_target_pairs={{0,4},{4,0},{1,5},{5,1},{2,6},{6,2},{3,7},{7,3},{8,12},{12,8},{9,1... | collective-permute-start | bytes 5013512 | tf_op jit(solution)/shard_map/ppermute | solution.py:60
  362.6 44.2 %collective-permute-start.34 = (bf16[2,272,1536]{2,1,0:T(8,128)(2,1)}, bf16[2,272,1536]{2,1,0:T(8,128)(2,1)}, u32[]{:S(2)}, u32[]{:S(2)}) collective-permute-start(bf16[2,272,1536]{2,1,0:T(8,128)(2,1)} %get-tuple-element.133), channel_id=1, source_target_pairs={{0,4},{4,0},{1,5},{5,1},{2,6},{6,2},{3,7},{7,3},{8,12},{12,8},{9,1... | collective-permute-start | bytes 5013512 | tf_op jit(solution)/shard_map/ppermute | solution.py:60
  405.3 20.0 %collective-permute-start.39 = (bf16[272,1536]{1,0:T(8,128)(2,1)}, bf16[272,1536]{1,0:T(8,128)(2,1)}, u32[]{:S(2)}, u32[]{:S(2)}) collective-permute-start(bf16[272,1536]{1,0:T(8,128)(2,1)} %fusion.28), channel_id=1, source_target_pairs={{0,8},{8,0},{16,24},{24,16},{1,9},{9,1},{17,25},{25,17},{2,10},{10... | collective-permute-start | bytes 2506760 | tf_op jit(solution)/shard_map/ppermute | solution.py:56
  412.2 19.9 %collective-permute-start.37 = (bf16[272,1536]{1,0:T(8,128)(2,1)}, bf16[272,1536]{1,0:T(8,128)(2,1)}, u32[]{:S(2)}, u32[]{:S(2)}) collective-permute-start(bf16[272,1536]{1,0:T(8,128)(2,1)} %fusion.27), channel_id=1, source_target_pairs={{0,16},{8,24},{16,0},{24,8},{1,17},{9,25},{17,1},{25,9},{2,18},{10... | collective-permute-start | bytes 2506760 | tf_op jit(solution)/shard_map/ppermute | solution.py:56
  412.9 175.2 %reduce-scatter.9.cloned.1.call-start = ((), (), s32[]{:S(2)}) async-start(), calls=%async_computation.6 | async-start | bytes 983040 | tf_op jit(solution)/shard_map/reduce_scatter | solution.py:765
  434.1 43.1 %collective-permute-start.42 = (bf16[2,256,1536]{2,1,0:T(8,128)(2,1)}, bf16[2,256,1536]{2,1,0:T(8,128)(2,1)}, u32[]{:S(2)}, u32[]{:S(2)}) collective-permute-start(bf16[2,256,1536]{2,1,0:T(8,128)(2,1)} %get-tuple-element.157), channel_id=1, source_target_pairs={{0,8},{8,0},{16,24},{24,16},{1,9},{9,1},{17,25},{25,17},{2,10},{10... | collective-permute-start | bytes 4718600 | tf_op jit(solution)/shard_map/ppermute | solution.py:56
  434.6 42.6 %collective-permute-start.43 = (bf16[2,256,1536]{2,1,0:T(8,128)(2,1)}, bf16[2,256,1536]{2,1,0:T(8,128)(2,1)}, u32[]{:S(2)}, u32[]{:S(2)}) collective-permute-start(bf16[2,256,1536]{2,1,0:T(8,128)(2,1)} %get-tuple-element.158), channel_id=1, source_target_pairs={{0,16},{8,24},{16,0},{24,8},{1,17},{9,25},{17,1},{25,9},{2,18},{10... | collective-permute-start | bytes 4718600 | tf_op jit(solution)/shard_map/ppermute | solution.py:56
  477.2 14.4 %collective-permute-start.41 = (bf16[4,4,48,1536]{3,2,1,0:T(8,128)(2,1)}, bf16[4,4,48,1536]{3,2,1,0:T(8,128)(2,1)}, u32[]{:S(2)}, u32[]{:S(2)}) collective-permute-start(bf16[4,4,48,1536]{3,2,1,0:T(8,128)(2,1)} %dynamic-slice_bitcast_fusion.1), channel_id=1, source_target_pairs={{0,4},{4,0},{1,5},{5,1},{2,6},{6,2},{3,7},{7,3},{8,12},{12,8},{9,1... | collective-permute-start | bytes 7077896 | tf_op jit(solution)/shard_map/ppermute | solution.py:60
  500.1 37.5 %collective-permute-start.48 = (bf16[2,2,48,2048]{3,2,1,0:T(8,128)(2,1)}, bf16[2,2,48,2048]{3,2,1,0:T(8,128)(2,1)}, u32[]{:S(2)}, u32[]{:S(2)}) collective-permute-start(bf16[2,2,48,2048]{3,2,1,0:T(8,128)(2,1)} %get-tuple-element.160), channel_id=1, source_target_pairs={{0,8},{8,0},{16,24},{24,16},{1,9},{9,1},{17,25},{25,17},{2,10},{10... | collective-permute-start | bytes 2359304 | tf_op jit(solution)/shard_map/ppermute | solution.py:56
  501.8 35.8 %collective-permute-start.49 = (bf16[2,2,48,2048]{3,2,1,0:T(8,128)(2,1)}, bf16[2,2,48,2048]{3,2,1,0:T(8,128)(2,1)}, u32[]{:S(2)}, u32[]{:S(2)}) collective-permute-start(bf16[2,2,48,2048]{3,2,1,0:T(8,128)(2,1)} %get-tuple-element.161), channel_id=1, source_target_pairs={{0,16},{8,24},{16,0},{24,8},{1,17},{9,25},{17,1},{25,9},{2,18},{10... | collective-permute-start | bytes 2359304 | tf_op jit(solution)/shard_map/ppermute | solution.py:56
  505.8 29.1 %collective-permute-start.64 = (bf16[3,192,768]{2,1,0:T(8,128)(2,1)}, bf16[3,192,768]{2,1,0:T(8,128)(2,1)}, u32[]{:S(2)}, u32[]{:S(2)}) collective-permute-start(bf16[3,192,768]{2,1,0:T(8,128)(2,1)} %select_bitcast_fusion.1), channel_id=1, source_target_pairs={{0,4},{4,0},{1,5},{5,1},{2,6},{6,2},{3,7},{7,3},{8,12},{12,8},{9,1... | collective-permute-start | bytes 2654216 | tf_op jit(solution)/shard_map/ppermute | solution.py:60
  513.1 24.6 %collective-permute-start.46 = (bf16[4,4,48,1536]{3,2,1,0:T(8,128)(2,1)}, bf16[4,4,48,1536]{3,2,1,0:T(8,128)(2,1)}, u32[]{:S(2)}, u32[]{:S(2)}) collective-permute-start(bf16[4,4,48,1536]{3,2,1,0:T(8,128)(2,1)} %dynamic-slice_bitcast_fusion), channel_id=1, source_target_pairs={{0,4},{4,0},{1,5},{5,1},{2,6},{6,2},{3,7},{7,3},{8,12},{12,8},{9,1... | collective-permute-start | bytes 7077896 | tf_op jit(solution)/shard_map/ppermute | solution.py:60
  539.6 13.0 %collective-permute-start.50 = (bf16[2,48,2048]{2,1,0:T(8,128)(2,1)}, bf16[2,48,2048]{2,1,0:T(8,128)(2,1)}, u32[]{:S(2)}, u32[]{:S(2)}) collective-permute-start(bf16[2,48,2048]{2,1,0:T(8,128)(2,1)} %fusion.35), channel_id=1, source_target_pairs={{0,16},{8,24},{16,0},{24,8},{1,17},{9,25},{17,1},{25,9},{2,18},{10... | collective-permute-start | bytes 1179656 | tf_op jit(solution)/shard_map/ppermute | solution.py:56
  541.9 12.3 %collective-permute-start.51 = (bf16[2,48,2048]{2,1,0:T(8,128)(2,1)}, bf16[2,48,2048]{2,1,0:T(8,128)(2,1)}, u32[]{:S(2)}, u32[]{:S(2)}) collective-permute-start(bf16[2,48,2048]{2,1,0:T(8,128)(2,1)} %fusion.36), channel_id=1, source_target_pairs={{0,8},{8,0},{16,24},{24,16},{1,9},{9,1},{17,25},{25,17},{2,10},{10... | collective-permute-start | bytes 1179656 | tf_op jit(solution)/shard_map/ppermute | solution.py:56
  549.6 17.6 %collective-permute-start.52 = (bf16[2,2,48,1664]{3,2,1,0:T(8,128)(2,1)}, bf16[2,2,48,1664]{3,2,1,0:T(8,128)(2,1)}, u32[]{:S(2)}, u32[]{:S(2)}) collective-permute-start(bf16[2,2,48,1664]{3,2,1,0:T(8,128)(2,1)} %get-tuple-element.176), channel_id=1, source_target_pairs={{0,8},{8,0},{16,24},{24,16},{1,9},{9,1},{17,25},{25,17},{2,10},{10... | collective-permute-start | bytes 1916936 | tf_op jit(solution)/shard_map/ppermute | solution.py:56
  551.1 18.9 %collective-permute-start.54 = (bf16[2,2,48,1664]{3,2,1,0:T(8,128)(2,1)}, bf16[2,2,48,1664]{3,2,1,0:T(8,128)(2,1)}, u32[]{:S(2)}, u32[]{:S(2)}) collective-permute-start(bf16[2,2,48,1664]{3,2,1,0:T(8,128)(2,1)} %get-tuple-element.177), channel_id=1, source_target_pairs={{0,16},{8,24},{16,0},{24,8},{1,17},{9,25},{17,1},{25,9},{2,18},{10... | collective-permute-start | bytes 1916936 | tf_op jit(solution)/shard_map/ppermute | solution.py:56
  558.9 23.0 %collective-permute-start.65 = (bf16[3,192,768]{2,1,0:T(8,128)(2,1)}, bf16[3,192,768]{2,1,0:T(8,128)(2,1)}, u32[]{:S(2)}, u32[]{:S(2)}) collective-permute-start(bf16[3,192,768]{2,1,0:T(8,128)(2,1)} %select_bitcast_fusion), channel_id=1, source_target_pairs={{0,4},{4,0},{1,5},{5,1},{2,6},{6,2},{3,7},{7,3},{8,12},{12,8},{9,1... | collective-permute-start | bytes 2654216 | tf_op jit(solution)/shard_map/ppermute | solution.py:60
  558.9 52.3 %reduce-scatter.11.cloned.1.call-start = ((), (), s32[]{:S(2)}) async-start(), calls=%async_computation.7 | async-start | bytes 798720 | tf_op jit(solution)/shard_map/reduce_scatter | solution.py:765
  568.3 8.9 %collective-permute-start.53 = (bf16[2,48,1664]{2,1,0:T(8,128)(2,1)S(1)}, bf16[2,48,1664]{2,1,0:T(8,128)(2,1)S(1)}, u32[]{:S(2)}, u32[]{:S(2)}) collective-permute-start(bf16[2,48,1664]{2,1,0:T(8,128)(2,1)S(1)} %fusion.39), channel_id=1, source_target_pairs={{0,16},{8,24},{16,0},{24,8},{1,17},{9,25},{17,1},{25,9},{2,18},{10... | collective-permute-start | bytes 958472 | tf_op jit(solution)/shard_map/ppermute | solution.py:56
  571.1 8.7 %collective-permute-start.55 = (bf16[2,48,1664]{2,1,0:T(8,128)(2,1)S(1)}, bf16[2,48,1664]{2,1,0:T(8,128)(2,1)S(1)}, u32[]{:S(2)}, u32[]{:S(2)}) collective-permute-start(bf16[2,48,1664]{2,1,0:T(8,128)(2,1)S(1)} %fusion.40), channel_id=1, source_target_pairs={{0,8},{8,0},{16,24},{24,16},{1,9},{9,1},{17,25},{25,17},{2,10},{10... | collective-permute-start | bytes 958472 | tf_op jit(solution)/shard_map/ppermute | solution.py:56
  588.1 8.9 %collective-permute-start.61 = (bf16[48,2048]{1,0:T(8,128)(2,1)}, bf16[48,2048]{1,0:T(8,128)(2,1)S(1)}, u32[]{:S(2)}, u32[]{:S(2)}) collective-permute-start(bf16[48,2048]{1,0:T(8,128)(2,1)} %bitcast.260), channel_id=1, source_target_pairs={{0,8},{8,0},{16,24},{24,16},{1,9},{9,1},{17,25},{25,17},{2,10},{10... | collective-permute-start | bytes 589832 | tf_op jit(solution)/shard_map/ppermute | solution.py:56
  588.7 11.5 %collective-permute-start.63 = (bf16[48,2048]{1,0:T(8,128)(2,1)}, bf16[48,2048]{1,0:T(8,128)(2,1)}, u32[]{:S(2)}, u32[]{:S(2)}) collective-permute-start(bf16[48,2048]{1,0:T(8,128)(2,1)} %bitcast.262), channel_id=1, source_target_pairs={{0,24},{8,16},{16,8},{24,0},{1,25},{9,17},{17,9},{25,1},{2,26},{10... | collective-permute-start | bytes 589832 | tf_op jit(solution)/shard_map/ppermute | solution.py:56
  594.2 23.1 %collective-permute-start.57 = (bf16[256,1536]{1,0:T(8,128)(2,1)}, bf16[256,1536]{1,0:T(8,128)(2,1)}, u32[]{:S(2)}, u32[]{:S(2)}) collective-permute-start(bf16[256,1536]{1,0:T(8,128)(2,1)} %fusion.30), channel_id=1, source_target_pairs={{0,8},{8,0},{16,24},{24,16},{1,9},{9,1},{17,25},{25,17},{2,10},{10... | collective-permute-start | bytes 2359304 | tf_op jit(solution)/shard_map/ppermute | solution.py:56
  596.7 21.4 %collective-permute-start.56 = (bf16[256,1536]{1,0:T(8,128)(2,1)}, bf16[256,1536]{1,0:T(8,128)(2,1)}, u32[]{:S(2)}, u32[]{:S(2)}) collective-permute-start(bf16[256,1536]{1,0:T(8,128)(2,1)} %fusion.29), channel_id=1, source_target_pairs={{0,16},{8,24},{16,0},{24,8},{1,17},{9,25},{17,1},{25,9},{2,18},{10... | collective-permute-start | bytes 2359304 | tf_op jit(solution)/shard_map/ppermute | solution.py:56
  611.2 12.1 %collective-permute-start.58 = (bf16[48,1664]{1,0:T(8,128)(2,1)}, bf16[48,1664]{1,0:T(8,128)(2,1)S(1)}, u32[]{:S(2)}, u32[]{:S(2)}) collective-permute-start(bf16[48,1664]{1,0:T(8,128)(2,1)} %bitcast.265), channel_id=1, source_target_pairs={{0,8},{8,0},{16,24},{24,16},{1,9},{9,1},{17,25},{25,17},{2,10},{10... | collective-permute-start | bytes 479240 | tf_op jit(solution)/shard_map/ppermute | solution.py:56
  612.7 10.6 %collective-permute-start.59 = (bf16[48,1664]{1,0:T(8,128)(2,1)}, bf16[48,1664]{1,0:T(8,128)(2,1)S(1)}, u32[]{:S(2)}, u32[]{:S(2)}) collective-permute-start(bf16[48,1664]{1,0:T(8,128)(2,1)} %bitcast.266), channel_id=1, source_target_pairs={{0,16},{8,24},{16,0},{24,8},{1,17},{9,25},{17,1},{25,9},{2,18},{10... | collective-permute-start | bytes 479240 | tf_op jit(solution)/shard_map/ppermute | solution.py:56
  614.3 9.0 %collective-permute-start.60 = (bf16[48,1664]{1,0:T(8,128)(2,1)}, bf16[48,1664]{1,0:T(8,128)(2,1)S(1)}, u32[]{:S(2)}, u32[]{:S(2)}) collective-permute-start(bf16[48,1664]{1,0:T(8,128)(2,1)} %bitcast.267), channel_id=1, source_target_pairs={{0,24},{8,16},{16,8},{24,0},{1,25},{9,17},{17,9},{25,1},{2,26},{10... | collective-permute-start | bytes 479240 | tf_op jit(solution)/shard_map/ppermute | solution.py:56
  (71 other events, 1205.1 us)
Sparse Core Ops, SparseCore 0:
  10.2 31.4 all-gather.7
  43.9 128.0 all-gather.9
  174.1 127.8 all-gather.11
  304.1 121.7 reduce-scatter.4
  428.0 123.9 reduce-scatter.6
  559.0 21.6 reduce-scatter.8
  591.7 19.4 reduce-scatter.10

commit v5 on v4

--- a/solution.py
+++ b/solution.py
@@ -760,12 +760,22 @@
     return total
 
 
-def finish_dense(total, expert):
+def scatter_line(total):
+    z = lax.axis_size("dp")
+    me = lax.axis_index("dp")
+    share = lax.dynamic_index_in_dim(total, me, 0, keepdims=False).astype(f32)
+    for s in range(1, z):
+        sent = lax.dynamic_index_in_dim(total, lax.rem(me + s, z), 0, keepdims=False)
+        came = lax.ppermute(sent, "dp", [(i, (i + s) % z) for i in range(z)])
+        share = share + came.astype(f32)
+    return share.astype(bf16)
+
+
+def join_rows(share, expert):
     count = lax.axis_size("expert")
-    share = lax.psum_scatter(total, "dp", scatter_dimension=0, tiled=False)
     blocks = jnp.stack([share] + [flip(share, k) for k in range(1, count)])
     pieces = [lax.dynamic_index_in_dim(blocks, expert ^ e, 0, keepdims=False) for e in range(count)]
-    return jnp.concatenate(pieces, axis=0).astype(f32), share
+    return jnp.concatenate(pieces, axis=0).astype(f32)
 
 
 def local(
@@ -916,7 +926,7 @@
         grads = weight_grads(x, gdy, hidden, dgate, dup, z, rows, False)
         (place,), grads = tie_lists((place + step,), grads)
         if final:
-            d_came, grads = tie_lists(d_came, grads)
+            d_came, grads, d_parts = tie_lists(d_came, grads, d_parts)
             d_last = scatter_second(d_parts, d_came)
             y_parts = block_parts(y_own, y_other)
             d_last, y_parts, shares[-1] = tie_lists(d_last, y_parts, shares[-1])
@@ -940,6 +950,7 @@
     )
     (far_grad,), y_came = tie_lists((far_grad,), y_came)
     came = lax.ppermute(far_grad, "context", [(1, 0)])
+    y_last = scatter_second(y_parts, y_came)
     grad_query = dot(act_one, dquery, ((0,), (0,))).astype(bf16)
     dkv = key_value_back(near_grad, came, cos_wide, sin_wide)
     grad_kv = dot(act_one, dkv, ((0,), (0,))).astype(bf16)
@@ -947,9 +958,11 @@
     first_parts = dense_parts(halves, context, expert)
     first_came = scatter_first(first_parts)
 
-    first_parts, (dquery, dkv, dlogits, dresid_b), shares[0] = tie_lists(
-        first_parts, (dquery, dkv, dlogits, dresid_b), shares[0]
+    first_parts, (dquery, dkv, dlogits, dresid_b), y_last, shares[0] = tie_lists(
+        first_parts, (dquery, dkv, dlogits, dresid_b), y_last, shares[0]
     )
+    y_sum = scatter_total(y_parts, y_came, y_last)
+    block_out = (resid_one + y_sum).astype(bf16)[None]
     out_halves = swap_halves(dot(mixed, dresid_b, ((0,), (0,))), context)
     dact_one = dot(dquery, qkv_w[:, :Q_WIDTH], ((1,), (1,)))
     dact_one = dact_one + dot(dkv, qkv_w[:, Q_WIDTH:], ((1,), (1,)))
@@ -975,16 +988,11 @@
     (first_total,), shares[-1], out_parts = tie_lists(
         (first_total.astype(bf16),), shares[-1], out_parts
     )
-    first, first_share = finish_dense(first_total, expert)
+    first_share = lax.psum_scatter(first_total, "dp", scatter_dimension=0, tiled=False)
     out_total = scatter_total(out_parts, out_came, scatter_second(out_parts, out_came))
-    (out_total, first_share, grad_in), y_came = tie_lists(
-        (out_total.astype(bf16), first_share, grad_in), y_came
-    )
-    last, out_share = finish_dense(out_total, expert)
-    y_last = scatter_second(y_parts, y_came)
-    y_last, (out_share,) = tie_lists(y_last, (out_share,))
-    y_sum = scatter_total(y_parts, y_came, y_last)
-    block_out = (resid_one + y_sum).astype(bf16)[None]
+    out_total, first_share = tie(out_total.astype(bf16), first_share)
+    first = join_rows(first_share, expert)
+    last = join_rows(scatter_line(out_total), expert)
     kv_at = Q_WIDTH + KV_WIDTH
 
     finals = []

time: 641 us -> 629 us (0.981)
  waiting for transfers between devices: 176 us -> 167 us
  other arithmetic: 61.4 us -> 53 us
  local copies, waits for them, and re-layouts: 51.6 us -> 58.8 us
    reduce_scatter x2 -> x1, waiting for transfers between devices: 7.81 us -> 0.01 us  [local(): lax.psum_scatter(first_total, 'dp', scatter_dimension=0, tiled=False)]
  transfers between devices with their start and end apart: 73 -> 75, of which waited for: 30 -> 27; matrix products, arithmetic and copies ran while one was open for 22% -> 21% of each run, Pallas kernels for 33% -> 33%
where the time goes in v5:
time: 629 us; the launch traced here: 622 us
  Pallas kernels  208 us (33%)
  waiting for transfers between devices  167 us (27%)
  local copies, waits for them, and re-layouts  58.8 us (9%)
  starting transfers between devices  56.1 us (9%)
  other arithmetic  53 us (8%)
  matrix products  40.1 us (6%)
  blocking collectives  23 us (4%)
  between operations  15.6 us (2%)
    ppermute x38, waiting for transfers between devices, flip(): return lax.ppermute(value, 'expert', [(i, i ^ step) for i in range(count)])  149 us
    pallas_call x2, Pallas kernels, run_expert(): pl.pallas_call(functools.partial(expert_kernel, count, tokens, capacity,...  89.1 us
    ppermute x38, starting transfers between devices, flip(): return lax.ppermute(value, 'expert', [(i, i ^ step) for i in range(count)])  41.1 us
    dot_general x12, matrix products, dot(): return lax.dot_general(a, b, (dims, ((), ())), preferred_element_type=f32)  40.1 us
    pallas_call x2, Pallas kernels, weight_grads(): pl.pallas_call(functools.partial(weight_grad_kernel, per), out_shape=shap...  29.6 us
    pallas_call x3, Pallas kernels, fold(): pl.pallas_call(functools.partial(fold_kernel, dense, len(pairs)), out_sha...  25.1 us
    pallas_call x1, Pallas kernels, attention_back(): pl.pallas_call(attend_back_kernel, out_shape=(jax.ShapeDtypeStruct((token...  23.8 us
    all_gather x1, blocking collectives, local(): first_z = lax.all_gather(first_pack, 'dp', axis=0, tiled=False)  23 us
  transfers between devices with their start and end apart: 75, of which 27 were waited for; matrix products, arithmetic and copies ran while one was open for 21% of the time, Pallas kernels for 33%

profile of v5, /device:TPU:0, one launch (start us, length us, event | category | flops | bytes accessed | tf_op | source)
XLA Modules:
  0.0 621.5 jit_solution(6894687961488394553)
XLA Ops:
  12.3 1.9 convert.47
  24.7 23.0 %all-gather = bf16[192,2176]{1,0:T(8,128)(2,1)S(1)} all-gather(bf16[48,2176]{1,0:T(8,128)(2,1)S(1)} %copy-done.36), channel_id=2, replica_groups=mesh['expert'=4,'context'=2,'dp'=4] {'dp'}, dimensions={0}, use_global_device_ids=true | all-gather | bytes 1044480 | tf_op jit(solution)/shard_map/all_gather | solution.py:836
  50.6 17.1 %collective-permute-done.refs_1_ = bf16[4,48,2176]{2,1,0:T(8,128)(2,1)} collective-permute-done((bf16[4,48,2176]{2,1,0:T(8,128)(2,1)S(1)}, bf16[4,48,2176]{2,1,0:T(8,128)(2,1)}, u32[]{:S(2)}, u32[]{:S(2)}) %collective-permute-start) | collective-permute-done | bytes 835616 | tf_op jit(solution)/shard_map/ppermute | solution.py:56
  73.4 5.5 collective-permute-done.2
  83.1 2.2 dynamic-slice_bitcast_fusion.3
  87.3 6.4 %assemble.2 = bf16[2,4,4,48,2176]{4,3,2,1,0:T(8,128)(2,1)} custom-call(s32[2]{0:T(128)} %pad_add_fusion.place, bf16[4,48,2176]{2,1,0:T(8,128)(2,1)} %bitcast.265, bf16[4,48,2176]{2,1,0:T(8,128)(2,1)} %collective-permute-done.refs_1_, bf16[4,48,2176]{2,1,0:T(8,128)(2,1)} %collective-permute-done.1.refs_2_, ...), custom_call_target="tpu_custom_call" | custom-call | bytes 13369344 | tf_op jit(solution)/shard_map/assemble/pallas_call | solution.py:115
  95.0 7.9 %fusion.x_ref.q_ref = f32[512,2048]{1,0:T(8,128)} fusion(bf16[1536,2176]{1,0:T(8,128)(2,1)} %bitcast.238, bf16[1,512,1536]{2,1,0:T(8,128)(2,1)S(1)} %copy-done.16, f32[1536]{0:T(1024)S(1)} %get-tuple-element.249, f32[512]{0:T(512)S(1)} %add_rsqrt_fusion.1), kind=kOutput, calls=%fused_computation.2 | convolution fusion | flops 3224371200 | bytes 12066816 | tf_op jit(solution)/shard_map/dot_general | solution.py:43
  107.2 5.8 collective-permute-done.11
  113.0 2.2 collective-permute-done.12
  118.5 2.4 key_value.1.ko_ref.vo_ref
  124.7 11.9 %attention.1 = (bf16[512,1536]{1,0:T(8,128)(2,1)}, bf16[512,1536]{1,0:T(8,128)(2,1)}, f32[12,1,512]{2,1,0:T(1,128)}) custom-call(s32[1]{0:T(128)} %bitcast.1.place, f32[512,2048]{1,0:T(8,128)} %fusion.x_ref.q_ref, bf16[512,512]{1,0:T(8,128)(2,1)} %key_value.1.ko_ref.vo_ref, bf16[512,512]{1,0:T(8,128)(2,1)} %key_value.1.ko_ref.vo_ref, ...), custom_call_target="tpu_custom_call" | custom-call | flops 3221225472 | bytes 7864320 | tf_op jit(solution)/shard_map/attention/pallas_call | solution.py:647
  137.6 5.3 assemble.3
  143.0 7.5 %collective-permute-done.13.refs_9_ = bf16[512,1536]{1,0:T(8,128)(2,1)} collective-permute-done((bf16[512,1536]{1,0:T(8,128)(2,1)S(1)}, bf16[512,1536]{1,0:T(8,128)(2,1)}, u32[]{:S(2)}, u32[]{:S(2)}) %collective-permute-start.13) | collective-permute-done | bytes 1572896 | tf_op jit(solution)/shard_map/ppermute | solution.py:56
  155.4 4.6 multiply_reduce_fusion.2
  163.7 5.6 collective-permute-done.18
  175.0 32.3 %collective-permute-done.20.refs_1_ = bf16[544,1536]{1,0:T(8,128)(2,1)} collective-permute-done((bf16[544,1536]{1,0:T(8,128)(2,1)}, bf16[544,1536]{1,0:T(8,128)(2,1)}, u32[]{:S(2)}, u32[]{:S(2)}) %collective-permute-start.20) | collective-permute-done | bytes 1671200 | tf_op jit(solution)/shard_map/ppermute | solution.py:56
  212.3 13.7 %collective-permute-done.22 = bf16[272,1536]{1,0:T(8,128)(2,1)S(1)} collective-permute-done((bf16[272,1536]{1,0:T(8,128)(2,1)S(1)}, bf16[272,1536]{1,0:T(8,128)(2,1)S(1)}, u32[]{:S(2)}, u32[]{:S(2)}) %collective-permute-start.22) | collective-permute-done | bytes 835616 | tf_op jit(solution)/shard_map/ppermute | solution.py:56
  230.8 9.2 %collective-permute-done.31.refs_15_ = bf16[512,1536]{1,0:T(8,128)(2,1)} collective-permute-done((bf16[512,1536]{1,0:T(8,128)(2,1)}, bf16[512,1536]{1,0:T(8,128)(2,1)}, u32[]{:S(2)}, u32[]{:S(2)}) %collective-permute-start.31) | collective-permute-done | bytes 1572896 | tf_op jit(solution)/shard_map/ppermute | solution.py:60
  240.0 41.6 %experts.2 = (bf16[4,512,1536]{2,1,0:T(8,128)(2,1)}, bf16[4,512,1536]{2,1,0:T(8,128)(2,1)}, bf16[4,544,1536]{2,1,0:T(8,128)(2,1)}, bf16[4,544,1536]{2,1,0:T(8,12...) custom-call(s32[2]{0:T(128)} %get-tuple-element.251.place, ...), custom_call_target="tpu_custom_call" | custom-call | flops 26172456960 | bytes 72744960 | tf_op jit(solution)/shard_map/experts/pallas_call | solution.py:451
  281.6 14.8 %weight_grads.2 = bf16[4,2,3,192,768]{4,3,2,1,0:T(8,128)(2,1)} custom-call(bf16[1280,1536]{1,0:T(8,128)(2,1)} %get-tuple-element.115.x_ref, bf16[1280,1536]{1,0:T(8,128)(2,1)} %get-tuple-element.116.gdy_ref, bf16[1280,768]{1,0:T(8,128)(2,1)} %get-tuple-element.117.h_ref, bf16[1280,768]{1,0:T(8,128)(2,1)} %get-tuple-element.118.dg_ref, ...), custom_call_target="tpu_custom_call" | custom-call | flops 9059696640 | bytes 20840448 | tf_op jit(solution)/shard_map/weight_grads/pallas_call | solution.py:520
  296.4 2.9 all-gather.12.cloned.1.call-done
  299.4 47.6 %experts.3 = (bf16[4,512,1536]{2,1,0:T(8,128)(2,1)}, bf16[4,512,1536]{2,1,0:T(8,128)(2,1)}, bf16[4,544,1536]{2,1,0:T(8,128)(2,1)}, bf16[2,272,1536]{2,1,0:T(8,12...) custom-call(s32[2]{0:T(128)} %get-tuple-element.120.place, ...), custom_call_target="tpu_custom_call" | custom-call | flops 26172456960 | bytes 72744960 | tf_op jit(solution)/shard_map/experts/pallas_call | solution.py:451
  347.5 3.4 collective-permute-done.34.came_ref
  350.9 2.9 fold_half.5
  353.8 3.0 fold_half.4
  360.5 14.8 %weight_grads.3 = bf16[4,2,3,192,768]{4,3,2,1,0:T(8,128)(2,1)} custom-call(bf16[1280,1536]{1,0:T(8,128)(2,1)} %get-tuple-element.133.x_ref, bf16[1280,1536]{1,0:T(8,128)(2,1)} %get-tuple-element.134.gdy_ref, bf16[1280,768]{1,0:T(8,128)(2,1)} %get-tuple-element.135.h_ref, bf16[1280,768]{1,0:T(8,128)(2,1)} %get-tuple-element.136.dg_ref, ...), custom_call_target="tpu_custom_call" | custom-call | flops 9059696640 | bytes 20840448 | tf_op jit(solution)/shard_map/weight_grads/pallas_call | solution.py:520
  375.3 2.9 fold_half.7
  378.2 2.9 fold_half.6
  381.1 15.4 %collective-permute-done.35 = bf16[2,272,1536]{2,1,0:T(8,128)(2,1)} collective-permute-done((bf16[2,272,1536]{2,1,0:T(8,128)(2,1)}, bf16[2,272,1536]{2,1,0:T(8,128)(2,1)}, u32[]{:S(2)}, u32[]{:S(2)}) %collective-permute-start.35) | collective-permute-done | bytes 1671200 | tf_op jit(solution)/shard_map/ppermute | solution.py:56
  397.8 2.5 fusion.29
  401.8 2.2 fusion.28
  405.2 10.4 %fold.3 = (bf16[2,256,1536]{2,1,0:T(8,128)(2,1)}, bf16[2,256,1536]{2,1,0:T(8,128)(2,1)}, bf16[2,256,1536]{2,1,0:T(8,128)(2,1)}, bf16[2,256,1536]{2,1,0:T(8,128)(2,1)}) custom-call(s32[2]{0:T(128)} %broadcast_3_place.2.place, bf16[4,512,1536]{2,1,0:T(8,128)(2,1)} %get-tuple-element.144.refs_0_, bf16[4,512,1536]{2,1,0:T(8,128)(2,1)} %collective-permute-done.40.refs_1_), custom_call_target="tpu_custom_call" | custom-call | flops 3145728 | bytes 18874368 | tf_op jit(solution)/shard_map/fold/pallas_call | solution.py:205
  415.6 4.7 collective-permute-done.39
  420.3 3.4 collective-permute-done.38
  423.8 2.1 bitcast_add_fusion.1
  430.4 2.8 multiply_reduce_fusion
  434.9 3.7 convolution_convert_fusion.3.dout_ref
  438.7 23.8 %attention_back.1 = (bf16[512,1536]{1,0:T(8,128)(2,1)}, f32[512,512]{1,0:T(8,128)}, bf16[512,512]{1,0:T(8,128)(2,1)}) custom-call(s32[1]{0:T(128)} %bitcast.1.place, bf16[512,1536]{1,0:T(8,128)(2,1)} %get-tuple-element.152.q_ref, bf16[512,1536]{1,0:T(8,128)(2,1)} %convolution_convert_fusion.3.dout_ref, bf16[512,512]{1,0:T(8,128)(2,1)} %key_value.1.ko_ref.vo_ref, ...), custom_call_target="tpu_custom_call" | custom-call | flops 8053063680 | bytes 6291456 | tf_op jit(solution)/shard_map/attention_back/pallas_call | solution.py:732
  462.5 4.7 convolution_convert_fusion.1
  471.5 2.2 fusion.31
  475.6 2.6 key_value_back.1
  478.2 2.6 convolution_convert_fusion.2
  483.1 2.2 fusion.30
  487.5 7.6 %fold.4 = (bf16[2,2,48,2048]{3,2,1,0:T(8,128)(2,1)}, bf16[2,2,48,2048]{3,2,1,0:T(8,128)(2,1)}, bf16[2,2,48,2048]{3,2,1,0:T(8,128)(2,1)}, bf16[2,2,48,2048]{3,2,1,0:T(8,128)(2,1)}) custom-call(s32[2]{0:T(128)} %pad_add_fusion.place, bf16[2,4,4,48,1536]{4,3,2,1,0:T(8,128)(2,1)} %bitcast.244, bf16[4,4,48,1536]{3,2,1,0:T(8,128)(2,1)} %collective-permute-done.43.refs_1_, ...), custom_call_target="tpu_custom_call" | custom-call | flops 1572864 | bytes 9437184 | tf_op jit(solution)/shard_map/fold/pallas_call | solution.py:205
  497.2 8.8 %collective-permute-done.46 = bf16[256,1536]{1,0:T(8,128)(2,1)} collective-permute-done((bf16[256,1536]{1,0:T(8,128)(2,1)}, bf16[256,1536]{1,0:T(8,128)(2,1)}, u32[]{:S(2)}, u32[]{:S(2)}) %collective-permute-start.46) | collective-permute-done | bytes 786464 | tf_op jit(solution)/shard_map/ppermute | solution.py:56
  506.0 2.4 select_bitcast_fusion.1
  511.1 2.7 fusion.21
  513.9 5.2 fusion.17
  520.5 2.9 convolution_convert_fusion
  523.6 2.0 copy-done.7
  530.4 3.9 fusion.16
  537.3 1.8 fusion.36
  539.8 1.9 fusion.37
  542.9 7.1 %fold.5 = (bf16[2,2,48,1664]{3,2,1,0:T(8,128)(2,1)}, bf16[2,2,48,1664]{3,2,1,0:T(8,128)(2,1)}, bf16[2,2,48,1664]{3,2,1,0:T(8,128)(2,1)}, bf16[2,2,48,1664]{3,2,1,0:T(8,128)(2,1)}) custom-call(s32[2]{0:T(128)} %pad_add_fusion.place, bf16[2,4,4,48,1536]{4,3,2,1,0:T(8,128)(2,1)} %bitcast.246, bf16[4,4,48,1536]{3,2,1,0:T(8,128)(2,1)} %copy-done.27, ...), custom_call_target="tpu_custom_call" | custom-call | flops 1277952 | bytes 7667712 | tf_op jit(solution)/shard_map/fold/pallas_call | solution.py:205
  555.6 2.5 select_bitcast_fusion
  558.1 8.6 %collective-permute-done.54 = bf16[2,2,48,1664]{3,2,1,0:T(8,128)(2,1)} collective-permute-done((bf16[2,2,48,1664]{3,2,1,0:T(8,128)(2,1)}, bf16[2,2,48,1664]{3,2,1,0:T(8,128)(2,1)}, u32[]{:S(2)}, u32[]{:S(2)}) %collective-permute-start.54) | collective-permute-done | bytes 639008 | tf_op jit(solution)/shard_map/ppermute | solution.py:56
  571.1 5.6 collective-permute-done.55
  580.5 3.3 maximum_convert_fusion
  585.3 1.9 collective-permute-start.59
  587.3 2.6 collective-permute-start.60
  589.9 6.2 slice_bitcast_fusion
  597.3 2.3 collective-permute-start.66
  601.0 3.0 collective-permute-done.64
  604.6 3.5 collective-permute-done.66
  (356 shorter events, 133.7 us)
Async XLA Ops:
  7.2 75.9 %all-gather.8.cloned.1.call-start = ((), (), s32[]{:S(2)}) async-start(), calls=%async_computation.6 | async-start | bytes 1327104 | tf_op jit(solution)/shard_map/all_gather | solution.py:833
  9.2 230.9 %all-gather.10.cloned.1.call-start = ((), (), s32[]{:S(2)}) async-start(), calls=%async_computation.7 | async-start | bytes 15925248 | tf_op jit(solution)/shard_map/all_gather | solution.py:838
  24.6 274.8 %all-gather.12.cloned.1.call-start = ((), (), s32[]{:S(2)}) async-start(), calls=%async_computation.8 | async-start | bytes 15925248 | tf_op jit(solution)/shard_map/all_gather | solution.py:841
  47.7 376.1 %reduce-scatter.4.cloned.1.call-start = ((), (), s32[]{:S(2)}) async-start(), calls=%async_computation.3 | async-start | bytes 8847360 | tf_op jit(solution)/shard_map/reduce_scatter | solution.py:933
  47.7 20.0 %collective-permute-start = (bf16[4,48,2176]{2,1,0:T(8,128)(2,1)S(1)}, bf16[4,48,2176]{2,1,0:T(8,128)(2,1)}, u32[]{:S(2)}, u32[]{:S(2)}) collective-permute-start(bf16[4,48,2176]{2,1,0:T(8,128)(2,1)S(1)} %bitcast.262), channel_id=1, source_target_pairs={{0,8},{8,0},{16,24},{24,16},{1,9},{9,1},{17,25},{25,17},{2,10},{10... | collective-permute-start | bytes 2506760 | tf_op jit(solution)/shard_map/ppermute | solution.py:56
  49.2 21.1 %collective-permute-start.1 = (bf16[4,48,2176]{2,1,0:T(8,128)(2,1)S(1)}, bf16[4,48,2176]{2,1,0:T(8,128)(2,1)}, u32[]{:S(2)}, u32[]{:S(2)}) collective-permute-start(bf16[4,48,2176]{2,1,0:T(8,128)(2,1)S(1)} %bitcast.263), channel_id=1, source_target_pairs={{0,16},{8,24},{16,0},{24,8},{1,17},{9,25},{17,1},{25,9},{2,18},{10... | collective-permute-start | bytes 2506760 | tf_op jit(solution)/shard_map/ppermute | solution.py:56
  68.8 10.1 %collective-permute-start.2 = (bf16[2,48,2176]{2,1,0:T(8,128)(2,1)S(1)}, bf16[2,48,2176]{2,1,0:T(8,128)(2,1)S(1)}, u32[]{:S(2)}, u32[]{:S(2)}) collective-permute-start(bf16[2,48,2176]{2,1,0:T(8,128)(2,1)S(1)} %slice.329), channel_id=1, source_target_pairs={{0,16},{8,24},{16,0},{24,8},{1,17},{9,25},{17,1},{25,9},{2,18},{10... | collective-permute-start | bytes 1253384 | tf_op jit(solution)/shard_map/ppermute | solution.py:56
  71.3 9.9 %collective-permute-start.3 = (bf16[2,48,2176]{2,1,0:T(8,128)(2,1)S(1)}, bf16[2,48,2176]{2,1,0:T(8,128)(2,1)S(1)}, u32[]{:S(2)}, u32[]{:S(2)}) collective-permute-start(bf16[2,48,2176]{2,1,0:T(8,128)(2,1)S(1)} %slice.330), channel_id=1, source_target_pairs={{0,8},{8,0},{16,24},{24,16},{1,9},{9,1},{17,25},{25,17},{2,10},{10... | collective-permute-start | bytes 1253384 | tf_op jit(solution)/shard_map/ppermute | solution.py:56
  72.9 13.8 %collective-permute-start.4 = (bf16[4,48,2176]{2,1,0:T(8,128)(2,1)S(1)}, bf16[4,48,2176]{2,1,0:T(8,128)(2,1)}, u32[]{:S(2)}, u32[]{:S(2)}) collective-permute-start(bf16[4,48,2176]{2,1,0:T(8,128)(2,1)S(1)} %bitcast.264), channel_id=1, source_target_pairs={{0,4},{4,0},{1,5},{5,1},{2,6},{6,2},{3,7},{7,3},{8,12},{12,8},{9,1... | collective-permute-start | bytes 2506760 | tf_op jit(solution)/shard_map/ppermute | solution.py:60
  72.9 14.4 %collective-permute-start.5 = (bf16[4,48,2176]{2,1,0:T(8,128)(2,1)}, bf16[4,48,2176]{2,1,0:T(8,128)(2,1)}, u32[]{:S(2)}, u32[]{:S(2)}) collective-permute-start(bf16[4,48,2176]{2,1,0:T(8,128)(2,1)} %collective-permute-done.refs_1_), channel_id=1, source_target_pairs={{0,4},{4,0},{1,5},{5,1},{2,6},{6,2},{3,7},{7,3},{8,12},{12,8},{9,1... | collective-permute-start | bytes 2506760 | tf_op jit(solution)/shard_map/ppermute | solution.py:60
  73.4 13.9 %collective-permute-start.6 = (bf16[4,48,2176]{2,1,0:T(8,128)(2,1)}, bf16[4,48,2176]{2,1,0:T(8,128)(2,1)}, u32[]{:S(2)}, u32[]{:S(2)}) collective-permute-start(bf16[4,48,2176]{2,1,0:T(8,128)(2,1)} %collective-permute-done.1.refs_2_), channel_id=1, source_target_pairs={{0,4},{4,0},{1,5},{5,1},{2,6},{6,2},{3,7},{7,3},{8,12},{12,8},{9,1... | collective-permute-start | bytes 2506760 | tf_op jit(solution)/shard_map/ppermute | solution.py:60
  85.2 17.7 %collective-permute-start.8 = (bf16[4,48,1536]{2,1,0:T(8,128)(2,1)S(1)}, bf16[4,48,1536]{2,1,0:T(8,128)(2,1)}, u32[]{:S(2)}, u32[]{:S(2)}) collective-permute-start(bf16[4,48,1536]{2,1,0:T(8,128)(2,1)S(1)} %get-tuple-element.104.refs_0_), channel_id=1, source_target_pairs={{0,8},{8,0},{16,24},{24,16},{1,9},{9,1},{17,25},{25,17},{2,10},{10... | collective-permute-start | bytes 1769480 | tf_op jit(solution)/shard_map/ppermute | solution.py:56
  86.7 16.2 %collective-permute-start.9 = (bf16[4,48,1536]{2,1,0:T(8,128)(2,1)S(1)}, bf16[4,48,1536]{2,1,0:T(8,128)(2,1)}, u32[]{:S(2)}, u32[]{:S(2)}) collective-permute-start(bf16[4,48,1536]{2,1,0:T(8,128)(2,1)S(1)} %get-tuple-element.104.refs_0_), channel_id=1, source_target_pairs={{0,16},{8,24},{16,0},{24,8},{1,17},{9,25},{17,1},{25,9},{2,18},{10... | collective-permute-start | bytes 1769480 | tf_op jit(solution)/shard_map/ppermute | solution.py:56
  104.0 8.9 %collective-permute-start.11 = (bf16[2,48,1536]{2,1,0:T(8,128)(2,1)S(1)}, bf16[2,48,1536]{2,1,0:T(8,128)(2,1)S(1)}, u32[]{:S(2)}, u32[]{:S(2)}) collective-permute-start(bf16[2,48,1536]{2,1,0:T(8,128)(2,1)S(1)} %slice.258), channel_id=1, source_target_pairs={{0,16},{8,24},{16,0},{24,8},{1,17},{9,25},{17,1},{25,9},{2,18},{10... | collective-permute-start | bytes 884744 | tf_op jit(solution)/shard_map/ppermute | solution.py:56
  115.2 35.3 %collective-permute-start.13 = (bf16[512,1536]{1,0:T(8,128)(2,1)S(1)}, bf16[512,1536]{1,0:T(8,128)(2,1)}, u32[]{:S(2)}, u32[]{:S(2)}) collective-permute-start(bf16[512,1536]{1,0:T(8,128)(2,1)S(1)} %bitcast.253), channel_id=1, source_target_pairs={{0,8},{8,0},{16,24},{24,16},{1,9},{9,1},{17,25},{25,17},{2,10},{10... | collective-permute-start | bytes 4718600 | tf_op jit(solution)/shard_map/ppermute | solution.py:56
  115.9 35.0 %collective-permute-start.14 = (bf16[512,1536]{1,0:T(8,128)(2,1)S(1)}, bf16[512,1536]{1,0:T(8,128)(2,1)}, u32[]{:S(2)}, u32[]{:S(2)}) collective-permute-start(bf16[512,1536]{1,0:T(8,128)(2,1)S(1)} %bitcast.254), channel_id=1, source_target_pairs={{0,16},{8,24},{16,0},{24,8},{1,17},{9,25},{17,1},{25,9},{2,18},{10... | collective-permute-start | bytes 4718600 | tf_op jit(solution)/shard_map/ppermute | solution.py:56
  122.4 14.2 %collective-permute-start.15 = (bf16[4,48,1536]{2,1,0:T(8,128)(2,1)}, bf16[4,48,1536]{2,1,0:T(8,128)(2,1)S(1)}, u32[]{:S(2)}, u32[]{:S(2)}) collective-permute-start(bf16[4,48,1536]{2,1,0:T(8,128)(2,1)} %collective-permute-done.8.refs_1_), channel_id=1, source_target_pairs={{0,4},{4,0},{1,5},{5,1},{2,6},{6,2},{3,7},{7,3},{8,12},{12,8},{9,1... | collective-permute-start | bytes 1769480 | tf_op jit(solution)/shard_map/ppermute | solution.py:60
  122.5 14.1 %collective-permute-start.16 = (bf16[4,48,1536]{2,1,0:T(8,128)(2,1)}, bf16[4,48,1536]{2,1,0:T(8,128)(2,1)S(1)}, u32[]{:S(2)}, u32[]{:S(2)}) collective-permute-start(bf16[4,48,1536]{2,1,0:T(8,128)(2,1)} %collective-permute-done.9.refs_2_), channel_id=1, source_target_pairs={{0,4},{4,0},{1,5},{5,1},{2,6},{6,2},{3,7},{7,3},{8,12},{12,8},{9,1... | collective-permute-start | bytes 1769480 | tf_op jit(solution)/shard_map/ppermute | solution.py:60
  123.9 12.8 %collective-permute-start.17 = (bf16[4,48,1536]{2,1,0:T(8,128)(2,1)S(1)}, bf16[4,48,1536]{2,1,0:T(8,128)(2,1)}, u32[]{:S(2)}, u32[]{:S(2)}) collective-permute-start(bf16[4,48,1536]{2,1,0:T(8,128)(2,1)S(1)} %constant_dynamic-update-slice_fusion.2.refs_3_), channel_id=1, source_target_pairs={{0,4},{4,0},{1,5},{5,1},{2,6},{6,2},{3,7},{7,3},{8,12},{12,8},{9,1... | collective-permute-start | bytes 1769480 | tf_op jit(solution)/shard_map/ppermute | solution.py:60
  152.1 17.2 %collective-permute-start.18 = (bf16[256,1536]{1,0:T(8,128)(2,1)S(1)}, bf16[256,1536]{1,0:T(8,128)(2,1)S(1)}, u32[]{:S(2)}, u32[]{:S(2)}) collective-permute-start(bf16[256,1536]{1,0:T(8,128)(2,1)S(1)} %slice.262), channel_id=1, source_target_pairs={{0,16},{8,24},{16,0},{24,8},{1,17},{9,25},{17,1},{25,9},{2,18},{10... | collective-permute-start | bytes 2359304 | tf_op jit(solution)/shard_map/ppermute | solution.py:56
  154.0 17.0 %collective-permute-start.19 = (bf16[256,1536]{1,0:T(8,128)(2,1)S(1)}, bf16[256,1536]{1,0:T(8,128)(2,1)S(1)}, u32[]{:S(2)}, u32[]{:S(2)}) collective-permute-start(bf16[256,1536]{1,0:T(8,128)(2,1)S(1)} %slice.263), channel_id=1, source_target_pairs={{0,8},{8,0},{16,24},{24,16},{1,9},{9,1},{17,25},{25,17},{2,10},{10... | collective-permute-start | bytes 2359304 | tf_op jit(solution)/shard_map/ppermute | solution.py:56
  172.0 35.4 %collective-permute-start.20 = (bf16[544,1536]{1,0:T(8,128)(2,1)}, bf16[544,1536]{1,0:T(8,128)(2,1)}, u32[]{:S(2)}, u32[]{:S(2)}) collective-permute-start(bf16[544,1536]{1,0:T(8,128)(2,1)} %pad_maximum_fusion.1.refs_0_), channel_id=1, source_target_pairs={{0,8},{8,0},{16,24},{24,16},{1,9},{9,1},{17,25},{25,17},{2,10},{10... | collective-permute-start | bytes 5013512 | tf_op jit(solution)/shard_map/ppermute | solution.py:56
  173.2 36.7 %collective-permute-start.21 = (bf16[544,1536]{1,0:T(8,128)(2,1)}, bf16[544,1536]{1,0:T(8,128)(2,1)}, u32[]{:S(2)}, u32[]{:S(2)}) collective-permute-start(bf16[544,1536]{1,0:T(8,128)(2,1)} %pad_maximum_fusion.1.refs_0_), channel_id=1, source_target_pairs={{0,16},{8,24},{16,0},{24,8},{1,17},{9,25},{17,1},{25,9},{2,18},{10... | collective-permute-start | bytes 5013512 | tf_op jit(solution)/shard_map/ppermute | solution.py:56
  174.5 54.0 %collective-permute-start.28 = (bf16[512,1536]{1,0:T(8,128)(2,1)S(1)}, bf16[512,1536]{1,0:T(8,128)(2,1)S(1)}, u32[]{:S(2)}, u32[]{:S(2)}) collective-permute-start(bf16[512,1536]{1,0:T(8,128)(2,1)S(1)} %bitcast.255), channel_id=1, source_target_pairs={{0,4},{4,0},{1,5},{5,1},{2,6},{6,2},{3,7},{7,3},{8,12},{12,8},{9,1... | collective-permute-start | bytes 4718600 | tf_op jit(solution)/shard_map/ppermute | solution.py:60
  174.5 55.2 %collective-permute-start.29 = (bf16[512,1536]{1,0:T(8,128)(2,1)}, bf16[512,1536]{1,0:T(8,128)(2,1)}, u32[]{:S(2)}, u32[]{:S(2)}) collective-permute-start(bf16[512,1536]{1,0:T(8,128)(2,1)} %collective-permute-done.13.refs_9_), channel_id=1, source_target_pairs={{0,4},{4,0},{1,5},{5,1},{2,6},{6,2},{3,7},{7,3},{8,12},{12,8},{9,1... | collective-permute-start | bytes 4718600 | tf_op jit(solution)/shard_map/ppermute | solution.py:60
  175.0 55.1 %collective-permute-start.30 = (bf16[512,1536]{1,0:T(8,128)(2,1)}, bf16[512,1536]{1,0:T(8,128)(2,1)}, u32[]{:S(2)}, u32[]{:S(2)}) collective-permute-start(bf16[512,1536]{1,0:T(8,128)(2,1)} %collective-permute-done.14.refs_10_), channel_id=1, source_target_pairs={{0,4},{4,0},{1,5},{5,1},{2,6},{6,2},{3,7},{7,3},{8,12},{12,8},{9,1... | collective-permute-start | bytes 4718600 | tf_op jit(solution)/shard_map/ppermute | solution.py:60
  208.6 17.5 %collective-permute-start.22 = (bf16[272,1536]{1,0:T(8,128)(2,1)S(1)}, bf16[272,1536]{1,0:T(8,128)(2,1)S(1)}, u32[]{:S(2)}, u32[]{:S(2)}) collective-permute-start(bf16[272,1536]{1,0:T(8,128)(2,1)S(1)} %slice.336), channel_id=1, source_target_pairs={{0,16},{8,24},{16,0},{24,8},{1,17},{9,25},{17,1},{25,9},{2,18},{10... | collective-permute-start | bytes 2506760 | tf_op jit(solution)/shard_map/ppermute | solution.py:56
  211.1 16.0 %collective-permute-start.23 = (bf16[272,1536]{1,0:T(8,128)(2,1)S(1)}, bf16[272,1536]{1,0:T(8,128)(2,1)S(1)}, u32[]{:S(2)}, u32[]{:S(2)}) collective-permute-start(bf16[272,1536]{1,0:T(8,128)(2,1)S(1)} %slice.337), channel_id=1, source_target_pairs={{0,8},{8,0},{16,24},{24,16},{1,9},{9,1},{17,25},{25,17},{2,10},{10... | collective-permute-start | bytes 2506760 | tf_op jit(solution)/shard_map/ppermute | solution.py:56
  226.1 13.9 %collective-permute-start.24 = (bf16[544,1536]{1,0:T(8,128)(2,1)}, bf16[544,1536]{1,0:T(8,128)(2,1)}, u32[]{:S(2)}, u32[]{:S(2)}) collective-permute-start(bf16[544,1536]{1,0:T(8,128)(2,1)} %pad_maximum_fusion.1.refs_0_), channel_id=1, source_target_pairs={{0,4},{4,0},{1,5},{5,1},{2,6},{6,2},{3,7},{7,3},{8,12},{12,8},{9,1... | collective-permute-start | bytes 5013512 | tf_op jit(solution)/shard_map/ppermute | solution.py:60
  227.0 13.0 %collective-permute-start.25 = (bf16[544,1536]{1,0:T(8,128)(2,1)}, bf16[544,1536]{1,0:T(8,128)(2,1)}, u32[]{:S(2)}, u32[]{:S(2)}) collective-permute-start(bf16[544,1536]{1,0:T(8,128)(2,1)} %collective-permute-done.20.refs_1_), channel_id=1, source_target_pairs={{0,4},{4,0},{1,5},{5,1},{2,6},{6,2},{3,7},{7,3},{8,12},{12,8},{9,1... | collective-permute-start | bytes 5013512 | tf_op jit(solution)/shard_map/ppermute | solution.py:60
  229.6 10.4 %collective-permute-start.26 = (bf16[544,1536]{1,0:T(8,128)(2,1)}, bf16[544,1536]{1,0:T(8,128)(2,1)}, u32[]{:S(2)}, u32[]{:S(2)}) collective-permute-start(bf16[544,1536]{1,0:T(8,128)(2,1)} %collective-permute-done.21.refs_2_), channel_id=1, source_target_pairs={{0,4},{4,0},{1,5},{5,1},{2,6},{6,2},{3,7},{7,3},{8,12},{12,8},{9,1... | collective-permute-start | bytes 5013512 | tf_op jit(solution)/shard_map/ppermute | solution.py:60
  229.7 10.3 %collective-permute-start.27 = (bf16[544,1536]{1,0:T(8,128)(2,1)}, bf16[544,1536]{1,0:T(8,128)(2,1)}, u32[]{:S(2)}, u32[]{:S(2)}) collective-permute-start(bf16[544,1536]{1,0:T(8,128)(2,1)} %constant_dynamic-update-slice_fusion.6.refs_3_), channel_id=1, source_target_pairs={{0,4},{4,0},{1,5},{5,1},{2,6},{6,2},{3,7},{7,3},{8,12},{12,8},{9,1... | collective-permute-start | bytes 5013512 | tf_op jit(solution)/shard_map/ppermute | solution.py:60
  230.2 9.8 %collective-permute-start.31 = (bf16[512,1536]{1,0:T(8,128)(2,1)}, bf16[512,1536]{1,0:T(8,128)(2,1)}, u32[]{:S(2)}, u32[]{:S(2)}) collective-permute-start(bf16[512,1536]{1,0:T(8,128)(2,1)} %constant_dynamic-update-slice_fusion.4.refs_11_), channel_id=1, source_target_pairs={{0,4},{4,0},{1,5},{5,1},{2,6},{6,2},{3,7},{7,3},{8,12},{12,8},{9,1... | collective-permute-start | bytes 4718600 | tf_op jit(solution)/shard_map/ppermute | solution.py:60
  296.4 259.2 %reduce-scatter.6.cloned.1.call-start = ((), (), s32[]{:S(2)}) async-start(), calls=%async_computation.4 | async-start | bytes 8847360 | tf_op jit(solution)/shard_map/reduce_scatter | solution.py:933
  356.8 47.9 %collective-permute-start.40 = (bf16[4,512,1536]{2,1,0:T(8,128)(2,1)}, bf16[4,512,1536]{2,1,0:T(8,128)(2,1)}, u32[]{:S(2)}, u32[]{:S(2)}) collective-permute-start(bf16[4,512,1536]{2,1,0:T(8,128)(2,1)} %get-tuple-element.145), channel_id=1, source_target_pairs={{0,4},{4,0},{1,5},{5,1},{2,6},{6,2},{3,7},{7,3},{8,12},{12,8},{9,1... | collective-permute-start | bytes 18874376 | tf_op jit(solution)/shard_map/ppermute | solution.py:60
  357.0 18.3 %collective-permute-start.37 = (bf16[2,272,1536]{2,1,0:T(8,128)(2,1)}, bf16[2,272,1536]{2,1,0:T(8,128)(2,1)}, u32[]{:S(2)}, u32[]{:S(2)}) collective-permute-start(bf16[2,272,1536]{2,1,0:T(8,128)(2,1)} %get-tuple-element.139), channel_id=1, source_target_pairs={{0,4},{4,0},{1,5},{5,1},{2,6},{6,2},{3,7},{7,3},{8,12},{12,8},{9,1... | collective-permute-start | bytes 5013512 | tf_op jit(solution)/shard_map/ppermute | solution.py:60
  357.3 20.9 %collective-permute-start.36 = (bf16[2,272,1536]{2,1,0:T(8,128)(2,1)}, bf16[2,272,1536]{2,1,0:T(8,128)(2,1)}, u32[]{:S(2)}, u32[]{:S(2)}) collective-permute-start(bf16[2,272,1536]{2,1,0:T(8,128)(2,1)} %get-tuple-element.138), channel_id=1, source_target_pairs={{0,4},{4,0},{1,5},{5,1},{2,6},{6,2},{3,7},{7,3},{8,12},{12,8},{9,1... | collective-permute-start | bytes 5013512 | tf_op jit(solution)/shard_map/ppermute | solution.py:60
  357.5 39.0 %collective-permute-start.35 = (bf16[2,272,1536]{2,1,0:T(8,128)(2,1)}, bf16[2,272,1536]{2,1,0:T(8,128)(2,1)}, u32[]{:S(2)}, u32[]{:S(2)}) collective-permute-start(bf16[2,272,1536]{2,1,0:T(8,128)(2,1)} %fold_half.5), channel_id=1, source_target_pairs={{0,16},{8,24},{16,0},{24,8},{1,17},{9,25},{17,1},{25,9},{2,18},{10... | collective-permute-start | bytes 5013512 | tf_op jit(solution)/shard_map/ppermute | solution.py:56
  359.0 38.8 %collective-permute-start.33 = (bf16[2,272,1536]{2,1,0:T(8,128)(2,1)}, bf16[2,272,1536]{2,1,0:T(8,128)(2,1)}, u32[]{:S(2)}, u32[]{:S(2)}) collective-permute-start(bf16[2,272,1536]{2,1,0:T(8,128)(2,1)} %fold_half.4), channel_id=1, source_target_pairs={{0,8},{8,0},{16,24},{24,16},{1,9},{9,1},{17,25},{25,17},{2,10},{10... | collective-permute-start | bytes 5013512 | tf_op jit(solution)/shard_map/ppermute | solution.py:56
  400.3 20.0 %collective-permute-start.39 = (bf16[272,1536]{1,0:T(8,128)(2,1)}, bf16[272,1536]{1,0:T(8,128)(2,1)}, u32[]{:S(2)}, u32[]{:S(2)}) collective-permute-start(bf16[272,1536]{1,0:T(8,128)(2,1)} %fusion.29), channel_id=1, source_target_pairs={{0,8},{8,0},{16,24},{24,16},{1,9},{9,1},{17,25},{25,17},{2,10},{10... | collective-permute-start | bytes 2506760 | tf_op jit(solution)/shard_map/ppermute | solution.py:56
  404.0 19.7 %collective-permute-start.38 = (bf16[272,1536]{1,0:T(8,128)(2,1)}, bf16[272,1536]{1,0:T(8,128)(2,1)}, u32[]{:S(2)}, u32[]{:S(2)}) collective-permute-start(bf16[272,1536]{1,0:T(8,128)(2,1)} %fusion.28), channel_id=1, source_target_pairs={{0,16},{8,24},{16,0},{24,8},{1,17},{9,25},{17,1},{25,9},{2,18},{10... | collective-permute-start | bytes 2506760 | tf_op jit(solution)/shard_map/ppermute | solution.py:56
  404.6 179.2 %reduce-scatter.8.cloned.1.call-start = ((), (), s32[]{:S(2)}) async-start(), calls=%async_computation.5 | async-start | bytes 983040 | tf_op jit(solution)/shard_map/reduce_scatter | solution.py:991
  427.9 42.3 %collective-permute-start.41 = (bf16[2,256,1536]{2,1,0:T(8,128)(2,1)}, bf16[2,256,1536]{2,1,0:T(8,128)(2,1)}, u32[]{:S(2)}, u32[]{:S(2)}) collective-permute-start(bf16[2,256,1536]{2,1,0:T(8,128)(2,1)} %get-tuple-element.157), channel_id=1, source_target_pairs={{0,8},{8,0},{16,24},{24,16},{1,9},{9,1},{17,25},{25,17},{2,10},{10... | collective-permute-start | bytes 4718600 | tf_op jit(solution)/shard_map/ppermute | solution.py:56
  428.9 41.3 %collective-permute-start.42 = (bf16[2,256,1536]{2,1,0:T(8,128)(2,1)}, bf16[2,256,1536]{2,1,0:T(8,128)(2,1)}, u32[]{:S(2)}, u32[]{:S(2)}) collective-permute-start(bf16[2,256,1536]{2,1,0:T(8,128)(2,1)} %get-tuple-element.158), channel_id=1, source_target_pairs={{0,16},{8,24},{16,0},{24,8},{1,17},{9,25},{17,1},{25,9},{2,18},{10... | collective-permute-start | bytes 4718600 | tf_op jit(solution)/shard_map/ppermute | solution.py:56
  470.2 17.3 %collective-permute-start.43 = (bf16[4,4,48,1536]{3,2,1,0:T(8,128)(2,1)}, bf16[4,4,48,1536]{3,2,1,0:T(8,128)(2,1)}, u32[]{:S(2)}, u32[]{:S(2)}) collective-permute-start(bf16[4,4,48,1536]{3,2,1,0:T(8,128)(2,1)} %dynamic-slice_bitcast_fusion.1), channel_id=1, source_target_pairs={{0,4},{4,0},{1,5},{5,1},{2,6},{6,2},{3,7},{7,3},{8,12},{12,8},{9,1... | collective-permute-start | bytes 7077896 | tf_op jit(solution)/shard_map/ppermute | solution.py:60
  473.7 23.4 %collective-permute-start.47 = (bf16[256,1536]{1,0:T(8,128)(2,1)}, bf16[256,1536]{1,0:T(8,128)(2,1)}, u32[]{:S(2)}, u32[]{:S(2)}) collective-permute-start(bf16[256,1536]{1,0:T(8,128)(2,1)} %fusion.31), channel_id=1, source_target_pairs={{0,8},{8,0},{16,24},{24,16},{1,9},{9,1},{17,25},{25,17},{2,10},{10... | collective-permute-start | bytes 2359304 | tf_op jit(solution)/shard_map/ppermute | solution.py:56
  485.3 20.7 %collective-permute-start.46 = (bf16[256,1536]{1,0:T(8,128)(2,1)}, bf16[256,1536]{1,0:T(8,128)(2,1)}, u32[]{:S(2)}, u32[]{:S(2)}) collective-permute-start(bf16[256,1536]{1,0:T(8,128)(2,1)} %fusion.30), channel_id=1, source_target_pairs={{0,16},{8,24},{16,0},{24,8},{1,17},{9,25},{17,1},{25,9},{2,18},{10... | collective-permute-start | bytes 2359304 | tf_op jit(solution)/shard_map/ppermute | solution.py:56
  495.1 40.8 %collective-permute-start.50 = (bf16[2,2,48,2048]{3,2,1,0:T(8,128)(2,1)}, bf16[2,2,48,2048]{3,2,1,0:T(8,128)(2,1)}, u32[]{:S(2)}, u32[]{:S(2)}) collective-permute-start(bf16[2,2,48,2048]{3,2,1,0:T(8,128)(2,1)} %get-tuple-element.163), channel_id=1, source_target_pairs={{0,8},{8,0},{16,24},{24,16},{1,9},{9,1},{17,25},{25,17},{2,10},{10... | collective-permute-start | bytes 2359304 | tf_op jit(solution)/shard_map/ppermute | solution.py:56
  496.4 39.5 %collective-permute-start.51 = (bf16[2,2,48,2048]{3,2,1,0:T(8,128)(2,1)}, bf16[2,2,48,2048]{3,2,1,0:T(8,128)(2,1)}, u32[]{:S(2)}, u32[]{:S(2)}) collective-permute-start(bf16[2,2,48,2048]{3,2,1,0:T(8,128)(2,1)} %get-tuple-element.164), channel_id=1, source_target_pairs={{0,16},{8,24},{16,0},{24,8},{1,17},{9,25},{17,1},{25,9},{2,18},{10... | collective-permute-start | bytes 2359304 | tf_op jit(solution)/shard_map/ppermute | solution.py:56
  508.4 26.0 %collective-permute-start.67 = (bf16[3,192,768]{2,1,0:T(8,128)(2,1)}, bf16[3,192,768]{2,1,0:T(8,128)(2,1)}, u32[]{:S(2)}, u32[]{:S(2)}) collective-permute-start(bf16[3,192,768]{2,1,0:T(8,128)(2,1)} %select_bitcast_fusion.1), channel_id=1, source_target_pairs={{0,4},{4,0},{1,5},{5,1},{2,6},{6,2},{3,7},{7,3},{8,12},{12,8},{9,1... | collective-permute-start | bytes 2654216 | tf_op jit(solution)/shard_map/ppermute | solution.py:60
  519.8 16.0 %collective-permute-start.49 = (bf16[4,4,48,128]{3,2,1,0:T(8,128)(2,1)S(1)}, bf16[4,4,48,128]{3,2,1,0:T(8,128)(2,1)S(1)}, u32[]{:S(2)}, u32[]{:S(2)}) collective-permute-start(bf16[4,4,48,128]{3,2,1,0:T(8,128)(2,1)S(1)} %dynamic-slice_bitcast_fusion.9), channel_id=1, source_target_pairs={{0,4},{4,0},{1,5},{5,1},{2,6},{6,2},{3,7},{7,3},{8,12},{12,8},{9,1... | collective-permute-start | bytes 589832 | tf_op jit(solution)/shard_map/ppermute | solution.py:60
  525.6 10.3 %collective-permute-start.48 = (bf16[4,4,48,1536]{3,2,1,0:T(8,128)(2,1)S(1)}, bf16[4,4,48,1536]{3,2,1,0:T(8,128)(2,1)S(1)}, u32[]{:S(2)}, u32[]{:S(2)}) collective-permute-start(bf16[4,4,48,1536]{3,2,1,0:T(8,128)(2,1)S(1)} %dynamic-slice_bitcast_fusion), channel_id=1, source_target_pairs={{0,4},{4,0},{1,5},{5,1},{2,6},{6,2},{3,7},{7,3},{8,12},{12,8},{9,1... | collective-permute-start | bytes 7077896 | tf_op jit(solution)/shard_map/ppermute | solution.py:60
  539.2 13.0 %collective-permute-start.52 = (bf16[2,48,2048]{2,1,0:T(8,128)(2,1)}, bf16[2,48,2048]{2,1,0:T(8,128)(2,1)}, u32[]{:S(2)}, u32[]{:S(2)}) collective-permute-start(bf16[2,48,2048]{2,1,0:T(8,128)(2,1)} %fusion.36), channel_id=1, source_target_pairs={{0,16},{8,24},{16,0},{24,8},{1,17},{9,25},{17,1},{25,9},{2,18},{10... | collective-permute-start | bytes 1179656 | tf_op jit(solution)/shard_map/ppermute | solution.py:56
  541.7 11.8 %collective-permute-start.53 = (bf16[2,48,2048]{2,1,0:T(8,128)(2,1)}, bf16[2,48,2048]{2,1,0:T(8,128)(2,1)S(1)}, u32[]{:S(2)}, u32[]{:S(2)}) collective-permute-start(bf16[2,48,2048]{2,1,0:T(8,128)(2,1)} %fusion.37), channel_id=1, source_target_pairs={{0,8},{8,0},{16,24},{24,16},{1,9},{9,1},{17,25},{25,17},{2,10},{10... | collective-permute-start | bytes 1179656 | tf_op jit(solution)/shard_map/ppermute | solution.py:56
  550.0 16.8 %collective-permute-start.54 = (bf16[2,2,48,1664]{3,2,1,0:T(8,128)(2,1)}, bf16[2,2,48,1664]{3,2,1,0:T(8,128)(2,1)}, u32[]{:S(2)}, u32[]{:S(2)}) collective-permute-start(bf16[2,2,48,1664]{3,2,1,0:T(8,128)(2,1)} %get-tuple-element.183), channel_id=1, source_target_pairs={{0,8},{8,0},{16,24},{24,16},{1,9},{9,1},{17,25},{25,17},{2,10},{10... | collective-permute-start | bytes 1916936 | tf_op jit(solution)/shard_map/ppermute | solution.py:56
  550.8 18.7 %collective-permute-start.56 = (bf16[2,2,48,1664]{3,2,1,0:T(8,128)(2,1)}, bf16[2,2,48,1664]{3,2,1,0:T(8,128)(2,1)}, u32[]{:S(2)}, u32[]{:S(2)}) collective-permute-start(bf16[2,2,48,1664]{3,2,1,0:T(8,128)(2,1)} %get-tuple-element.184), channel_id=1, source_target_pairs={{0,16},{8,24},{16,0},{24,8},{1,17},{9,25},{17,1},{25,9},{2,18},{10... | collective-permute-start | bytes 1916936 | tf_op jit(solution)/shard_map/ppermute | solution.py:56
  558.1 22.2 %collective-permute-start.68 = (bf16[3,192,768]{2,1,0:T(8,128)(2,1)}, bf16[3,192,768]{2,1,0:T(8,128)(2,1)S(1)}, u32[]{:S(2)}, u32[]{:S(2)}) collective-permute-start(bf16[3,192,768]{2,1,0:T(8,128)(2,1)} %select_bitcast_fusion), channel_id=1, source_target_pairs={{0,4},{4,0},{1,5},{5,1},{2,6},{6,2},{3,7},{7,3},{8,12},{12,8},{9,1... | collective-permute-start | bytes 2654216 | tf_op jit(solution)/shard_map/ppermute | solution.py:60
  567.9 8.8 %collective-permute-start.55 = (bf16[2,48,1664]{2,1,0:T(8,128)(2,1)S(1)}, bf16[2,48,1664]{2,1,0:T(8,128)(2,1)S(1)}, u32[]{:S(2)}, u32[]{:S(2)}) collective-permute-start(bf16[2,48,1664]{2,1,0:T(8,128)(2,1)S(1)} %fusion.40), channel_id=1, source_target_pairs={{0,16},{8,24},{16,0},{24,8},{1,17},{9,25},{17,1},{25,9},{2,18},{10... | collective-permute-start | bytes 958472 | tf_op jit(solution)/shard_map/ppermute | solution.py:56
  583.8 13.5 %collective-permute-start.58 = (bf16[48,1664]{1,0:T(8,128)(2,1)S(1)}, bf16[48,1664]{1,0:T(8,128)(2,1)S(1)}, u32[]{:S(2)}, u32[]{:S(2)}) collective-permute-start(bf16[48,1664]{1,0:T(8,128)(2,1)S(1)} %get-tuple-element.285), channel_id=1, source_target_pairs={{0,1},{1,2},{2,3},{3,0},{4,5},{5,6},{6,7},{7,4},{8,9},{9,10},{10,1... | collective-permute-start | bytes 479240 | tf_op jit(solution)/shard_map/ppermute | solution.py:769
  585.3 14.2 %collective-permute-start.59 = (bf16[48,1664]{1,0:T(8,128)(2,1)S(1)}, bf16[48,1664]{1,0:T(8,128)(2,1)S(1)}, u32[]{:S(2)}, u32[]{:S(2)}) collective-permute-start(bf16[48,1664]{1,0:T(8,128)(2,1)S(1)} %get-tuple-element.287), channel_id=1, source_target_pairs={{0,2},{1,3},{2,0},{3,1},{4,6},{5,7},{6,4},{7,5},{8,10},{9,11},{10,... | collective-permute-start | bytes 479240 | tf_op jit(solution)/shard_map/ppermute | solution.py:769
  587.3 12.3 %collective-permute-start.60 = (bf16[48,1664]{1,0:T(8,128)(2,1)S(1)}, bf16[48,1664]{1,0:T(8,128)(2,1)S(1)}, u32[]{:S(2)}, u32[]{:S(2)}) collective-permute-start(bf16[48,1664]{1,0:T(8,128)(2,1)S(1)} %get-tuple-element.286), channel_id=1, source_target_pairs={{0,3},{1,0},{2,1},{3,2},{4,7},{5,4},{6,5},{7,6},{8,11},{9,8},{10,9... | collective-permute-start | bytes 479240 | tf_op jit(solution)/shard_map/ppermute | solution.py:769
  597.3 10.7 %collective-permute-start.66 = (bf16[48,2048]{1,0:T(8,128)(2,1)S(1)}, bf16[48,2048]{1,0:T(8,128)(2,1)S(1)}, u32[]{:S(2)}, u32[]{:S(2)}) collective-permute-start(bf16[48,2048]{1,0:T(8,128)(2,1)S(1)} %bitcast.273), channel_id=1, source_target_pairs={{0,24},{8,16},{16,8},{24,0},{1,25},{9,17},{17,9},{25,1},{2,26},{10... | collective-permute-start | bytes 589832 | tf_op jit(solution)/shard_map/ppermute | solution.py:56
  599.7 10.6 %collective-permute-start.61 = (bf16[48,1664]{1,0:T(8,128)(2,1)S(1)}, bf16[48,1664]{1,0:T(8,128)(2,1)S(1)}, u32[]{:S(2)}, u32[]{:S(2)}) collective-permute-start(bf16[48,1664]{1,0:T(8,128)(2,1)S(1)} %fusion.44), channel_id=1, source_target_pairs={{0,8},{8,0},{16,24},{24,16},{1,9},{9,1},{17,25},{25,17},{2,10},{10... | collective-permute-start | bytes 479240 | tf_op jit(solution)/shard_map/ppermute | solution.py:56
  600.0 10.3 %collective-permute-start.62 = (bf16[48,1664]{1,0:T(8,128)(2,1)S(1)}, bf16[48,1664]{1,0:T(8,128)(2,1)S(1)}, u32[]{:S(2)}, u32[]{:S(2)}) collective-permute-start(bf16[48,1664]{1,0:T(8,128)(2,1)S(1)} %fusion.44), channel_id=1, source_target_pairs={{0,16},{8,24},{16,0},{24,8},{1,17},{9,25},{17,1},{25,9},{2,18},{10... | collective-permute-start | bytes 479240 | tf_op jit(solution)/shard_map/ppermute | solution.py:56
  (73 other events, 1241.0 us)
Sparse Core Ops, SparseCore 0:
  10.2 29.1 all-gather.7
  41.6 127.6 all-gather.9
  171.5 127.8 all-gather.11
  301.5 121.7 reduce-scatter.3
  425.4 123.9 reduce-scatter.5
  558.2 23.4 reduce-scatter.7

commit v6 on v5

--- a/solution.py
+++ b/solution.py
@@ -307,9 +307,9 @@
     acts, dys = refs[: 2 * count], refs[2 * count : 4 * count]
     w_ref, refs = refs[4 * count], refs[4 * count + 1 :]
     sums = 7 if apart else 4
-    earlier, refs = refs[: len(refs) - sums - 8], refs[len(refs) - sums - 8 :]
+    earlier, refs = refs[: len(refs) - sums - 10], refs[len(refs) - sums - 10 :]
     y_refs, d_refs = refs[:2], refs[2:sums]
-    x_ref, gdy_ref, h_ref, dg_ref, du_ref, abuf, dbuf, sems = refs[sums:]
+    x_ref, gdy_ref, h_ref, dg_ref, du_ref, abuf, dbuf, wbuf, sems, wsems = refs[sums:]
     step = pl.program_id(0)
     slot = lax.rem(step, 2)
 
@@ -320,9 +320,14 @@
             out.append(pltpu.make_async_copy(dys[s * count + k], dbuf.at[at, s], sems.at[at, 2 + s]))
         return out
 
+    def weight_copies():
+        return [
+            pltpu.make_async_copy(w_ref.at[:, place[1], i], wbuf.at[i], wsems.at[i]) for i in range(3)
+        ]
+
     @pl.when(step == 0)
     def _():
-        for c in copies(0, 0):
+        for c in copies(0, 0) + weight_copies():
             c.start()
 
     for k in range(1, count):
@@ -358,10 +363,12 @@
         x_ref[at, :] = dot(one, abuf[slot, s, :tokens, :]).astype(bf16)
         gdy_ref[at, :] = dot(one, dbuf[slot, s]).astype(bf16)
     gate_col = jnp.concatenate(gate_cols, axis=0)
-    wide = w_ref.shape[0] * w_ref.shape[3]
-    w_gate = w_ref[:, 0, 0].reshape(wide, FF)
-    w_up = w_ref[:, 0, 1].reshape(wide, FF)
-    w_down = w_ref[:, 0, 2].reshape(wide, FF)
+    @pl.when(step == 0)
+    def _():
+        for c in weight_copies():
+            c.wait()
+
+    w_gate, w_up, w_down = (wbuf[i].reshape(-1, FF) for i in range(3))
     x = x_ref[...]
     dy = gdy_ref[...]
     gate_h = dot(x, w_gate)
@@ -455,19 +462,15 @@
             num_scalar_prefetch=1,
             grid=(count,),
             in_specs=[pl.BlockSpec(memory_space=pl.ANY)] * (4 * count)
-            + [
-                pl.BlockSpec(
-                    (cz, 1, 3, local, FF),
-                    lambda i, place: (0, place[1], 0, 0, 0),
-                    pipeline_mode=pl.Buffered(1),
-                )
-            ]
+            + [pl.BlockSpec(memory_space=pl.ANY)]
             + (sums if earlier else []),
             out_specs=(*outs, *(pl.BlockSpec((slots, n), lambda i, place: (i, 0)) for n in widths)),
             scratch_shapes=[
                 pltpu.VMEM((2, 2, rows, MODEL_WIDTH), bf16),
                 pltpu.VMEM((2, 2, tokens, MODEL_WIDTH), bf16),
+                pltpu.VMEM((3, cz, local, FF), bf16),
                 pltpu.SemaphoreType.DMA((2, 4)),
+                pltpu.SemaphoreType.DMA((3,)),
             ],
         ),
         compiler_params=pltpu.CompilerParams(

time: 629 us -> 629 us (level)
  transfers between devices with their start and end apart: 75 -> 75, of which waited for: 27 -> 28; matrix products, arithmetic and copies ran while one was open for 21% -> 21% of each run, Pallas kernels for 33% -> 34%
where the time goes in v6:
time: 629 us; the launch traced here: 622 us
  Pallas kernels  210 us (33%)
  waiting for transfers between devices  164 us (26%)
  local copies, waits for them, and re-layouts  58.7 us (9%)
  starting transfers between devices  57 us (9%)
  other arithmetic  53 us (8%)
  matrix products  40.1 us (6%)
  blocking collectives  23 us (4%)
  between operations  15.6 us (2%)
    ppermute x38, waiting for transfers between devices, flip(): return lax.ppermute(value, 'expert', [(i, i ^ step) for i in range(count)])  148 us
    pallas_call x2, Pallas kernels, run_expert(): pl.pallas_call(functools.partial(expert_kernel, count, tokens, capacity,...  91.1 us
    ppermute x38, starting transfers between devices, flip(): return lax.ppermute(value, 'expert', [(i, i ^ step) for i in range(count)])  41.4 us
    dot_general x12, matrix products, dot(): return lax.dot_general(a, b, (dims, ((), ())), preferred_element_type=f32)  40.1 us
    pallas_call x2, Pallas kernels, weight_grads(): pl.pallas_call(functools.partial(weight_grad_kernel, per), out_shape=shap...  29.6 us
    pallas_call x3, Pallas kernels, fold(): pl.pallas_call(functools.partial(fold_kernel, dense, len(pairs)), out_sha...  25.1 us
    pallas_call x1, Pallas kernels, attention_back(): pl.pallas_call(attend_back_kernel, out_shape=(jax.ShapeDtypeStruct((token...  23.8 us
    all_gather x1, blocking collectives, local(): first_z = lax.all_gather(first_pack, 'dp', axis=0, tiled=False)  23 us
  transfers between devices with their start and end apart: 75, of which 28 were waited for; matrix products, arithmetic and copies ran while one was open for 21% of the time, Pallas kernels for 34%

profile of v6, /device:TPU:0, one launch (start us, length us, event | category | flops | bytes accessed | tf_op | source)
XLA Modules:
  0.0 621.5 jit_solution(15068990233298325329)
XLA Ops:
  12.3 1.9 convert.47
  24.7 23.0 %all-gather = bf16[192,2176]{1,0:T(8,128)(2,1)S(1)} all-gather(bf16[48,2176]{1,0:T(8,128)(2,1)S(1)} %copy-done.36), channel_id=2, replica_groups=mesh['expert'=4,'context'=2,'dp'=4] {'dp'}, dimensions={0}, use_global_device_ids=true | all-gather | bytes 1044480 | tf_op jit(solution)/shard_map/all_gather | solution.py:839
  50.6 17.1 %collective-permute-done.refs_1_ = bf16[4,48,2176]{2,1,0:T(8,128)(2,1)} collective-permute-done((bf16[4,48,2176]{2,1,0:T(8,128)(2,1)S(1)}, bf16[4,48,2176]{2,1,0:T(8,128)(2,1)}, u32[]{:S(2)}, u32[]{:S(2)}) %collective-permute-start) | collective-permute-done | bytes 835616 | tf_op jit(solution)/shard_map/ppermute | solution.py:56
  73.4 5.5 collective-permute-done.2
  83.1 2.2 dynamic-slice_bitcast_fusion.3
  87.3 6.4 %assemble.2 = bf16[2,4,4,48,2176]{4,3,2,1,0:T(8,128)(2,1)} custom-call(s32[2]{0:T(128)} %pad_add_fusion.place, bf16[4,48,2176]{2,1,0:T(8,128)(2,1)} %bitcast.265, bf16[4,48,2176]{2,1,0:T(8,128)(2,1)} %collective-permute-done.refs_1_, bf16[4,48,2176]{2,1,0:T(8,128)(2,1)} %collective-permute-done.1.refs_2_, ...), custom_call_target="tpu_custom_call" | custom-call | bytes 13369344 | tf_op jit(solution)/shard_map/assemble/pallas_call | solution.py:115
  95.0 7.9 %fusion.x_ref.q_ref = f32[512,2048]{1,0:T(8,128)} fusion(bf16[1536,2176]{1,0:T(8,128)(2,1)} %bitcast.238, bf16[1,512,1536]{2,1,0:T(8,128)(2,1)S(1)} %copy-done.16, f32[1536]{0:T(1024)S(1)} %get-tuple-element.249, f32[512]{0:T(512)S(1)} %add_rsqrt_fusion.1), kind=kOutput, calls=%fused_computation.2 | convolution fusion | flops 3224371200 | bytes 12066816 | tf_op jit(solution)/shard_map/dot_general | solution.py:43
  107.2 5.8 collective-permute-done.11
  113.0 2.2 collective-permute-done.12
  118.5 2.4 key_value.1.ko_ref.vo_ref
  124.7 11.9 %attention.1 = (bf16[512,1536]{1,0:T(8,128)(2,1)}, bf16[512,1536]{1,0:T(8,128)(2,1)}, f32[12,1,512]{2,1,0:T(1,128)}) custom-call(s32[1]{0:T(128)} %bitcast.1.place, f32[512,2048]{1,0:T(8,128)} %fusion.x_ref.q_ref, bf16[512,512]{1,0:T(8,128)(2,1)} %key_value.1.ko_ref.vo_ref, bf16[512,512]{1,0:T(8,128)(2,1)} %key_value.1.ko_ref.vo_ref, ...), custom_call_target="tpu_custom_call" | custom-call | flops 3221225472 | bytes 7864320 | tf_op jit(solution)/shard_map/attention/pallas_call | solution.py:650
  137.6 5.3 assemble.3
  143.0 7.5 %collective-permute-done.13.refs_9_ = bf16[512,1536]{1,0:T(8,128)(2,1)} collective-permute-done((bf16[512,1536]{1,0:T(8,128)(2,1)S(1)}, bf16[512,1536]{1,0:T(8,128)(2,1)}, u32[]{:S(2)}, u32[]{:S(2)}) %collective-permute-start.13) | collective-permute-done | bytes 1572896 | tf_op jit(solution)/shard_map/ppermute | solution.py:56
  155.4 4.6 multiply_reduce_fusion.2
  163.7 5.6 collective-permute-done.18
  175.0 32.3 %collective-permute-done.20.refs_1_ = bf16[544,1536]{1,0:T(8,128)(2,1)} collective-permute-done((bf16[544,1536]{1,0:T(8,128)(2,1)}, bf16[544,1536]{1,0:T(8,128)(2,1)}, u32[]{:S(2)}, u32[]{:S(2)}) %collective-permute-start.20) | collective-permute-done | bytes 1671200 | tf_op jit(solution)/shard_map/ppermute | solution.py:56
  212.3 13.7 %collective-permute-done.22 = bf16[272,1536]{1,0:T(8,128)(2,1)S(1)} collective-permute-done((bf16[272,1536]{1,0:T(8,128)(2,1)S(1)}, bf16[272,1536]{1,0:T(8,128)(2,1)S(1)}, u32[]{:S(2)}, u32[]{:S(2)}) %collective-permute-start.22) | collective-permute-done | bytes 835616 | tf_op jit(solution)/shard_map/ppermute | solution.py:56
  230.8 9.2 %collective-permute-done.31.refs_15_ = bf16[512,1536]{1,0:T(8,128)(2,1)} collective-permute-done((bf16[512,1536]{1,0:T(8,128)(2,1)}, bf16[512,1536]{1,0:T(8,128)(2,1)}, u32[]{:S(2)}, u32[]{:S(2)}) %collective-permute-start.31) | collective-permute-done | bytes 1572896 | tf_op jit(solution)/shard_map/ppermute | solution.py:60
  240.0 42.0 %experts.2 = (bf16[4,512,1536]{2,1,0:T(8,128)(2,1)}, bf16[4,512,1536]{2,1,0:T(8,128)(2,1)}, bf16[4,544,1536]{2,1,0:T(8,128)(2,1)}, bf16[4,544,1536]{2,1,0:T(8,12...) custom-call(s32[2]{0:T(128)} %get-tuple-element.251.place, ...), custom_call_target="tpu_custom_call" | custom-call | flops 26172456960 | bytes 72744960 | tf_op jit(solution)/shard_map/experts/pallas_call | solution.py:458
  282.0 14.7 %weight_grads.2 = bf16[4,2,3,192,768]{4,3,2,1,0:T(8,128)(2,1)} custom-call(bf16[1280,1536]{1,0:T(8,128)(2,1)} %get-tuple-element.115.x_ref, bf16[1280,1536]{1,0:T(8,128)(2,1)} %get-tuple-element.116.gdy_ref, bf16[1280,768]{1,0:T(8,128)(2,1)} %get-tuple-element.117.h_ref, bf16[1280,768]{1,0:T(8,128)(2,1)} %get-tuple-element.118.dg_ref, ...), custom_call_target="tpu_custom_call" | custom-call | flops 9059696640 | bytes 20840448 | tf_op jit(solution)/shard_map/weight_grads/pallas_call | solution.py:523
  296.8 2.5 all-gather.12.cloned.1.call-done
  299.4 49.1 %experts.3 = (bf16[4,512,1536]{2,1,0:T(8,128)(2,1)}, bf16[4,512,1536]{2,1,0:T(8,128)(2,1)}, bf16[4,544,1536]{2,1,0:T(8,128)(2,1)}, bf16[2,272,1536]{2,1,0:T(8,12...) custom-call(s32[2]{0:T(128)} %get-tuple-element.120.place, ...), custom_call_target="tpu_custom_call" | custom-call | flops 26172456960 | bytes 72744960 | tf_op jit(solution)/shard_map/experts/pallas_call | solution.py:458
  349.1 3.4 collective-permute-done.34.came_ref
  352.4 2.9 fold_half.5
  355.4 2.9 fold_half.4
  362.0 14.9 %weight_grads.3 = bf16[4,2,3,192,768]{4,3,2,1,0:T(8,128)(2,1)} custom-call(bf16[1280,1536]{1,0:T(8,128)(2,1)} %get-tuple-element.133.x_ref, bf16[1280,1536]{1,0:T(8,128)(2,1)} %get-tuple-element.134.gdy_ref, bf16[1280,768]{1,0:T(8,128)(2,1)} %get-tuple-element.135.h_ref, bf16[1280,768]{1,0:T(8,128)(2,1)} %get-tuple-element.136.dg_ref, ...), custom_call_target="tpu_custom_call" | custom-call | flops 9059696640 | bytes 20840448 | tf_op jit(solution)/shard_map/weight_grads/pallas_call | solution.py:523
  376.9 2.9 fold_half.7
  379.8 2.9 fold_half.6
  382.7 15.3 %collective-permute-done.35 = bf16[2,272,1536]{2,1,0:T(8,128)(2,1)} collective-permute-done((bf16[2,272,1536]{2,1,0:T(8,128)(2,1)}, bf16[2,272,1536]{2,1,0:T(8,128)(2,1)}, u32[]{:S(2)}, u32[]{:S(2)}) %collective-permute-start.35) | collective-permute-done | bytes 1671200 | tf_op jit(solution)/shard_map/ppermute | solution.py:56
  399.2 2.5 fusion.29
  403.1 2.3 fusion.28
  406.5 10.4 %fold.3 = (bf16[2,256,1536]{2,1,0:T(8,128)(2,1)}, bf16[2,256,1536]{2,1,0:T(8,128)(2,1)}, bf16[2,256,1536]{2,1,0:T(8,128)(2,1)}, bf16[2,256,1536]{2,1,0:T(8,128)(2,1)}) custom-call(s32[2]{0:T(128)} %broadcast_3_place.2.place, bf16[4,512,1536]{2,1,0:T(8,128)(2,1)} %get-tuple-element.144.refs_0_, bf16[4,512,1536]{2,1,0:T(8,128)(2,1)} %collective-permute-done.40.refs_1_), custom_call_target="tpu_custom_call" | custom-call | flops 3145728 | bytes 18874368 | tf_op jit(solution)/shard_map/fold/pallas_call | solution.py:205
  416.9 4.6 collective-permute-done.39
  421.5 3.4 collective-permute-done.38
  425.0 2.1 bitcast_add_fusion.1
  430.4 2.8 multiply_reduce_fusion
  434.9 3.7 convolution_convert_fusion.3.dout_ref
  438.7 23.8 %attention_back.1 = (bf16[512,1536]{1,0:T(8,128)(2,1)}, f32[512,512]{1,0:T(8,128)}, bf16[512,512]{1,0:T(8,128)(2,1)}) custom-call(s32[1]{0:T(128)} %bitcast.1.place, bf16[512,1536]{1,0:T(8,128)(2,1)} %get-tuple-element.152.q_ref, bf16[512,1536]{1,0:T(8,128)(2,1)} %convolution_convert_fusion.3.dout_ref, bf16[512,512]{1,0:T(8,128)(2,1)} %key_value.1.ko_ref.vo_ref, ...), custom_call_target="tpu_custom_call" | custom-call | flops 8053063680 | bytes 6291456 | tf_op jit(solution)/shard_map/attention_back/pallas_call | solution.py:735
  462.5 4.6 convolution_convert_fusion.1
  471.5 2.2 fusion.31
  475.6 2.6 key_value_back.1
  478.2 2.6 convolution_convert_fusion.2
  483.1 2.2 fusion.30
  488.2 7.6 %fold.4 = (bf16[2,2,48,2048]{3,2,1,0:T(8,128)(2,1)}, bf16[2,2,48,2048]{3,2,1,0:T(8,128)(2,1)}, bf16[2,2,48,2048]{3,2,1,0:T(8,128)(2,1)}, bf16[2,2,48,2048]{3,2,1,0:T(8,128)(2,1)}) custom-call(s32[2]{0:T(128)} %pad_add_fusion.place, bf16[2,4,4,48,1536]{4,3,2,1,0:T(8,128)(2,1)} %bitcast.244, bf16[4,4,48,1536]{3,2,1,0:T(8,128)(2,1)} %collective-permute-done.43.refs_1_, ...), custom_call_target="tpu_custom_call" | custom-call | flops 1572864 | bytes 9437184 | tf_op jit(solution)/shard_map/fold/pallas_call | solution.py:205
  498.0 7.8 %collective-permute-done.46 = bf16[256,1536]{1,0:T(8,128)(2,1)} collective-permute-done((bf16[256,1536]{1,0:T(8,128)(2,1)}, bf16[256,1536]{1,0:T(8,128)(2,1)}, u32[]{:S(2)}, u32[]{:S(2)}) %collective-permute-start.46) | collective-permute-done | bytes 786464 | tf_op jit(solution)/shard_map/ppermute | solution.py:56
  505.7 2.4 select_bitcast_fusion.1
  511.5 2.7 fusion.21
  514.3 5.2 fusion.17
  520.9 2.9 convolution_convert_fusion
  524.0 2.0 copy-done.7
  530.6 3.9 fusion.16
  537.6 1.8 fusion.36
  540.8 1.8 fusion.37
  543.8 7.1 %fold.5 = (bf16[2,2,48,1664]{3,2,1,0:T(8,128)(2,1)}, bf16[2,2,48,1664]{3,2,1,0:T(8,128)(2,1)}, bf16[2,2,48,1664]{3,2,1,0:T(8,128)(2,1)}, bf16[2,2,48,1664]{3,2,1,0:T(8,128)(2,1)}) custom-call(s32[2]{0:T(128)} %pad_add_fusion.place, bf16[2,4,4,48,1536]{4,3,2,1,0:T(8,128)(2,1)} %bitcast.246, bf16[4,4,48,1536]{3,2,1,0:T(8,128)(2,1)} %copy-done.27, ...), custom_call_target="tpu_custom_call" | custom-call | flops 1277952 | bytes 7667712 | tf_op jit(solution)/shard_map/fold/pallas_call | solution.py:205
  556.0 2.5 select_bitcast_fusion
  558.6 9.0 %collective-permute-done.54 = bf16[2,2,48,1664]{3,2,1,0:T(8,128)(2,1)} collective-permute-done((bf16[2,2,48,1664]{3,2,1,0:T(8,128)(2,1)}, bf16[2,2,48,1664]{3,2,1,0:T(8,128)(2,1)}, u32[]{:S(2)}, u32[]{:S(2)}) %collective-permute-start.54) | collective-permute-done | bytes 639008 | tf_op jit(solution)/shard_map/ppermute | solution.py:56
  571.9 5.5 collective-permute-done.55
  580.4 3.3 maximum_convert_fusion
  585.3 2.0 collective-permute-start.59
  587.3 2.6 collective-permute-start.60
  589.9 6.2 slice_bitcast_fusion
  597.3 2.3 collective-permute-start.66
  600.9 3.0 collective-permute-done.64
  604.5 3.5 collective-permute-done.66
  (356 shorter events, 132.9 us)
Async XLA Ops:
  7.2 75.9 %all-gather.8.cloned.1.call-start = ((), (), s32[]{:S(2)}) async-start(), calls=%async_computation.6 | async-start | bytes 1327104 | tf_op jit(solution)/shard_map/all_gather | solution.py:836
  9.2 230.9 %all-gather.10.cloned.1.call-start = ((), (), s32[]{:S(2)}) async-start(), calls=%async_computation.7 | async-start | bytes 15925248 | tf_op jit(solution)/shard_map/all_gather | solution.py:841
  24.6 274.8 %all-gather.12.cloned.1.call-start = ((), (), s32[]{:S(2)}) async-start(), calls=%async_computation.8 | async-start | bytes 15925248 | tf_op jit(solution)/shard_map/all_gather | solution.py:844
  47.7 377.3 %reduce-scatter.4.cloned.1.call-start = ((), (), s32[]{:S(2)}) async-start(), calls=%async_computation.3 | async-start | bytes 8847360 | tf_op jit(solution)/shard_map/reduce_scatter | solution.py:936
  47.7 20.0 %collective-permute-start = (bf16[4,48,2176]{2,1,0:T(8,128)(2,1)S(1)}, bf16[4,48,2176]{2,1,0:T(8,128)(2,1)}, u32[]{:S(2)}, u32[]{:S(2)}) collective-permute-start(bf16[4,48,2176]{2,1,0:T(8,128)(2,1)S(1)} %bitcast.262), channel_id=1, source_target_pairs={{0,8},{8,0},{16,24},{24,16},{1,9},{9,1},{17,25},{25,17},{2,10},{10... | collective-permute-start | bytes 2506760 | tf_op jit(solution)/shard_map/ppermute | solution.py:56
  49.2 21.1 %collective-permute-start.1 = (bf16[4,48,2176]{2,1,0:T(8,128)(2,1)S(1)}, bf16[4,48,2176]{2,1,0:T(8,128)(2,1)}, u32[]{:S(2)}, u32[]{:S(2)}) collective-permute-start(bf16[4,48,2176]{2,1,0:T(8,128)(2,1)S(1)} %bitcast.263), channel_id=1, source_target_pairs={{0,16},{8,24},{16,0},{24,8},{1,17},{9,25},{17,1},{25,9},{2,18},{10... | collective-permute-start | bytes 2506760 | tf_op jit(solution)/shard_map/ppermute | solution.py:56
  68.8 10.1 %collective-permute-start.2 = (bf16[2,48,2176]{2,1,0:T(8,128)(2,1)S(1)}, bf16[2,48,2176]{2,1,0:T(8,128)(2,1)S(1)}, u32[]{:S(2)}, u32[]{:S(2)}) collective-permute-start(bf16[2,48,2176]{2,1,0:T(8,128)(2,1)S(1)} %slice.329), channel_id=1, source_target_pairs={{0,16},{8,24},{16,0},{24,8},{1,17},{9,25},{17,1},{25,9},{2,18},{10... | collective-permute-start | bytes 1253384 | tf_op jit(solution)/shard_map/ppermute | solution.py:56
  71.3 9.9 %collective-permute-start.3 = (bf16[2,48,2176]{2,1,0:T(8,128)(2,1)S(1)}, bf16[2,48,2176]{2,1,0:T(8,128)(2,1)S(1)}, u32[]{:S(2)}, u32[]{:S(2)}) collective-permute-start(bf16[2,48,2176]{2,1,0:T(8,128)(2,1)S(1)} %slice.330), channel_id=1, source_target_pairs={{0,8},{8,0},{16,24},{24,16},{1,9},{9,1},{17,25},{25,17},{2,10},{10... | collective-permute-start | bytes 1253384 | tf_op jit(solution)/shard_map/ppermute | solution.py:56
  72.9 13.8 %collective-permute-start.4 = (bf16[4,48,2176]{2,1,0:T(8,128)(2,1)S(1)}, bf16[4,48,2176]{2,1,0:T(8,128)(2,1)}, u32[]{:S(2)}, u32[]{:S(2)}) collective-permute-start(bf16[4,48,2176]{2,1,0:T(8,128)(2,1)S(1)} %bitcast.264), channel_id=1, source_target_pairs={{0,4},{4,0},{1,5},{5,1},{2,6},{6,2},{3,7},{7,3},{8,12},{12,8},{9,1... | collective-permute-start | bytes 2506760 | tf_op jit(solution)/shard_map/ppermute | solution.py:60
  72.9 14.4 %collective-permute-start.5 = (bf16[4,48,2176]{2,1,0:T(8,128)(2,1)}, bf16[4,48,2176]{2,1,0:T(8,128)(2,1)}, u32[]{:S(2)}, u32[]{:S(2)}) collective-permute-start(bf16[4,48,2176]{2,1,0:T(8,128)(2,1)} %collective-permute-done.refs_1_), channel_id=1, source_target_pairs={{0,4},{4,0},{1,5},{5,1},{2,6},{6,2},{3,7},{7,3},{8,12},{12,8},{9,1... | collective-permute-start | bytes 2506760 | tf_op jit(solution)/shard_map/ppermute | solution.py:60
  73.4 13.9 %collective-permute-start.6 = (bf16[4,48,2176]{2,1,0:T(8,128)(2,1)}, bf16[4,48,2176]{2,1,0:T(8,128)(2,1)}, u32[]{:S(2)}, u32[]{:S(2)}) collective-permute-start(bf16[4,48,2176]{2,1,0:T(8,128)(2,1)} %collective-permute-done.1.refs_2_), channel_id=1, source_target_pairs={{0,4},{4,0},{1,5},{5,1},{2,6},{6,2},{3,7},{7,3},{8,12},{12,8},{9,1... | collective-permute-start | bytes 2506760 | tf_op jit(solution)/shard_map/ppermute | solution.py:60
  85.2 17.7 %collective-permute-start.8 = (bf16[4,48,1536]{2,1,0:T(8,128)(2,1)S(1)}, bf16[4,48,1536]{2,1,0:T(8,128)(2,1)}, u32[]{:S(2)}, u32[]{:S(2)}) collective-permute-start(bf16[4,48,1536]{2,1,0:T(8,128)(2,1)S(1)} %get-tuple-element.104.refs_0_), channel_id=1, source_target_pairs={{0,8},{8,0},{16,24},{24,16},{1,9},{9,1},{17,25},{25,17},{2,10},{10... | collective-permute-start | bytes 1769480 | tf_op jit(solution)/shard_map/ppermute | solution.py:56
  86.7 16.2 %collective-permute-start.9 = (bf16[4,48,1536]{2,1,0:T(8,128)(2,1)S(1)}, bf16[4,48,1536]{2,1,0:T(8,128)(2,1)}, u32[]{:S(2)}, u32[]{:S(2)}) collective-permute-start(bf16[4,48,1536]{2,1,0:T(8,128)(2,1)S(1)} %get-tuple-element.104.refs_0_), channel_id=1, source_target_pairs={{0,16},{8,24},{16,0},{24,8},{1,17},{9,25},{17,1},{25,9},{2,18},{10... | collective-permute-start | bytes 1769480 | tf_op jit(solution)/shard_map/ppermute | solution.py:56
  104.0 8.9 %collective-permute-start.11 = (bf16[2,48,1536]{2,1,0:T(8,128)(2,1)S(1)}, bf16[2,48,1536]{2,1,0:T(8,128)(2,1)S(1)}, u32[]{:S(2)}, u32[]{:S(2)}) collective-permute-start(bf16[2,48,1536]{2,1,0:T(8,128)(2,1)S(1)} %slice.258), channel_id=1, source_target_pairs={{0,16},{8,24},{16,0},{24,8},{1,17},{9,25},{17,1},{25,9},{2,18},{10... | collective-permute-start | bytes 884744 | tf_op jit(solution)/shard_map/ppermute | solution.py:56
  115.2 35.3 %collective-permute-start.13 = (bf16[512,1536]{1,0:T(8,128)(2,1)S(1)}, bf16[512,1536]{1,0:T(8,128)(2,1)}, u32[]{:S(2)}, u32[]{:S(2)}) collective-permute-start(bf16[512,1536]{1,0:T(8,128)(2,1)S(1)} %bitcast.253), channel_id=1, source_target_pairs={{0,8},{8,0},{16,24},{24,16},{1,9},{9,1},{17,25},{25,17},{2,10},{10... | collective-permute-start | bytes 4718600 | tf_op jit(solution)/shard_map/ppermute | solution.py:56
  115.9 35.0 %collective-permute-start.14 = (bf16[512,1536]{1,0:T(8,128)(2,1)S(1)}, bf16[512,1536]{1,0:T(8,128)(2,1)}, u32[]{:S(2)}, u32[]{:S(2)}) collective-permute-start(bf16[512,1536]{1,0:T(8,128)(2,1)S(1)} %bitcast.254), channel_id=1, source_target_pairs={{0,16},{8,24},{16,0},{24,8},{1,17},{9,25},{17,1},{25,9},{2,18},{10... | collective-permute-start | bytes 4718600 | tf_op jit(solution)/shard_map/ppermute | solution.py:56
  122.4 14.2 %collective-permute-start.15 = (bf16[4,48,1536]{2,1,0:T(8,128)(2,1)}, bf16[4,48,1536]{2,1,0:T(8,128)(2,1)S(1)}, u32[]{:S(2)}, u32[]{:S(2)}) collective-permute-start(bf16[4,48,1536]{2,1,0:T(8,128)(2,1)} %collective-permute-done.8.refs_1_), channel_id=1, source_target_pairs={{0,4},{4,0},{1,5},{5,1},{2,6},{6,2},{3,7},{7,3},{8,12},{12,8},{9,1... | collective-permute-start | bytes 1769480 | tf_op jit(solution)/shard_map/ppermute | solution.py:60
  122.5 14.1 %collective-permute-start.16 = (bf16[4,48,1536]{2,1,0:T(8,128)(2,1)}, bf16[4,48,1536]{2,1,0:T(8,128)(2,1)S(1)}, u32[]{:S(2)}, u32[]{:S(2)}) collective-permute-start(bf16[4,48,1536]{2,1,0:T(8,128)(2,1)} %collective-permute-done.9.refs_2_), channel_id=1, source_target_pairs={{0,4},{4,0},{1,5},{5,1},{2,6},{6,2},{3,7},{7,3},{8,12},{12,8},{9,1... | collective-permute-start | bytes 1769480 | tf_op jit(solution)/shard_map/ppermute | solution.py:60
  123.9 12.8 %collective-permute-start.17 = (bf16[4,48,1536]{2,1,0:T(8,128)(2,1)S(1)}, bf16[4,48,1536]{2,1,0:T(8,128)(2,1)}, u32[]{:S(2)}, u32[]{:S(2)}) collective-permute-start(bf16[4,48,1536]{2,1,0:T(8,128)(2,1)S(1)} %constant_dynamic-update-slice_fusion.2.refs_3_), channel_id=1, source_target_pairs={{0,4},{4,0},{1,5},{5,1},{2,6},{6,2},{3,7},{7,3},{8,12},{12,8},{9,1... | collective-permute-start | bytes 1769480 | tf_op jit(solution)/shard_map/ppermute | solution.py:60
  152.1 17.2 %collective-permute-start.18 = (bf16[256,1536]{1,0:T(8,128)(2,1)S(1)}, bf16[256,1536]{1,0:T(8,128)(2,1)S(1)}, u32[]{:S(2)}, u32[]{:S(2)}) collective-permute-start(bf16[256,1536]{1,0:T(8,128)(2,1)S(1)} %slice.262), channel_id=1, source_target_pairs={{0,16},{8,24},{16,0},{24,8},{1,17},{9,25},{17,1},{25,9},{2,18},{10... | collective-permute-start | bytes 2359304 | tf_op jit(solution)/shard_map/ppermute | solution.py:56
  154.0 17.0 %collective-permute-start.19 = (bf16[256,1536]{1,0:T(8,128)(2,1)S(1)}, bf16[256,1536]{1,0:T(8,128)(2,1)S(1)}, u32[]{:S(2)}, u32[]{:S(2)}) collective-permute-start(bf16[256,1536]{1,0:T(8,128)(2,1)S(1)} %slice.263), channel_id=1, source_target_pairs={{0,8},{8,0},{16,24},{24,16},{1,9},{9,1},{17,25},{25,17},{2,10},{10... | collective-permute-start | bytes 2359304 | tf_op jit(solution)/shard_map/ppermute | solution.py:56
  172.0 35.4 %collective-permute-start.20 = (bf16[544,1536]{1,0:T(8,128)(2,1)}, bf16[544,1536]{1,0:T(8,128)(2,1)}, u32[]{:S(2)}, u32[]{:S(2)}) collective-permute-start(bf16[544,1536]{1,0:T(8,128)(2,1)} %pad_maximum_fusion.1.refs_0_), channel_id=1, source_target_pairs={{0,8},{8,0},{16,24},{24,16},{1,9},{9,1},{17,25},{25,17},{2,10},{10... | collective-permute-start | bytes 5013512 | tf_op jit(solution)/shard_map/ppermute | solution.py:56
  173.2 36.7 %collective-permute-start.21 = (bf16[544,1536]{1,0:T(8,128)(2,1)}, bf16[544,1536]{1,0:T(8,128)(2,1)}, u32[]{:S(2)}, u32[]{:S(2)}) collective-permute-start(bf16[544,1536]{1,0:T(8,128)(2,1)} %pad_maximum_fusion.1.refs_0_), channel_id=1, source_target_pairs={{0,16},{8,24},{16,0},{24,8},{1,17},{9,25},{17,1},{25,9},{2,18},{10... | collective-permute-start | bytes 5013512 | tf_op jit(solution)/shard_map/ppermute | solution.py:56
  174.5 54.0 %collective-permute-start.28 = (bf16[512,1536]{1,0:T(8,128)(2,1)S(1)}, bf16[512,1536]{1,0:T(8,128)(2,1)S(1)}, u32[]{:S(2)}, u32[]{:S(2)}) collective-permute-start(bf16[512,1536]{1,0:T(8,128)(2,1)S(1)} %bitcast.255), channel_id=1, source_target_pairs={{0,4},{4,0},{1,5},{5,1},{2,6},{6,2},{3,7},{7,3},{8,12},{12,8},{9,1... | collective-permute-start | bytes 4718600 | tf_op jit(solution)/shard_map/ppermute | solution.py:60
  174.5 55.2 %collective-permute-start.29 = (bf16[512,1536]{1,0:T(8,128)(2,1)}, bf16[512,1536]{1,0:T(8,128)(2,1)}, u32[]{:S(2)}, u32[]{:S(2)}) collective-permute-start(bf16[512,1536]{1,0:T(8,128)(2,1)} %collective-permute-done.13.refs_9_), channel_id=1, source_target_pairs={{0,4},{4,0},{1,5},{5,1},{2,6},{6,2},{3,7},{7,3},{8,12},{12,8},{9,1... | collective-permute-start | bytes 4718600 | tf_op jit(solution)/shard_map/ppermute | solution.py:60
  175.0 55.1 %collective-permute-start.30 = (bf16[512,1536]{1,0:T(8,128)(2,1)}, bf16[512,1536]{1,0:T(8,128)(2,1)}, u32[]{:S(2)}, u32[]{:S(2)}) collective-permute-start(bf16[512,1536]{1,0:T(8,128)(2,1)} %collective-permute-done.14.refs_10_), channel_id=1, source_target_pairs={{0,4},{4,0},{1,5},{5,1},{2,6},{6,2},{3,7},{7,3},{8,12},{12,8},{9,1... | collective-permute-start | bytes 4718600 | tf_op jit(solution)/shard_map/ppermute | solution.py:60
  208.6 17.5 %collective-permute-start.22 = (bf16[272,1536]{1,0:T(8,128)(2,1)S(1)}, bf16[272,1536]{1,0:T(8,128)(2,1)S(1)}, u32[]{:S(2)}, u32[]{:S(2)}) collective-permute-start(bf16[272,1536]{1,0:T(8,128)(2,1)S(1)} %slice.336), channel_id=1, source_target_pairs={{0,16},{8,24},{16,0},{24,8},{1,17},{9,25},{17,1},{25,9},{2,18},{10... | collective-permute-start | bytes 2506760 | tf_op jit(solution)/shard_map/ppermute | solution.py:56
  211.1 16.0 %collective-permute-start.23 = (bf16[272,1536]{1,0:T(8,128)(2,1)S(1)}, bf16[272,1536]{1,0:T(8,128)(2,1)S(1)}, u32[]{:S(2)}, u32[]{:S(2)}) collective-permute-start(bf16[272,1536]{1,0:T(8,128)(2,1)S(1)} %slice.337), channel_id=1, source_target_pairs={{0,8},{8,0},{16,24},{24,16},{1,9},{9,1},{17,25},{25,17},{2,10},{10... | collective-permute-start | bytes 2506760 | tf_op jit(solution)/shard_map/ppermute | solution.py:56
  226.1 13.9 %collective-permute-start.24 = (bf16[544,1536]{1,0:T(8,128)(2,1)}, bf16[544,1536]{1,0:T(8,128)(2,1)}, u32[]{:S(2)}, u32[]{:S(2)}) collective-permute-start(bf16[544,1536]{1,0:T(8,128)(2,1)} %pad_maximum_fusion.1.refs_0_), channel_id=1, source_target_pairs={{0,4},{4,0},{1,5},{5,1},{2,6},{6,2},{3,7},{7,3},{8,12},{12,8},{9,1... | collective-permute-start | bytes 5013512 | tf_op jit(solution)/shard_map/ppermute | solution.py:60
  227.0 13.0 %collective-permute-start.25 = (bf16[544,1536]{1,0:T(8,128)(2,1)}, bf16[544,1536]{1,0:T(8,128)(2,1)}, u32[]{:S(2)}, u32[]{:S(2)}) collective-permute-start(bf16[544,1536]{1,0:T(8,128)(2,1)} %collective-permute-done.20.refs_1_), channel_id=1, source_target_pairs={{0,4},{4,0},{1,5},{5,1},{2,6},{6,2},{3,7},{7,3},{8,12},{12,8},{9,1... | collective-permute-start | bytes 5013512 | tf_op jit(solution)/shard_map/ppermute | solution.py:60
  229.6 10.4 %collective-permute-start.26 = (bf16[544,1536]{1,0:T(8,128)(2,1)}, bf16[544,1536]{1,0:T(8,128)(2,1)}, u32[]{:S(2)}, u32[]{:S(2)}) collective-permute-start(bf16[544,1536]{1,0:T(8,128)(2,1)} %collective-permute-done.21.refs_2_), channel_id=1, source_target_pairs={{0,4},{4,0},{1,5},{5,1},{2,6},{6,2},{3,7},{7,3},{8,12},{12,8},{9,1... | collective-permute-start | bytes 5013512 | tf_op jit(solution)/shard_map/ppermute | solution.py:60
  229.7 10.3 %collective-permute-start.27 = (bf16[544,1536]{1,0:T(8,128)(2,1)}, bf16[544,1536]{1,0:T(8,128)(2,1)}, u32[]{:S(2)}, u32[]{:S(2)}) collective-permute-start(bf16[544,1536]{1,0:T(8,128)(2,1)} %constant_dynamic-update-slice_fusion.6.refs_3_), channel_id=1, source_target_pairs={{0,4},{4,0},{1,5},{5,1},{2,6},{6,2},{3,7},{7,3},{8,12},{12,8},{9,1... | collective-permute-start | bytes 5013512 | tf_op jit(solution)/shard_map/ppermute | solution.py:60
  230.2 9.8 %collective-permute-start.31 = (bf16[512,1536]{1,0:T(8,128)(2,1)}, bf16[512,1536]{1,0:T(8,128)(2,1)}, u32[]{:S(2)}, u32[]{:S(2)}) collective-permute-start(bf16[512,1536]{1,0:T(8,128)(2,1)} %constant_dynamic-update-slice_fusion.4.refs_11_), channel_id=1, source_target_pairs={{0,4},{4,0},{1,5},{5,1},{2,6},{6,2},{3,7},{7,3},{8,12},{12,8},{9,1... | collective-permute-start | bytes 4718600 | tf_op jit(solution)/shard_map/ppermute | solution.py:60
  296.8 259.2 %reduce-scatter.6.cloned.1.call-start = ((), (), s32[]{:S(2)}) async-start(), calls=%async_computation.4 | async-start | bytes 8847360 | tf_op jit(solution)/shard_map/reduce_scatter | solution.py:936
  358.3 47.7 %collective-permute-start.40 = (bf16[4,512,1536]{2,1,0:T(8,128)(2,1)}, bf16[4,512,1536]{2,1,0:T(8,128)(2,1)}, u32[]{:S(2)}, u32[]{:S(2)}) collective-permute-start(bf16[4,512,1536]{2,1,0:T(8,128)(2,1)} %get-tuple-element.145), channel_id=1, source_target_pairs={{0,4},{4,0},{1,5},{5,1},{2,6},{6,2},{3,7},{7,3},{8,12},{12,8},{9,1... | collective-permute-start | bytes 18874376 | tf_op jit(solution)/shard_map/ppermute | solution.py:60
  358.6 18.4 %collective-permute-start.37 = (bf16[2,272,1536]{2,1,0:T(8,128)(2,1)}, bf16[2,272,1536]{2,1,0:T(8,128)(2,1)}, u32[]{:S(2)}, u32[]{:S(2)}) collective-permute-start(bf16[2,272,1536]{2,1,0:T(8,128)(2,1)} %get-tuple-element.139), channel_id=1, source_target_pairs={{0,4},{4,0},{1,5},{5,1},{2,6},{6,2},{3,7},{7,3},{8,12},{12,8},{9,1... | collective-permute-start | bytes 5013512 | tf_op jit(solution)/shard_map/ppermute | solution.py:60
  358.8 21.1 %collective-permute-start.36 = (bf16[2,272,1536]{2,1,0:T(8,128)(2,1)}, bf16[2,272,1536]{2,1,0:T(8,128)(2,1)}, u32[]{:S(2)}, u32[]{:S(2)}) collective-permute-start(bf16[2,272,1536]{2,1,0:T(8,128)(2,1)} %get-tuple-element.138), channel_id=1, source_target_pairs={{0,4},{4,0},{1,5},{5,1},{2,6},{6,2},{3,7},{7,3},{8,12},{12,8},{9,1... | collective-permute-start | bytes 5013512 | tf_op jit(solution)/shard_map/ppermute | solution.py:60
  359.1 38.9 %collective-permute-start.35 = (bf16[2,272,1536]{2,1,0:T(8,128)(2,1)}, bf16[2,272,1536]{2,1,0:T(8,128)(2,1)}, u32[]{:S(2)}, u32[]{:S(2)}) collective-permute-start(bf16[2,272,1536]{2,1,0:T(8,128)(2,1)} %fold_half.5), channel_id=1, source_target_pairs={{0,16},{8,24},{16,0},{24,8},{1,17},{9,25},{17,1},{25,9},{2,18},{10... | collective-permute-start | bytes 5013512 | tf_op jit(solution)/shard_map/ppermute | solution.py:56
  360.5 38.6 %collective-permute-start.33 = (bf16[2,272,1536]{2,1,0:T(8,128)(2,1)}, bf16[2,272,1536]{2,1,0:T(8,128)(2,1)}, u32[]{:S(2)}, u32[]{:S(2)}) collective-permute-start(bf16[2,272,1536]{2,1,0:T(8,128)(2,1)} %fold_half.4), channel_id=1, source_target_pairs={{0,8},{8,0},{16,24},{24,16},{1,9},{9,1},{17,25},{25,17},{2,10},{10... | collective-permute-start | bytes 5013512 | tf_op jit(solution)/shard_map/ppermute | solution.py:56
  401.7 19.9 %collective-permute-start.39 = (bf16[272,1536]{1,0:T(8,128)(2,1)}, bf16[272,1536]{1,0:T(8,128)(2,1)}, u32[]{:S(2)}, u32[]{:S(2)}) collective-permute-start(bf16[272,1536]{1,0:T(8,128)(2,1)} %fusion.29), channel_id=1, source_target_pairs={{0,8},{8,0},{16,24},{24,16},{1,9},{9,1},{17,25},{25,17},{2,10},{10... | collective-permute-start | bytes 2506760 | tf_op jit(solution)/shard_map/ppermute | solution.py:56
  405.4 19.6 %collective-permute-start.38 = (bf16[272,1536]{1,0:T(8,128)(2,1)}, bf16[272,1536]{1,0:T(8,128)(2,1)}, u32[]{:S(2)}, u32[]{:S(2)}) collective-permute-start(bf16[272,1536]{1,0:T(8,128)(2,1)} %fusion.28), channel_id=1, source_target_pairs={{0,16},{8,24},{16,0},{24,8},{1,17},{9,25},{17,1},{25,9},{2,18},{10... | collective-permute-start | bytes 2506760 | tf_op jit(solution)/shard_map/ppermute | solution.py:56
  406.0 177.7 %reduce-scatter.8.cloned.1.call-start = ((), (), s32[]{:S(2)}) async-start(), calls=%async_computation.5 | async-start | bytes 983040 | tf_op jit(solution)/shard_map/reduce_scatter | solution.py:994
  429.1 41.1 %collective-permute-start.41 = (bf16[2,256,1536]{2,1,0:T(8,128)(2,1)}, bf16[2,256,1536]{2,1,0:T(8,128)(2,1)}, u32[]{:S(2)}, u32[]{:S(2)}) collective-permute-start(bf16[2,256,1536]{2,1,0:T(8,128)(2,1)} %get-tuple-element.157), channel_id=1, source_target_pairs={{0,8},{8,0},{16,24},{24,16},{1,9},{9,1},{17,25},{25,17},{2,10},{10... | collective-permute-start | bytes 4718600 | tf_op jit(solution)/shard_map/ppermute | solution.py:56
  429.7 40.5 %collective-permute-start.42 = (bf16[2,256,1536]{2,1,0:T(8,128)(2,1)}, bf16[2,256,1536]{2,1,0:T(8,128)(2,1)}, u32[]{:S(2)}, u32[]{:S(2)}) collective-permute-start(bf16[2,256,1536]{2,1,0:T(8,128)(2,1)} %get-tuple-element.158), channel_id=1, source_target_pairs={{0,16},{8,24},{16,0},{24,8},{1,17},{9,25},{17,1},{25,9},{2,18},{10... | collective-permute-start | bytes 4718600 | tf_op jit(solution)/shard_map/ppermute | solution.py:56
  470.2 18.0 %collective-permute-start.43 = (bf16[4,4,48,1536]{3,2,1,0:T(8,128)(2,1)}, bf16[4,4,48,1536]{3,2,1,0:T(8,128)(2,1)}, u32[]{:S(2)}, u32[]{:S(2)}) collective-permute-start(bf16[4,4,48,1536]{3,2,1,0:T(8,128)(2,1)} %dynamic-slice_bitcast_fusion.1), channel_id=1, source_target_pairs={{0,4},{4,0},{1,5},{5,1},{2,6},{6,2},{3,7},{7,3},{8,12},{12,8},{9,1... | collective-permute-start | bytes 7077896 | tf_op jit(solution)/shard_map/ppermute | solution.py:60
  473.7 24.3 %collective-permute-start.47 = (bf16[256,1536]{1,0:T(8,128)(2,1)}, bf16[256,1536]{1,0:T(8,128)(2,1)}, u32[]{:S(2)}, u32[]{:S(2)}) collective-permute-start(bf16[256,1536]{1,0:T(8,128)(2,1)} %fusion.31), channel_id=1, source_target_pairs={{0,8},{8,0},{16,24},{24,16},{1,9},{9,1},{17,25},{25,17},{2,10},{10... | collective-permute-start | bytes 2359304 | tf_op jit(solution)/shard_map/ppermute | solution.py:56
  485.3 20.5 %collective-permute-start.46 = (bf16[256,1536]{1,0:T(8,128)(2,1)}, bf16[256,1536]{1,0:T(8,128)(2,1)}, u32[]{:S(2)}, u32[]{:S(2)}) collective-permute-start(bf16[256,1536]{1,0:T(8,128)(2,1)} %fusion.30), channel_id=1, source_target_pairs={{0,16},{8,24},{16,0},{24,8},{1,17},{9,25},{17,1},{25,9},{2,18},{10... | collective-permute-start | bytes 2359304 | tf_op jit(solution)/shard_map/ppermute | solution.py:56
  495.8 40.3 %collective-permute-start.50 = (bf16[2,2,48,2048]{3,2,1,0:T(8,128)(2,1)}, bf16[2,2,48,2048]{3,2,1,0:T(8,128)(2,1)}, u32[]{:S(2)}, u32[]{:S(2)}) collective-permute-start(bf16[2,2,48,2048]{3,2,1,0:T(8,128)(2,1)} %get-tuple-element.163), channel_id=1, source_target_pairs={{0,8},{8,0},{16,24},{24,16},{1,9},{9,1},{17,25},{25,17},{2,10},{10... | collective-permute-start | bytes 2359304 | tf_op jit(solution)/shard_map/ppermute | solution.py:56
  497.3 38.8 %collective-permute-start.51 = (bf16[2,2,48,2048]{3,2,1,0:T(8,128)(2,1)}, bf16[2,2,48,2048]{3,2,1,0:T(8,128)(2,1)}, u32[]{:S(2)}, u32[]{:S(2)}) collective-permute-start(bf16[2,2,48,2048]{3,2,1,0:T(8,128)(2,1)} %get-tuple-element.164), channel_id=1, source_target_pairs={{0,16},{8,24},{16,0},{24,8},{1,17},{9,25},{17,1},{25,9},{2,18},{10... | collective-permute-start | bytes 2359304 | tf_op jit(solution)/shard_map/ppermute | solution.py:56
  508.2 26.4 %collective-permute-start.67 = (bf16[3,192,768]{2,1,0:T(8,128)(2,1)}, bf16[3,192,768]{2,1,0:T(8,128)(2,1)}, u32[]{:S(2)}, u32[]{:S(2)}) collective-permute-start(bf16[3,192,768]{2,1,0:T(8,128)(2,1)} %select_bitcast_fusion.1), channel_id=1, source_target_pairs={{0,4},{4,0},{1,5},{5,1},{2,6},{6,2},{3,7},{7,3},{8,12},{12,8},{9,1... | collective-permute-start | bytes 2654216 | tf_op jit(solution)/shard_map/ppermute | solution.py:60
  520.2 15.8 %collective-permute-start.49 = (bf16[4,4,48,128]{3,2,1,0:T(8,128)(2,1)S(1)}, bf16[4,4,48,128]{3,2,1,0:T(8,128)(2,1)S(1)}, u32[]{:S(2)}, u32[]{:S(2)}) collective-permute-start(bf16[4,4,48,128]{3,2,1,0:T(8,128)(2,1)S(1)} %dynamic-slice_bitcast_fusion.9), channel_id=1, source_target_pairs={{0,4},{4,0},{1,5},{5,1},{2,6},{6,2},{3,7},{7,3},{8,12},{12,8},{9,1... | collective-permute-start | bytes 589832 | tf_op jit(solution)/shard_map/ppermute | solution.py:60
  526.1 10.1 %collective-permute-start.48 = (bf16[4,4,48,1536]{3,2,1,0:T(8,128)(2,1)S(1)}, bf16[4,4,48,1536]{3,2,1,0:T(8,128)(2,1)S(1)}, u32[]{:S(2)}, u32[]{:S(2)}) collective-permute-start(bf16[4,4,48,1536]{3,2,1,0:T(8,128)(2,1)S(1)} %dynamic-slice_bitcast_fusion), channel_id=1, source_target_pairs={{0,4},{4,0},{1,5},{5,1},{2,6},{6,2},{3,7},{7,3},{8,12},{12,8},{9,1... | collective-permute-start | bytes 7077896 | tf_op jit(solution)/shard_map/ppermute | solution.py:60
  539.4 13.0 %collective-permute-start.52 = (bf16[2,48,2048]{2,1,0:T(8,128)(2,1)}, bf16[2,48,2048]{2,1,0:T(8,128)(2,1)}, u32[]{:S(2)}, u32[]{:S(2)}) collective-permute-start(bf16[2,48,2048]{2,1,0:T(8,128)(2,1)} %fusion.36), channel_id=1, source_target_pairs={{0,16},{8,24},{16,0},{24,8},{1,17},{9,25},{17,1},{25,9},{2,18},{10... | collective-permute-start | bytes 1179656 | tf_op jit(solution)/shard_map/ppermute | solution.py:56
  542.6 11.3 %collective-permute-start.53 = (bf16[2,48,2048]{2,1,0:T(8,128)(2,1)}, bf16[2,48,2048]{2,1,0:T(8,128)(2,1)S(1)}, u32[]{:S(2)}, u32[]{:S(2)}) collective-permute-start(bf16[2,48,2048]{2,1,0:T(8,128)(2,1)} %fusion.37), channel_id=1, source_target_pairs={{0,8},{8,0},{16,24},{24,16},{1,9},{9,1},{17,25},{25,17},{2,10},{10... | collective-permute-start | bytes 1179656 | tf_op jit(solution)/shard_map/ppermute | solution.py:56
  550.9 16.7 %collective-permute-start.54 = (bf16[2,2,48,1664]{3,2,1,0:T(8,128)(2,1)}, bf16[2,2,48,1664]{3,2,1,0:T(8,128)(2,1)}, u32[]{:S(2)}, u32[]{:S(2)}) collective-permute-start(bf16[2,2,48,1664]{3,2,1,0:T(8,128)(2,1)} %get-tuple-element.183), channel_id=1, source_target_pairs={{0,8},{8,0},{16,24},{24,16},{1,9},{9,1},{17,25},{25,17},{2,10},{10... | collective-permute-start | bytes 1916936 | tf_op jit(solution)/shard_map/ppermute | solution.py:56
  551.7 17.8 %collective-permute-start.56 = (bf16[2,2,48,1664]{3,2,1,0:T(8,128)(2,1)}, bf16[2,2,48,1664]{3,2,1,0:T(8,128)(2,1)}, u32[]{:S(2)}, u32[]{:S(2)}) collective-permute-start(bf16[2,2,48,1664]{3,2,1,0:T(8,128)(2,1)} %get-tuple-element.184), channel_id=1, source_target_pairs={{0,16},{8,24},{16,0},{24,8},{1,17},{9,25},{17,1},{25,9},{2,18},{10... | collective-permute-start | bytes 1916936 | tf_op jit(solution)/shard_map/ppermute | solution.py:56
  558.5 21.7 %collective-permute-start.68 = (bf16[3,192,768]{2,1,0:T(8,128)(2,1)}, bf16[3,192,768]{2,1,0:T(8,128)(2,1)S(1)}, u32[]{:S(2)}, u32[]{:S(2)}) collective-permute-start(bf16[3,192,768]{2,1,0:T(8,128)(2,1)} %select_bitcast_fusion), channel_id=1, source_target_pairs={{0,4},{4,0},{1,5},{5,1},{2,6},{6,2},{3,7},{7,3},{8,12},{12,8},{9,1... | collective-permute-start | bytes 2654216 | tf_op jit(solution)/shard_map/ppermute | solution.py:60
  568.7 8.7 %collective-permute-start.55 = (bf16[2,48,1664]{2,1,0:T(8,128)(2,1)S(1)}, bf16[2,48,1664]{2,1,0:T(8,128)(2,1)S(1)}, u32[]{:S(2)}, u32[]{:S(2)}) collective-permute-start(bf16[2,48,1664]{2,1,0:T(8,128)(2,1)S(1)} %fusion.40), channel_id=1, source_target_pairs={{0,16},{8,24},{16,0},{24,8},{1,17},{9,25},{17,1},{25,9},{2,18},{10... | collective-permute-start | bytes 958472 | tf_op jit(solution)/shard_map/ppermute | solution.py:56
  583.8 13.5 %collective-permute-start.58 = (bf16[48,1664]{1,0:T(8,128)(2,1)S(1)}, bf16[48,1664]{1,0:T(8,128)(2,1)S(1)}, u32[]{:S(2)}, u32[]{:S(2)}) collective-permute-start(bf16[48,1664]{1,0:T(8,128)(2,1)S(1)} %get-tuple-element.285), channel_id=1, source_target_pairs={{0,1},{1,2},{2,3},{3,0},{4,5},{5,6},{6,7},{7,4},{8,9},{9,10},{10,1... | collective-permute-start | bytes 479240 | tf_op jit(solution)/shard_map/ppermute | solution.py:772
  585.3 14.2 %collective-permute-start.59 = (bf16[48,1664]{1,0:T(8,128)(2,1)S(1)}, bf16[48,1664]{1,0:T(8,128)(2,1)S(1)}, u32[]{:S(2)}, u32[]{:S(2)}) collective-permute-start(bf16[48,1664]{1,0:T(8,128)(2,1)S(1)} %get-tuple-element.287), channel_id=1, source_target_pairs={{0,2},{1,3},{2,0},{3,1},{4,6},{5,7},{6,4},{7,5},{8,10},{9,11},{10,... | collective-permute-start | bytes 479240 | tf_op jit(solution)/shard_map/ppermute | solution.py:772
  587.3 12.3 %collective-permute-start.60 = (bf16[48,1664]{1,0:T(8,128)(2,1)S(1)}, bf16[48,1664]{1,0:T(8,128)(2,1)S(1)}, u32[]{:S(2)}, u32[]{:S(2)}) collective-permute-start(bf16[48,1664]{1,0:T(8,128)(2,1)S(1)} %get-tuple-element.286), channel_id=1, source_target_pairs={{0,3},{1,0},{2,1},{3,2},{4,7},{5,4},{6,5},{7,6},{8,11},{9,8},{10,9... | collective-permute-start | bytes 479240 | tf_op jit(solution)/shard_map/ppermute | solution.py:772
  597.3 10.8 %collective-permute-start.66 = (bf16[48,2048]{1,0:T(8,128)(2,1)S(1)}, bf16[48,2048]{1,0:T(8,128)(2,1)S(1)}, u32[]{:S(2)}, u32[]{:S(2)}) collective-permute-start(bf16[48,2048]{1,0:T(8,128)(2,1)S(1)} %bitcast.273), channel_id=1, source_target_pairs={{0,24},{8,16},{16,8},{24,0},{1,25},{9,17},{17,9},{25,1},{2,26},{10... | collective-permute-start | bytes 589832 | tf_op jit(solution)/shard_map/ppermute | solution.py:56
  599.7 10.6 %collective-permute-start.61 = (bf16[48,1664]{1,0:T(8,128)(2,1)S(1)}, bf16[48,1664]{1,0:T(8,128)(2,1)S(1)}, u32[]{:S(2)}, u32[]{:S(2)}) collective-permute-start(bf16[48,1664]{1,0:T(8,128)(2,1)S(1)} %fusion.44), channel_id=1, source_target_pairs={{0,8},{8,0},{16,24},{24,16},{1,9},{9,1},{17,25},{25,17},{2,10},{10... | collective-permute-start | bytes 479240 | tf_op jit(solution)/shard_map/ppermute | solution.py:56
  600.0 10.3 %collective-permute-start.62 = (bf16[48,1664]{1,0:T(8,128)(2,1)S(1)}, bf16[48,1664]{1,0:T(8,128)(2,1)S(1)}, u32[]{:S(2)}, u32[]{:S(2)}) collective-permute-start(bf16[48,1664]{1,0:T(8,128)(2,1)S(1)} %fusion.44), channel_id=1, source_target_pairs={{0,16},{8,24},{16,0},{24,8},{1,17},{9,25},{17,1},{25,9},{2,18},{10... | collective-permute-start | bytes 479240 | tf_op jit(solution)/shard_map/ppermute | solution.py:56
  (73 other events, 1236.3 us)
Sparse Core Ops, SparseCore 0:
  10.2 29.1 all-gather.7
  41.6 127.6 all-gather.9
  171.5 127.8 all-gather.11
  301.5 121.7 reduce-scatter.3
  425.4 123.9 reduce-scatter.5
  558.7 23.0 reduce-scatter.7
